TPU v7x, 512 devices: a whole 4x8x8 slice. The times are simulated.
512 devices in a mesh: tm: 32 (over z_lo, x, core), chan: 16 (over z_hi, y).
Axes of the slice: x: 4, y: 8, z: 8 (z_hi: 2, z_lo: 4; z = z_hi * 4 + z_lo), core: 2. Of those that a mesh axis runs over, the one named last changes fastest.
Arguments:
- arrived: bfloat16 [2048, 512, 128], P('tm', 'chan')
- row_target: int32 [2048], P('tm'), may hold values from 0 to 2047, as said below
- clip_lengths: int32 [4], replicated, may hold values from 1 to 32, 64 in all
- conv_weight: bfloat16 [3, 3, 3, 512, 512], P(None, None, None, 'chan'), may hold values from -0.0546875 to 0.0546875
- gn_gain: float32 [512], replicated, may hold values from 0.1 to 1.9
- gn_bias: float32 [512], replicated, may hold values from -3 to 3
Outputs:
- features: bfloat16 [16, 64, 64, 512], P('chan', 'tm')
Inputs may be any that keep to these rules, and one draw needn't show every extreme that they name: `row_target`: a permutation of the 2048 packed frame rows; the 64 rows arrived on one device of tm go to 17 owners of time slabs of 64 consecutive packed rows, at most 4 to one owner, and exactly 4 to some.
All inputs are finite; a program needn't handle non-finite values.
Results may differ from a plain program's by a relative error of at most 0.001.
Values may be sent and summed in bfloat16 or wider, within the bound.
No kernel may reach another device: no remote copies, remote signals or barrier semaphores. Data moves between devices by JAX's collectives and lax.ppermute only.
A program may use at most 64 MiB of HBM per device.

v0:
```python
import jax
import jax.numpy as jnp
from jax import lax
from jax.sharding import PartitionSpec as P

COUT = 512
GROUPS = 32
WIN_H = 32


EPSILON = 1e-05


def passed_along(shard, axis, by):
    devices = lax.axis_size(axis)
    pairs = [(i, i + by) for i in range(devices) if 0 <= i + by < devices]
    return lax.ppermute(shard, axis, pairs)


def spatial_taps(frames):
    frame_total, row_total, chan_total, col_total = frames.shape
    paired_rows = frames.reshape(frame_total, row_total // 2, 2, chan_total, col_total)
    even_rows = paired_rows[:, :, 0]
    odd_rows = paired_rows[:, :, 1]
    upper_rows = jnp.concatenate([jnp.zeros_like(odd_rows[:, :1]), odd_rows[:, :-1]], axis=1)
    tapped = []
    for picked in (upper_rows, even_rows, odd_rows):
        paired_cols = picked.reshape(frame_total, row_total // 2, chan_total, col_total // 2, 2)
        even_cols = paired_cols[..., 0]
        odd_cols = paired_cols[..., 1]
        left_cols = jnp.concatenate([jnp.zeros_like(odd_cols[..., :1]), odd_cols[..., :-1]], axis=3)
        tapped.extend([left_cols, even_cols, odd_cols])
    return tapped


def clip_masks(first_frame, frame_total, clip_lengths, value_type):
    clip_ends = jnp.cumsum(clip_lengths)
    starts = clip_ends - clip_lengths
    frame_ids = first_frame + jnp.arange(frame_total, dtype=jnp.int32)
    member = (frame_ids[:, None] >= starts[None, :]) & (frame_ids[:, None] < clip_ends[None, :])
    clip_first = jnp.sum(jnp.where(member, starts[None, :], 0), axis=1)
    allowed = jnp.stack([frame_ids - (2 - offset) >= clip_first for offset in range(3)])
    return (member.astype(jnp.float32), allowed.astype(value_type))


def build_patches(frames, allowed, frame_total):
    spatial = spatial_taps(frames)
    pieces = []
    for offset in range(3):
        frame_mask = allowed[offset][:, None, None, None]
        for tapped in spatial:
            pieces.append(tapped[offset : offset + frame_total] * frame_mask)
    return jnp.stack(pieces)


def slot_places(owners, wanted, slabs, capacity):
    slab_ids = jnp.arange(slabs, dtype=jnp.int32)
    onehot = ((owners[:, None] == slab_ids[None, :]) & wanted[:, None]).astype(jnp.int32)
    ranks = jnp.sum((jnp.cumsum(onehot, axis=0) - onehot) * onehot, axis=1)
    return jnp.where(wanted, owners * capacity + ranks, slabs * capacity)


def pack_rows(rows_in, places, slot_total):
    empty = jnp.zeros((slot_total,) + rows_in.shape[1:], rows_in.dtype)
    return empty.at[places].set(rows_in, mode="drop")


def place_rows(got_rows, got_places, total_rows):
    flat_rows = got_rows.reshape((-1,) + got_rows.shape[2:])
    empty = jnp.zeros((total_rows,) + got_rows.shape[2:], got_rows.dtype)
    return empty.at[got_places.reshape(-1)].set(flat_rows, mode="drop")


def clip_statistics(sums, squares, entries):
    clip_mean = sums / entries
    clip_var = squares / entries - clip_mean * clip_mean
    return (clip_mean, lax.rsqrt(clip_var + EPSILON))


def body(arrived, row_target, clip_lengths, conv_weight, gn_gain, gn_bias):
    slabs = lax.axis_size("tm")
    slab_index = lax.axis_index("tm")
    rows_dev = arrived.shape[0]
    chan_dev = arrived.shape[1]
    col_total = arrived.shape[2]
    frames_dev = rows_dev // WIN_H
    capacity = 2 * rows_dev // slabs
    owners = row_target // rows_dev
    local_rows = row_target % rows_dev
    everyone = jnp.ones(owners.shape, dtype=bool)
    places = slot_places(owners, everyone, slabs, capacity)
    send_rows = pack_rows(arrived, places, slabs * capacity).reshape(
        slabs, capacity, chan_dev, col_total
    )
    send_places = (
        jnp.full((slabs * capacity,), rows_dev, jnp.int32)
        .at[places]
        .set(local_rows, mode="drop")
        .reshape(slabs, capacity)
    )
    got_rows, got_places = (
        lax.all_to_all(send_rows, "tm", split_axis=0, concat_axis=0, tiled=True),
        lax.all_to_all(send_places, "tm", split_axis=0, concat_axis=0, tiled=True),
    )
    slab_rows = place_rows(got_rows, got_places, rows_dev)
    before = passed_along(slab_rows, "tm", 1)
    frames = jnp.concatenate([before, slab_rows], axis=0).reshape(
        frames_dev + 2, WIN_H, chan_dev, col_total
    )
    member, allowed = clip_masks(slab_index * frames_dev, frames_dev, clip_lengths, arrived.dtype)
    patches = build_patches(frames, allowed, frames_dev)
    kernel = conv_weight.reshape(27, chan_dev, COUT)
    out_rows = WIN_H // 2
    out_cols = col_total // 2
    group_size = COUT // GROUPS
    entries = clip_lengths.astype(jnp.float32) * float(out_rows * out_cols * group_size)
    conv = lax.psum_scatter(
        jnp.einsum("ktncw,kcd->ntwd", patches, kernel, preferred_element_type=jnp.float32),
        "chan",
        scatter_dimension=0,
        tiled=True,
    )
    grouped = conv.reshape(conv.shape[0], frames_dev, out_cols, GROUPS, group_size)
    frame_sums = jnp.sum(grouped, axis=(0, 2, 4))
    frame_squares = jnp.sum(grouped * grouped, axis=(0, 2, 4))
    part_sums = jnp.dot(member.T, frame_sums, precision=lax.Precision.HIGHEST)
    part_squares = jnp.dot(member.T, frame_squares, precision=lax.Precision.HIGHEST)
    clip_sums, clip_squares = lax.psum((part_sums, part_squares), ("tm", "chan"))
    clip_mean, clip_scale = clip_statistics(clip_sums, clip_squares, entries[:, None])
    frame_mean = jnp.dot(member, clip_mean, precision=lax.Precision.HIGHEST)
    frame_scale = jnp.dot(member, clip_scale, precision=lax.Precision.HIGHEST)
    centred = (grouped - frame_mean[None, :, None, :, None]) * frame_scale[None, :, None, :, None]
    shaped = centred.reshape(conv.shape) * gn_gain + gn_bias
    return jax.nn.silu(shaped).astype(jnp.bfloat16)


def solution(mesh):
    in_specs = (P("tm", "chan", None), P("tm"), P(), P(None, None, None, "chan", None), P(), P())
    out_specs = P("chan", "tm", None, None)
    return jax.shard_map(body, mesh=mesh, in_specs=in_specs, out_specs=out_specs, check_vma=False)
```

profile of v0, /device:TPU:1, one launch (start us, length us, event | category | flops | bytes accessed | tf_op | source)
XLA Modules:
  0.0 501.2 jit_solution(846538479693409804)
XLA Ops:
  6.5 0.7 and_select_fusion
  7.6 0.8 scatter_custom_fusion
  8.4 0.7 all_to_all.9
  9.1 11.4 %all-to-all-start = ((s32[32,1,4]{2,1,0:T(1,128)}), s32[32,1,4]{2,1,0:T(1,128)S(1)}, u32[]{:S(2)}, u32[]{:S(2)}) async-start(s32[32,1,4]{2,1,0:T(1,128)} %bitcast), calls=%async_computation | async-start | bytes 32768 | tf_op jit(solution)/shard_map/all_to_all | solution.py:103
  20.5 1.1 broadcast_in_dim.19
  21.7 7.9 %scatter_fusion = bf16[128,32,128]{2,1,0:T(8,128)(2,1)} fusion(bf16[128,32,128]{2,1,0:T(8,128)(2,1)} %broadcast_in_dim.19, s32[64]{0:T(128)S(1)} %compare_select_fusion.1, bf16[64,32,128]{2,1,0:T(8,128)(2,1)} %param.6), kind=kCustom, calls=%fused_computation.1 | custom fusion | bytes 1573120 | tf_op jit(solution)/shard_map/scatter | solution.py:65
  29.6 7.7 %all-to-all-start.1 = ((bf16[32,4,32,128]{3,2,1,0:T(8,128)(2,1)}), bf16[32,4,32,128]{3,2,1,0:T(8,128)(2,1)S(1)}, u32[]{:S(2)}, u32[]{:S(2)}) async-start(bf16[32,4,32,128]{3,2,1,0:T(8,128)(2,1)} %bitcast.2), calls=%async_computation.1 | async-start | bytes 2097152 | tf_op jit(solution)/shard_map/all_to_all | solution.py:102
  37.4 0.8 reduce-window.8
  38.2 0.7 bitcast_subtract_fusion
  39.1 0.5 broadcast.279
  39.6 0.7 reduce.8
  40.4 23.5 %all-to-all-done.1 = bf16[32,4,32,128]{3,2,1,0:T(8,128)(2,1)S(1)} async-done(((bf16[32,4,32,128]{3,2,1,0:T(8,128)(2,1)}), bf16[32,4,32,128]{3,2,1,0:T(8,128)(2,1)S(1)}, u32[]{:S(2)}, u32[]{:S(2)}) %all-to-all-start.1) | async-done | bytes 1048608 | tf_op jit(solution)/shard_map/all_to_all | solution.py:102
  64.0 4.7 scatter_fusion.1
  68.7 2.9 collective-permute-start
  71.6 6.1 %collective-permute-done = bf16[64,32,128]{2,1,0:T(8,128)(2,1)S(1)} collective-permute-done((bf16[64,32,128]{2,1,0:T(8,128)(2,1)S(1)}, bf16[64,32,128]{2,1,0:T(8,128)(2,1)S(1)}, u32[]{:S(2)}, u32[]{:S(2)}) %collective-permute-start) | collective-permute-done | bytes 524320 | tf_op jit(solution)/shard_map/ppermute | solution.py:17
  77.8 1.4 fusion.60
  79.2 2.5 copy.144
  81.7 1.2 slice.260
  82.9 1.7 fusion.57
  84.6 0.9 slice.250
  85.5 2.5 copy.194
  88.1 0.8 concatenate.16.clone
  88.9 1.2 slice.251
  90.1 1.7 fusion.59
  91.8 1.8 copy.140
  93.7 1.2 slice.256
  94.8 1.8 fusion.58
  96.6 2.1 copy.179
  98.7 2.2 copy.193
  100.9 2.1 copy.192
  103.1 2.1 copy.187
  105.2 2.2 copy.186
  107.4 2.2 copy.181
  109.5 2.1 copy.180
  111.7 2.0 copy.173
  113.7 2.2 copy.189
  115.8 2.1 copy.188
  118.0 2.2 copy.183
  120.2 2.1 copy.182
  122.3 2.1 copy.175
  124.4 1.2 copy.174
  125.6 0.9 copy.176
  126.5 2.2 copy.191
  128.6 2.2 copy.190
  130.9 2.1 copy.185
  133.0 2.2 copy.184
  135.2 2.2 copy.178
  137.4 2.1 copy.177
  139.7 1.2 fusion.44
  140.9 1.1 fusion.43
  142.2 1.1 fusion.42
  143.3 1.1 fusion.41
  144.6 1.1 fusion.40
  145.7 1.1 fusion.39
  147.0 1.1 fusion.38
  148.1 1.1 fusion.37
  150.2 0.4 fusion.8
  151.9 4.4 convolution_bitcast_fusion
  156.3 1.2 dynamic-slice
  157.6 225.6 %all-reduce.8.cloned.1.call-done = f32[16,2,64,512]{3,2,0,1:T(8,128)} async-done(((f32[16,2,64,512]{3,2,0,1:T(8,128)}), f32[16,2,64,512]{3,2,0,1:T(8,128)}) %all-reduce.8.cloned.1.call-update) | async-done | bytes 4194320
  383.2 1.6 dynamic-slice_reduce_fusion
  385.3 0.2 fusion.62
  385.5 105.9 %all-reduce.5 = (f32[4,32]{1,0:T(4,128)S(1)}, f32[4,32]{1,0:T(4,128)S(1)}) all-reduce(f32[4,32]{1,0:T(4,128)S(1)} %fusion.62, f32[4,32]{1,0:T(4,128)S(1)} %fusion.61), channel_id=1, replica_groups=mesh['tm'=32,'chan'=16] {'tm','chan'}, use_global_device_ids=true, to_apply=%region_13.14 | all-reduce | flops 256 | bytes 2048 | tf_op jit(solution)/shard_map/psum | solution.py:128
  492.1 2.3 fusion.45
  (80 shorter events, 5.1 us)
Async XLA Ops:
  6.5 145.3 %copy-start = (bf16[3,3,3,32,512]{4,3,2,1,0:T(8,128)(2,1)S(1)}, bf16[3,3,3,32,512]{4,3,2,1,0:T(8,128)(2,1)}, u32[]{:S(2)}) copy-start(bf16[3,3,3,32,512]{4,3,2,1,0:T(8,128)(2,1)} %param.9) | copy-start | bytes 2654212
  9.1 20.5 %all-to-all-start = ((s32[32,1,4]{2,1,0:T(1,128)}), s32[32,1,4]{2,1,0:T(1,128)S(1)}, u32[]{:S(2)}, u32[]{:S(2)}) async-start(s32[32,1,4]{2,1,0:T(1,128)} %bitcast), calls=%async_computation | async-start | bytes 32768 | tf_op jit(solution)/shard_map/all_to_all | solution.py:103
  29.6 34.3 %all-to-all-start.1 = ((bf16[32,4,32,128]{3,2,1,0:T(8,128)(2,1)}), bf16[32,4,32,128]{3,2,1,0:T(8,128)(2,1)S(1)}, u32[]{:S(2)}, u32[]{:S(2)}) async-start(bf16[32,4,32,128]{3,2,1,0:T(8,128)(2,1)} %bitcast.2), calls=%async_computation.1 | async-start | bytes 2097152 | tf_op jit(solution)/shard_map/all_to_all | solution.py:102
  37.3 345.8 %all-reduce.8.cloned.1.call-start = ((), (), s32[]{:S(2)}) async-start(), calls=%async_computation.2 | async-start | bytes 8388608
  68.7 9.0 %collective-permute-start = (bf16[64,32,128]{2,1,0:T(8,128)(2,1)S(1)}, bf16[64,32,128]{2,1,0:T(8,128)(2,1)S(1)}, u32[]{:S(2)}, u32[]{:S(2)}) collective-permute-start(bf16[64,32,128]{2,1,0:T(8,128)(2,1)S(1)} %scatter_fusion.1), channel_id=1, source_target_pairs={{0,16},{16,32},{32,48},{48,64},{64,80},{80,96},{96,112},{112,128},... | collective-permute-start | bytes 1572872 | tf_op jit(solution)/shard_map/ppermute | solution.py:17
  81.7 2.9 copy-start.3
  96.6 27.8 %copy-start.2 = (bf16[2,16,32,64,1]{2,1,4,3,0:T(8,128)(2,1)S(1)}, bf16[2,16,32,64,1]{2,1,4,3,0:T(8,128)(2,1)}, u32[]{:S(2)}) copy-start(bf16[2,16,32,64,1]{2,1,4,3,0:T(8,128)(2,1)} %get-tuple-element.28) | copy-start | bytes 393220
  96.6 29.0 %copy-start.1 = (bf16[4,16,32,64,1]{2,1,4,3,0:T(8,128)(2,1)S(1)}, bf16[4,16,32,64,1]{2,1,4,3,0:T(8,128)(2,1)}, u32[]{:S(2)}) copy-start(bf16[4,16,32,64,1]{2,1,4,3,0:T(8,128)(2,1)} %slice.256) | copy-start | bytes 786436
  128.6 21.2 %copy-start.8 = (bf16[2,16,32,64,1]{3,2,1,0,4:T(8,128)(2,1)S(1)}, bf16[2,16,32,64,1]{3,2,1,0,4:T(8,128)(2,1)}, u32[]{:S(2)}) copy-start(bf16[2,16,32,64,1]{3,2,1,0,4:T(8,128)(2,1)} %copy.186) | copy-start | bytes 393220
  128.6 21.4 %copy-start.6 = (bf16[2,16,32,64,1]{3,2,1,0,4:T(8,128)(2,1)S(1)}, bf16[2,16,32,64,1]{3,2,1,0,4:T(8,128)(2,1)}, u32[]{:S(2)}) copy-start(bf16[2,16,32,64,1]{3,2,1,0,4:T(8,128)(2,1)} %copy.187) | copy-start | bytes 393220
  133.0 17.6 %copy-start.9 = (bf16[2,16,32,64,1]{3,2,1,0,4:T(8,128)(2,1)S(1)}, bf16[2,16,32,64,1]{3,2,1,0,4:T(8,128)(2,1)}, u32[]{:S(2)}) copy-start(bf16[2,16,32,64,1]{3,2,1,0,4:T(8,128)(2,1)} %copy.188) | copy-start | bytes 393220
  135.2 15.5 %copy-start.7 = (bf16[2,16,32,64,1]{3,2,1,0,4:T(8,128)(2,1)S(1)}, bf16[2,16,32,64,1]{3,2,1,0,4:T(8,128)(2,1)}, u32[]{:S(2)}) copy-start(bf16[2,16,32,64,1]{3,2,1,0,4:T(8,128)(2,1)} %copy.189) | copy-start | bytes 393220
  139.5 9.8 %copy-start.13 = (bf16[2,16,32,64,1]{3,2,1,0,4:T(8,128)(2,1)S(1)}, bf16[2,16,32,64,1]{3,2,1,0,4:T(8,128)(2,1)}, u32[]{:S(2)}) copy-start(bf16[2,16,32,64,1]{3,2,1,0,4:T(8,128)(2,1)} %copy.184) | copy-start | bytes 393220
  139.5 10.0 %copy-start.12 = (bf16[2,16,32,64,1]{3,2,1,0,4:T(8,128)(2,1)S(1)}, bf16[2,16,32,64,1]{3,2,1,0,4:T(8,128)(2,1)}, u32[]{:S(2)}) copy-start(bf16[2,16,32,64,1]{3,2,1,0,4:T(8,128)(2,1)} %copy.185) | copy-start | bytes 393220
  139.5 11.5 %copy-start.11 = (bf16[2,16,32,64,1]{3,2,1,0,4:T(8,128)(2,1)S(1)}, bf16[2,16,32,64,1]{3,2,1,0,4:T(8,128)(2,1)}, u32[]{:S(2)}) copy-start(bf16[2,16,32,64,1]{3,2,1,0,4:T(8,128)(2,1)} %copy.190) | copy-start | bytes 393220
  139.6 11.7 %copy-start.10 = (bf16[2,16,32,64,1]{3,2,1,0,4:T(8,128)(2,1)S(1)}, bf16[2,16,32,64,1]{3,2,1,0,4:T(8,128)(2,1)}, u32[]{:S(2)}) copy-start(bf16[2,16,32,64,1]{3,2,1,0,4:T(8,128)(2,1)} %copy.191) | copy-start | bytes 393220
  140.9 10.7 %copy-start.5 = (bf16[2,16,32,64,1]{3,2,1,0,4:T(8,128)(2,1)S(1)}, bf16[2,16,32,64,1]{3,2,1,0,4:T(8,128)(2,1)}, u32[]{:S(2)}) copy-start(bf16[2,16,32,64,1]{3,2,1,0,4:T(8,128)(2,1)} %copy.192) | copy-start | bytes 393220
  142.0 9.7 %copy-start.4 = (bf16[2,16,32,64,1]{3,2,1,0,4:T(8,128)(2,1)S(1)}, bf16[2,16,32,64,1]{3,2,1,0,4:T(8,128)(2,1)}, u32[]{:S(2)}) copy-start(bf16[2,16,32,64,1]{3,2,1,0,4:T(8,128)(2,1)} %copy.193) | copy-start | bytes 393220
  151.9 5.7 %copy-start.16 = (s32[4]{0:T(128)S(1)}, s32[4]{0:T(128)}, u32[]{:S(2)}) copy-start(s32[4]{0:T(128)} %param.8) | copy-start | bytes 52
  151.9 340.2 %copy-start.14 = (f32[512]{0:T(512)S(1)}, f32[512]{0:T(512)}, u32[]{:S(2)}) copy-start(f32[512]{0:T(512)} %param.11) | copy-start | bytes 6148
  151.9 340.2 %copy-start.15 = (f32[512]{0:T(512)S(1)}, f32[512]{0:T(512)}, u32[]{:S(2)}) copy-start(f32[512]{0:T(512)} %param.10) | copy-start | bytes 6148
Sparse Core Ops, SparseCore 0:
  156.5 226.6 all-reduce.7
where the time goes:
time: 503 us; the launch traced here: 501 us
  waiting for transfers between devices  255 us (51%)
  blocking collectives  106 us (21%)
  local copies, waits for them, and re-layouts  79.4 us (16%)
  starting transfers between devices  22 us (4%)
  other arithmetic  19.7 us (4%)
  between operations  13.8 us (3%)
  matrix products  5.17 us (1%)
    unnamed x2, waiting for transfers between devices  226 us
    psum x1, blocking collectives, body(): lax.psum((part_sums, part_squares), ('tm', 'chan'))  106 us
    unnamed x57, local copies, waits for them, and re-layouts  46.7 us
    all_to_all x1, waiting for transfers between devices, body(): lax.all_to_all(send_rows, 'tm', split_axis=0, concat_axis=0, tiled=True)  23.5 us
    unnamed x26, other arithmetic  12 us
    all_to_all x1, starting transfers between devices, body(): lax.all_to_all(send_places, 'tm', split_axis=0, concat_axis=0, tiled=True)  11.4 us
  transfers between devices with their start and end apart: 4, of which 3 were waited for; matrix products, arithmetic and copies ran while one was open for 3% of the time, Pallas kernels for 0%

commit v1 on v0

v1 whole, which is shorter than its diff:
```python
import jax
import jax.numpy as jnp
from jax import lax
from jax.experimental import pallas as pl
from jax.experimental.pallas import tpu as pltpu
from jax.sharding import Mesh, PartitionSpec as P

TM = ("zl", "x", "co")
CH = ("zh", "y")
SLABS = 32
ROWS = 64
CAP = 4
CH_DEV = 32
NY = 8
OUT_ROWS = 16
COUT = 512
GROUPS = 32
GROUP_SIZE = 16
EPSILON = 1e-05
BF = jnp.bfloat16
F32 = jnp.float32
HIGHEST = lax.Precision.HIGHEST

VMEM = pl.BlockSpec(memory_space=pltpu.VMEM)
SMEM = pl.BlockSpec(memory_space=pltpu.SMEM)


def params(mib):
    return pltpu.CompilerParams(vmem_limit_bytes=mib * 1024 * 1024)


def pack_kernel(target, arrived, send, counts, places):
    places[...] = jnp.full(places.shape, float(ROWS), F32)

    def clear(i, carry):
        counts[i] = 0
        return carry

    lax.fori_loop(0, SLABS, clear, 0)

    def one(i, carry):
        t = target[i]
        owner = lax.shift_right_logical(t, 6)
        rank = counts[owner]
        counts[owner] = rank + 1
        send[owner, pl.ds(pl.multiple_of(rank * CH_DEV, CH_DEV), CH_DEV), :] = arrived[i]
        place = lax.bitwise_and(t, ROWS - 1).astype(F32)
        places[owner, pl.ds(rank, 1), :] = jnp.full((1, 128), place, F32)
        return carry

    lax.fori_loop(0, ROWS, one, 0)
    send[:, CAP * CH_DEV:, :] = places[...].astype(BF)


def place_kernel(got, out, table, table_s, sem):
    zh = lax.axis_index("zh")
    lane = lax.broadcasted_iota(jnp.int32, (16, 128), 1)
    acc = jnp.zeros((16, 128), F32)
    for s in range(SLABS):
        acc = jnp.where(lane == s, got[s, CAP * CH_DEV:, :].astype(F32), acc)
    table[...] = acc.astype(jnp.int32)
    copy = pltpu.make_async_copy(table, table_s, sem)
    copy.start()
    copy.wait()
    for f in range(2):
        first = f * 6 + (1 - lax.bitwise_xor(0, zh)) * 3
        out[first] = jnp.zeros((CH_DEV, 128), BF)

    def spot(i, f, b):
        half = 1 - lax.bitwise_xor(lax.shift_right_logical(i, 3), zh)
        return lax.bitwise_and(i, NY - 1) * 12 + f * 6 + half * 3 + b

    def one(s, carry):
        for r in range(CAP):
            place = table_s[r, s]

            @pl.when(place < ROWS)
            def _():
                row = got[s, r * CH_DEV:(r + 1) * CH_DEV, :]
                f = lax.shift_right_logical(place, 5)
                h = lax.bitwise_and(place, 31)
                odd = lax.bitwise_and(h, 1)
                i = lax.shift_right_logical(h, 1)
                out[spot(i, f, 1 + odd)] = row

                @pl.when((odd == 1) & (i < OUT_ROWS - 1))
                def _():
                    out[spot(i + 1, f, 0)] = row
        return carry

    lax.fori_loop(0, SLABS, one, 0)


def clip_start_of(lengths, frame):
    first = jnp.int32(0)
    end = jnp.int32(0)
    for k in range(4):
        start = end
        end = end + lengths[k]
        first = jnp.where((frame >= start) & (frame < end), start, first)
    return first


def conv_kernel(lengths, own, before, *rest):
    weights, (out_far, out_near, taps, acc) = rest[:NY], rest[NY:]
    step = pl.program_id(0)
    y = lax.axis_index("y")
    core = lax.axis_index("co")
    slab = (lax.axis_index("zl") * 4 + lax.axis_index("x")) * 2 + core
    sign = 2 * core - 1
    sources = [y]
    for s in range(1, 4):
        sources += [y + sign * s, y - sign * s]
    sources.append(y + 4)
    sources = [lax.bitwise_and(s + NY, NY - 1) for s in sources]

    @pl.when(step == 0)
    def _():
        acc[...] = jnp.zeros(acc.shape, F32)
        j = lax.broadcasted_iota(jnp.int32, (192, 128), 0)
        w = lax.broadcasted_iota(jnp.int32, (192, 128), 1)
        wanted = jnp.where(j < 64, 2 * j - 1, jnp.where(j < 128, 2 * j - 128, 2 * j - 255))
        pick = (w == wanted).astype(F32).astype(BF)
        for f in range(4):
            block = before if f < 2 else own
            for sb in range(6):
                at = (f % 2) * 6 + sb
                x = jnp.concatenate([block[s, at] for s in sources], axis=0)
                t = lax.dot_general(pick, x, (((1,), (1,)), ((), ())),
                                    preferred_element_type=F32).astype(BF)
                for e in range(3):
                    taps[f, sb, :, e * 256:(e + 1) * 256] = t[e * 64:(e + 1) * 64]

    a = step // 3
    b = step % 3
    w = jnp.concatenate([ref[e] for e in range(3) for ref in weights], axis=0)
    blocks = []
    for f in range(2):
        frame = slab * 2 + f
        allowed = frame - 2 + a >= clip_start_of(lengths, frame)
        gate = jnp.full((64, 768), jnp.where(allowed, 1.0, 0.0), F32).astype(BF)
        for half in range(2):
            blocks.append(taps[f + a, half * 3 + b] * gate)
    lhs = jnp.concatenate([blocks[0], blocks[2], blocks[1], blocks[3]], axis=0)
    acc[...] += jnp.dot(lhs, w, preferred_element_type=F32)

    @pl.when(step == 8)
    def _():
        out_far[...] = acc[:128]
        out_near[...] = acc[128:]


def group_matrix(channels_first):
    shape = (COUT, 128) if channels_first else (128, COUT)
    c = lax.broadcasted_iota(jnp.int32, shape, 0 if channels_first else 1)
    g = lax.broadcasted_iota(jnp.int32, shape, 1 if channels_first else 0)
    return (lax.shift_right_logical(c, 4) == g).astype(F32)


def member_of(lengths, frame):
    end = jnp.int32(0)
    flags = []
    for k in range(4):
        start = end
        end = end + lengths[k]
        flags.append(jnp.where((frame >= start) & (frame < end), 1.0, 0.0).astype(F32))
    return flags


def stat_kernel(lengths, near, far, conv_out, stats):
    slab = (lax.axis_index("zl") * 4 + lax.axis_index("x")) * 2 + lax.axis_index("co")
    conv = near[...] + far[...]
    conv_out[...] = conv
    rows = []
    for f in range(2):
        part = conv[f * 64:(f + 1) * 64]
        rows.append(jnp.sum(part, axis=0, keepdims=True))
        rows.append(jnp.sum(part * part, axis=0, keepdims=True))
    rows = jnp.concatenate(rows + rows, axis=0)
    grouped = jnp.dot(rows, group_matrix(True), precision=HIGHEST, preferred_element_type=F32)
    m0 = member_of(lengths, slab * 2)
    m1 = member_of(lengths, slab * 2 + 1)
    sums = [grouped[0:1] * m0[k] + grouped[2:3] * m1[k] for k in range(4)]
    squares = [grouped[1:2] * m0[k] + grouped[3:4] * m1[k] for k in range(4)]
    tile = jnp.concatenate(sums + squares, axis=0)
    stats[...] = jnp.broadcast_to(tile[None], stats.shape)


def middle_kernel(got, out):
    out[...] = jnp.broadcast_to(jnp.sum(got[...], axis=0)[None], out.shape)


def final_kernel(lengths, got, conv, gain, bias, out):
    slab = (lax.axis_index("zl") * 4 + lax.axis_index("x")) * 2 + lax.axis_index("co")
    total = jnp.sum(got[...], axis=0)
    spread = group_matrix(False)
    for f in range(2):
        flags = member_of(lengths, slab * 2 + f)
        sums = jnp.zeros((1, 128), F32)
        squares = jnp.zeros((1, 128), F32)
        frames = jnp.float32(0)
        for k in range(4):
            sums = sums + total[k:k + 1] * flags[k]
            squares = squares + total[4 + k:5 + k] * flags[k]
            frames = frames + flags[k] * lengths[k].astype(F32)
        entries = jnp.full((1, 128), frames * float(OUT_ROWS * 64 * GROUP_SIZE), F32)
        mean = sums / entries
        var = squares / entries - mean * mean
        scale = lax.rsqrt(var + EPSILON)
        both = jnp.concatenate([mean, scale] * 4, axis=0)
        wide = jnp.dot(both, spread, precision=HIGHEST, preferred_element_type=F32)
        part = conv[f * 64:(f + 1) * 64]
        v = ((part - wide[0:1]) * wide[1:2]) * gain[...] + bias[...]
        out[f] = (v / (1.0 + jnp.exp(-v))).astype(BF)


def shuffle(x, axis):
    return lax.all_to_all(x, axis, split_axis=0, concat_axis=0, tiled=True)


def gathered_weights(kernel):
    ring = [(c * NY + y, c * NY + (y + (1 if c == 0 else NY - 1)) % NY)
            for c in range(2) for y in range(NY)]
    swap = [(0, 1), (1, 0)]
    shards = [kernel]
    moving = kernel
    for _ in range(3):
        moving = lax.ppermute(moving, ("co", "y"), ring)
        shards += [moving, lax.ppermute(moving, "co", swap)]
    shards.append(lax.ppermute(moving, ("co", "y"), ring))
    return shards


def body(arrived, row_target, clip_lengths, conv_weight, gn_gain, gn_bias):
    weights = gathered_weights(conv_weight.reshape(27, CH_DEV, COUT))
    send = pl.pallas_call(
        pack_kernel,
        out_shape=jax.ShapeDtypeStruct((SLABS, 144, 128), BF),
        in_specs=[SMEM, VMEM],
        out_specs=VMEM,
        scratch_shapes=[pltpu.SMEM((SLABS,), jnp.int32), pltpu.VMEM((SLABS, 16, 128), F32)],
        compiler_params=params(16),
    )(row_target, arrived)
    got = shuffle(send, TM)
    placed = pl.pallas_call(
        place_kernel,
        out_shape=jax.ShapeDtypeStruct((NY * 12, CH_DEV, 128), BF),
        in_specs=[VMEM],
        out_specs=VMEM,
        scratch_shapes=[
            pltpu.VMEM((16, 128), jnp.int32),
            pltpu.SMEM((16, 128), jnp.int32),
            pltpu.SemaphoreType.DMA,
        ],
        compiler_params=params(16),
    )(got)
    own = shuffle(placed.reshape(NY, 12, CH_DEV, 128), "y")
    before = lax.ppermute(own, TM, [(i, i + 1) for i in range(SLABS - 1)])
    whole = pl.BlockSpec((NY, 12, CH_DEV, 128), lambda t: (0, 0, 0, 0))
    tap = pl.BlockSpec((3, CH_DEV, COUT), lambda t: (t, 0, 0))
    part = pl.BlockSpec((128, COUT), lambda t: (0, 0))
    far, near = pl.pallas_call(
        conv_kernel,
        grid=(9,),
        out_shape=[jax.ShapeDtypeStruct((128, COUT), F32)] * 2,
        in_specs=[SMEM, whole, whole] + [tap] * NY,
        out_specs=[part, part],
        scratch_shapes=[pltpu.VMEM((4, 6, 64, 768), BF), pltpu.VMEM((256, COUT), F32)],
        compiler_params=params(32),
    )(clip_lengths, own, before, *weights)
    far = lax.ppermute(far, "zh", [(0, 1), (1, 0)])
    conv, stats = pl.pallas_call(
        stat_kernel,
        out_shape=[jax.ShapeDtypeStruct((128, COUT), F32), jax.ShapeDtypeStruct((16, 8, 128), F32)],
        in_specs=[SMEM, VMEM, VMEM],
        out_specs=[VMEM, VMEM],
        compiler_params=params(16),
    )(clip_lengths, near, far)
    stats = shuffle(stats, CH)
    stats = pl.pallas_call(
        middle_kernel,
        out_shape=jax.ShapeDtypeStruct((SLABS, 8, 128), F32),
        in_specs=[VMEM],
        out_specs=VMEM,
    )(stats)
    stats = shuffle(stats, TM)
    out = pl.pallas_call(
        final_kernel,
        out_shape=jax.ShapeDtypeStruct((2, 64, COUT), BF),
        in_specs=[SMEM, VMEM, VMEM, VMEM, VMEM],
        out_specs=VMEM,
        compiler_params=params(16),
    )(clip_lengths, stats, conv, gn_gain.reshape(1, COUT), gn_bias.reshape(1, COUT))
    return out.reshape(1, 2, 64, COUT)


def solution(mesh):
    fine = Mesh(mesh.devices.reshape(4, 4, 2, 2, 8), TM + CH)
    in_specs = (P(TM, CH, None), P(TM), P(), P(None, None, None, CH, None), P(), P())
    out_specs = P(CH, TM, None, None)
    return jax.shard_map(body, mesh=fine, in_specs=in_specs, out_specs=out_specs, check_vma=False)
```

time: 503 us -> 172 us (0.34)
  waiting for transfers between devices: 255 us -> 52.8 us
  local copies, waits for them, and re-layouts: 79.4 us -> 1.72 us
  blocking collectives: 106 us -> 44.1 us
  starting transfers between devices: 22 us -> 54.3 us
  other arithmetic: 19.7 us -> 0 us
  Pallas kernels: 0 us -> 18.4 us
  between operations: 13.8 us -> 0.18 us
  matrix products: 5.17 us -> 0 us
    unnamed x2 -> x0, waiting for transfers between devices: 226 us -> none
    psum x1 -> x0, blocking collectives: 106 us -> none  [body(): lax.psum((part_sums, part_squares), ('tm', 'chan'))]
    unnamed x57 -> x12, local copies, waits for them, and re-layouts: 46.7 us -> 1.72 us
    all_to_all x0 -> x2, blocking collectives: none -> 44.1 us  [shuffle(): return lax.all_to_all(x, axis, split_axis=0, concat_axis=0, tiled=True)]
    ppermute x1 -> x9, waiting for transfers between devices: 6.06 us -> 44.1 us  [the longest x3 30.2 us: gathered_weights(): moving = lax.ppermute(moving, ('co', 'y'), ring)]
    ppermute x1 -> x9, starting transfers between devices: 2.89 us -> 35.9 us  [the longest x3 15.1 us: gathered_weights(): moving = lax.ppermute(moving, ('co', 'y'), ring)]
    pallas_call x0 -> x6, Pallas kernels: none -> 18.4 us  [the longest x1 8.55 us: body(): pl.pallas_call(conv_kernel, grid=(9,), out_shape=[jax.ShapeDtypeStruct((1...]
    slice x10 -> x0, local copies, waits for them, and re-layouts: 15.4 us -> none  [the longest x3 5.29 us: build_patches(): pieces.append(tapped[offset:offset + frame_total] * frame_mask)]
  transfers between devices with their start and end apart: 4 -> 11, of which waited for: 3 -> 5; matrix products, arithmetic and copies ran while one was open for 3% -> 0% of each run, Pallas kernels for 0% -> 2%
where the time goes in v1:
time: 172 us; the launch traced here: 171 us
  starting transfers between devices  54.3 us (32%)
  waiting for transfers between devices  52.8 us (31%)
  blocking collectives  44.1 us (26%)
  Pallas kernels  18.4 us (11%)
  local copies, waits for them, and re-layouts  1.72 us (1%)
    all_to_all x2, blocking collectives, shuffle(): return lax.all_to_all(x, axis, split_axis=0, concat_axis=0, tiled=True)  44.1 us
    ppermute x3, waiting for transfers between devices, gathered_weights(): moving = lax.ppermute(moving, ('co', 'y'), ring)  30.2 us
    all_to_all x2, starting transfers between devices, shuffle(): return lax.all_to_all(x, axis, split_axis=0, concat_axis=0, tiled=True)  18.3 us
    ppermute x3, starting transfers between devices, gathered_weights(): moving = lax.ppermute(moving, ('co', 'y'), ring)  15.1 us
    ppermute x1, waiting for transfers between devices, gathered_weights(): shards.append(lax.ppermute(moving, ('co', 'y'), ring))  9.29 us
    all_to_all x2, waiting for transfers between devices, shuffle(): return lax.all_to_all(x, axis, split_axis=0, concat_axis=0, tiled=True)  8.76 us
    pallas_call x1, Pallas kernels, body(): pl.pallas_call(conv_kernel, grid=(9,), out_shape=[jax.ShapeDtypeStruct((1...  8.55 us
    ppermute x1, starting transfers between devices, body(): far = lax.ppermute(far, 'zh', [(0, 1), (1, 0)])  7.94 us
  transfers between devices with their start and end apart: 11, of which 5 were waited for; matrix products, arithmetic and copies ran while one was open for 0% of the time, Pallas kernels for 2%

profile of v1, /device:TPU:1, one launch (start us, length us, event | category | flops | bytes accessed | tf_op | source)
XLA Modules:
  0.0 171.5 jit_solution(14383055112245508032)
XLA Ops:
  0.0 0.0 copy-start.1
  0.0 1.0 copy-done.1
  1.0 0.0 copy-start.5
  1.0 0.7 copy-done.5
  1.7 2.5 %shard_map.64 = bf16[32,144,128]{2,1,0:T(8,128)(2,1)} custom-call(s32[64]{0:T(128)S(1)} %copy-done.5, bf16[64,32,128]{2,1,0:T(8,128)(2,1)S(1)} %copy-done.1), custom_call_target="tpu_custom_call" | custom-call | tf_op jit(solution)/shard_map/pallas_call | solution.py:236
  4.2 0.0 copy-start
  4.2 11.5 %all-to-all-start = ((bf16[32,144,128]{2,1,0:T(8,128)(2,1)}), bf16[32,144,128]{2,1,0:T(8,128)(2,1)S(1)}, u32[]{:S(2)}, u32[]{:S(2)}) async-start(bf16[32,144,128]{2,1,0:T(8,128)(2,1)} %shard_map.64), calls=%async_computation | async-start | bytes 2359296 | tf_op jit(solution)/shard_map/all_to_all | solution.py:218
  15.7 0.0 copy-done
  15.7 5.1 %collective-permute-start.1 = (bf16[27,32,512]{2,1,0:T(8,128)(2,1)S(1)}, bf16[27,32,512]{2,1,0:T(8,128)(2,1)S(1)}, u32[]{:S(2)}, u32[]{:S(2)}) collective-permute-start(bf16[27,32,512]{2,1,0:T(8,128)(2,1)S(1)} %bitcast.5), channel_id=1, source_target_pairs={{0,1},{1,2},{2,3},{3,4},{4,5},{5,6},{6,7},{7,0},{16,23},{17,16},{1... | collective-permute-start | bytes 2654216 | tf_op jit(solution)/shard_map/ppermute | solution.py:228
  20.8 10.0 %collective-permute-done.1.rest_1_ = bf16[27,32,512]{2,1,0:T(8,128)(2,1)S(1)} collective-permute-done((bf16[27,32,512]{2,1,0:T(8,128)(2,1)S(1)}, bf16[27,32,512]{2,1,0:T(8,128)(2,1)S(1)}, u32[]{:S(2)}, u32[]{:S(2)}) %collective-permute-start.1) | collective-permute-done | bytes 884768 | tf_op jit(solution)/shard_map/ppermute | solution.py:228
  30.8 5.3 %collective-permute-start.3 = (bf16[27,32,512]{2,1,0:T(8,128)(2,1)S(1)}, bf16[27,32,512]{2,1,0:T(8,128)(2,1)}, u32[]{:S(2)}, u32[]{:S(2)}) collective-permute-start(bf16[27,32,512]{2,1,0:T(8,128)(2,1)S(1)} %collective-permute-done.1.rest_1_), channel_id=1, source_target_pairs={{0,1},{1,2},{2,3},{3,4},{4,5},{5,6},{6,7},{7,0},{16,23},{17,16},{1... | collective-permute-start | bytes 2654216 | tf_op jit(solution)/shard_map/ppermute | solution.py:228
  36.1 8.8 %all-to-all-done.got = bf16[32,144,128]{2,1,0:T(8,128)(2,1)S(1)} async-done(((bf16[32,144,128]{2,1,0:T(8,128)(2,1)}), bf16[32,144,128]{2,1,0:T(8,128)(2,1)S(1)}, u32[]{:S(2)}, u32[]{:S(2)}) %all-to-all-start) | async-done | bytes 1179680 | tf_op jit(solution)/shard_map/all_to_all | solution.py:218
  44.8 3.5 %shard_map.65 = bf16[96,32,128]{2,1,0:T(8,128)(2,1)} custom-call(bf16[32,144,128]{2,1,0:T(8,128)(2,1)S(1)} %all-to-all-done.got), custom_call_target="tpu_custom_call" | custom-call | tf_op jit(solution)/shard_map/pallas_call | solution.py:245
  48.3 0.0 copy-start.2
  48.3 6.8 %all-to-all-start.1 = ((bf16[8,12,32,128]{3,2,1,0:T(8,128)(2,1)}), bf16[8,12,32,128]{3,2,1,0:T(8,128)(2,1)S(1)}, u32[]{:S(2)}, u32[]{:S(2)}) async-start(bf16[8,12,32,128]{3,2,1,0:T(8,128)(2,1)} %bitcast), calls=%async_computation.1 | async-start | bytes 1572864 | tf_op jit(solution)/shard_map/all_to_all | solution.py:218
  55.1 0.0 copy-start.3
  55.1 0.0 copy-start.4
  55.2 0.0 collective-permute-done.3.rest_3_
  55.2 4.7 %collective-permute-start.5 = (bf16[27,32,512]{2,1,0:T(8,128)(2,1)}, bf16[27,32,512]{2,1,0:T(8,128)(2,1)}, u32[]{:S(2)}, u32[]{:S(2)}) collective-permute-start(bf16[27,32,512]{2,1,0:T(8,128)(2,1)} %collective-permute-done.3.rest_3_), channel_id=1, source_target_pairs={{0,1},{1,2},{2,3},{3,4},{4,5},{5,6},{6,7},{7,0},{16,23},{17,16},{1... | collective-permute-start | bytes 2654216 | tf_op jit(solution)/shard_map/ppermute | solution.py:228
  59.9 1.9 %collective-permute-start.2 = (bf16[27,32,512]{2,1,0:T(8,128)(2,1)S(1)}, bf16[27,32,512]{2,1,0:T(8,128)(2,1)}, u32[]{:S(2)}, u32[]{:S(2)}) collective-permute-start(bf16[27,32,512]{2,1,0:T(8,128)(2,1)S(1)} %collective-permute-done.1.rest_1_), channel_id=1, source_target_pairs={{0,16},{16,0},{1,17},{17,1},{2,18},{18,2},{3,19},{19,3},{4,20},{20... | collective-permute-start | bytes 2654216 | tf_op jit(solution)/shard_map/ppermute | solution.py:229
  61.8 2.4 %collective-permute-start.4 = (bf16[27,32,512]{2,1,0:T(8,128)(2,1)}, bf16[27,32,512]{2,1,0:T(8,128)(2,1)}, u32[]{:S(2)}, u32[]{:S(2)}) collective-permute-start(bf16[27,32,512]{2,1,0:T(8,128)(2,1)} %collective-permute-done.3.rest_3_), channel_id=1, source_target_pairs={{0,16},{16,0},{1,17},{17,1},{2,18},{18,2},{3,19},{19,3},{4,20},{20... | collective-permute-start | bytes 2654216 | tf_op jit(solution)/shard_map/ppermute | solution.py:229
  64.2 20.3 %collective-permute-done.5.rest_5_ = bf16[27,32,512]{2,1,0:T(8,128)(2,1)} collective-permute-done((bf16[27,32,512]{2,1,0:T(8,128)(2,1)}, bf16[27,32,512]{2,1,0:T(8,128)(2,1)}, u32[]{:S(2)}, u32[]{:S(2)}) %collective-permute-start.5) | collective-permute-done | bytes 884768 | tf_op jit(solution)/shard_map/ppermute | solution.py:228
  84.5 3.5 %collective-permute-start.6 = (bf16[27,32,512]{2,1,0:T(8,128)(2,1)}, bf16[27,32,512]{2,1,0:T(8,128)(2,1)}, u32[]{:S(2)}, u32[]{:S(2)}) collective-permute-start(bf16[27,32,512]{2,1,0:T(8,128)(2,1)} %collective-permute-done.5.rest_5_), channel_id=1, source_target_pairs={{0,16},{16,0},{1,17},{17,1},{2,18},{18,2},{3,19},{19,3},{4,20},{20... | collective-permute-start | bytes 2654216 | tf_op jit(solution)/shard_map/ppermute | solution.py:229
  88.0 3.1 %collective-permute-start.7 = (bf16[27,32,512]{2,1,0:T(8,128)(2,1)}, bf16[27,32,512]{2,1,0:T(8,128)(2,1)}, u32[]{:S(2)}, u32[]{:S(2)}) collective-permute-start(bf16[27,32,512]{2,1,0:T(8,128)(2,1)} %collective-permute-done.5.rest_5_), channel_id=1, source_target_pairs={{0,1},{1,2},{2,3},{3,4},{4,5},{5,6},{6,7},{7,0},{16,23},{17,16},{1... | collective-permute-start | bytes 2654216 | tf_op jit(solution)/shard_map/ppermute | solution.py:230
  91.1 0.0 all-to-all-done.1.own
  91.2 1.9 %collective-permute-start = (bf16[8,12,32,128]{3,2,1,0:T(8,128)(2,1)S(1)}, bf16[8,12,32,128]{3,2,1,0:T(8,128)(2,1)S(1)}, u32[]{:S(2)}, u32[]{:S(2)}) collective-permute-start(bf16[8,12,32,128]{3,2,1,0:T(8,128)(2,1)S(1)} %all-to-all-done.1.own), channel_id=1, source_target_pairs={{0,16},{16,32},{32,48},{48,64},{64,80},{80,96},{96,112},{112,128},... | collective-permute-start | bytes 2359304 | tf_op jit(solution)/shard_map/ppermute | solution.py:258
  93.1 0.0 collective-permute-done.2.rest_2_
  93.1 0.0 collective-permute-done.4.rest_4_
  93.1 0.0 collective-permute-done.6.rest_6_
  93.1 9.3 %collective-permute-done.7.rest_7_ = bf16[27,32,512]{2,1,0:T(8,128)(2,1)} collective-permute-done((bf16[27,32,512]{2,1,0:T(8,128)(2,1)}, bf16[27,32,512]{2,1,0:T(8,128)(2,1)}, u32[]{:S(2)}, u32[]{:S(2)}) %collective-permute-start.7) | collective-permute-done | bytes 884768 | tf_op jit(solution)/shard_map/ppermute | solution.py:230
  102.4 0.0 collective-permute-done.before
  102.4 0.0 copy-done.2
  102.4 8.6 %shard_map.66 = (f32[128,512]{1,0:T(8,128)S(1)}, f32[128,512]{1,0:T(8,128)S(1)}) custom-call(s32[4]{0:T(128)S(1)} %copy-done.2, bf16[8,12,32,128]{3,2,1,0:T(8,128)(2,1)S(1)} %all-to-all-done.1.own, bf16[8,12,32,128]{3,2,1,0:T(8,128)(2,1)S(1)} %collective-permute-done.before, bf16[27,32,512]{2,1,0:T(8,128)(2,1)S(1)} %bitcast.6, ...), custom_call_target="tpu_custom_call" | custom-call | tf_op jit(solution)/shard_map/pallas_call | solution.py:262
  111.0 7.9 %collective-permute-start.8 = (f32[128,512]{1,0:T(8,128)S(1)}, f32[128,512]{1,0:T(8,128)S(1)}, u32[]{:S(2)}, u32[]{:S(2)}) collective-permute-start(f32[128,512]{1,0:T(8,128)S(1)} %get-tuple-element.10), channel_id=1, source_target_pairs={{0,8},{8,0},{1,9},{9,1},{2,10},{10,2},{3,11},{11,3},{4,12},{12,4},... | collective-permute-start | bytes 786440 | tf_op jit(solution)/shard_map/ppermute | solution.py:271
  118.9 4.5 %collective-permute-done.8.far = f32[128,512]{1,0:T(8,128)S(1)} collective-permute-done((f32[128,512]{1,0:T(8,128)S(1)}, f32[128,512]{1,0:T(8,128)S(1)}, u32[]{:S(2)}, u32[]{:S(2)}) %collective-permute-start.8) | collective-permute-done | bytes 262176 | tf_op jit(solution)/shard_map/ppermute | solution.py:271
  123.4 0.9 shard_map.67
  124.3 26.0 %all_to_all.20.got = f32[16,8,128]{2,1,0:T(8,128)} all-to-all(f32[16,8,128]{2,1,0:T(8,128)S(1)} %get-tuple-element.11), channel_id=1, replica_groups=mesh['zl'=4,'x'=4,'co'=2,'zh'=2,'y'=8] {'zh','y'}, dimensions={0} | all-to-all | bytes 131072 | tf_op jit(solution)/shard_map/all_to_all | solution.py:218
  150.3 1.5 shard_map.68
  151.9 18.1 %all_to_all.21.got = f32[32,8,128]{2,1,0:T(8,128)S(1)} all-to-all(f32[32,8,128]{2,1,0:T(8,128)} %shard_map.68), channel_id=1, replica_groups=mesh['zl'=4,'x'=4,'co'=2,'zh'=2,'y'=8] {'zl','x','co'}, dimensions={0} | all-to-all | bytes 262144 | tf_op jit(solution)/shard_map/all_to_all | solution.py:218
  170.0 0.0 copy-done.3
  170.0 0.0 copy-done.4
  170.0 1.5 shard_map.69
Async XLA Ops:
  0.0 1.0 copy-start.1
  1.0 0.7 copy-start.5
  4.2 11.5 %copy-start = (bf16[3,3,3,32,512]{4,3,2,1,0:T(8,128)(2,1)S(1)}, bf16[3,3,3,32,512]{4,3,2,1,0:T(8,128)(2,1)}, u32[]{:S(2)}) copy-start(bf16[3,3,3,32,512]{4,3,2,1,0:T(8,128)(2,1)} %param.9) | copy-start | bytes 2654212
  4.2 40.7 %all-to-all-start = ((bf16[32,144,128]{2,1,0:T(8,128)(2,1)}), bf16[32,144,128]{2,1,0:T(8,128)(2,1)S(1)}, u32[]{:S(2)}, u32[]{:S(2)}) async-start(bf16[32,144,128]{2,1,0:T(8,128)(2,1)} %shard_map.64), calls=%async_computation | async-start | bytes 2359296 | tf_op jit(solution)/shard_map/all_to_all | solution.py:218
  15.7 15.1 %collective-permute-start.1 = (bf16[27,32,512]{2,1,0:T(8,128)(2,1)S(1)}, bf16[27,32,512]{2,1,0:T(8,128)(2,1)S(1)}, u32[]{:S(2)}, u32[]{:S(2)}) collective-permute-start(bf16[27,32,512]{2,1,0:T(8,128)(2,1)S(1)} %bitcast.5), channel_id=1, source_target_pairs={{0,1},{1,2},{2,3},{3,4},{4,5},{5,6},{6,7},{7,0},{16,23},{17,16},{1... | collective-permute-start | bytes 2654216 | tf_op jit(solution)/shard_map/ppermute | solution.py:228
  30.8 24.4 %collective-permute-start.3 = (bf16[27,32,512]{2,1,0:T(8,128)(2,1)S(1)}, bf16[27,32,512]{2,1,0:T(8,128)(2,1)}, u32[]{:S(2)}, u32[]{:S(2)}) collective-permute-start(bf16[27,32,512]{2,1,0:T(8,128)(2,1)S(1)} %collective-permute-done.1.rest_1_), channel_id=1, source_target_pairs={{0,1},{1,2},{2,3},{3,4},{4,5},{5,6},{6,7},{7,0},{16,23},{17,16},{1... | collective-permute-start | bytes 2654216 | tf_op jit(solution)/shard_map/ppermute | solution.py:228
  48.3 54.1 %copy-start.2 = (s32[4]{0:T(128)S(1)}, s32[4]{0:T(128)}, u32[]{:S(2)}) copy-start(s32[4]{0:T(128)} %lengths.5) | copy-start | bytes 52
  48.3 42.8 %all-to-all-start.1 = ((bf16[8,12,32,128]{3,2,1,0:T(8,128)(2,1)}), bf16[8,12,32,128]{3,2,1,0:T(8,128)(2,1)S(1)}, u32[]{:S(2)}, u32[]{:S(2)}) async-start(bf16[8,12,32,128]{3,2,1,0:T(8,128)(2,1)} %bitcast), calls=%async_computation.1 | async-start | bytes 1572864 | tf_op jit(solution)/shard_map/all_to_all | solution.py:218
  55.1 114.8 %copy-start.3 = (f32[512]{0:T(512)S(1)}, f32[512]{0:T(512)}, u32[]{:S(2)}) copy-start(f32[512]{0:T(512)} %param.10) | copy-start | bytes 6148
  55.1 114.8 %copy-start.4 = (f32[512]{0:T(512)S(1)}, f32[512]{0:T(512)}, u32[]{:S(2)}) copy-start(f32[512]{0:T(512)} %param.11) | copy-start | bytes 6148
  55.2 29.3 %collective-permute-start.5 = (bf16[27,32,512]{2,1,0:T(8,128)(2,1)}, bf16[27,32,512]{2,1,0:T(8,128)(2,1)}, u32[]{:S(2)}, u32[]{:S(2)}) collective-permute-start(bf16[27,32,512]{2,1,0:T(8,128)(2,1)} %collective-permute-done.3.rest_3_), channel_id=1, source_target_pairs={{0,1},{1,2},{2,3},{3,4},{4,5},{5,6},{6,7},{7,0},{16,23},{17,16},{1... | collective-permute-start | bytes 2654216 | tf_op jit(solution)/shard_map/ppermute | solution.py:228
  59.9 33.2 %collective-permute-start.2 = (bf16[27,32,512]{2,1,0:T(8,128)(2,1)S(1)}, bf16[27,32,512]{2,1,0:T(8,128)(2,1)}, u32[]{:S(2)}, u32[]{:S(2)}) collective-permute-start(bf16[27,32,512]{2,1,0:T(8,128)(2,1)S(1)} %collective-permute-done.1.rest_1_), channel_id=1, source_target_pairs={{0,16},{16,0},{1,17},{17,1},{2,18},{18,2},{3,19},{19,3},{4,20},{20... | collective-permute-start | bytes 2654216 | tf_op jit(solution)/shard_map/ppermute | solution.py:229
  61.8 31.3 %collective-permute-start.4 = (bf16[27,32,512]{2,1,0:T(8,128)(2,1)}, bf16[27,32,512]{2,1,0:T(8,128)(2,1)}, u32[]{:S(2)}, u32[]{:S(2)}) collective-permute-start(bf16[27,32,512]{2,1,0:T(8,128)(2,1)} %collective-permute-done.3.rest_3_), channel_id=1, source_target_pairs={{0,16},{16,0},{1,17},{17,1},{2,18},{18,2},{3,19},{19,3},{4,20},{20... | collective-permute-start | bytes 2654216 | tf_op jit(solution)/shard_map/ppermute | solution.py:229
  84.5 8.6 %collective-permute-start.6 = (bf16[27,32,512]{2,1,0:T(8,128)(2,1)}, bf16[27,32,512]{2,1,0:T(8,128)(2,1)}, u32[]{:S(2)}, u32[]{:S(2)}) collective-permute-start(bf16[27,32,512]{2,1,0:T(8,128)(2,1)} %collective-permute-done.5.rest_5_), channel_id=1, source_target_pairs={{0,16},{16,0},{1,17},{17,1},{2,18},{18,2},{3,19},{19,3},{4,20},{20... | collective-permute-start | bytes 2654216 | tf_op jit(solution)/shard_map/ppermute | solution.py:229
  88.0 14.4 %collective-permute-start.7 = (bf16[27,32,512]{2,1,0:T(8,128)(2,1)}, bf16[27,32,512]{2,1,0:T(8,128)(2,1)}, u32[]{:S(2)}, u32[]{:S(2)}) collective-permute-start(bf16[27,32,512]{2,1,0:T(8,128)(2,1)} %collective-permute-done.5.rest_5_), channel_id=1, source_target_pairs={{0,1},{1,2},{2,3},{3,4},{4,5},{5,6},{6,7},{7,0},{16,23},{17,16},{1... | collective-permute-start | bytes 2654216 | tf_op jit(solution)/shard_map/ppermute | solution.py:230
  91.2 11.2 %collective-permute-start = (bf16[8,12,32,128]{3,2,1,0:T(8,128)(2,1)S(1)}, bf16[8,12,32,128]{3,2,1,0:T(8,128)(2,1)S(1)}, u32[]{:S(2)}, u32[]{:S(2)}) collective-permute-start(bf16[8,12,32,128]{3,2,1,0:T(8,128)(2,1)S(1)} %all-to-all-done.1.own), channel_id=1, source_target_pairs={{0,16},{16,32},{32,48},{48,64},{64,80},{80,96},{96,112},{112,128},... | collective-permute-start | bytes 2359304 | tf_op jit(solution)/shard_map/ppermute | solution.py:258
  111.0 12.5 %collective-permute-start.8 = (f32[128,512]{1,0:T(8,128)S(1)}, f32[128,512]{1,0:T(8,128)S(1)}, u32[]{:S(2)}, u32[]{:S(2)}) collective-permute-start(f32[128,512]{1,0:T(8,128)S(1)} %get-tuple-element.10), channel_id=1, source_target_pairs={{0,8},{8,0},{1,9},{9,1},{2,10},{10,2},{3,11},{11,3},{4,12},{12,4},... | collective-permute-start | bytes 786440 | tf_op jit(solution)/shard_map/ppermute | solution.py:271

commit v2 on v1

v2 whole, which is shorter than its diff:
```python
import functools

import jax
import jax.numpy as jnp
from jax import lax
from jax.experimental import pallas as pl
from jax.experimental.pallas import tpu as pltpu
from jax.sharding import Mesh, PartitionSpec as P

TM = ("zl", "x", "co")
CH = ("zh", "y")
SLABS = 32
ROWS = 64
CAP = 4
CH_DEV = 32
NY = 8
OUT_ROWS = 16
COUT = 512
GROUPS = 32
GROUP_SIZE = 16
EPSILON = 1e-05
BF = jnp.bfloat16
F32 = jnp.float32
HIGHEST = lax.Precision.HIGHEST

VMEM = pl.BlockSpec(memory_space=pltpu.VMEM)
SMEM = pl.BlockSpec(memory_space=pltpu.SMEM)


def params(mib):
    return pltpu.CompilerParams(vmem_limit_bytes=mib * 1024 * 1024)


def pack_kernel(target, arrived, send, places, counts, sem):
    places[...] = jnp.full(places.shape, float(ROWS), F32)

    def clear(i, carry):
        counts[i] = 0
        return carry

    lax.fori_loop(0, SLABS, clear, 0)

    def one(i, carry):
        t = target[i]
        owner = lax.shift_right_logical(t, 6)
        rank = counts[owner]
        counts[owner] = rank + 1
        pltpu.make_async_copy(arrived.at[i], send.at[owner * CAP + rank], sem).start()
        place = lax.bitwise_and(t, ROWS - 1).astype(F32)
        places[owner, pl.ds(rank, 1), :] = jnp.full((1, 128), place, F32)
        return carry

    lax.fori_loop(0, ROWS, one, 0)
    pltpu.make_async_copy(arrived, send.at[pl.ds(0, ROWS)], sem).wait()


def spot(zh, i, f, b):
    near = 1 - lax.bitwise_xor(lax.shift_right_logical(i, 3), zh)
    return near * 48 + lax.bitwise_and(i, NY - 1) * 6 + f * 3 + b


def table_kernel(got, moves, table, table_s, sem):
    zh = lax.axis_index("zh")
    lane = lax.broadcasted_iota(jnp.int32, (8, 128), 1)
    acc = jnp.zeros((8, 128), F32)
    for s in range(SLABS):
        acc = jnp.where(lane == s, got[s], acc)
    table[...] = acc.astype(jnp.int32)
    copy = pltpu.make_async_copy(table, table_s, sem)
    copy.start()
    copy.wait()

    def one(s, n):
        for r in range(CAP):
            place = table_s[r, s]
            f = lax.shift_right_logical(place, 5)
            h = lax.bitwise_and(place, 31)
            odd = lax.bitwise_and(h, 1)
            i = lax.shift_right_logical(h, 1)
            first = spot(zh, i, f, 1 + odd)
            shared = (odd == 1) & (i < OUT_ROWS - 1)
            moves[0, n] = s * CAP + r
            moves[1, n] = first
            moves[2, n] = jnp.where(shared, spot(zh, i + 1, f, 0), first)
            n = jnp.where(place < ROWS, n + 1, n)
        return n

    lax.fori_loop(0, SLABS, one, jnp.int32(0))


def place_kernel(moves, got, far, near, both):
    zh = lax.axis_index("zh")
    for f in range(2):
        both[spot(zh, jnp.int32(0), f, 0)] = jnp.zeros((CH_DEV, 128), BF)

    def some(n, carry):
        for k in range(8):
            row = got[moves[0, n * 8 + k]]
            both[moves[1, n * 8 + k]] = row
            both[moves[2, n * 8 + k]] = row
        return carry

    lax.fori_loop(0, ROWS // 8, some, 0)
    far[...] = both[:48]
    near[...] = both[48:]


def clip_start_of(lengths, frame):
    first = jnp.int32(0)
    end = jnp.int32(0)
    for k in range(4):
        start = end
        end = end + lengths[k]
        first = jnp.where((frame >= start) & (frame < end), start, first)
    return first


def conv_kernel(late, lengths, frames, *rest):
    weights, rest = rest[:NY], rest[NY:]
    out, taps = rest[-2:]
    y = lax.axis_index("y")
    core = lax.axis_index("co")
    slab = (lax.axis_index("zl") * 4 + lax.axis_index("x")) * 2 + core
    sign = 2 * core - 1
    sources = [y]
    for s in range(1, 4):
        sources += [y + sign * s, y - sign * s]
    sources.append(y + 4)
    sources = [lax.bitwise_and(s + NY, NY - 1) for s in sources]
    j = lax.broadcasted_iota(jnp.int32, (192, 128), 0)
    w = lax.broadcasted_iota(jnp.int32, (192, 128), 1)
    wanted = jnp.where(j < 64, 2 * j - 1, jnp.where(j < 128, 2 * j - 128, 2 * j - 255))
    pick = (w == wanted).astype(F32).astype(BF)
    for t in range(2):
        for b in range(3):
            x = jnp.concatenate([frames[s, t * 3 + b] for s in sources], axis=0)
            picked = lax.dot_general(pick, x, (((1,), (1,)), ((), ())),
                                     preferred_element_type=F32).astype(BF)
            for e in range(3):
                taps[t, b, :, e * 256:(e + 1) * 256] = picked[e * 64:(e + 1) * 64]
    out[...] = jnp.zeros(out.shape, F32) if late else rest[0][...]

    def gate(f, a):
        frame = slab * 2 + f
        allowed = frame - 2 + a >= clip_start_of(lengths, frame)
        return jnp.full((64, 768), jnp.where(allowed, 1.0, 0.0), F32).astype(BF)

    plan = [(2, [(0, 0), (1, 1)]), (1, [(1, 0)])] if late else [(0, [(0, 0), (1, 1)]), (1, [(0, 1)])]

    def row_tap(b, carry):
        for a, pairs in plan:
            tap = (a * 3 + b) * 3
            kernel = jnp.concatenate([ref[tap + e] for e in range(3) for ref in weights], axis=0)
            lhs = jnp.concatenate([taps[t, b] * gate(f, a) for f, t in pairs], axis=0)
            first = pairs[0][0] * 64
            rows = slice(first, first + 64 * len(pairs))
            out[rows] += jnp.dot(lhs, kernel, preferred_element_type=F32)
        return carry

    lax.fori_loop(0, 3, row_tap, 0)


def group_matrix(channels_first):
    shape = (COUT, 128) if channels_first else (128, COUT)
    c = lax.broadcasted_iota(jnp.int32, shape, 0 if channels_first else 1)
    g = lax.broadcasted_iota(jnp.int32, shape, 1 if channels_first else 0)
    return (lax.shift_right_logical(c, 4) == g).astype(F32)


def member_of(lengths, frame):
    end = jnp.int32(0)
    flags = []
    for k in range(4):
        start = end
        end = end + lengths[k]
        flags.append(jnp.where((frame >= start) & (frame < end), 1.0, 0.0).astype(F32))
    return flags


def stat_kernel(lengths, near, far, conv_out, stats):
    slab = (lax.axis_index("zl") * 4 + lax.axis_index("x")) * 2 + lax.axis_index("co")
    conv = near[...] + far[...]
    conv_out[...] = conv
    rows = []
    for f in range(2):
        part = conv[f * 64:(f + 1) * 64]
        rows.append(jnp.sum(part, axis=0, keepdims=True))
        rows.append(jnp.sum(part * part, axis=0, keepdims=True))
    rows = jnp.concatenate(rows + rows, axis=0)
    grouped = jnp.dot(rows, group_matrix(True), precision=HIGHEST, preferred_element_type=F32)
    m0 = member_of(lengths, slab * 2)
    m1 = member_of(lengths, slab * 2 + 1)
    sums = [grouped[0:1] * m0[k] + grouped[2:3] * m1[k] for k in range(4)]
    squares = [grouped[1:2] * m0[k] + grouped[3:4] * m1[k] for k in range(4)]
    tile = jnp.concatenate(sums + squares, axis=0)
    stats[...] = jnp.broadcast_to(tile[None], stats.shape)


def middle_kernel(got, out):
    out[...] = jnp.broadcast_to(jnp.sum(got[...], axis=0)[None], out.shape)


def final_kernel(lengths, got, conv, gain, bias, out):
    slab = (lax.axis_index("zl") * 4 + lax.axis_index("x")) * 2 + lax.axis_index("co")
    total = jnp.sum(got[...], axis=0)
    spread = group_matrix(False)
    for f in range(2):
        flags = member_of(lengths, slab * 2 + f)
        sums = jnp.zeros((1, 128), F32)
        squares = jnp.zeros((1, 128), F32)
        frames = jnp.float32(0)
        for k in range(4):
            sums = sums + total[k:k + 1] * flags[k]
            squares = squares + total[4 + k:5 + k] * flags[k]
            frames = frames + flags[k] * lengths[k].astype(F32)
        entries = jnp.full((1, 128), frames * float(OUT_ROWS * 64 * GROUP_SIZE), F32)
        mean = sums / entries
        var = squares / entries - mean * mean
        scale = lax.rsqrt(var + EPSILON)
        both = jnp.concatenate([mean, scale] * 4, axis=0)
        wide = jnp.dot(both, spread, precision=HIGHEST, preferred_element_type=F32)
        part = conv[f * 64:(f + 1) * 64]
        v = ((part - wide[0:1]) * wide[1:2]) * gain[...] + bias[...]
        out[f] = (v / (1.0 + jnp.exp(-v))).astype(BF)


def shuffle(x, axis):
    return lax.all_to_all(x, axis, split_axis=0, concat_axis=0, tiled=True)


def gathered_weights(kernel):
    ring = [(c * NY + y, c * NY + (y + (1 if c == 0 else NY - 1)) % NY)
            for c in range(2) for y in range(NY)]
    swap = [(0, 1), (1, 0)]
    moved = [kernel]
    swapped = []
    for step in range(4):
        moved.append(lax.ppermute(moved[-1], ("co", "y"), ring))
        if step < 3:
            swapped.append(lax.ppermute(moved[-1], "co", swap))
    return moved, swapped


def convolve(late, lengths, frames, weights, start=()):
    return pl.pallas_call(
        functools.partial(conv_kernel, late),
        out_shape=jax.ShapeDtypeStruct((128, COUT), F32),
        in_specs=[SMEM] + [VMEM] * (1 + NY + len(start)),
        out_specs=VMEM,
        scratch_shapes=[pltpu.VMEM((2, 3, 64, 768), BF)],
        compiler_params=params(24),
    )(lengths, frames, *weights, *start)


def body(arrived, row_target, clip_lengths, conv_weight, gn_gain, gn_bias):
    moved, swapped = gathered_weights(conv_weight.reshape(27, CH_DEV, COUT))
    send, places = pl.pallas_call(
        pack_kernel,
        out_shape=[
            jax.ShapeDtypeStruct((SLABS * CAP, CH_DEV, 128), BF),
            jax.ShapeDtypeStruct((SLABS, 8, 128), F32),
        ],
        in_specs=[SMEM, pl.BlockSpec(memory_space=pl.ANY)],
        out_specs=[pl.BlockSpec(memory_space=pl.ANY), VMEM],
        scratch_shapes=[pltpu.SMEM((SLABS,), jnp.int32), pltpu.SemaphoreType.DMA],
        compiler_params=params(8),
    )(row_target, arrived)
    got = shuffle(send, TM)
    places = shuffle(places, TM)
    moves = pl.pallas_call(
        table_kernel,
        out_shape=jax.ShapeDtypeStruct((3, 128), jnp.int32),
        in_specs=[VMEM],
        out_specs=SMEM,
        scratch_shapes=[
            pltpu.VMEM((8, 128), jnp.int32),
            pltpu.SMEM((8, 128), jnp.int32),
            pltpu.SemaphoreType.DMA,
        ],
    )(places)
    got, moved[3] = lax.optimization_barrier((got, moved[3]))
    far, near = pl.pallas_call(
        place_kernel,
        out_shape=[jax.ShapeDtypeStruct((NY * 6, CH_DEV, 128), BF)] * 2,
        in_specs=[SMEM, VMEM],
        out_specs=[VMEM, VMEM],
        scratch_shapes=[pltpu.VMEM((96, CH_DEV, 128), BF)],
        compiler_params=params(8),
    )(moves, got)
    weights = [moved[0], moved[1], swapped[0], moved[2], swapped[1], moved[3], swapped[2], moved[4]]
    sums = []
    owns = [shuffle(rows.reshape(NY, 6, CH_DEV, 128), "y") for rows in (far, near)]
    befores = [lax.ppermute(own, TM, [(i, i + 1) for i in range(SLABS - 1)]) for own in owns]
    for own, before in zip(owns, befores):
        part = convolve(True, clip_lengths, own, weights)
        sums.append(convolve(False, clip_lengths, before, weights, (part,)))
    far, near = sums
    far = lax.ppermute(far, "zh", [(0, 1), (1, 0)])
    conv, stats = pl.pallas_call(
        stat_kernel,
        out_shape=[jax.ShapeDtypeStruct((128, COUT), F32), jax.ShapeDtypeStruct((16, 8, 128), F32)],
        in_specs=[SMEM, VMEM, VMEM],
        out_specs=[VMEM, VMEM],
        compiler_params=params(16),
    )(clip_lengths, near, far)
    stats = shuffle(stats, ("y", "co"))
    stats = pl.pallas_call(
        middle_kernel,
        out_shape=jax.ShapeDtypeStruct((SLABS, 8, 128), F32),
        in_specs=[VMEM],
        out_specs=VMEM,
    )(stats)
    stats = shuffle(stats, ("zl", "zh", "x"))
    out = pl.pallas_call(
        final_kernel,
        out_shape=jax.ShapeDtypeStruct((2, 64, COUT), BF),
        in_specs=[SMEM, VMEM, VMEM, VMEM, VMEM],
        out_specs=VMEM,
        compiler_params=params(16),
    )(clip_lengths, stats, conv, gn_gain.reshape(1, COUT), gn_bias.reshape(1, COUT))
    return out.reshape(1, 2, 64, COUT)


def solution(mesh):
    fine = Mesh(mesh.devices.reshape(4, 4, 2, 2, 8), TM + CH)
    in_specs = (P(TM, CH, None), P(TM), P(), P(None, None, None, CH, None), P(), P())
    out_specs = P(CH, TM, None, None)
    return jax.shard_map(body, mesh=fine, in_specs=in_specs, out_specs=out_specs, check_vma=False)
```

time: 172 us -> 175 us (1.017)
  waiting for transfers between devices: 52.8 us -> 30.4 us
  blocking collectives: 44.1 us -> 52.6 us
  Pallas kernels: 18.4 us -> 25.6 us
  starting transfers between devices: 54.3 us -> 61.4 us
  local copies, waits for them, and re-layouts: 1.72 us -> 3.94 us
    ppermute x8 -> x9, waiting for transfers between devices: 39.5 us -> 12.5 us  [the longest x4 12.5 us: gathered_weights(): moved.append(lax.ppermute(moved[-1], ('co', 'y'), ring))]
    ppermute x8 -> x9, starting transfers between devices: 28 us -> 37.9 us  [the longest x4 17.8 us: gathered_weights(): moved.append(lax.ppermute(moved[-1], ('co', 'y'), ring))]
    all_to_all x2 -> x3, blocking collectives: 44.1 us -> 52.6 us  [shuffle(): return lax.all_to_all(x, axis, split_axis=0, concat_axis=0, tiled=True)]
    pallas_call x3 -> x7, Pallas kernels: 14.5 us -> 21.7 us  [the longest x4 14.2 us: convolve(): pl.pallas_call(functools.partial(conv_kernel, late), out_shape=jax.ShapeD...]
    all_to_all x2 -> x3, waiting for transfers between devices: 8.76 us -> 14.5 us  [shuffle(): return lax.all_to_all(x, axis, split_axis=0, concat_axis=0, tiled=True)]
    all_to_all x2 -> x3, starting transfers between devices: 18.3 us -> 15.6 us  [shuffle(): return lax.all_to_all(x, axis, split_axis=0, concat_axis=0, tiled=True)]
    unnamed x12 -> x18, local copies, waits for them, and re-layouts: 1.72 us -> 3.94 us
  transfers between devices with their start and end apart: 11 -> 13, of which waited for: 5 -> 5; matrix products, arithmetic and copies ran while one was open for 0% -> 0% of each run, Pallas kernels for 2% -> 11%
where the time goes in v2:
time: 175 us; the launch traced here: 174 us
  starting transfers between devices  61.4 us (35%)
  blocking collectives  52.6 us (30%)
  waiting for transfers between devices  30.4 us (17%)
  Pallas kernels  25.6 us (15%)
  local copies, waits for them, and re-layouts  3.94 us (2%)
    all_to_all x3, blocking collectives, shuffle(): return lax.all_to_all(x, axis, split_axis=0, concat_axis=0, tiled=True)  52.6 us
    ppermute x4, starting transfers between devices, gathered_weights(): moved.append(lax.ppermute(moved[-1], ('co', 'y'), ring))  17.8 us
    all_to_all x3, starting transfers between devices, shuffle(): return lax.all_to_all(x, axis, split_axis=0, concat_axis=0, tiled=True)  15.6 us
    all_to_all x3, waiting for transfers between devices, shuffle(): return lax.all_to_all(x, axis, split_axis=0, concat_axis=0, tiled=True)  14.5 us
    pallas_call x4, Pallas kernels, convolve(): pl.pallas_call(functools.partial(conv_kernel, late), out_shape=jax.ShapeD...  14.2 us
    ppermute x4, waiting for transfers between devices, gathered_weights(): moved.append(lax.ppermute(moved[-1], ('co', 'y'), ring))  12.5 us
    ppermute x2, starting transfers between devices, body(): lax.ppermute(own, TM, [(i, i + 1) for i in range(SLABS - 1)])  10.8 us
    ppermute x3, starting transfers between devices, gathered_weights(): swapped.append(lax.ppermute(moved[-1], 'co', swap))  9.34 us
  transfers between devices with their start and end apart: 13, of which 5 were waited for; matrix products, arithmetic and copies ran while one was open for 0% of the time, Pallas kernels for 11%

profile of v2, /device:TPU:1, one launch (start us, length us, event | category | flops | bytes accessed | tf_op | source)
XLA Modules:
  0.0 174.1 jit_solution(6587107909232023260)
XLA Ops:
  0.0 0.0 copy-start.8
  0.0 6.0 %collective-permute-start = (bf16[27,32,512]{2,1,0:T(8,128)(2,1)}, bf16[27,32,512]{2,1,0:T(8,128)(2,1)S(1)}, u32[]{:S(2)}, u32[]{:S(2)}) collective-permute-start(bf16[27,32,512]{2,1,0:T(8,128)(2,1)} %bitcast.6), channel_id=1, source_target_pairs={{0,1},{1,2},{2,3},{3,4},{4,5},{5,6},{6,7},{7,0},{16,23},{17,16},{1... | collective-permute-start | bytes 2654216 | tf_op jit(solution)/shard_map/ppermute | solution.py:238
  6.1 0.0 copy-done.8
  6.1 0.0 copy-start.1
  6.1 1.0 copy-done.1
  7.1 2.0 %shard_map.64 = (bf16[128,32,128]{2,1,0:T(8,128)(2,1)}, f32[32,8,128]{2,1,0:T(8,128)S(1)}) custom-call(s32[64]{0:T(128)S(1)} %copy-done.8, bf16[64,32,128]{2,1,0:T(8,128)(2,1)S(1)} %copy-done.1), custom_call_target="tpu_custom_call" | custom-call | tf_op jit(solution)/shard_map/pallas_call | solution.py:257
  9.1 18.4 %all_to_all.30.got = f32[32,8,128]{2,1,0:T(8,128)} all-to-all(f32[32,8,128]{2,1,0:T(8,128)S(1)} %get-tuple-element.13), channel_id=1, replica_groups=mesh['zl'=4,'x'=4,'co'=2,'zh'=2,'y'=8] {'zl','x','co'}, dimensions={0} | all-to-all | bytes 262144 | tf_op jit(solution)/shard_map/all_to_all | solution.py:228
  27.6 4.6 %all-to-all-start.1 = ((bf16[128,32,128]{2,1,0:T(8,128)(2,1)}), bf16[128,32,128]{2,1,0:T(8,128)(2,1)}, u32[]{:S(2)}, u32[]{:S(2)}) async-start(bf16[128,32,128]{2,1,0:T(8,128)(2,1)} %get-tuple-element.14), calls=%async_computation.1 | async-start | bytes 2097152 | tf_op jit(solution)/shard_map/all_to_all | solution.py:228
  32.2 0.0 collective-permute-done.rest_1_
  32.2 3.0 %collective-permute-start.1 = (bf16[27,32,512]{2,1,0:T(8,128)(2,1)S(1)}, bf16[27,32,512]{2,1,0:T(8,128)(2,1)S(1)}, u32[]{:S(2)}, u32[]{:S(2)}) collective-permute-start(bf16[27,32,512]{2,1,0:T(8,128)(2,1)S(1)} %collective-permute-done.rest_1_), channel_id=1, source_target_pairs={{0,1},{1,2},{2,3},{3,4},{4,5},{5,6},{6,7},{7,0},{16,23},{17,16},{1... | collective-permute-start | bytes 2654216 | tf_op jit(solution)/shard_map/ppermute | solution.py:238
  35.2 11.1 %collective-permute-done.1.rest_3_ = bf16[27,32,512]{2,1,0:T(8,128)(2,1)S(1)} collective-permute-done((bf16[27,32,512]{2,1,0:T(8,128)(2,1)S(1)}, bf16[27,32,512]{2,1,0:T(8,128)(2,1)S(1)}, u32[]{:S(2)}, u32[]{:S(2)}) %collective-permute-start.1) | collective-permute-done | bytes 884768 | tf_op jit(solution)/shard_map/ppermute | solution.py:238
  46.3 3.9 %collective-permute-start.2 = (bf16[27,32,512]{2,1,0:T(8,128)(2,1)S(1)}, bf16[27,32,512]{2,1,0:T(8,128)(2,1)S(1)}, u32[]{:S(2)}, u32[]{:S(2)}) collective-permute-start(bf16[27,32,512]{2,1,0:T(8,128)(2,1)S(1)} %collective-permute-done.1.rest_3_), channel_id=1, source_target_pairs={{0,1},{1,2},{2,3},{3,4},{4,5},{5,6},{6,7},{7,0},{16,23},{17,16},{1... | collective-permute-start | bytes 2654216 | tf_op jit(solution)/shard_map/ppermute | solution.py:238
  50.2 3.8 %shard_map.65.moves = s32[3,128]{1,0:T(4,128)} custom-call(f32[32,8,128]{2,1,0:T(8,128)} %all_to_all.30.got), custom_call_target="tpu_custom_call" | custom-call | tf_op jit(solution)/shard_map/pallas_call | solution.py:270
  54.0 4.9 %all-to-all-done.1.got = bf16[128,32,128]{2,1,0:T(8,128)(2,1)} async-done(((bf16[128,32,128]{2,1,0:T(8,128)(2,1)}), bf16[128,32,128]{2,1,0:T(8,128)(2,1)}, u32[]{:S(2)}, u32[]{:S(2)}) %all-to-all-start.1) | async-done | bytes 1048608 | tf_op jit(solution)/shard_map/all_to_all | solution.py:228
  58.9 1.4 collective-permute-done.2.rest_5_
  60.4 0.0 copy-start.5
  60.4 0.7 copy-done.5
  61.0 1.7 shard_map.66
  62.8 0.0 copy-start.2
  62.8 0.8 copy-done.2
  63.5 0.0 copy-start.3
  63.5 0.8 copy-done.3
  64.3 0.0 copy-start
  64.3 6.7 %all-to-all-start.3 = ((bf16[8,6,32,128]{3,2,1,0:T(8,128)(2,1)}), bf16[8,6,32,128]{3,2,1,0:T(8,128)(2,1)}, u32[]{:S(2)}, u32[]{:S(2)}) async-start(bf16[8,6,32,128]{3,2,1,0:T(8,128)(2,1)} %bitcast.12), calls=%async_computation.3 | async-start | bytes 786432 | tf_op jit(solution)/shard_map/all_to_all | solution.py:228
  71.0 5.0 %collective-permute-start.4 = (bf16[27,32,512]{2,1,0:T(8,128)(2,1)S(1)}, bf16[27,32,512]{2,1,0:T(8,128)(2,1)}, u32[]{:S(2)}, u32[]{:S(2)}) collective-permute-start(bf16[27,32,512]{2,1,0:T(8,128)(2,1)S(1)} %collective-permute-done.rest_1_), channel_id=1, source_target_pairs={{0,16},{16,0},{1,17},{17,1},{2,18},{18,2},{3,19},{19,3},{4,20},{20... | collective-permute-start | bytes 2654216 | tf_op jit(solution)/shard_map/ppermute | solution.py:240
  76.0 1.9 %collective-permute-start.5 = (bf16[27,32,512]{2,1,0:T(8,128)(2,1)S(1)}, bf16[27,32,512]{2,1,0:T(8,128)(2,1)}, u32[]{:S(2)}, u32[]{:S(2)}) collective-permute-start(bf16[27,32,512]{2,1,0:T(8,128)(2,1)S(1)} %collective-permute-done.1.rest_3_), channel_id=1, source_target_pairs={{0,16},{16,0},{1,17},{17,1},{2,18},{18,2},{3,19},{19,3},{4,20},{20... | collective-permute-start | bytes 2654216 | tf_op jit(solution)/shard_map/ppermute | solution.py:240
  77.9 2.4 %collective-permute-start.6 = (bf16[27,32,512]{2,1,0:T(8,128)(2,1)S(1)}, bf16[27,32,512]{2,1,0:T(8,128)(2,1)}, u32[]{:S(2)}, u32[]{:S(2)}) collective-permute-start(bf16[27,32,512]{2,1,0:T(8,128)(2,1)S(1)} %collective-permute-done.2.rest_5_), channel_id=1, source_target_pairs={{0,16},{16,0},{1,17},{17,1},{2,18},{18,2},{3,19},{19,3},{4,20},{20... | collective-permute-start | bytes 2654216 | tf_op jit(solution)/shard_map/ppermute | solution.py:240
  80.4 4.9 %collective-permute-start.7 = (bf16[27,32,512]{2,1,0:T(8,128)(2,1)S(1)}, bf16[27,32,512]{2,1,0:T(8,128)(2,1)}, u32[]{:S(2)}, u32[]{:S(2)}) collective-permute-start(bf16[27,32,512]{2,1,0:T(8,128)(2,1)S(1)} %collective-permute-done.2.rest_5_), channel_id=1, source_target_pairs={{0,1},{1,2},{2,3},{3,4},{4,5},{5,6},{6,7},{7,0},{16,23},{17,16},{1... | collective-permute-start | bytes 2654216 | tf_op jit(solution)/shard_map/ppermute | solution.py:238
  85.2 0.0 all-to-all-done.3.frames
  85.2 0.0 copy-start.4
  85.3 4.3 %all-to-all-start.2 = ((bf16[8,6,32,128]{3,2,1,0:T(8,128)(2,1)}), bf16[8,6,32,128]{3,2,1,0:T(8,128)(2,1)}, u32[]{:S(2)}, u32[]{:S(2)}) async-start(bf16[8,6,32,128]{3,2,1,0:T(8,128)(2,1)} %bitcast.11), calls=%async_computation.2 | async-start | bytes 786432 | tf_op jit(solution)/shard_map/all_to_all | solution.py:228
  89.5 4.6 %collective-permute-start.8 = (bf16[8,6,32,128]{3,2,1,0:T(8,128)(2,1)}, bf16[8,6,32,128]{3,2,1,0:T(8,128)(2,1)}, u32[]{:S(2)}, u32[]{:S(2)}) collective-permute-start(bf16[8,6,32,128]{3,2,1,0:T(8,128)(2,1)} %all-to-all-done.3.frames), channel_id=1, source_target_pairs={{0,16},{16,32},{32,48},{48,64},{64,80},{80,96},{96,112},{112,128},... | collective-permute-start | bytes 1179656 | tf_op jit(solution)/shard_map/ppermute | solution.py:293
  94.2 0.0 collective-permute-done.4.rest_2_
  94.2 9.5 %all-to-all-done.2.frames = bf16[8,6,32,128]{3,2,1,0:T(8,128)(2,1)} async-done(((bf16[8,6,32,128]{3,2,1,0:T(8,128)(2,1)}), bf16[8,6,32,128]{3,2,1,0:T(8,128)(2,1)}, u32[]{:S(2)}, u32[]{:S(2)}) %all-to-all-start.2) | async-done | bytes 393248 | tf_op jit(solution)/shard_map/all_to_all | solution.py:228
  103.7 6.2 %collective-permute-start.3 = (bf16[8,6,32,128]{3,2,1,0:T(8,128)(2,1)}, bf16[8,6,32,128]{3,2,1,0:T(8,128)(2,1)S(1)}, u32[]{:S(2)}, u32[]{:S(2)}) collective-permute-start(bf16[8,6,32,128]{3,2,1,0:T(8,128)(2,1)} %all-to-all-done.2.frames), channel_id=1, source_target_pairs={{0,16},{16,32},{32,48},{48,64},{64,80},{80,96},{96,112},{112,128},... | collective-permute-start | bytes 1179656 | tf_op jit(solution)/shard_map/ppermute | solution.py:293
  109.9 0.0 collective-permute-done.5.rest_4_
  109.9 0.0 collective-permute-done.6.rest_6_
  109.9 0.0 collective-permute-done.7.rest_7_
  109.9 0.0 copy-done
  109.9 0.0 copy-done.4
  109.9 3.6 %shard_map.69.rest_8_ = f32[128,512]{1,0:T(8,128)S(1)} custom-call(s32[4]{0:T(128)S(1)} %copy-done.4, bf16[8,6,32,128]{3,2,1,0:T(8,128)(2,1)} %all-to-all-done.3.frames, bf16[27,32,512]{2,1,0:T(8,128)(2,1)S(1)} %bitcast.7, bf16[27,32,512]{2,1,0:T(8,128)(2,1)S(1)} %collective-permute-done.rest_1_, bf16[27,32,512]{2,1,0:T(8,128)(2,1)} %collective-permute-done.4.rest_2_, ...), custom_call_target="tpu_custom_call" | custom-call | tf_op jit(solution)/shard_map/pallas_call | solution.py:245
  113.5 0.0 collective-permute-done.8.frames
  113.5 3.6 %shard_map.70 = f32[128,512]{1,0:T(8,128)S(1)} custom-call(s32[4]{0:T(128)S(1)} %copy-done.4, bf16[8,6,32,128]{3,2,1,0:T(8,128)(2,1)} %collective-permute-done.8.frames, bf16[27,32,512]{2,1,0:T(8,128)(2,1)S(1)} %bitcast.8, bf16[27,32,512]{2,1,0:T(8,128)(2,1)S(1)} %collective-permute-done.rest_1_, bf16[27,32,512]{2,1,0:T(8,128)(2,1)} %collective-permute-done.4.rest_2_, ...), custom_call_target="tpu_custom_call" | custom-call | tf_op jit(solution)/shard_map/pallas_call | solution.py:245
  117.1 7.9 %collective-permute-start.9 = (f32[128,512]{1,0:T(8,128)S(1)}, f32[128,512]{1,0:T(8,128)S(1)}, u32[]{:S(2)}, u32[]{:S(2)}) collective-permute-start(f32[128,512]{1,0:T(8,128)S(1)} %shard_map.70), channel_id=1, source_target_pairs={{0,8},{8,0},{1,9},{9,1},{2,10},{10,2},{3,11},{11,3},{4,12},{12,4},... | collective-permute-start | bytes 786440 | tf_op jit(solution)/shard_map/ppermute | solution.py:298
  125.1 3.6 %shard_map.67.rest_8_ = f32[128,512]{1,0:T(8,128)S(1)} custom-call(s32[4]{0:T(128)S(1)} %copy-done.4, bf16[8,6,32,128]{3,2,1,0:T(8,128)(2,1)} %all-to-all-done.2.frames, bf16[27,32,512]{2,1,0:T(8,128)(2,1)S(1)} %bitcast.9, bf16[27,32,512]{2,1,0:T(8,128)(2,1)S(1)} %collective-permute-done.rest_1_, bf16[27,32,512]{2,1,0:T(8,128)(2,1)} %collective-permute-done.4.rest_2_, ...), custom_call_target="tpu_custom_call" | custom-call | tf_op jit(solution)/shard_map/pallas_call | solution.py:245
  128.6 0.0 collective-permute-done.3.frames
  128.6 3.5 %shard_map.68.near = f32[128,512]{1,0:T(8,128)S(1)} custom-call(s32[4]{0:T(128)S(1)} %copy-done.4, bf16[8,6,32,128]{3,2,1,0:T(8,128)(2,1)S(1)} %collective-permute-done.3.frames, bf16[27,32,512]{2,1,0:T(8,128)(2,1)S(1)} %bitcast.10, bf16[27,32,512]{2,1,0:T(8,128)(2,1)S(1)} %collective-permute-done.rest_1_, ...), custom_call_target="tpu_custom_call" | custom-call | tf_op jit(solution)/shard_map/pallas_call | solution.py:245
  132.1 3.3 %collective-permute-done.9.far = f32[128,512]{1,0:T(8,128)S(1)} collective-permute-done((f32[128,512]{1,0:T(8,128)S(1)}, f32[128,512]{1,0:T(8,128)S(1)}, u32[]{:S(2)}, u32[]{:S(2)}) %collective-permute-start.9) | collective-permute-done | bytes 262176 | tf_op jit(solution)/shard_map/ppermute | solution.py:298
  135.4 0.9 shard_map.71
  136.3 13.3 %all_to_all.31.got = f32[16,8,128]{2,1,0:T(8,128)} all-to-all(f32[16,8,128]{2,1,0:T(8,128)S(1)} %get-tuple-element.19), channel_id=1, replica_groups=mesh['zl'=4,'x'=4,'co'=2,'zh'=2,'y'=8] {'y','co'}, dimensions={0} | all-to-all | bytes 131072 | tf_op jit(solution)/shard_map/all_to_all | solution.py:228
  149.6 1.5 shard_map.72
  151.1 20.8 %all_to_all.32.got = f32[32,8,128]{2,1,0:T(8,128)S(1)} all-to-all(f32[32,8,128]{2,1,0:T(8,128)} %shard_map.72), channel_id=1, replica_groups=mesh['zl'=4,'x'=4,'co'=2,'zh'=2,'y'=8] {'zl','zh','x'}, dimensions={0} | all-to-all | bytes 262144 | tf_op jit(solution)/shard_map/all_to_all | solution.py:228
  171.9 0.0 copy-start.7
  171.9 0.0 copy-start.6
  171.9 0.7 copy-done.7
  172.6 0.0 copy-done.6
  172.6 1.5 shard_map.73
Async XLA Ops:
  0.0 6.1 %copy-start.8 = (s32[64]{0:T(128)S(1)}, s32[64]{0:T(128)}, u32[]{:S(2)}) copy-start(s32[64]{0:T(128)} %target.1) | copy-start | bytes 772
  0.0 32.2 %collective-permute-start = (bf16[27,32,512]{2,1,0:T(8,128)(2,1)}, bf16[27,32,512]{2,1,0:T(8,128)(2,1)S(1)}, u32[]{:S(2)}, u32[]{:S(2)}) collective-permute-start(bf16[27,32,512]{2,1,0:T(8,128)(2,1)} %bitcast.6), channel_id=1, source_target_pairs={{0,1},{1,2},{2,3},{3,4},{4,5},{5,6},{6,7},{7,0},{16,23},{17,16},{1... | collective-permute-start | bytes 2654216 | tf_op jit(solution)/shard_map/ppermute | solution.py:238
  6.1 1.0 copy-start.1
  27.6 31.4 %all-to-all-start.1 = ((bf16[128,32,128]{2,1,0:T(8,128)(2,1)}), bf16[128,32,128]{2,1,0:T(8,128)(2,1)}, u32[]{:S(2)}, u32[]{:S(2)}) async-start(bf16[128,32,128]{2,1,0:T(8,128)(2,1)} %get-tuple-element.14), calls=%async_computation.1 | async-start | bytes 2097152 | tf_op jit(solution)/shard_map/all_to_all | solution.py:228
  32.2 14.1 %collective-permute-start.1 = (bf16[27,32,512]{2,1,0:T(8,128)(2,1)S(1)}, bf16[27,32,512]{2,1,0:T(8,128)(2,1)S(1)}, u32[]{:S(2)}, u32[]{:S(2)}) collective-permute-start(bf16[27,32,512]{2,1,0:T(8,128)(2,1)S(1)} %collective-permute-done.rest_1_), channel_id=1, source_target_pairs={{0,1},{1,2},{2,3},{3,4},{4,5},{5,6},{6,7},{7,0},{16,23},{17,16},{1... | collective-permute-start | bytes 2654216 | tf_op jit(solution)/shard_map/ppermute | solution.py:238
  46.3 14.1 %collective-permute-start.2 = (bf16[27,32,512]{2,1,0:T(8,128)(2,1)S(1)}, bf16[27,32,512]{2,1,0:T(8,128)(2,1)S(1)}, u32[]{:S(2)}, u32[]{:S(2)}) collective-permute-start(bf16[27,32,512]{2,1,0:T(8,128)(2,1)S(1)} %collective-permute-done.1.rest_3_), channel_id=1, source_target_pairs={{0,1},{1,2},{2,3},{3,4},{4,5},{5,6},{6,7},{7,0},{16,23},{17,16},{1... | collective-permute-start | bytes 2654216 | tf_op jit(solution)/shard_map/ppermute | solution.py:238
  60.4 0.7 copy-start.5
  62.8 0.8 copy-start.2
  63.5 0.8 copy-start.3
  64.3 45.6 %copy-start = (bf16[3,3,3,32,512]{4,3,2,1,0:T(8,128)(2,1)S(1)}, bf16[3,3,3,32,512]{4,3,2,1,0:T(8,128)(2,1)}, u32[]{:S(2)}) copy-start(bf16[3,3,3,32,512]{4,3,2,1,0:T(8,128)(2,1)} %param.9) | copy-start | bytes 2654212
  64.3 20.9 %all-to-all-start.3 = ((bf16[8,6,32,128]{3,2,1,0:T(8,128)(2,1)}), bf16[8,6,32,128]{3,2,1,0:T(8,128)(2,1)}, u32[]{:S(2)}, u32[]{:S(2)}) async-start(bf16[8,6,32,128]{3,2,1,0:T(8,128)(2,1)} %bitcast.12), calls=%async_computation.3 | async-start | bytes 786432 | tf_op jit(solution)/shard_map/all_to_all | solution.py:228
  71.0 23.2 %collective-permute-start.4 = (bf16[27,32,512]{2,1,0:T(8,128)(2,1)S(1)}, bf16[27,32,512]{2,1,0:T(8,128)(2,1)}, u32[]{:S(2)}, u32[]{:S(2)}) collective-permute-start(bf16[27,32,512]{2,1,0:T(8,128)(2,1)S(1)} %collective-permute-done.rest_1_), channel_id=1, source_target_pairs={{0,16},{16,0},{1,17},{17,1},{2,18},{18,2},{3,19},{19,3},{4,20},{20... | collective-permute-start | bytes 2654216 | tf_op jit(solution)/shard_map/ppermute | solution.py:240
  76.0 33.9 %collective-permute-start.5 = (bf16[27,32,512]{2,1,0:T(8,128)(2,1)S(1)}, bf16[27,32,512]{2,1,0:T(8,128)(2,1)}, u32[]{:S(2)}, u32[]{:S(2)}) collective-permute-start(bf16[27,32,512]{2,1,0:T(8,128)(2,1)S(1)} %collective-permute-done.1.rest_3_), channel_id=1, source_target_pairs={{0,16},{16,0},{1,17},{17,1},{2,18},{18,2},{3,19},{19,3},{4,20},{20... | collective-permute-start | bytes 2654216 | tf_op jit(solution)/shard_map/ppermute | solution.py:240
  77.9 32.0 %collective-permute-start.6 = (bf16[27,32,512]{2,1,0:T(8,128)(2,1)S(1)}, bf16[27,32,512]{2,1,0:T(8,128)(2,1)}, u32[]{:S(2)}, u32[]{:S(2)}) collective-permute-start(bf16[27,32,512]{2,1,0:T(8,128)(2,1)S(1)} %collective-permute-done.2.rest_5_), channel_id=1, source_target_pairs={{0,16},{16,0},{1,17},{17,1},{2,18},{18,2},{3,19},{19,3},{4,20},{20... | collective-permute-start | bytes 2654216 | tf_op jit(solution)/shard_map/ppermute | solution.py:240
  80.4 29.6 %collective-permute-start.7 = (bf16[27,32,512]{2,1,0:T(8,128)(2,1)S(1)}, bf16[27,32,512]{2,1,0:T(8,128)(2,1)}, u32[]{:S(2)}, u32[]{:S(2)}) collective-permute-start(bf16[27,32,512]{2,1,0:T(8,128)(2,1)S(1)} %collective-permute-done.2.rest_5_), channel_id=1, source_target_pairs={{0,1},{1,2},{2,3},{3,4},{4,5},{5,6},{6,7},{7,0},{16,23},{17,16},{1... | collective-permute-start | bytes 2654216 | tf_op jit(solution)/shard_map/ppermute | solution.py:238
  85.2 24.7 %copy-start.4 = (s32[4]{0:T(128)S(1)}, s32[4]{0:T(128)}, u32[]{:S(2)}) copy-start(s32[4]{0:T(128)} %lengths.11) | copy-start | bytes 52
  85.3 18.5 %all-to-all-start.2 = ((bf16[8,6,32,128]{3,2,1,0:T(8,128)(2,1)}), bf16[8,6,32,128]{3,2,1,0:T(8,128)(2,1)}, u32[]{:S(2)}, u32[]{:S(2)}) async-start(bf16[8,6,32,128]{3,2,1,0:T(8,128)(2,1)} %bitcast.11), calls=%async_computation.2 | async-start | bytes 786432 | tf_op jit(solution)/shard_map/all_to_all | solution.py:228
  89.5 24.0 %collective-permute-start.8 = (bf16[8,6,32,128]{3,2,1,0:T(8,128)(2,1)}, bf16[8,6,32,128]{3,2,1,0:T(8,128)(2,1)}, u32[]{:S(2)}, u32[]{:S(2)}) collective-permute-start(bf16[8,6,32,128]{3,2,1,0:T(8,128)(2,1)} %all-to-all-done.3.frames), channel_id=1, source_target_pairs={{0,16},{16,32},{32,48},{48,64},{64,80},{80,96},{96,112},{112,128},... | collective-permute-start | bytes 1179656 | tf_op jit(solution)/shard_map/ppermute | solution.py:293
  103.7 24.9 %collective-permute-start.3 = (bf16[8,6,32,128]{3,2,1,0:T(8,128)(2,1)}, bf16[8,6,32,128]{3,2,1,0:T(8,128)(2,1)S(1)}, u32[]{:S(2)}, u32[]{:S(2)}) collective-permute-start(bf16[8,6,32,128]{3,2,1,0:T(8,128)(2,1)} %all-to-all-done.2.frames), channel_id=1, source_target_pairs={{0,16},{16,32},{32,48},{48,64},{64,80},{80,96},{96,112},{112,128},... | collective-permute-start | bytes 1179656 | tf_op jit(solution)/shard_map/ppermute | solution.py:293
  117.1 18.3 %collective-permute-start.9 = (f32[128,512]{1,0:T(8,128)S(1)}, f32[128,512]{1,0:T(8,128)S(1)}, u32[]{:S(2)}, u32[]{:S(2)}) collective-permute-start(f32[128,512]{1,0:T(8,128)S(1)} %shard_map.70), channel_id=1, source_target_pairs={{0,8},{8,0},{1,9},{9,1},{2,10},{10,2},{3,11},{11,3},{4,12},{12,4},... | collective-permute-start | bytes 786440 | tf_op jit(solution)/shard_map/ppermute | solution.py:298
  171.9 0.7 copy-start.7
  171.9 0.7 copy-start.6

commit v3 on v2

v3 whole, which is shorter than its diff:
```python
import functools

import jax
import jax.numpy as jnp
from jax import lax
from jax.experimental import pallas as pl
from jax.experimental.pallas import tpu as pltpu
from jax.sharding import Mesh, PartitionSpec as P

TM = ("zl", "x", "co")
CH = ("zh", "y")
SLABS = 32
ROWS = 64
CAP = 4
CH_DEV = 32
NY = 8
OUT_ROWS = 16
COUT = 512
GROUPS = 32
GROUP_SIZE = 16
EPSILON = 1e-05
BF = jnp.bfloat16
F32 = jnp.float32
HIGHEST = lax.Precision.HIGHEST

VMEM = pl.BlockSpec(memory_space=pltpu.VMEM)
SMEM = pl.BlockSpec(memory_space=pltpu.SMEM)
HBM = pl.BlockSpec(memory_space=pltpu.HBM)


def params(mib):
    return pltpu.CompilerParams(vmem_limit_bytes=mib * 1024 * 1024)


def pack_kernel(target, arrived, send, counts, places, rounded, sems):
    places[...] = jnp.full(places.shape, float(ROWS), F32)

    def clear(i, carry):
        counts[i] = 0
        return carry

    lax.fori_loop(0, SLABS, clear, 0)

    def one(i, carry):
        t = target[i]
        owner = lax.shift_right_logical(t, 6)
        rank = counts[owner]
        counts[owner] = rank + 1
        slot = pl.ds(pl.multiple_of(rank * CH_DEV, CH_DEV), CH_DEV)
        pltpu.make_async_copy(arrived.at[i], send.at[owner, slot], sems.at[0]).start()
        place = lax.bitwise_and(t, ROWS - 1).astype(F32)
        places[owner, pl.ds(rank, 1), :] = jnp.full((1, 128), place, F32)
        return carry

    lax.fori_loop(0, ROWS, one, 0)
    rounded[...] = places[...].astype(BF)
    listed = pltpu.make_async_copy(rounded, send.at[:, pl.ds(CAP * CH_DEV, 16)], sems.at[1])
    listed.start()
    pltpu.make_async_copy(arrived, arrived, sems.at[0]).wait()
    listed.wait()


def my_slab():
    return (lax.axis_index("zl") * 4 + lax.axis_index("x")) * 2 + lax.axis_index("co")


def spot(zh, i, f, b):
    near = 1 - lax.bitwise_xor(lax.shift_right_logical(i, 3), zh)
    return near * 48 + lax.bitwise_and(i, NY - 1) * 6 + f * 3 + b


def place_kernel(got, far, near, both, table, moves, sems):
    zh = lax.axis_index("zh")
    lane = lax.broadcasted_iota(jnp.int32, (16, 128), 1)
    place = jnp.full((16, 128), float(ROWS), F32)
    for s in range(SLABS):
        place = jnp.where(lane == s, got[s, CAP * CH_DEV:, :].astype(F32), place)
    place = place.astype(jnp.int32)
    f = lax.shift_right_logical(place, 5)
    h = lax.bitwise_and(place, 31)
    odd = lax.bitwise_and(h, 1)
    i = lax.shift_right_logical(h, 1)
    first = spot(zh, i, f, 1 + odd)
    second = jnp.where((odd == 1) & (i < OUT_ROWS - 1), spot(zh, i + 1, f, 0), first)
    table[...] = jnp.where(place < ROWS, first * 128 + second, 96 * 128 + 96)
    copy = pltpu.make_async_copy(table, moves, sems.at[0])
    copy.start()
    for f in range(2):
        both[spot(zh, jnp.int32(0), f, 0)] = jnp.zeros((CH_DEV, 128), BF)
    copy.wait()

    def some(s, carry):
        for source in (2 * s, 2 * s + 1):
            for r in range(CAP):
                move = moves[r, source]
                row = got[source, r * CH_DEV:(r + 1) * CH_DEV, :]
                both[lax.shift_right_logical(move, 7)] = row
                both[lax.bitwise_and(move, 127)] = row
        return carry

    lax.fori_loop(0, SLABS // 2, some, 0)
    copies = [
        pltpu.make_async_copy(both.at[pl.ds(48 * k, 48)], out, sems.at[k])
        for k, out in enumerate((far, near))
    ]
    for copy in copies:
        copy.start()
    for copy in copies:
        copy.wait()


def clip_start_of(lengths, frame):
    first = jnp.int32(0)
    end = jnp.int32(0)
    for k in range(4):
        start = end
        end = end + lengths[k]
        first = jnp.where((frame >= start) & (frame < end), start, first)
    return first


def conv_kernel(lengths, frames, *rest):
    weights, (own, after, taps) = rest[:NY], rest[NY:]
    y = lax.axis_index("y")
    core = lax.axis_index("co")
    slab = my_slab()
    sign = 2 * core - 1
    sources = [y]
    for s in range(1, 4):
        sources += [y + sign * s, y - sign * s]
    sources.append(y + 4)
    sources = [lax.bitwise_and(s + NY, NY - 1) for s in sources]
    j = lax.broadcasted_iota(jnp.int32, (192, 128), 0)
    w = lax.broadcasted_iota(jnp.int32, (192, 128), 1)
    wanted = jnp.where(j < 64, 2 * j - 1, jnp.where(j < 128, 2 * j - 128, 2 * j - 255))
    pick = (w == wanted).astype(F32).astype(BF)
    for t in range(2):
        for b in range(3):
            x = jnp.concatenate([frames[s, t * 3 + b] for s in sources], axis=0)
            picked = lax.dot_general(pick, x, (((1,), (1,)), ((), ())),
                                     preferred_element_type=F32).astype(BF)
            for e in range(3):
                taps[b, t * 64:(t + 1) * 64, e * 256:(e + 1) * 256] = picked[e * 64:(e + 1) * 64]
    own[...] = jnp.zeros(own.shape, F32)
    after[...] = jnp.zeros(after.shape, F32)

    def gates(a):
        parts = []
        for t in range(2):
            frame = slab * 2 + t
            allowed = frame >= clip_start_of(lengths, frame + 2 - a)
            parts.append(jnp.full((64, 768), jnp.where(allowed, 1.0, 0.0), F32).astype(BF))
        return jnp.concatenate(parts, axis=0)

    def row_tap(b, carry):
        lhs = taps[b]
        for a in range(3):
            tap = (a * 3 + b) * 3
            kernel = jnp.concatenate([ref[tap + e] for e in range(3) for ref in weights], axis=0)
            part = jnp.dot(lhs * gates(a), kernel, preferred_element_type=F32)
            if a == 0:
                after[...] += part
            elif a == 1:
                own[64:] += part[:64]
                after[:64] += part[64:]
            else:
                own[...] += part
        return carry

    lax.fori_loop(0, 3, row_tap, 0)


def group_matrix(channels_first):
    shape = (COUT, 128) if channels_first else (128, COUT)
    c = lax.broadcasted_iota(jnp.int32, shape, 0 if channels_first else 1)
    g = lax.broadcasted_iota(jnp.int32, shape, 1 if channels_first else 0)
    return (lax.shift_right_logical(c, 4) == g).astype(F32)


def member_of(lengths, frame):
    end = jnp.int32(0)
    flags = []
    for k in range(4):
        start = end
        end = end + lengths[k]
        flags.append(jnp.where((frame >= start) & (frame < end), 1.0, 0.0).astype(F32))
    return flags


def stat_kernel(lengths, near, before, conv_out, stats):
    slab = my_slab()
    conv = near[...] + before[...]
    conv_out[...] = conv
    rows = []
    for f in range(2):
        part = conv[f * 64:(f + 1) * 64]
        rows.append(jnp.sum(part, axis=0, keepdims=True))
        rows.append(jnp.sum(part * part, axis=0, keepdims=True))
    rows = jnp.concatenate(rows + rows, axis=0)
    grouped = jnp.dot(rows, group_matrix(True), precision=HIGHEST, preferred_element_type=F32)
    m0 = member_of(lengths, slab * 2)
    m1 = member_of(lengths, slab * 2 + 1)
    sums = [grouped[0:1] * m0[k] + grouped[2:3] * m1[k] for k in range(4)]
    squares = [grouped[1:2] * m0[k] + grouped[3:4] * m1[k] for k in range(4)]
    tile = jnp.concatenate(sums + squares, axis=0)
    stats[...] = jnp.broadcast_to(tile[None], stats.shape)


def middle_kernel(got, out):
    out[...] = jnp.broadcast_to(jnp.sum(got[...], axis=0)[None], out.shape)


def final_kernel(lengths, got, conv, gain, bias, out):
    slab = my_slab()
    total = jnp.sum(got[...], axis=0)
    spread = group_matrix(False)
    for f in range(2):
        flags = member_of(lengths, slab * 2 + f)
        sums = jnp.zeros((1, 128), F32)
        squares = jnp.zeros((1, 128), F32)
        frames = jnp.float32(0)
        for k in range(4):
            sums = sums + total[k:k + 1] * flags[k]
            squares = squares + total[4 + k:5 + k] * flags[k]
            frames = frames + flags[k] * lengths[k].astype(F32)
        entries = jnp.full((1, 128), frames * float(OUT_ROWS * 64 * GROUP_SIZE), F32)
        mean = sums / entries
        var = squares / entries - mean * mean
        scale = lax.rsqrt(var + EPSILON)
        both = jnp.concatenate([mean, scale] * 4, axis=0)
        wide = jnp.dot(both, spread, precision=HIGHEST, preferred_element_type=F32)
        part = conv[f * 64:(f + 1) * 64]
        v = ((part - wide[0:1]) * wide[1:2]) * gain[...] + bias[...]
        out[f] = (v / (1.0 + jnp.exp(-v))).astype(BF)


def shuffle(x, axis):
    return lax.all_to_all(x, axis, split_axis=0, concat_axis=0, tiled=True)


def gathered_weights(kernel):
    ring = [(c * NY + y, c * NY + (y + (1 if c == 0 else NY - 1)) % NY)
            for c in range(2) for y in range(NY)]
    swap = [(0, 1), (1, 0)]
    moved = [kernel]
    swapped = []
    for step in range(4):
        moved.append(lax.ppermute(moved[-1], ("co", "y"), ring))
        if step < 3:
            swapped.append(lax.ppermute(moved[-1], "co", swap))
    return moved, swapped


def convolve(lengths, frames, weights):
    return pl.pallas_call(
        conv_kernel,
        out_shape=[jax.ShapeDtypeStruct((128, COUT), F32)] * 2,
        in_specs=[SMEM] + [VMEM] * (1 + NY),
        out_specs=[VMEM, VMEM],
        scratch_shapes=[pltpu.VMEM((3, 128, 768), BF)],
        compiler_params=params(24),
    )(lengths, frames, *weights)


def body(arrived, row_target, clip_lengths, conv_weight, gn_gain, gn_bias):
    moved, swapped = gathered_weights(conv_weight.reshape(27, CH_DEV, COUT))
    send = pl.pallas_call(
        pack_kernel,
        out_shape=jax.ShapeDtypeStruct((SLABS, 144, 128), BF),
        in_specs=[SMEM, HBM],
        out_specs=HBM,
        scratch_shapes=[
            pltpu.SMEM((SLABS,), jnp.int32),
            pltpu.VMEM((SLABS, 16, 128), F32),
            pltpu.VMEM((SLABS, 16, 128), BF),
            pltpu.SemaphoreType.DMA((2,)),
        ],
        compiler_params=params(60),
    )(row_target, arrived)
    got = shuffle(send, TM)
    got, moved[3], swapped[0], swapped[1] = lax.optimization_barrier(
        (got, moved[3], swapped[0], swapped[1])
    )
    far, near = pl.pallas_call(
        place_kernel,
        out_shape=[jax.ShapeDtypeStruct((NY * 6, CH_DEV, 128), BF)] * 2,
        in_specs=[VMEM],
        out_specs=[HBM, HBM],
        scratch_shapes=[
            pltpu.VMEM((97, CH_DEV, 128), BF),
            pltpu.VMEM((16, 128), jnp.int32),
            pltpu.SMEM((16, 128), jnp.int32),
            pltpu.SemaphoreType.DMA((2,)),
        ],
        compiler_params=params(8),
    )(got)
    weights = [moved[0], moved[1], swapped[0], moved[2], swapped[1], moved[3], swapped[2], moved[4]]
    onward = [(i, i + 1) for i in range(SLABS - 1)]
    far = shuffle(far.reshape(NY, 6, CH_DEV, 128), "y")
    near = shuffle(near.reshape(NY, 6, CH_DEV, 128), "y")
    far, far_after = convolve(clip_lengths, far, weights)
    far_before = lax.ppermute(far_after, TM, onward)
    near, near_after = convolve(clip_lengths, near, weights)
    near_before = lax.ppermute(near_after, TM, onward)
    far = lax.ppermute(far + far_before, "zh", [(0, 1), (1, 0)])
    near = near + far
    conv, stats = pl.pallas_call(
        stat_kernel,
        out_shape=[jax.ShapeDtypeStruct((128, COUT), F32), jax.ShapeDtypeStruct((16, 8, 128), F32)],
        in_specs=[SMEM, VMEM, VMEM],
        out_specs=[VMEM, VMEM],
        compiler_params=params(16),
    )(clip_lengths, near, near_before)
    stats = shuffle(stats, ("y", "co"))
    stats = pl.pallas_call(
        middle_kernel,
        out_shape=jax.ShapeDtypeStruct((SLABS, 8, 128), F32),
        in_specs=[VMEM],
        out_specs=VMEM,
    )(stats)
    stats = shuffle(stats, ("zl", "zh", "x"))
    out = pl.pallas_call(
        final_kernel,
        out_shape=jax.ShapeDtypeStruct((2, 64, COUT), BF),
        in_specs=[SMEM, VMEM, VMEM, VMEM, VMEM],
        out_specs=VMEM,
        compiler_params=params(16),
    )(clip_lengths, stats, conv, gn_gain.reshape(1, COUT), gn_bias.reshape(1, COUT))
    return out.reshape(1, 2, 64, COUT)


def solution(mesh):
    fine = Mesh(mesh.devices.reshape(4, 4, 2, 2, 8), TM + CH)
    in_specs = (P(TM, CH, None), P(TM), P(), P(None, None, None, CH, None), P(), P())
    out_specs = P(CH, TM, None, None)
    return jax.shard_map(body, mesh=fine, in_specs=in_specs, out_specs=out_specs, check_vma=False)
```

time: 175 us -> 172 us (0.983)
  blocking collectives: 52.6 us -> 38 us
  starting transfers between devices: 61.4 us -> 68 us
  Pallas kernels: 25.6 us -> 32 us
    all_to_all x3 -> x2, blocking collectives: 52.6 us -> 38 us  [shuffle(): return lax.all_to_all(x, axis, split_axis=0, concat_axis=0, tiled=True)]
    pallas_call x6 -> x3, Pallas kernels: 20 us -> 26 us  [the longest x1 17.9 us: body(): pl.pallas_call(pack_kernel, out_shape=jax.ShapeDtypeStruct((SLABS, 144, 1...]
    all_to_all x3, waiting for transfers between devices: 14.5 us -> 9.3 us  [shuffle(): return lax.all_to_all(x, axis, split_axis=0, concat_axis=0, tiled=True)]
    all_to_all x3, starting transfers between devices: 15.6 us -> 19.8 us  [shuffle(): return lax.all_to_all(x, axis, split_axis=0, concat_axis=0, tiled=True)]
    ppermute x3, starting transfers between devices: 18.7 us -> 21.4 us  [the longest x1 8.8 us: body(): far_before = lax.ppermute(far_after, TM, onward)]
    ppermute x3, waiting for transfers between devices: 3.33 us -> 5.58 us  [the longest x1 3.29 us: body(): far_before = lax.ppermute(far_after, TM, onward)]
    ppermute x4, waiting for transfers between devices: 12.5 us -> 14.7 us  [gathered_weights(): moved.append(lax.ppermute(moved[-1], ('co', 'y'), ring))]
    unnamed x18 -> x16, local copies, waits for them, and re-layouts: 3.94 us -> 2.72 us
  transfers between devices with their start and end apart: 13 -> 13, of which waited for: 5 -> 6; matrix products, arithmetic and copies ran while one was open for 0% -> 1% of each run, Pallas kernels for 11% -> 15%
where the time goes in v3:
time: 172 us
  starting transfers between devices  68 us (40%)
  blocking collectives  38 us (22%)
  Pallas kernels  32 us (19%)
  waiting for transfers between devices  29.6 us (17%)
  local copies, waits for them, and re-layouts  2.72 us (2%)
    all_to_all x2, blocking collectives, shuffle(): return lax.all_to_all(x, axis, split_axis=0, concat_axis=0, tiled=True)  38 us
    all_to_all x3, starting transfers between devices, shuffle(): return lax.all_to_all(x, axis, split_axis=0, concat_axis=0, tiled=True)  19.8 us
    pallas_call x1, Pallas kernels, body(): pl.pallas_call(pack_kernel, out_shape=jax.ShapeDtypeStruct((SLABS, 144, 1...  17.9 us
    ppermute x4, starting transfers between devices, gathered_weights(): moved.append(lax.ppermute(moved[-1], ('co', 'y'), ring))  17.8 us
    ppermute x4, waiting for transfers between devices, gathered_weights(): moved.append(lax.ppermute(moved[-1], ('co', 'y'), ring))  14.7 us
    all_to_all x3, waiting for transfers between devices, shuffle(): return lax.all_to_all(x, axis, split_axis=0, concat_axis=0, tiled=True)  9.3 us
    ppermute x3, starting transfers between devices, gathered_weights(): swapped.append(lax.ppermute(moved[-1], 'co', swap))  8.94 us
    ppermute x1, starting transfers between devices, body(): far_before = lax.ppermute(far_after, TM, onward)  8.8 us
  transfers between devices with their start and end apart: 13, of which 6 were waited for; matrix products, arithmetic and copies ran while one was open for 1% of the time, Pallas kernels for 15%

profile of v3, /device:TPU:1, one launch (start us, length us, event | category | flops | bytes accessed | tf_op | source)
XLA Modules:
  0.0 171.6 jit_solution(3221660262492102377)
XLA Ops:
  0.0 5.9 %collective-permute-start = (bf16[27,32,512]{2,1,0:T(8,128)(2,1)}, bf16[27,32,512]{2,1,0:T(8,128)(2,1)S(1)}, u32[]{:S(2)}, u32[]{:S(2)}) collective-permute-start(bf16[27,32,512]{2,1,0:T(8,128)(2,1)} %bitcast.6), channel_id=1, source_target_pairs={{0,1},{1,2},{2,3},{3,4},{4,5},{5,6},{6,7},{7,0},{16,23},{17,16},{1... | collective-permute-start | bytes 2654216 | tf_op jit(solution)/shard_map/ppermute | solution.py:248
  5.9 17.9 %shard_map.64 = bf16[32,144,128]{2,1,0:T(8,128)(2,1)} custom-call(s32[64]{0:T(128)} %target.1, bf16[64,32,128]{2,1,0:T(8,128)(2,1)} %arrived.1), custom_call_target="tpu_custom_call" | custom-call | tf_op jit(solution)/shard_map/pallas_call | solution.py:267
  23.8 10.0 %all-to-all-start = ((bf16[32,144,128]{2,1,0:T(8,128)(2,1)}), bf16[32,144,128]{2,1,0:T(8,128)(2,1)S(1)}, u32[]{:S(2)}, u32[]{:S(2)}) async-start(bf16[32,144,128]{2,1,0:T(8,128)(2,1)} %shard_map.64), calls=%async_computation | async-start | bytes 2359296 | tf_op jit(solution)/shard_map/all_to_all | solution.py:238
  33.9 0.0 copy-start
  33.9 0.0 copy-start.5
  33.9 0.0 collective-permute-done.rest_1_
  33.9 3.1 %collective-permute-start.1 = (bf16[27,32,512]{2,1,0:T(8,128)(2,1)S(1)}, bf16[27,32,512]{2,1,0:T(8,128)(2,1)}, u32[]{:S(2)}, u32[]{:S(2)}) collective-permute-start(bf16[27,32,512]{2,1,0:T(8,128)(2,1)S(1)} %collective-permute-done.rest_1_), channel_id=1, source_target_pairs={{0,1},{1,2},{2,3},{3,4},{4,5},{5,6},{6,7},{7,0},{16,23},{17,16},{1... | collective-permute-start | bytes 2654216 | tf_op jit(solution)/shard_map/ppermute | solution.py:248
  37.0 1.9 %collective-permute-start.3 = (bf16[27,32,512]{2,1,0:T(8,128)(2,1)S(1)}, bf16[27,32,512]{2,1,0:T(8,128)(2,1)S(1)}, u32[]{:S(2)}, u32[]{:S(2)}) collective-permute-start(bf16[27,32,512]{2,1,0:T(8,128)(2,1)S(1)} %collective-permute-done.rest_1_), channel_id=1, source_target_pairs={{0,16},{16,0},{1,17},{17,1},{2,18},{18,2},{3,19},{19,3},{4,20},{20... | collective-permute-start | bytes 2654216 | tf_op jit(solution)/shard_map/ppermute | solution.py:250
  38.9 9.3 %collective-permute-done.1.rest_3_ = bf16[27,32,512]{2,1,0:T(8,128)(2,1)} collective-permute-done((bf16[27,32,512]{2,1,0:T(8,128)(2,1)S(1)}, bf16[27,32,512]{2,1,0:T(8,128)(2,1)}, u32[]{:S(2)}, u32[]{:S(2)}) %collective-permute-start.1) | collective-permute-done | bytes 884768 | tf_op jit(solution)/shard_map/ppermute | solution.py:248
  48.2 3.9 %collective-permute-start.2 = (bf16[27,32,512]{2,1,0:T(8,128)(2,1)}, bf16[27,32,512]{2,1,0:T(8,128)(2,1)}, u32[]{:S(2)}, u32[]{:S(2)}) collective-permute-start(bf16[27,32,512]{2,1,0:T(8,128)(2,1)} %collective-permute-done.1.rest_3_), channel_id=1, source_target_pairs={{0,1},{1,2},{2,3},{3,4},{4,5},{5,6},{6,7},{7,0},{16,23},{17,16},{1... | collective-permute-start | bytes 2654216 | tf_op jit(solution)/shard_map/ppermute | solution.py:248
  52.1 2.2 %collective-permute-start.4 = (bf16[27,32,512]{2,1,0:T(8,128)(2,1)}, bf16[27,32,512]{2,1,0:T(8,128)(2,1)}, u32[]{:S(2)}, u32[]{:S(2)}) collective-permute-start(bf16[27,32,512]{2,1,0:T(8,128)(2,1)} %collective-permute-done.1.rest_3_), channel_id=1, source_target_pairs={{0,16},{16,0},{1,17},{17,1},{2,18},{18,2},{3,19},{19,3},{4,20},{20... | collective-permute-start | bytes 2654216 | tf_op jit(solution)/shard_map/ppermute | solution.py:250
  54.3 0.0 collective-permute-done.3.rest_2_
  54.4 0.0 copy-start.1
  54.4 1.0 copy-done.1
  55.3 7.7 %all-to-all-done.got = bf16[32,144,128]{2,1,0:T(8,128)(2,1)S(1)} async-done(((bf16[32,144,128]{2,1,0:T(8,128)(2,1)}), bf16[32,144,128]{2,1,0:T(8,128)(2,1)S(1)}, u32[]{:S(2)}, u32[]{:S(2)}) %all-to-all-start) | async-done | bytes 1179680 | tf_op jit(solution)/shard_map/all_to_all | solution.py:238
  63.0 0.0 collective-permute-done.2.rest_5_
  63.0 0.0 collective-permute-done.4.rest_4_
  63.0 2.1 %shard_map.65 = (bf16[48,32,128]{2,1,0:T(8,128)(2,1)}, bf16[48,32,128]{2,1,0:T(8,128)(2,1)}) custom-call(bf16[32,144,128]{2,1,0:T(8,128)(2,1)S(1)} %all-to-all-done.got), custom_call_target="tpu_custom_call" | custom-call | tf_op jit(solution)/shard_map/pallas_call | solution.py:284
  65.1 0.0 copy-start.2
  65.1 6.4 %all-to-all-start.2 = ((bf16[8,6,32,128]{3,2,1,0:T(8,128)(2,1)}), bf16[8,6,32,128]{3,2,1,0:T(8,128)(2,1)S(1)}, u32[]{:S(2)}, u32[]{:S(2)}) async-start(bf16[8,6,32,128]{3,2,1,0:T(8,128)(2,1)} %bitcast.2), calls=%async_computation.2 | async-start | bytes 786432 | tf_op jit(solution)/shard_map/all_to_all | solution.py:238
  71.5 4.8 %collective-permute-start.5 = (bf16[27,32,512]{2,1,0:T(8,128)(2,1)}, bf16[27,32,512]{2,1,0:T(8,128)(2,1)}, u32[]{:S(2)}, u32[]{:S(2)}) collective-permute-start(bf16[27,32,512]{2,1,0:T(8,128)(2,1)} %collective-permute-done.2.rest_5_), channel_id=1, source_target_pairs={{0,16},{16,0},{1,17},{17,1},{2,18},{18,2},{3,19},{19,3},{4,20},{20... | collective-permute-start | bytes 2654216 | tf_op jit(solution)/shard_map/ppermute | solution.py:250
  76.3 4.9 %collective-permute-start.6 = (bf16[27,32,512]{2,1,0:T(8,128)(2,1)}, bf16[27,32,512]{2,1,0:T(8,128)(2,1)}, u32[]{:S(2)}, u32[]{:S(2)}) collective-permute-start(bf16[27,32,512]{2,1,0:T(8,128)(2,1)} %collective-permute-done.2.rest_5_), channel_id=1, source_target_pairs={{0,1},{1,2},{2,3},{3,4},{4,5},{5,6},{6,7},{7,0},{16,23},{17,16},{1... | collective-permute-start | bytes 2654216 | tf_op jit(solution)/shard_map/ppermute | solution.py:248
  81.2 1.6 all-to-all-done.2.frames
  82.8 0.0 copy-start.3
  82.8 0.7 copy-done.3
  83.5 3.5 %all-to-all-start.1 = ((bf16[8,6,32,128]{3,2,1,0:T(8,128)(2,1)}), bf16[8,6,32,128]{3,2,1,0:T(8,128)(2,1)S(1)}, u32[]{:S(2)}, u32[]{:S(2)}) async-start(bf16[8,6,32,128]{3,2,1,0:T(8,128)(2,1)} %bitcast.1), calls=%async_computation.1 | async-start | bytes 786432 | tf_op jit(solution)/shard_map/all_to_all | solution.py:238
  87.0 0.0 collective-permute-done.5.rest_6_
  87.0 5.4 %collective-permute-done.6.rest_7_ = bf16[27,32,512]{2,1,0:T(8,128)(2,1)} collective-permute-done((bf16[27,32,512]{2,1,0:T(8,128)(2,1)}, bf16[27,32,512]{2,1,0:T(8,128)(2,1)}, u32[]{:S(2)}, u32[]{:S(2)}) %collective-permute-start.6) | collective-permute-done | bytes 884768 | tf_op jit(solution)/shard_map/ppermute | solution.py:248
  92.4 0.0 copy-done
  92.4 0.0 copy-done.5
  92.4 0.0 copy-done.2
  92.4 0.0 copy-start.4
  92.4 1.0 copy-done.4
  93.4 4.0 %shard_map.67 = (f32[128,512]{1,0:T(8,128)S(1)}, f32[128,512]{1,0:T(8,128)S(1)}) custom-call(s32[4]{0:T(128)S(1)} %copy-done.5, bf16[8,6,32,128]{3,2,1,0:T(8,128)(2,1)S(1)} %copy-done.4, bf16[27,32,512]{2,1,0:T(8,128)(2,1)S(1)} %bitcast.7, bf16[27,32,512]{2,1,0:T(8,128)(2,1)S(1)} %collective-permute-done.rest_1_, bf16[27,32,512]{2,1,0:T(8,128)(2,1)S(1)} %copy-done.2, ...), custom_call_target="tpu_custom_call" | custom-call | tf_op jit(solution)/shard_map/pallas_call | solution.py:255
  97.4 8.8 %collective-permute-start.7 = (f32[128,512]{1,0:T(8,128)S(1)}, f32[128,512]{1,0:T(8,128)S(1)}, u32[]{:S(2)}, u32[]{:S(2)}) collective-permute-start(f32[128,512]{1,0:T(8,128)S(1)} %get-tuple-element.25), channel_id=1, source_target_pairs={{0,16},{16,32},{32,48},{48,64},{64,80},{80,96},{96,112},{112,128},... | collective-permute-start | bytes 786440 | tf_op jit(solution)/shard_map/ppermute | solution.py:302
  106.3 3.3 %collective-permute-done.7 = f32[128,512]{1,0:T(8,128)S(1)} collective-permute-done((f32[128,512]{1,0:T(8,128)S(1)}, f32[128,512]{1,0:T(8,128)S(1)}, u32[]{:S(2)}, u32[]{:S(2)}) %collective-permute-start.7) | collective-permute-done | bytes 262176 | tf_op jit(solution)/shard_map/ppermute | solution.py:302
  109.6 7.9 %collective-permute-start.8 = (f32[128,512]{1,0:T(8,128)S(1)}, f32[128,512]{1,0:T(8,128)}, u32[]{:S(2)}, u32[]{:S(2)}) collective-permute-start(f32[128,512]{1,0:T(8,128)S(1)} %add.6), channel_id=1, source_target_pairs={{0,8},{8,0},{1,9},{9,1},{2,10},{10,2},{3,11},{11,3},{4,12},{12,4},... | collective-permute-start | bytes 786440 | tf_op jit(solution)/shard_map/ppermute | solution.py:305
  117.5 0.0 all-to-all-done.1.frames
  117.6 4.0 %shard_map.66 = (f32[128,512]{1,0:T(8,128)S(1)}, f32[128,512]{1,0:T(8,128)S(1)}) custom-call(s32[4]{0:T(128)S(1)} %copy-done.5, bf16[8,6,32,128]{3,2,1,0:T(8,128)(2,1)S(1)} %all-to-all-done.1.frames, bf16[27,32,512]{2,1,0:T(8,128)(2,1)S(1)} %bitcast.8, bf16[27,32,512]{2,1,0:T(8,128)(2,1)S(1)} %collective-permute-done.rest_1_, ...), custom_call_target="tpu_custom_call" | custom-call | tf_op jit(solution)/shard_map/pallas_call | solution.py:255
  121.6 0.0 copy-start.6
  121.6 0.0 copy-start.7
  121.6 4.7 %collective-permute-start.9 = (f32[128,512]{1,0:T(8,128)S(1)}, f32[128,512]{1,0:T(8,128)S(1)}, u32[]{:S(2)}, u32[]{:S(2)}) collective-permute-start(f32[128,512]{1,0:T(8,128)S(1)} %get-tuple-element.26), channel_id=1, source_target_pairs={{0,16},{16,32},{32,48},{48,64},{64,80},{80,96},{96,112},{112,128},... | collective-permute-start | bytes 786440 | tf_op jit(solution)/shard_map/ppermute | solution.py:304
  126.3 0.0 collective-permute-done.8
  126.3 1.0 add.7.near
  127.3 2.3 %collective-permute-done.9.before = f32[128,512]{1,0:T(8,128)S(1)} collective-permute-done((f32[128,512]{1,0:T(8,128)S(1)}, f32[128,512]{1,0:T(8,128)S(1)}, u32[]{:S(2)}, u32[]{:S(2)}) %collective-permute-start.9) | collective-permute-done | bytes 262176 | tf_op jit(solution)/shard_map/ppermute | solution.py:304
  129.6 0.9 shard_map.68
  130.5 15.7 %all_to_all.25.got = f32[16,8,128]{2,1,0:T(8,128)} all-to-all(f32[16,8,128]{2,1,0:T(8,128)S(1)} %get-tuple-element.27), channel_id=1, replica_groups=mesh['zl'=4,'x'=4,'co'=2,'zh'=2,'y'=8] {'y','co'}, dimensions={0} | all-to-all | bytes 131072 | tf_op jit(solution)/shard_map/all_to_all | solution.py:238
  146.2 1.5 shard_map.69
  147.7 22.3 %all_to_all.26.got = f32[32,8,128]{2,1,0:T(8,128)S(1)} all-to-all(f32[32,8,128]{2,1,0:T(8,128)} %shard_map.69), channel_id=1, replica_groups=mesh['zl'=4,'x'=4,'co'=2,'zh'=2,'y'=8] {'zl','zh','x'}, dimensions={0} | all-to-all | bytes 262144 | tf_op jit(solution)/shard_map/all_to_all | solution.py:238
  170.0 0.0 copy-done.6
  170.1 0.0 copy-done.7
  170.1 1.5 shard_map.70
  (1 shorter events, 0.0 us)
Async XLA Ops:
  0.0 33.9 %collective-permute-start = (bf16[27,32,512]{2,1,0:T(8,128)(2,1)}, bf16[27,32,512]{2,1,0:T(8,128)(2,1)S(1)}, u32[]{:S(2)}, u32[]{:S(2)}) collective-permute-start(bf16[27,32,512]{2,1,0:T(8,128)(2,1)} %bitcast.6), channel_id=1, source_target_pairs={{0,1},{1,2},{2,3},{3,4},{4,5},{5,6},{6,7},{7,0},{16,23},{17,16},{1... | collective-permute-start | bytes 2654216 | tf_op jit(solution)/shard_map/ppermute | solution.py:248
  23.8 39.1 %all-to-all-start = ((bf16[32,144,128]{2,1,0:T(8,128)(2,1)}), bf16[32,144,128]{2,1,0:T(8,128)(2,1)S(1)}, u32[]{:S(2)}, u32[]{:S(2)}) async-start(bf16[32,144,128]{2,1,0:T(8,128)(2,1)} %shard_map.64), calls=%async_computation | async-start | bytes 2359296 | tf_op jit(solution)/shard_map/all_to_all | solution.py:238
  33.9 58.6 %copy-start = (bf16[3,3,3,32,512]{4,3,2,1,0:T(8,128)(2,1)S(1)}, bf16[3,3,3,32,512]{4,3,2,1,0:T(8,128)(2,1)}, u32[]{:S(2)}) copy-start(bf16[3,3,3,32,512]{4,3,2,1,0:T(8,128)(2,1)} %param.9) | copy-start | bytes 2654212
  33.9 58.5 %copy-start.5 = (s32[4]{0:T(128)S(1)}, s32[4]{0:T(128)}, u32[]{:S(2)}) copy-start(s32[4]{0:T(128)} %lengths.7) | copy-start | bytes 52
  33.9 14.3 %collective-permute-start.1 = (bf16[27,32,512]{2,1,0:T(8,128)(2,1)S(1)}, bf16[27,32,512]{2,1,0:T(8,128)(2,1)}, u32[]{:S(2)}, u32[]{:S(2)}) collective-permute-start(bf16[27,32,512]{2,1,0:T(8,128)(2,1)S(1)} %collective-permute-done.rest_1_), channel_id=1, source_target_pairs={{0,1},{1,2},{2,3},{3,4},{4,5},{5,6},{6,7},{7,0},{16,23},{17,16},{1... | collective-permute-start | bytes 2654216 | tf_op jit(solution)/shard_map/ppermute | solution.py:248
  37.0 17.3 %collective-permute-start.3 = (bf16[27,32,512]{2,1,0:T(8,128)(2,1)S(1)}, bf16[27,32,512]{2,1,0:T(8,128)(2,1)S(1)}, u32[]{:S(2)}, u32[]{:S(2)}) collective-permute-start(bf16[27,32,512]{2,1,0:T(8,128)(2,1)S(1)} %collective-permute-done.rest_1_), channel_id=1, source_target_pairs={{0,16},{16,0},{1,17},{17,1},{2,18},{18,2},{3,19},{19,3},{4,20},{20... | collective-permute-start | bytes 2654216 | tf_op jit(solution)/shard_map/ppermute | solution.py:250
  48.2 14.8 %collective-permute-start.2 = (bf16[27,32,512]{2,1,0:T(8,128)(2,1)}, bf16[27,32,512]{2,1,0:T(8,128)(2,1)}, u32[]{:S(2)}, u32[]{:S(2)}) collective-permute-start(bf16[27,32,512]{2,1,0:T(8,128)(2,1)} %collective-permute-done.1.rest_3_), channel_id=1, source_target_pairs={{0,1},{1,2},{2,3},{3,4},{4,5},{5,6},{6,7},{7,0},{16,23},{17,16},{1... | collective-permute-start | bytes 2654216 | tf_op jit(solution)/shard_map/ppermute | solution.py:248
  52.1 10.9 %collective-permute-start.4 = (bf16[27,32,512]{2,1,0:T(8,128)(2,1)}, bf16[27,32,512]{2,1,0:T(8,128)(2,1)}, u32[]{:S(2)}, u32[]{:S(2)}) collective-permute-start(bf16[27,32,512]{2,1,0:T(8,128)(2,1)} %collective-permute-done.1.rest_3_), channel_id=1, source_target_pairs={{0,16},{16,0},{1,17},{17,1},{2,18},{18,2},{3,19},{19,3},{4,20},{20... | collective-permute-start | bytes 2654216 | tf_op jit(solution)/shard_map/ppermute | solution.py:250
  54.4 1.0 copy-start.1
  65.1 27.3 %copy-start.2 = (bf16[27,32,512]{2,1,0:T(8,128)(2,1)S(1)}, bf16[27,32,512]{2,1,0:T(8,128)(2,1)}, u32[]{:S(2)}) copy-start(bf16[27,32,512]{2,1,0:T(8,128)(2,1)} %copy-done.1) | copy-start | bytes 2654212
  65.1 17.7 %all-to-all-start.2 = ((bf16[8,6,32,128]{3,2,1,0:T(8,128)(2,1)}), bf16[8,6,32,128]{3,2,1,0:T(8,128)(2,1)S(1)}, u32[]{:S(2)}, u32[]{:S(2)}) async-start(bf16[8,6,32,128]{3,2,1,0:T(8,128)(2,1)} %bitcast.2), calls=%async_computation.2 | async-start | bytes 786432 | tf_op jit(solution)/shard_map/all_to_all | solution.py:238
  71.5 15.5 %collective-permute-start.5 = (bf16[27,32,512]{2,1,0:T(8,128)(2,1)}, bf16[27,32,512]{2,1,0:T(8,128)(2,1)}, u32[]{:S(2)}, u32[]{:S(2)}) collective-permute-start(bf16[27,32,512]{2,1,0:T(8,128)(2,1)} %collective-permute-done.2.rest_5_), channel_id=1, source_target_pairs={{0,16},{16,0},{1,17},{17,1},{2,18},{18,2},{3,19},{19,3},{4,20},{20... | collective-permute-start | bytes 2654216 | tf_op jit(solution)/shard_map/ppermute | solution.py:250
  76.3 16.1 %collective-permute-start.6 = (bf16[27,32,512]{2,1,0:T(8,128)(2,1)}, bf16[27,32,512]{2,1,0:T(8,128)(2,1)}, u32[]{:S(2)}, u32[]{:S(2)}) collective-permute-start(bf16[27,32,512]{2,1,0:T(8,128)(2,1)} %collective-permute-done.2.rest_5_), channel_id=1, source_target_pairs={{0,1},{1,2},{2,3},{3,4},{4,5},{5,6},{6,7},{7,0},{16,23},{17,16},{1... | collective-permute-start | bytes 2654216 | tf_op jit(solution)/shard_map/ppermute | solution.py:248
  82.8 0.7 copy-start.3
  83.5 34.0 %all-to-all-start.1 = ((bf16[8,6,32,128]{3,2,1,0:T(8,128)(2,1)}), bf16[8,6,32,128]{3,2,1,0:T(8,128)(2,1)S(1)}, u32[]{:S(2)}, u32[]{:S(2)}) async-start(bf16[8,6,32,128]{3,2,1,0:T(8,128)(2,1)} %bitcast.1), calls=%async_computation.1 | async-start | bytes 786432 | tf_op jit(solution)/shard_map/all_to_all | solution.py:238
  92.4 1.0 copy-start.4
  97.4 12.1 %collective-permute-start.7 = (f32[128,512]{1,0:T(8,128)S(1)}, f32[128,512]{1,0:T(8,128)S(1)}, u32[]{:S(2)}, u32[]{:S(2)}) collective-permute-start(f32[128,512]{1,0:T(8,128)S(1)} %get-tuple-element.25), channel_id=1, source_target_pairs={{0,16},{16,32},{32,48},{48,64},{64,80},{80,96},{96,112},{112,128},... | collective-permute-start | bytes 786440 | tf_op jit(solution)/shard_map/ppermute | solution.py:302
  109.6 16.7 %collective-permute-start.8 = (f32[128,512]{1,0:T(8,128)S(1)}, f32[128,512]{1,0:T(8,128)}, u32[]{:S(2)}, u32[]{:S(2)}) collective-permute-start(f32[128,512]{1,0:T(8,128)S(1)} %add.6), channel_id=1, source_target_pairs={{0,8},{8,0},{1,9},{9,1},{2,10},{10,2},{3,11},{11,3},{4,12},{12,4},... | collective-permute-start | bytes 786440 | tf_op jit(solution)/shard_map/ppermute | solution.py:305
  121.6 48.4 %copy-start.6 = (f32[512]{0:T(512)S(1)}, f32[512]{0:T(512)}, u32[]{:S(2)}) copy-start(f32[512]{0:T(512)} %param.10) | copy-start | bytes 6148
  121.6 48.4 %copy-start.7 = (f32[512]{0:T(512)S(1)}, f32[512]{0:T(512)}, u32[]{:S(2)}) copy-start(f32[512]{0:T(512)} %param.11) | copy-start | bytes 6148
  121.6 8.0 %collective-permute-start.9 = (f32[128,512]{1,0:T(8,128)S(1)}, f32[128,512]{1,0:T(8,128)S(1)}, u32[]{:S(2)}, u32[]{:S(2)}) collective-permute-start(f32[128,512]{1,0:T(8,128)S(1)} %get-tuple-element.26), channel_id=1, source_target_pairs={{0,16},{16,32},{32,48},{48,64},{64,80},{80,96},{96,112},{112,128},... | collective-permute-start | bytes 786440 | tf_op jit(solution)/shard_map/ppermute | solution.py:304

commit v4 on v3

--- a/solution.py
+++ b/solution.py
@@ -243,11 +243,9 @@
             for c in range(2) for y in range(NY)]
     swap = [(0, 1), (1, 0)]
     moved = [kernel]
-    swapped = []
-    for step in range(4):
+    for _ in range(4):
         moved.append(lax.ppermute(moved[-1], ("co", "y"), ring))
-        if step < 3:
-            swapped.append(lax.ppermute(moved[-1], "co", swap))
+    swapped = [lax.ppermute(shard, "co", swap) for shard in moved[1:4]]
     return moved, swapped
 
 
@@ -275,7 +273,7 @@
             pltpu.VMEM((SLABS, 16, 128), BF),
             pltpu.SemaphoreType.DMA((2,)),
         ],
-        compiler_params=params(60),
+        compiler_params=params(8),
     )(row_target, arrived)
     got = shuffle(send, TM)
     got, moved[3], swapped[0], swapped[1] = lax.optimization_barrier(

time: 172 us -> 160 us (0.930)
  Pallas kernels: 32 us -> 16.2 us
  starting transfers between devices: 68 us -> 75.9 us
  waiting for transfers between devices: 29.6 us -> 23.2 us
    pallas_call x1, Pallas kernels: 17.9 us -> 2.14 us  [body(): pl.pallas_call(pack_kernel, out_shape=jax.ShapeDtypeStruct((SLABS, 144, 1...]
    ppermute x3, starting transfers between devices: 8.94 us -> 15.5 us  [gathered_weights(): swapped = [lax.ppermute(shard, 'co', swap) for shard in moved[1:4]]]
    all_to_all x3, waiting for transfers between devices: 9.3 us -> 4.64 us  [shuffle(): return lax.all_to_all(x, axis, split_axis=0, concat_axis=0, tiled=True)]
    unnamed x16 -> x20, local copies, waits for them, and re-layouts: 2.72 us -> 4.41 us
  transfers between devices with their start and end apart: 13 -> 13, of which waited for: 6 -> 5; matrix products, arithmetic and copies ran while one was open for 1% -> 1% of each run, Pallas kernels for 15% -> 6%
where the time goes in v4:
time: 160 us; the launch traced here: 159 us
  starting transfers between devices  75.9 us (47%)
  blocking collectives  38.3 us (24%)
  waiting for transfers between devices  23.2 us (14%)
  Pallas kernels  16.2 us (10%)
  local copies, waits for them, and re-layouts  4.41 us (3%)
    all_to_all x2, blocking collectives, shuffle(): return lax.all_to_all(x, axis, split_axis=0, concat_axis=0, tiled=True)  38.3 us
    all_to_all x3, starting transfers between devices, shuffle(): return lax.all_to_all(x, axis, split_axis=0, concat_axis=0, tiled=True)  20.6 us
    ppermute x4, starting transfers between devices, gathered_weights(): moved.append(lax.ppermute(moved[-1], ('co', 'y'), ring))  17.7 us
    ppermute x3, starting transfers between devices, gathered_weights(): swapped = [lax.ppermute(shard, 'co', swap) for shard in moved[1:4]]  15.5 us
    ppermute x4, waiting for transfers between devices, gathered_weights(): moved.append(lax.ppermute(moved[-1], ('co', 'y'), ring))  13 us
    ppermute x1, starting transfers between devices, body(): far = lax.ppermute(far + far_before, 'zh', [(0, 1), (1, 0)])  9.51 us
    pallas_call x2, Pallas kernels, convolve(): pl.pallas_call(conv_kernel, out_shape=[jax.ShapeDtypeStruct((128, COUT),...  8.07 us
    ppermute x1, starting transfers between devices, body(): far_before = lax.ppermute(far_after, TM, onward)  7.85 us
  transfers between devices with their start and end apart: 13, of which 5 were waited for; matrix products, arithmetic and copies ran while one was open for 1% of the time, Pallas kernels for 6%

profile of v4, /device:TPU:1, one launch (start us, length us, event | category | flops | bytes accessed | tf_op | source)
XLA Modules:
  0.0 159.3 jit_solution(13606049964375276635)
XLA Ops:
  0.0 5.9 %collective-permute-start = (bf16[27,32,512]{2,1,0:T(8,128)(2,1)}, bf16[27,32,512]{2,1,0:T(8,128)(2,1)S(1)}, u32[]{:S(2)}, u32[]{:S(2)}) collective-permute-start(bf16[27,32,512]{2,1,0:T(8,128)(2,1)} %bitcast.6), channel_id=1, source_target_pairs={{0,1},{1,2},{2,3},{3,4},{4,5},{5,6},{6,7},{7,0},{16,23},{17,16},{1... | collective-permute-start | bytes 2654216 | tf_op jit(solution)/shard_map/ppermute | solution.py:247
  5.9 0.0 copy-start.5
  5.9 1.0 copy-done.5
  7.0 0.0 copy-start.9
  7.0 0.7 copy-done.9
  7.6 2.1 %shard_map.64 = bf16[32,144,128]{2,1,0:T(8,128)(2,1)} custom-call(s32[64]{0:T(128)S(1)} %copy-done.9, bf16[64,32,128]{2,1,0:T(8,128)(2,1)S(1)} %copy-done.5), custom_call_target="tpu_custom_call" | custom-call | tf_op jit(solution)/shard_map/pallas_call | solution.py:265
  9.8 10.0 %all-to-all-start = ((bf16[32,144,128]{2,1,0:T(8,128)(2,1)}), bf16[32,144,128]{2,1,0:T(8,128)(2,1)S(1)}, u32[]{:S(2)}, u32[]{:S(2)}) async-start(bf16[32,144,128]{2,1,0:T(8,128)(2,1)} %shard_map.64), calls=%async_computation | async-start | bytes 2359296 | tf_op jit(solution)/shard_map/all_to_all | solution.py:238
  19.8 0.0 copy-start
  19.8 0.0 copy-start.6
  19.8 0.0 collective-permute-done.rest_1_
  19.8 3.1 %collective-permute-start.1 = (bf16[27,32,512]{2,1,0:T(8,128)(2,1)S(1)}, bf16[27,32,512]{2,1,0:T(8,128)(2,1)}, u32[]{:S(2)}, u32[]{:S(2)}) collective-permute-start(bf16[27,32,512]{2,1,0:T(8,128)(2,1)S(1)} %collective-permute-done.rest_1_), channel_id=1, source_target_pairs={{0,1},{1,2},{2,3},{3,4},{4,5},{5,6},{6,7},{7,0},{16,23},{17,16},{1... | collective-permute-start | bytes 2654216 | tf_op jit(solution)/shard_map/ppermute | solution.py:247
  22.9 4.1 %collective-permute-start.3 = (bf16[27,32,512]{2,1,0:T(8,128)(2,1)S(1)}, bf16[27,32,512]{2,1,0:T(8,128)(2,1)S(1)}, u32[]{:S(2)}, u32[]{:S(2)}) collective-permute-start(bf16[27,32,512]{2,1,0:T(8,128)(2,1)S(1)} %collective-permute-done.rest_1_), channel_id=1, source_target_pairs={{0,16},{16,0},{1,17},{17,1},{2,18},{18,2},{3,19},{19,3},{4,20},{20... | collective-permute-start | bytes 2654216 | tf_op jit(solution)/shard_map/ppermute | solution.py:248
  27.1 7.1 %collective-permute-done.1.rest_3_ = bf16[27,32,512]{2,1,0:T(8,128)(2,1)} collective-permute-done((bf16[27,32,512]{2,1,0:T(8,128)(2,1)S(1)}, bf16[27,32,512]{2,1,0:T(8,128)(2,1)}, u32[]{:S(2)}, u32[]{:S(2)}) %collective-permute-start.1) | collective-permute-done | bytes 884768 | tf_op jit(solution)/shard_map/ppermute | solution.py:247
  34.1 3.9 %collective-permute-start.2 = (bf16[27,32,512]{2,1,0:T(8,128)(2,1)}, bf16[27,32,512]{2,1,0:T(8,128)(2,1)}, u32[]{:S(2)}, u32[]{:S(2)}) collective-permute-start(bf16[27,32,512]{2,1,0:T(8,128)(2,1)} %collective-permute-done.1.rest_3_), channel_id=1, source_target_pairs={{0,1},{1,2},{2,3},{3,4},{4,5},{5,6},{6,7},{7,0},{16,23},{17,16},{1... | collective-permute-start | bytes 2654216 | tf_op jit(solution)/shard_map/ppermute | solution.py:247
  38.0 5.3 %collective-permute-start.4 = (bf16[27,32,512]{2,1,0:T(8,128)(2,1)}, bf16[27,32,512]{2,1,0:T(8,128)(2,1)}, u32[]{:S(2)}, u32[]{:S(2)}) collective-permute-start(bf16[27,32,512]{2,1,0:T(8,128)(2,1)} %collective-permute-done.1.rest_3_), channel_id=1, source_target_pairs={{0,16},{16,0},{1,17},{17,1},{2,18},{18,2},{3,19},{19,3},{4,20},{20... | collective-permute-start | bytes 2654216 | tf_op jit(solution)/shard_map/ppermute | solution.py:248
  43.3 0.0 collective-permute-done.3.rest_2_
  43.3 0.0 copy-start.1
  43.3 0.9 copy-done.1
  44.3 4.6 %all-to-all-done.got = bf16[32,144,128]{2,1,0:T(8,128)(2,1)S(1)} async-done(((bf16[32,144,128]{2,1,0:T(8,128)(2,1)}), bf16[32,144,128]{2,1,0:T(8,128)(2,1)S(1)}, u32[]{:S(2)}, u32[]{:S(2)}) %all-to-all-start) | async-done | bytes 1179680 | tf_op jit(solution)/shard_map/all_to_all | solution.py:238
  48.9 0.0 collective-permute-done.2.rest_5_
  48.9 0.0 collective-permute-done.4.rest_4_
  48.9 2.1 %shard_map.65 = (bf16[48,32,128]{2,1,0:T(8,128)(2,1)}, bf16[48,32,128]{2,1,0:T(8,128)(2,1)}) custom-call(bf16[32,144,128]{2,1,0:T(8,128)(2,1)S(1)} %all-to-all-done.got), custom_call_target="tpu_custom_call" | custom-call | tf_op jit(solution)/shard_map/pallas_call | solution.py:282
  51.0 0.0 copy-start.2
  51.0 6.4 %all-to-all-start.2 = ((bf16[8,6,32,128]{3,2,1,0:T(8,128)(2,1)}), bf16[8,6,32,128]{3,2,1,0:T(8,128)(2,1)S(1)}, u32[]{:S(2)}, u32[]{:S(2)}) async-start(bf16[8,6,32,128]{3,2,1,0:T(8,128)(2,1)} %bitcast.2), calls=%async_computation.2 | async-start | bytes 786432 | tf_op jit(solution)/shard_map/all_to_all | solution.py:238
  57.4 6.1 %collective-permute-start.5 = (bf16[27,32,512]{2,1,0:T(8,128)(2,1)}, bf16[27,32,512]{2,1,0:T(8,128)(2,1)}, u32[]{:S(2)}, u32[]{:S(2)}) collective-permute-start(bf16[27,32,512]{2,1,0:T(8,128)(2,1)} %collective-permute-done.2.rest_5_), channel_id=1, source_target_pairs={{0,16},{16,0},{1,17},{17,1},{2,18},{18,2},{3,19},{19,3},{4,20},{20... | collective-permute-start | bytes 2654216 | tf_op jit(solution)/shard_map/ppermute | solution.py:248
  63.6 4.8 %collective-permute-start.6 = (bf16[27,32,512]{2,1,0:T(8,128)(2,1)}, bf16[27,32,512]{2,1,0:T(8,128)(2,1)}, u32[]{:S(2)}, u32[]{:S(2)}) collective-permute-start(bf16[27,32,512]{2,1,0:T(8,128)(2,1)} %collective-permute-done.2.rest_5_), channel_id=1, source_target_pairs={{0,1},{1,2},{2,3},{3,4},{4,5},{5,6},{6,7},{7,0},{16,23},{17,16},{1... | collective-permute-start | bytes 2654216 | tf_op jit(solution)/shard_map/ppermute | solution.py:247
  68.4 0.0 all-to-all-done.2.frames
  68.4 0.0 copy-start.3
  68.4 0.7 copy-done.3
  69.1 4.2 %all-to-all-start.1 = ((bf16[8,6,32,128]{3,2,1,0:T(8,128)(2,1)}), bf16[8,6,32,128]{3,2,1,0:T(8,128)(2,1)S(1)}, u32[]{:S(2)}, u32[]{:S(2)}) async-start(bf16[8,6,32,128]{3,2,1,0:T(8,128)(2,1)} %bitcast.1), calls=%async_computation.1 | async-start | bytes 786432 | tf_op jit(solution)/shard_map/all_to_all | solution.py:238
  73.4 0.0 collective-permute-done.5.rest_6_
  73.4 5.9 %collective-permute-done.6.rest_7_ = bf16[27,32,512]{2,1,0:T(8,128)(2,1)} collective-permute-done((bf16[27,32,512]{2,1,0:T(8,128)(2,1)}, bf16[27,32,512]{2,1,0:T(8,128)(2,1)}, u32[]{:S(2)}, u32[]{:S(2)}) %collective-permute-start.6) | collective-permute-done | bytes 884768 | tf_op jit(solution)/shard_map/ppermute | solution.py:247
  79.3 0.0 copy-done
  79.3 0.0 copy-done.6
  79.3 0.0 copy-done.2
  79.3 0.0 copy-start.4
  79.3 1.0 copy-done.4
  80.3 4.0 %shard_map.67 = (f32[128,512]{1,0:T(8,128)S(1)}, f32[128,512]{1,0:T(8,128)S(1)}) custom-call(s32[4]{0:T(128)S(1)} %copy-done.6, bf16[8,6,32,128]{3,2,1,0:T(8,128)(2,1)S(1)} %copy-done.4, bf16[27,32,512]{2,1,0:T(8,128)(2,1)S(1)} %bitcast.7, bf16[27,32,512]{2,1,0:T(8,128)(2,1)S(1)} %collective-permute-done.rest_1_, bf16[27,32,512]{2,1,0:T(8,128)(2,1)S(1)} %copy-done.2, ...), custom_call_target="tpu_custom_call" | custom-call | tf_op jit(solution)/shard_map/pallas_call | solution.py:253
  84.3 7.8 %collective-permute-start.7 = (f32[128,512]{1,0:T(8,128)S(1)}, f32[128,512]{1,0:T(8,128)S(1)}, u32[]{:S(2)}, u32[]{:S(2)}) collective-permute-start(f32[128,512]{1,0:T(8,128)S(1)} %get-tuple-element.25), channel_id=1, source_target_pairs={{0,16},{16,32},{32,48},{48,64},{64,80},{80,96},{96,112},{112,128},... | collective-permute-start | bytes 786440 | tf_op jit(solution)/shard_map/ppermute | solution.py:300
  92.2 3.3 %collective-permute-done.7 = f32[128,512]{1,0:T(8,128)S(1)} collective-permute-done((f32[128,512]{1,0:T(8,128)S(1)}, f32[128,512]{1,0:T(8,128)S(1)}, u32[]{:S(2)}, u32[]{:S(2)}) %collective-permute-start.7) | collective-permute-done | bytes 262176 | tf_op jit(solution)/shard_map/ppermute | solution.py:300
  95.5 9.5 %collective-permute-start.8 = (f32[128,512]{1,0:T(8,128)S(1)}, f32[128,512]{1,0:T(8,128)}, u32[]{:S(2)}, u32[]{:S(2)}) collective-permute-start(f32[128,512]{1,0:T(8,128)S(1)} %add.6), channel_id=1, source_target_pairs={{0,8},{8,0},{1,9},{9,1},{2,10},{10,2},{3,11},{11,3},{4,12},{12,4},... | collective-permute-start | bytes 786440 | tf_op jit(solution)/shard_map/ppermute | solution.py:303
  105.0 0.0 all-to-all-done.1.frames
  105.0 4.0 %shard_map.66 = (f32[128,512]{1,0:T(8,128)S(1)}, f32[128,512]{1,0:T(8,128)S(1)}) custom-call(s32[4]{0:T(128)S(1)} %copy-done.6, bf16[8,6,32,128]{3,2,1,0:T(8,128)(2,1)S(1)} %all-to-all-done.1.frames, bf16[27,32,512]{2,1,0:T(8,128)(2,1)S(1)} %bitcast.8, bf16[27,32,512]{2,1,0:T(8,128)(2,1)S(1)} %collective-permute-done.rest_1_, ...), custom_call_target="tpu_custom_call" | custom-call | tf_op jit(solution)/shard_map/pallas_call | solution.py:253
  109.1 0.0 copy-start.7
  109.1 0.0 copy-start.8
  109.1 4.7 %collective-permute-start.9 = (f32[128,512]{1,0:T(8,128)S(1)}, f32[128,512]{1,0:T(8,128)S(1)}, u32[]{:S(2)}, u32[]{:S(2)}) collective-permute-start(f32[128,512]{1,0:T(8,128)S(1)} %get-tuple-element.26), channel_id=1, source_target_pairs={{0,16},{16,32},{32,48},{48,64},{64,80},{80,96},{96,112},{112,128},... | collective-permute-start | bytes 786440 | tf_op jit(solution)/shard_map/ppermute | solution.py:302
  113.8 0.0 collective-permute-done.8
  113.8 1.0 add.7.near
  114.8 2.3 %collective-permute-done.9.before = f32[128,512]{1,0:T(8,128)S(1)} collective-permute-done((f32[128,512]{1,0:T(8,128)S(1)}, f32[128,512]{1,0:T(8,128)S(1)}, u32[]{:S(2)}, u32[]{:S(2)}) %collective-permute-start.9) | collective-permute-done | bytes 262176 | tf_op jit(solution)/shard_map/ppermute | solution.py:302
  117.1 0.9 shard_map.68
  118.0 16.1 %all_to_all.25.got = f32[16,8,128]{2,1,0:T(8,128)} all-to-all(f32[16,8,128]{2,1,0:T(8,128)S(1)} %get-tuple-element.27), channel_id=1, replica_groups=mesh['zl'=4,'x'=4,'co'=2,'zh'=2,'y'=8] {'y','co'}, dimensions={0} | all-to-all | bytes 131072 | tf_op jit(solution)/shard_map/all_to_all | solution.py:238
  134.1 1.5 shard_map.69
  135.6 22.2 %all_to_all.26.got = f32[32,8,128]{2,1,0:T(8,128)S(1)} all-to-all(f32[32,8,128]{2,1,0:T(8,128)} %shard_map.69), channel_id=1, replica_groups=mesh['zl'=4,'x'=4,'co'=2,'zh'=2,'y'=8] {'zl','zh','x'}, dimensions={0} | all-to-all | bytes 262144 | tf_op jit(solution)/shard_map/all_to_all | solution.py:238
  157.8 0.0 copy-done.7
  157.8 0.0 copy-done.8
  157.8 1.5 shard_map.70
  (1 shorter events, 0.0 us)
Async XLA Ops:
  0.0 19.8 %collective-permute-start = (bf16[27,32,512]{2,1,0:T(8,128)(2,1)}, bf16[27,32,512]{2,1,0:T(8,128)(2,1)S(1)}, u32[]{:S(2)}, u32[]{:S(2)}) collective-permute-start(bf16[27,32,512]{2,1,0:T(8,128)(2,1)} %bitcast.6), channel_id=1, source_target_pairs={{0,1},{1,2},{2,3},{3,4},{4,5},{5,6},{6,7},{7,0},{16,23},{17,16},{1... | collective-permute-start | bytes 2654216 | tf_op jit(solution)/shard_map/ppermute | solution.py:247
  5.9 1.0 copy-start.5
  7.0 0.7 copy-start.9
  9.8 39.1 %all-to-all-start = ((bf16[32,144,128]{2,1,0:T(8,128)(2,1)}), bf16[32,144,128]{2,1,0:T(8,128)(2,1)S(1)}, u32[]{:S(2)}, u32[]{:S(2)}) async-start(bf16[32,144,128]{2,1,0:T(8,128)(2,1)} %shard_map.64), calls=%async_computation | async-start | bytes 2359296 | tf_op jit(solution)/shard_map/all_to_all | solution.py:238
  19.8 59.5 %copy-start = (bf16[3,3,3,32,512]{4,3,2,1,0:T(8,128)(2,1)S(1)}, bf16[3,3,3,32,512]{4,3,2,1,0:T(8,128)(2,1)}, u32[]{:S(2)}) copy-start(bf16[3,3,3,32,512]{4,3,2,1,0:T(8,128)(2,1)} %param.9) | copy-start | bytes 2654212
  19.8 59.5 %copy-start.6 = (s32[4]{0:T(128)S(1)}, s32[4]{0:T(128)}, u32[]{:S(2)}) copy-start(s32[4]{0:T(128)} %lengths.7) | copy-start | bytes 52
  19.8 14.3 %collective-permute-start.1 = (bf16[27,32,512]{2,1,0:T(8,128)(2,1)S(1)}, bf16[27,32,512]{2,1,0:T(8,128)(2,1)}, u32[]{:S(2)}, u32[]{:S(2)}) collective-permute-start(bf16[27,32,512]{2,1,0:T(8,128)(2,1)S(1)} %collective-permute-done.rest_1_), channel_id=1, source_target_pairs={{0,1},{1,2},{2,3},{3,4},{4,5},{5,6},{6,7},{7,0},{16,23},{17,16},{1... | collective-permute-start | bytes 2654216 | tf_op jit(solution)/shard_map/ppermute | solution.py:247
  22.9 20.4 %collective-permute-start.3 = (bf16[27,32,512]{2,1,0:T(8,128)(2,1)S(1)}, bf16[27,32,512]{2,1,0:T(8,128)(2,1)S(1)}, u32[]{:S(2)}, u32[]{:S(2)}) collective-permute-start(bf16[27,32,512]{2,1,0:T(8,128)(2,1)S(1)} %collective-permute-done.rest_1_), channel_id=1, source_target_pairs={{0,16},{16,0},{1,17},{17,1},{2,18},{18,2},{3,19},{19,3},{4,20},{20... | collective-permute-start | bytes 2654216 | tf_op jit(solution)/shard_map/ppermute | solution.py:248
  34.1 14.8 %collective-permute-start.2 = (bf16[27,32,512]{2,1,0:T(8,128)(2,1)}, bf16[27,32,512]{2,1,0:T(8,128)(2,1)}, u32[]{:S(2)}, u32[]{:S(2)}) collective-permute-start(bf16[27,32,512]{2,1,0:T(8,128)(2,1)} %collective-permute-done.1.rest_3_), channel_id=1, source_target_pairs={{0,1},{1,2},{2,3},{3,4},{4,5},{5,6},{6,7},{7,0},{16,23},{17,16},{1... | collective-permute-start | bytes 2654216 | tf_op jit(solution)/shard_map/ppermute | solution.py:247
  38.0 10.9 %collective-permute-start.4 = (bf16[27,32,512]{2,1,0:T(8,128)(2,1)}, bf16[27,32,512]{2,1,0:T(8,128)(2,1)}, u32[]{:S(2)}, u32[]{:S(2)}) collective-permute-start(bf16[27,32,512]{2,1,0:T(8,128)(2,1)} %collective-permute-done.1.rest_3_), channel_id=1, source_target_pairs={{0,16},{16,0},{1,17},{17,1},{2,18},{18,2},{3,19},{19,3},{4,20},{20... | collective-permute-start | bytes 2654216 | tf_op jit(solution)/shard_map/ppermute | solution.py:248
  43.3 1.0 copy-start.1
  51.0 28.3 %copy-start.2 = (bf16[27,32,512]{2,1,0:T(8,128)(2,1)S(1)}, bf16[27,32,512]{2,1,0:T(8,128)(2,1)}, u32[]{:S(2)}) copy-start(bf16[27,32,512]{2,1,0:T(8,128)(2,1)} %copy-done.1) | copy-start | bytes 2654212
  51.0 17.3 %all-to-all-start.2 = ((bf16[8,6,32,128]{3,2,1,0:T(8,128)(2,1)}), bf16[8,6,32,128]{3,2,1,0:T(8,128)(2,1)S(1)}, u32[]{:S(2)}, u32[]{:S(2)}) async-start(bf16[8,6,32,128]{3,2,1,0:T(8,128)(2,1)} %bitcast.2), calls=%async_computation.2 | async-start | bytes 786432 | tf_op jit(solution)/shard_map/all_to_all | solution.py:238
  57.4 16.0 %collective-permute-start.5 = (bf16[27,32,512]{2,1,0:T(8,128)(2,1)}, bf16[27,32,512]{2,1,0:T(8,128)(2,1)}, u32[]{:S(2)}, u32[]{:S(2)}) collective-permute-start(bf16[27,32,512]{2,1,0:T(8,128)(2,1)} %collective-permute-done.2.rest_5_), channel_id=1, source_target_pairs={{0,16},{16,0},{1,17},{17,1},{2,18},{18,2},{3,19},{19,3},{4,20},{20... | collective-permute-start | bytes 2654216 | tf_op jit(solution)/shard_map/ppermute | solution.py:248
  63.6 15.7 %collective-permute-start.6 = (bf16[27,32,512]{2,1,0:T(8,128)(2,1)}, bf16[27,32,512]{2,1,0:T(8,128)(2,1)}, u32[]{:S(2)}, u32[]{:S(2)}) collective-permute-start(bf16[27,32,512]{2,1,0:T(8,128)(2,1)} %collective-permute-done.2.rest_5_), channel_id=1, source_target_pairs={{0,1},{1,2},{2,3},{3,4},{4,5},{5,6},{6,7},{7,0},{16,23},{17,16},{1... | collective-permute-start | bytes 2654216 | tf_op jit(solution)/shard_map/ppermute | solution.py:247
  68.4 0.8 copy-start.3
  69.1 35.9 %all-to-all-start.1 = ((bf16[8,6,32,128]{3,2,1,0:T(8,128)(2,1)}), bf16[8,6,32,128]{3,2,1,0:T(8,128)(2,1)S(1)}, u32[]{:S(2)}, u32[]{:S(2)}) async-start(bf16[8,6,32,128]{3,2,1,0:T(8,128)(2,1)} %bitcast.1), calls=%async_computation.1 | async-start | bytes 786432 | tf_op jit(solution)/shard_map/all_to_all | solution.py:238
  79.3 1.0 copy-start.4
  84.3 11.1 %collective-permute-start.7 = (f32[128,512]{1,0:T(8,128)S(1)}, f32[128,512]{1,0:T(8,128)S(1)}, u32[]{:S(2)}, u32[]{:S(2)}) collective-permute-start(f32[128,512]{1,0:T(8,128)S(1)} %get-tuple-element.25), channel_id=1, source_target_pairs={{0,16},{16,32},{32,48},{48,64},{64,80},{80,96},{96,112},{112,128},... | collective-permute-start | bytes 786440 | tf_op jit(solution)/shard_map/ppermute | solution.py:300
  95.5 18.3 %collective-permute-start.8 = (f32[128,512]{1,0:T(8,128)S(1)}, f32[128,512]{1,0:T(8,128)}, u32[]{:S(2)}, u32[]{:S(2)}) collective-permute-start(f32[128,512]{1,0:T(8,128)S(1)} %add.6), channel_id=1, source_target_pairs={{0,8},{8,0},{1,9},{9,1},{2,10},{10,2},{3,11},{11,3},{4,12},{12,4},... | collective-permute-start | bytes 786440 | tf_op jit(solution)/shard_map/ppermute | solution.py:303
  109.1 48.7 %copy-start.7 = (f32[512]{0:T(512)S(1)}, f32[512]{0:T(512)}, u32[]{:S(2)}) copy-start(f32[512]{0:T(512)} %param.10) | copy-start | bytes 6148
  109.1 48.7 %copy-start.8 = (f32[512]{0:T(512)S(1)}, f32[512]{0:T(512)}, u32[]{:S(2)}) copy-start(f32[512]{0:T(512)} %param.11) | copy-start | bytes 6148
  109.1 8.0 %collective-permute-start.9 = (f32[128,512]{1,0:T(8,128)S(1)}, f32[128,512]{1,0:T(8,128)S(1)}, u32[]{:S(2)}, u32[]{:S(2)}) collective-permute-start(f32[128,512]{1,0:T(8,128)S(1)} %get-tuple-element.26), channel_id=1, source_target_pairs={{0,16},{16,32},{32,48},{48,64},{64,80},{80,96},{96,112},{112,128},... | collective-permute-start | bytes 786440 | tf_op jit(solution)/shard_map/ppermute | solution.py:302

commit v5 on v4

--- a/solution.py
+++ b/solution.py
@@ -13,6 +13,7 @@
 ROWS = 64
 CAP = 4
 CH_DEV = 32
+HALF = 16
 NY = 8
 OUT_ROWS = 16
 COUT = 512
@@ -120,7 +121,7 @@
 
 
 def conv_kernel(lengths, frames, *rest):
-    weights, (own, after, taps) = rest[:NY], rest[NY:]
+    weights, (own, after, taps) = rest[:NY + 1], rest[NY + 1:]
     y = lax.axis_index("y")
     core = lax.axis_index("co")
     slab = my_slab()
@@ -128,15 +129,19 @@
     sources = [y]
     for s in range(1, 4):
         sources += [y + sign * s, y - sign * s]
-    sources.append(y + 4)
+    sources += [y + 4, y + 4]
     sources = [lax.bitwise_and(s + NY, NY - 1) for s in sources]
+    whole = pl.ds(0, CH_DEV)
+    mine = pl.ds(pl.multiple_of(core * HALF, HALF), HALF)
+    other = pl.ds(pl.multiple_of((1 - core) * HALF, HALF), HALF)
+    sources = list(zip(sources, [whole] * 7 + [mine, other]))
     j = lax.broadcasted_iota(jnp.int32, (192, 128), 0)
     w = lax.broadcasted_iota(jnp.int32, (192, 128), 1)
     wanted = jnp.where(j < 64, 2 * j - 1, jnp.where(j < 128, 2 * j - 128, 2 * j - 255))
     pick = (w == wanted).astype(F32).astype(BF)
     for t in range(2):
         for b in range(3):
-            x = jnp.concatenate([frames[s, t * 3 + b] for s in sources], axis=0)
+            x = jnp.concatenate([frames[s, t * 3 + b, c] for s, c in sources], axis=0)
             picked = lax.dot_general(pick, x, (((1,), (1,)), ((), ())),
                                      preferred_element_type=F32).astype(BF)
             for e in range(3):
@@ -243,9 +248,12 @@
             for c in range(2) for y in range(NY)]
     swap = [(0, 1), (1, 0)]
     moved = [kernel]
-    for _ in range(4):
+    for _ in range(3):
         moved.append(lax.ppermute(moved[-1], ("co", "y"), ring))
-    swapped = [lax.ppermute(shard, "co", swap) for shard in moved[1:4]]
+    first = lax.axis_index("co") * HALF
+    half = lax.dynamic_slice_in_dim(moved[3], first, HALF, axis=1)
+    moved.append(lax.ppermute(half, ("co", "y"), ring))
+    swapped = [lax.ppermute(shard, "co", swap) for shard in moved[1:]]
     return moved, swapped
 
 
@@ -253,7 +261,7 @@
     return pl.pallas_call(
         conv_kernel,
         out_shape=[jax.ShapeDtypeStruct((128, COUT), F32)] * 2,
-        in_specs=[SMEM] + [VMEM] * (1 + NY),
+        in_specs=[SMEM] + [VMEM] * (2 + NY),
         out_specs=[VMEM, VMEM],
         scratch_shapes=[pltpu.VMEM((3, 128, 768), BF)],
         compiler_params=params(24),
@@ -276,9 +284,7 @@
         compiler_params=params(8),
     )(row_target, arrived)
     got = shuffle(send, TM)
-    got, moved[3], swapped[0], swapped[1] = lax.optimization_barrier(
-        (got, moved[3], swapped[0], swapped[1])
-    )
+    got, moved[2], swapped[0] = lax.optimization_barrier((got, moved[2], swapped[0]))
     far, near = pl.pallas_call(
         place_kernel,
         out_shape=[jax.ShapeDtypeStruct((NY * 6, CH_DEV, 128), BF)] * 2,
@@ -292,7 +298,8 @@
         ],
         compiler_params=params(8),
     )(got)
-    weights = [moved[0], moved[1], swapped[0], moved[2], swapped[1], moved[3], swapped[2], moved[4]]
+    weights = [moved[0], moved[1], swapped[0], moved[2], swapped[1], moved[3], swapped[2]]
+    weights += [moved[4], swapped[3]]
     onward = [(i, i + 1) for i in range(SLABS - 1)]
     far = shuffle(far.reshape(NY, 6, CH_DEV, 128), "y")
     near = shuffle(near.reshape(NY, 6, CH_DEV, 128), "y")

time: 160 us -> 151 us (0.944)
  starting transfers between devices: 75.9 us -> 65.1 us
  waiting for transfers between devices: 23.2 us -> 29.2 us
  blocking collectives: 38.3 us -> 34 us
    ppermute x3 -> x5, waiting for transfers between devices: 0.01 us -> 6.83 us  [the longest x1 6.82 us: gathered_weights(): moved.append(lax.ppermute(half, ('co', 'y'), ring))]
    ppermute x4 -> x3, waiting for transfers between devices: 13 us -> 6.91 us  [gathered_weights(): moved.append(lax.ppermute(moved[-1], ('co', 'y'), ring))]
    all_to_all x3, waiting for transfers between devices: 4.64 us -> 9.92 us  [shuffle(): return lax.all_to_all(x, axis, split_axis=0, concat_axis=0, tiled=True)]
    ppermute x4 -> x3, starting transfers between devices: 17.7 us -> 12.9 us  [gathered_weights(): moved.append(lax.ppermute(moved[-1], ('co', 'y'), ring))]
    ppermute x1, starting transfers between devices: 7.85 us -> 3.31 us  [body(): far_before = lax.ppermute(far_after, TM, onward)]
    all_to_all x2, blocking collectives: 38.3 us -> 34 us  [shuffle(): return lax.all_to_all(x, axis, split_axis=0, concat_axis=0, tiled=True)]
    ppermute x3 -> x5, starting transfers between devices: 15.5 us -> 17 us  [the longest x4 12.1 us: gathered_weights(): swapped = [lax.ppermute(shard, 'co', swap) for shard in moved[1:]]]
    unnamed x20 -> x18, local copies, waits for them, and re-layouts: 4.41 us -> 4.98 us
  transfers between devices with their start and end apart: 13 -> 14, of which waited for: 5 -> 5; matrix products, arithmetic and copies ran while one was open for 1% -> 1% of each run, Pallas kernels for 6% -> 8%
where the time goes in v5:
time: 151 us; the launch traced here: 150 us
  starting transfers between devices  65.1 us (43%)
  blocking collectives  34 us (23%)
  waiting for transfers between devices  29.2 us (19%)
  Pallas kernels  15.6 us (10%)
  local copies, waits for them, and re-layouts  5.01 us (3%)
    all_to_all x2, blocking collectives, shuffle(): return lax.all_to_all(x, axis, split_axis=0, concat_axis=0, tiled=True)  34 us
    all_to_all x3, starting transfers between devices, shuffle(): return lax.all_to_all(x, axis, split_axis=0, concat_axis=0, tiled=True)  19.3 us
    ppermute x3, starting transfers between devices, gathered_weights(): moved.append(lax.ppermute(moved[-1], ('co', 'y'), ring))  12.9 us
    ppermute x4, starting transfers between devices, gathered_weights(): swapped = [lax.ppermute(shard, 'co', swap) for shard in moved[1:]]  12.1 us
    all_to_all x3, waiting for transfers between devices, shuffle(): return lax.all_to_all(x, axis, split_axis=0, concat_axis=0, tiled=True)  9.92 us
    ppermute x1, starting transfers between devices, body(): far = lax.ppermute(far + far_before, 'zh', [(0, 1), (1, 0)])  7.94 us
    pallas_call x2, Pallas kernels, convolve(): pl.pallas_call(conv_kernel, out_shape=[jax.ShapeDtypeStruct((128, COUT),...  7.52 us
    ppermute x3, waiting for transfers between devices, gathered_weights(): moved.append(lax.ppermute(moved[-1], ('co', 'y'), ring))  6.91 us
  transfers between devices with their start and end apart: 14, of which 5 were waited for; matrix products, arithmetic and copies ran while one was open for 1% of the time, Pallas kernels for 8%

profile of v5, /device:TPU:1, one launch (start us, length us, event | category | flops | bytes accessed | tf_op | source)
XLA Modules:
  0.0 150.3 jit_solution(9461085759778663882)
XLA Ops:
  0.0 5.9 %collective-permute-start = (bf16[27,32,512]{2,1,0:T(8,128)(2,1)}, bf16[27,32,512]{2,1,0:T(8,128)(2,1)S(1)}, u32[]{:S(2)}, u32[]{:S(2)}) collective-permute-start(bf16[27,32,512]{2,1,0:T(8,128)(2,1)} %bitcast.6), channel_id=1, source_target_pairs={{0,1},{1,2},{2,3},{3,4},{4,5},{5,6},{6,7},{7,0},{16,23},{17,16},{1... | collective-permute-start | bytes 2654216 | tf_op jit(solution)/shard_map/ppermute | solution.py:252
  5.9 0.0 copy-start.4
  5.9 1.0 copy-done.4
  7.0 0.0 copy-start.8
  7.0 0.7 copy-done.8
  7.6 2.1 %shard_map.64 = bf16[32,144,128]{2,1,0:T(8,128)(2,1)} custom-call(s32[64]{0:T(128)S(1)} %copy-done.8, bf16[64,32,128]{2,1,0:T(8,128)(2,1)S(1)} %copy-done.4), custom_call_target="tpu_custom_call" | custom-call | tf_op jit(solution)/shard_map/pallas_call | solution.py:273
  9.8 10.0 %all-to-all-start = ((bf16[32,144,128]{2,1,0:T(8,128)(2,1)}), bf16[32,144,128]{2,1,0:T(8,128)(2,1)S(1)}, u32[]{:S(2)}, u32[]{:S(2)}) async-start(bf16[32,144,128]{2,1,0:T(8,128)(2,1)} %shard_map.64), calls=%async_computation | async-start | bytes 2359296 | tf_op jit(solution)/shard_map/all_to_all | solution.py:243
  19.8 0.0 collective-permute-done.rest_1_
  19.8 3.0 %collective-permute-start.1 = (bf16[27,32,512]{2,1,0:T(8,128)(2,1)S(1)}, bf16[27,32,512]{2,1,0:T(8,128)(2,1)}, u32[]{:S(2)}, u32[]{:S(2)}) collective-permute-start(bf16[27,32,512]{2,1,0:T(8,128)(2,1)S(1)} %collective-permute-done.rest_1_), channel_id=1, source_target_pairs={{0,1},{1,2},{2,3},{3,4},{4,5},{5,6},{6,7},{7,0},{16,23},{17,16},{1... | collective-permute-start | bytes 2654216 | tf_op jit(solution)/shard_map/ppermute | solution.py:252
  22.8 4.3 %collective-permute-start.2 = (bf16[27,32,512]{2,1,0:T(8,128)(2,1)S(1)}, bf16[27,32,512]{2,1,0:T(8,128)(2,1)S(1)}, u32[]{:S(2)}, u32[]{:S(2)}) collective-permute-start(bf16[27,32,512]{2,1,0:T(8,128)(2,1)S(1)} %collective-permute-done.rest_1_), channel_id=1, source_target_pairs={{0,16},{16,0},{1,17},{17,1},{2,18},{18,2},{3,19},{19,3},{4,20},{20... | collective-permute-start | bytes 2654216 | tf_op jit(solution)/shard_map/ppermute | solution.py:256
  27.1 6.9 %collective-permute-done.1.rest_3_ = bf16[27,32,512]{2,1,0:T(8,128)(2,1)} collective-permute-done((bf16[27,32,512]{2,1,0:T(8,128)(2,1)S(1)}, bf16[27,32,512]{2,1,0:T(8,128)(2,1)}, u32[]{:S(2)}, u32[]{:S(2)}) %collective-permute-start.1) | collective-permute-done | bytes 884768 | tf_op jit(solution)/shard_map/ppermute | solution.py:252
  34.0 4.0 %collective-permute-start.4 = (bf16[27,32,512]{2,1,0:T(8,128)(2,1)}, bf16[27,32,512]{2,1,0:T(8,128)(2,1)S(1)}, u32[]{:S(2)}, u32[]{:S(2)}) collective-permute-start(bf16[27,32,512]{2,1,0:T(8,128)(2,1)} %collective-permute-done.1.rest_3_), channel_id=1, source_target_pairs={{0,1},{1,2},{2,3},{3,4},{4,5},{5,6},{6,7},{7,0},{16,23},{17,16},{1... | collective-permute-start | bytes 2654216 | tf_op jit(solution)/shard_map/ppermute | solution.py:252
  38.0 0.0 collective-permute-done.2.rest_2_
  38.0 0.0 copy-start.1
  38.0 0.9 copy-done.1
  39.0 9.9 %all-to-all-done.got = bf16[32,144,128]{2,1,0:T(8,128)(2,1)S(1)} async-done(((bf16[32,144,128]{2,1,0:T(8,128)(2,1)}), bf16[32,144,128]{2,1,0:T(8,128)(2,1)S(1)}, u32[]{:S(2)}, u32[]{:S(2)}) %all-to-all-start) | async-done | bytes 1179680 | tf_op jit(solution)/shard_map/all_to_all | solution.py:243
  48.9 2.1 %shard_map.65 = (bf16[48,32,128]{2,1,0:T(8,128)(2,1)}, bf16[48,32,128]{2,1,0:T(8,128)(2,1)}) custom-call(bf16[32,144,128]{2,1,0:T(8,128)(2,1)S(1)} %all-to-all-done.got), custom_call_target="tpu_custom_call" | custom-call | tf_op jit(solution)/shard_map/pallas_call | solution.py:288
  51.0 0.0 copy-start
  51.0 0.0 copy-start.5
  51.0 5.0 %all-to-all-start.2 = ((bf16[8,6,32,128]{3,2,1,0:T(8,128)(2,1)}), bf16[8,6,32,128]{3,2,1,0:T(8,128)(2,1)}, u32[]{:S(2)}, u32[]{:S(2)}) async-start(bf16[8,6,32,128]{3,2,1,0:T(8,128)(2,1)} %bitcast.2), calls=%async_computation.2 | async-start | bytes 786432 | tf_op jit(solution)/shard_map/all_to_all | solution.py:243
  56.0 2.4 %collective-permute-start.3 = (bf16[27,32,512]{2,1,0:T(8,128)(2,1)}, bf16[27,32,512]{2,1,0:T(8,128)(2,1)}, u32[]{:S(2)}, u32[]{:S(2)}) collective-permute-start(bf16[27,32,512]{2,1,0:T(8,128)(2,1)} %collective-permute-done.1.rest_3_), channel_id=1, source_target_pairs={{0,16},{16,0},{1,17},{17,1},{2,18},{18,2},{3,19},{19,3},{4,20},{20... | collective-permute-start | bytes 2654216 | tf_op jit(solution)/shard_map/ppermute | solution.py:256
  58.4 0.0 collective-permute-done.4.rest_5_
  58.5 4.9 %collective-permute-start.6 = (bf16[27,16,512]{2,1,0:T(8,128)(2,1)S(1)}, bf16[27,16,512]{2,1,0:T(8,128)(2,1)S(1)}, u32[]{:S(2)}, u32[]{:S(2)}) collective-permute-start(bf16[27,16,512]{2,1,0:T(8,128)(2,1)S(1)} %constant_dynamic-slice_fusion), channel_id=1, source_target_pairs={{0,1},{1,2},{2,3},{3,4},{4,5},{5,6},{6,7},{7,0},{16,23},{17,16},{1... | collective-permute-start | bytes 1327112 | tf_op jit(solution)/shard_map/ppermute | solution.py:255
  63.4 1.9 %collective-permute-start.5 = (bf16[27,32,512]{2,1,0:T(8,128)(2,1)S(1)}, bf16[27,32,512]{2,1,0:T(8,128)(2,1)}, u32[]{:S(2)}, u32[]{:S(2)}) collective-permute-start(bf16[27,32,512]{2,1,0:T(8,128)(2,1)S(1)} %collective-permute-done.4.rest_5_), channel_id=1, source_target_pairs={{0,16},{16,0},{1,17},{17,1},{2,18},{18,2},{3,19},{19,3},{4,20},{20... | collective-permute-start | bytes 2654216 | tf_op jit(solution)/shard_map/ppermute | solution.py:256
  65.3 6.8 %collective-permute-done.6.rest_7_ = bf16[27,16,512]{2,1,0:T(8,128)(2,1)S(1)} collective-permute-done((bf16[27,16,512]{2,1,0:T(8,128)(2,1)S(1)}, bf16[27,16,512]{2,1,0:T(8,128)(2,1)S(1)}, u32[]{:S(2)}, u32[]{:S(2)}) %collective-permute-start.6) | collective-permute-done | bytes 442400 | tf_op jit(solution)/shard_map/ppermute | solution.py:255
  72.1 3.5 %collective-permute-start.7 = (bf16[27,16,512]{2,1,0:T(8,128)(2,1)S(1)}, bf16[27,16,512]{2,1,0:T(8,128)(2,1)}, u32[]{:S(2)}, u32[]{:S(2)}) collective-permute-start(bf16[27,16,512]{2,1,0:T(8,128)(2,1)S(1)} %collective-permute-done.6.rest_7_), channel_id=1, source_target_pairs={{0,16},{16,0},{1,17},{17,1},{2,18},{18,2},{3,19},{19,3},{4,20},{20... | collective-permute-start | bytes 1327112 | tf_op jit(solution)/shard_map/ppermute | solution.py:256
  75.6 0.0 all-to-all-done.2.frames
  75.6 4.3 %all-to-all-start.1 = ((bf16[8,6,32,128]{3,2,1,0:T(8,128)(2,1)}), bf16[8,6,32,128]{3,2,1,0:T(8,128)(2,1)}, u32[]{:S(2)}, u32[]{:S(2)}) async-start(bf16[8,6,32,128]{3,2,1,0:T(8,128)(2,1)} %bitcast.1), calls=%async_computation.1 | async-start | bytes 786432 | tf_op jit(solution)/shard_map/all_to_all | solution.py:243
  79.9 0.0 collective-permute-done.3.rest_4_
  79.9 0.0 collective-permute-done.7.rest_8_
  79.9 0.0 collective-permute-done.5.rest_6_
  79.9 0.0 copy-done
  79.9 0.0 copy-done.5
  80.0 0.0 copy-start.2
  80.0 1.2 copy-done.2
  81.1 3.8 %shard_map.67 = (f32[128,512]{1,0:T(8,128)S(1)}, f32[128,512]{1,0:T(8,128)S(1)}) custom-call(s32[4]{0:T(128)S(1)} %copy-done.5, bf16[8,6,32,128]{3,2,1,0:T(8,128)(2,1)} %all-to-all-done.2.frames, bf16[27,32,512]{2,1,0:T(8,128)(2,1)S(1)} %bitcast.7, bf16[27,32,512]{2,1,0:T(8,128)(2,1)S(1)} %collective-permute-done.rest_1_, ...), custom_call_target="tpu_custom_call" | custom-call | tf_op jit(solution)/shard_map/pallas_call | solution.py:261
  84.9 3.3 %collective-permute-start.8 = (f32[128,512]{1,0:T(8,128)S(1)}, f32[128,512]{1,0:T(8,128)S(1)}, u32[]{:S(2)}, u32[]{:S(2)}) collective-permute-start(f32[128,512]{1,0:T(8,128)S(1)} %get-tuple-element.23), channel_id=1, source_target_pairs={{0,16},{16,32},{32,48},{48,64},{64,80},{80,96},{96,112},{112,128},... | collective-permute-start | bytes 786440 | tf_op jit(solution)/shard_map/ppermute | solution.py:307
  88.2 3.3 %collective-permute-done.8 = f32[128,512]{1,0:T(8,128)S(1)} collective-permute-done((f32[128,512]{1,0:T(8,128)S(1)}, f32[128,512]{1,0:T(8,128)S(1)}, u32[]{:S(2)}, u32[]{:S(2)}) %collective-permute-start.8) | collective-permute-done | bytes 262176 | tf_op jit(solution)/shard_map/ppermute | solution.py:307
  91.6 7.9 %collective-permute-start.9 = (f32[128,512]{1,0:T(8,128)S(1)}, f32[128,512]{1,0:T(8,128)}, u32[]{:S(2)}, u32[]{:S(2)}) collective-permute-start(f32[128,512]{1,0:T(8,128)S(1)} %add.10), channel_id=1, source_target_pairs={{0,8},{8,0},{1,9},{9,1},{2,10},{10,2},{3,11},{11,3},{4,12},{12,4},... | collective-permute-start | bytes 786440 | tf_op jit(solution)/shard_map/ppermute | solution.py:310
  99.5 0.0 all-to-all-done.1.frames
  99.5 0.0 copy-start.3
  99.5 1.2 copy-done.3
  100.7 3.8 %shard_map.66 = (f32[128,512]{1,0:T(8,128)S(1)}, f32[128,512]{1,0:T(8,128)S(1)}) custom-call(s32[4]{0:T(128)S(1)} %copy-done.5, bf16[8,6,32,128]{3,2,1,0:T(8,128)(2,1)} %all-to-all-done.1.frames, bf16[27,32,512]{2,1,0:T(8,128)(2,1)S(1)} %bitcast.8, bf16[27,32,512]{2,1,0:T(8,128)(2,1)S(1)} %collective-permute-done.rest_1_, ...), custom_call_target="tpu_custom_call" | custom-call | tf_op jit(solution)/shard_map/pallas_call | solution.py:261
  104.5 0.0 copy-start.6
  104.5 0.0 copy-start.7
  104.5 4.7 %collective-permute-start.10 = (f32[128,512]{1,0:T(8,128)S(1)}, f32[128,512]{1,0:T(8,128)S(1)}, u32[]{:S(2)}, u32[]{:S(2)}) collective-permute-start(f32[128,512]{1,0:T(8,128)S(1)} %get-tuple-element.24), channel_id=1, source_target_pairs={{0,16},{16,32},{32,48},{48,64},{64,80},{80,96},{96,112},{112,128},... | collective-permute-start | bytes 786440 | tf_op jit(solution)/shard_map/ppermute | solution.py:309
  109.1 0.0 collective-permute-done.9
  109.2 1.0 add.11.near
  110.2 2.3 %collective-permute-done.10.before = f32[128,512]{1,0:T(8,128)S(1)} collective-permute-done((f32[128,512]{1,0:T(8,128)S(1)}, f32[128,512]{1,0:T(8,128)S(1)}, u32[]{:S(2)}, u32[]{:S(2)}) %collective-permute-start.10) | collective-permute-done | bytes 262176 | tf_op jit(solution)/shard_map/ppermute | solution.py:309
  112.4 0.9 shard_map.68
  113.3 15.0 %all_to_all.25.got = f32[16,8,128]{2,1,0:T(8,128)} all-to-all(f32[16,8,128]{2,1,0:T(8,128)S(1)} %get-tuple-element.25), channel_id=1, replica_groups=mesh['zl'=4,'x'=4,'co'=2,'zh'=2,'y'=8] {'y','co'}, dimensions={0} | all-to-all | bytes 131072 | tf_op jit(solution)/shard_map/all_to_all | solution.py:243
  128.4 1.5 %shard_map.69 = f32[32,8,128]{2,1,0:T(8,128)} custom-call(f32[16,8,128]{2,1,0:T(8,128)} %all_to_all.25.got), custom_call_target="tpu_custom_call" | custom-call | tf_op jit(solution)/shard_map/pallas_call | solution.py:320
  129.9 18.9 %all_to_all.26.got = f32[32,8,128]{2,1,0:T(8,128)S(1)} all-to-all(f32[32,8,128]{2,1,0:T(8,128)} %shard_map.69), channel_id=1, replica_groups=mesh['zl'=4,'x'=4,'co'=2,'zh'=2,'y'=8] {'zl','zh','x'}, dimensions={0} | all-to-all | bytes 262144 | tf_op jit(solution)/shard_map/all_to_all | solution.py:243
  148.8 0.0 copy-done.6
  148.8 0.0 copy-done.7
  148.8 1.5 shard_map.70
  (2 shorter events, 0.1 us)
Async XLA Ops:
  0.0 19.8 %collective-permute-start = (bf16[27,32,512]{2,1,0:T(8,128)(2,1)}, bf16[27,32,512]{2,1,0:T(8,128)(2,1)S(1)}, u32[]{:S(2)}, u32[]{:S(2)}) collective-permute-start(bf16[27,32,512]{2,1,0:T(8,128)(2,1)} %bitcast.6), channel_id=1, source_target_pairs={{0,1},{1,2},{2,3},{3,4},{4,5},{5,6},{6,7},{7,0},{16,23},{17,16},{1... | collective-permute-start | bytes 2654216 | tf_op jit(solution)/shard_map/ppermute | solution.py:252
  5.9 1.0 copy-start.4
  7.0 0.7 copy-start.8
  9.8 39.1 %all-to-all-start = ((bf16[32,144,128]{2,1,0:T(8,128)(2,1)}), bf16[32,144,128]{2,1,0:T(8,128)(2,1)S(1)}, u32[]{:S(2)}, u32[]{:S(2)}) async-start(bf16[32,144,128]{2,1,0:T(8,128)(2,1)} %shard_map.64), calls=%async_computation | async-start | bytes 2359296 | tf_op jit(solution)/shard_map/all_to_all | solution.py:243
  19.8 14.2 %collective-permute-start.1 = (bf16[27,32,512]{2,1,0:T(8,128)(2,1)S(1)}, bf16[27,32,512]{2,1,0:T(8,128)(2,1)}, u32[]{:S(2)}, u32[]{:S(2)}) collective-permute-start(bf16[27,32,512]{2,1,0:T(8,128)(2,1)S(1)} %collective-permute-done.rest_1_), channel_id=1, source_target_pairs={{0,1},{1,2},{2,3},{3,4},{4,5},{5,6},{6,7},{7,0},{16,23},{17,16},{1... | collective-permute-start | bytes 2654216 | tf_op jit(solution)/shard_map/ppermute | solution.py:252
  22.8 15.3 %collective-permute-start.2 = (bf16[27,32,512]{2,1,0:T(8,128)(2,1)S(1)}, bf16[27,32,512]{2,1,0:T(8,128)(2,1)S(1)}, u32[]{:S(2)}, u32[]{:S(2)}) collective-permute-start(bf16[27,32,512]{2,1,0:T(8,128)(2,1)S(1)} %collective-permute-done.rest_1_), channel_id=1, source_target_pairs={{0,16},{16,0},{1,17},{17,1},{2,18},{18,2},{3,19},{19,3},{4,20},{20... | collective-permute-start | bytes 2654216 | tf_op jit(solution)/shard_map/ppermute | solution.py:256
  34.0 24.5 %collective-permute-start.4 = (bf16[27,32,512]{2,1,0:T(8,128)(2,1)}, bf16[27,32,512]{2,1,0:T(8,128)(2,1)S(1)}, u32[]{:S(2)}, u32[]{:S(2)}) collective-permute-start(bf16[27,32,512]{2,1,0:T(8,128)(2,1)} %collective-permute-done.1.rest_3_), channel_id=1, source_target_pairs={{0,1},{1,2},{2,3},{3,4},{4,5},{5,6},{6,7},{7,0},{16,23},{17,16},{1... | collective-permute-start | bytes 2654216 | tf_op jit(solution)/shard_map/ppermute | solution.py:252
  38.0 0.9 copy-start.1
  51.0 28.9 %copy-start = (bf16[3,3,3,32,512]{4,3,2,1,0:T(8,128)(2,1)S(1)}, bf16[3,3,3,32,512]{4,3,2,1,0:T(8,128)(2,1)}, u32[]{:S(2)}) copy-start(bf16[3,3,3,32,512]{4,3,2,1,0:T(8,128)(2,1)} %param.9) | copy-start | bytes 2654212
  51.0 28.9 %copy-start.5 = (s32[4]{0:T(128)S(1)}, s32[4]{0:T(128)}, u32[]{:S(2)}) copy-start(s32[4]{0:T(128)} %lengths.7) | copy-start | bytes 52
  51.0 24.6 %all-to-all-start.2 = ((bf16[8,6,32,128]{3,2,1,0:T(8,128)(2,1)}), bf16[8,6,32,128]{3,2,1,0:T(8,128)(2,1)}, u32[]{:S(2)}, u32[]{:S(2)}) async-start(bf16[8,6,32,128]{3,2,1,0:T(8,128)(2,1)} %bitcast.2), calls=%async_computation.2 | async-start | bytes 786432 | tf_op jit(solution)/shard_map/all_to_all | solution.py:243
  56.0 23.9 %collective-permute-start.3 = (bf16[27,32,512]{2,1,0:T(8,128)(2,1)}, bf16[27,32,512]{2,1,0:T(8,128)(2,1)}, u32[]{:S(2)}, u32[]{:S(2)}) collective-permute-start(bf16[27,32,512]{2,1,0:T(8,128)(2,1)} %collective-permute-done.1.rest_3_), channel_id=1, source_target_pairs={{0,16},{16,0},{1,17},{17,1},{2,18},{18,2},{3,19},{19,3},{4,20},{20... | collective-permute-start | bytes 2654216 | tf_op jit(solution)/shard_map/ppermute | solution.py:256
  58.5 13.6 %collective-permute-start.6 = (bf16[27,16,512]{2,1,0:T(8,128)(2,1)S(1)}, bf16[27,16,512]{2,1,0:T(8,128)(2,1)S(1)}, u32[]{:S(2)}, u32[]{:S(2)}) collective-permute-start(bf16[27,16,512]{2,1,0:T(8,128)(2,1)S(1)} %constant_dynamic-slice_fusion), channel_id=1, source_target_pairs={{0,1},{1,2},{2,3},{3,4},{4,5},{5,6},{6,7},{7,0},{16,23},{17,16},{1... | collective-permute-start | bytes 1327112 | tf_op jit(solution)/shard_map/ppermute | solution.py:255
  63.4 16.6 %collective-permute-start.5 = (bf16[27,32,512]{2,1,0:T(8,128)(2,1)S(1)}, bf16[27,32,512]{2,1,0:T(8,128)(2,1)}, u32[]{:S(2)}, u32[]{:S(2)}) collective-permute-start(bf16[27,32,512]{2,1,0:T(8,128)(2,1)S(1)} %collective-permute-done.4.rest_5_), channel_id=1, source_target_pairs={{0,16},{16,0},{1,17},{17,1},{2,18},{18,2},{3,19},{19,3},{4,20},{20... | collective-permute-start | bytes 2654216 | tf_op jit(solution)/shard_map/ppermute | solution.py:256
  72.1 7.8 %collective-permute-start.7 = (bf16[27,16,512]{2,1,0:T(8,128)(2,1)S(1)}, bf16[27,16,512]{2,1,0:T(8,128)(2,1)}, u32[]{:S(2)}, u32[]{:S(2)}) collective-permute-start(bf16[27,16,512]{2,1,0:T(8,128)(2,1)S(1)} %collective-permute-done.6.rest_7_), channel_id=1, source_target_pairs={{0,16},{16,0},{1,17},{17,1},{2,18},{18,2},{3,19},{19,3},{4,20},{20... | collective-permute-start | bytes 1327112 | tf_op jit(solution)/shard_map/ppermute | solution.py:256
  75.6 23.9 %all-to-all-start.1 = ((bf16[8,6,32,128]{3,2,1,0:T(8,128)(2,1)}), bf16[8,6,32,128]{3,2,1,0:T(8,128)(2,1)}, u32[]{:S(2)}, u32[]{:S(2)}) async-start(bf16[8,6,32,128]{3,2,1,0:T(8,128)(2,1)} %bitcast.1), calls=%async_computation.1 | async-start | bytes 786432 | tf_op jit(solution)/shard_map/all_to_all | solution.py:243
  80.0 1.2 copy-start.2
  84.9 6.6 %collective-permute-start.8 = (f32[128,512]{1,0:T(8,128)S(1)}, f32[128,512]{1,0:T(8,128)S(1)}, u32[]{:S(2)}, u32[]{:S(2)}) collective-permute-start(f32[128,512]{1,0:T(8,128)S(1)} %get-tuple-element.23), channel_id=1, source_target_pairs={{0,16},{16,32},{32,48},{48,64},{64,80},{80,96},{96,112},{112,128},... | collective-permute-start | bytes 786440 | tf_op jit(solution)/shard_map/ppermute | solution.py:307
  91.6 17.6 %collective-permute-start.9 = (f32[128,512]{1,0:T(8,128)S(1)}, f32[128,512]{1,0:T(8,128)}, u32[]{:S(2)}, u32[]{:S(2)}) collective-permute-start(f32[128,512]{1,0:T(8,128)S(1)} %add.10), channel_id=1, source_target_pairs={{0,8},{8,0},{1,9},{9,1},{2,10},{10,2},{3,11},{11,3},{4,12},{12,4},... | collective-permute-start | bytes 786440 | tf_op jit(solution)/shard_map/ppermute | solution.py:310
  99.5 1.2 copy-start.3
  104.5 44.4 %copy-start.6 = (f32[512]{0:T(512)S(1)}, f32[512]{0:T(512)}, u32[]{:S(2)}) copy-start(f32[512]{0:T(512)} %param.10) | copy-start | bytes 6148
  104.5 44.4 %copy-start.7 = (f32[512]{0:T(512)S(1)}, f32[512]{0:T(512)}, u32[]{:S(2)}) copy-start(f32[512]{0:T(512)} %param.11) | copy-start | bytes 6148
  104.5 8.0 %collective-permute-start.10 = (f32[128,512]{1,0:T(8,128)S(1)}, f32[128,512]{1,0:T(8,128)S(1)}, u32[]{:S(2)}, u32[]{:S(2)}) collective-permute-start(f32[128,512]{1,0:T(8,128)S(1)} %get-tuple-element.24), channel_id=1, source_target_pairs={{0,16},{16,32},{32,48},{48,64},{64,80},{80,96},{96,112},{112,128},... | collective-permute-start | bytes 786440 | tf_op jit(solution)/shard_map/ppermute | solution.py:309

commit v6 on v5

--- a/solution.py
+++ b/solution.py
@@ -33,7 +33,9 @@
     return pltpu.CompilerParams(vmem_limit_bytes=mib * 1024 * 1024)
 
 
-def pack_kernel(target, arrived, send, counts, places, rounded, sems):
+def pack_kernel(target, arrived, send, rows, counts, places, rounded, sems):
+    fetch = pltpu.make_async_copy(arrived, rows, sems.at[0])
+    fetch.start()
     places[...] = jnp.full(places.shape, float(ROWS), F32)
 
     def clear(i, carry):
@@ -41,6 +43,7 @@
         return carry
 
     lax.fori_loop(0, SLABS, clear, 0)
+    fetch.wait()
 
     def one(i, carry):
         t = target[i]
@@ -48,7 +51,7 @@
         rank = counts[owner]
         counts[owner] = rank + 1
         slot = pl.ds(pl.multiple_of(rank * CH_DEV, CH_DEV), CH_DEV)
-        pltpu.make_async_copy(arrived.at[i], send.at[owner, slot], sems.at[0]).start()
+        pltpu.make_async_copy(rows.at[i], send.at[owner, slot], sems.at[0]).start()
         place = lax.bitwise_and(t, ROWS - 1).astype(F32)
         places[owner, pl.ds(rank, 1), :] = jnp.full((1, 128), place, F32)
         return carry
@@ -57,7 +60,7 @@
     rounded[...] = places[...].astype(BF)
     listed = pltpu.make_async_copy(rounded, send.at[:, pl.ds(CAP * CH_DEV, 16)], sems.at[1])
     listed.start()
-    pltpu.make_async_copy(arrived, arrived, sems.at[0]).wait()
+    pltpu.make_async_copy(rows, rows, sems.at[0]).wait()
     listed.wait()
 
 
@@ -70,8 +73,15 @@
     return near * 48 + lax.bitwise_and(i, NY - 1) * 6 + f * 3 + b
 
 
-def place_kernel(got, far, near, both, table, moves, sems):
+def place_kernel(arrived, far, near, got, both, table, moves, sems):
+    fetches = [
+        pltpu.make_async_copy(arrived.at[:, part], got.at[:, part], sems.at[k])
+        for k, part in enumerate((pl.ds(CAP * CH_DEV, 16), pl.ds(0, CAP * CH_DEV)))
+    ]
+    for fetch in fetches:
+        fetch.start()
     zh = lax.axis_index("zh")
+    fetches[0].wait()
     lane = lax.broadcasted_iota(jnp.int32, (16, 128), 1)
     place = jnp.full((16, 128), float(ROWS), F32)
     for s in range(SLABS):
@@ -89,6 +99,7 @@
     for f in range(2):
         both[spot(zh, jnp.int32(0), f, 0)] = jnp.zeros((CH_DEV, 128), BF)
     copy.wait()
+    fetches[1].wait()
 
     def some(s, carry):
         for source in (2 * s, 2 * s + 1):
@@ -276,32 +287,37 @@
         in_specs=[SMEM, HBM],
         out_specs=HBM,
         scratch_shapes=[
+            pltpu.VMEM((ROWS, CH_DEV, 128), BF),
             pltpu.SMEM((SLABS,), jnp.int32),
             pltpu.VMEM((SLABS, 16, 128), F32),
             pltpu.VMEM((SLABS, 16, 128), BF),
             pltpu.SemaphoreType.DMA((2,)),
         ],
-        compiler_params=params(8),
+        compiler_params=params(60),
     )(row_target, arrived)
     got = shuffle(send, TM)
-    got, moved[2], swapped[0] = lax.optimization_barrier((got, moved[2], swapped[0]))
+    got, moved[2], swapped[0], swapped[1] = lax.optimization_barrier(
+        (got, moved[2], swapped[0], swapped[1])
+    )
     far, near = pl.pallas_call(
         place_kernel,
         out_shape=[jax.ShapeDtypeStruct((NY * 6, CH_DEV, 128), BF)] * 2,
-        in_specs=[VMEM],
+        in_specs=[HBM],
         out_specs=[HBM, HBM],
         scratch_shapes=[
+            pltpu.VMEM((SLABS, 144, 128), BF),
             pltpu.VMEM((97, CH_DEV, 128), BF),
             pltpu.VMEM((16, 128), jnp.int32),
             pltpu.SMEM((16, 128), jnp.int32),
             pltpu.SemaphoreType.DMA((2,)),
         ],
-        compiler_params=params(8),
+        compiler_params=params(60),
     )(got)
     weights = [moved[0], moved[1], swapped[0], moved[2], swapped[1], moved[3], swapped[2]]
     weights += [moved[4], swapped[3]]
     onward = [(i, i + 1) for i in range(SLABS - 1)]
     far = shuffle(far.reshape(NY, 6, CH_DEV, 128), "y")
+    near, weights[-1] = lax.optimization_barrier((near, weights[-1]))
     near = shuffle(near.reshape(NY, 6, CH_DEV, 128), "y")
     far, far_after = convolve(clip_lengths, far, weights)
     far_before = lax.ppermute(far_after, TM, onward)

time: 151 us -> 156 us (1.033)
  starting transfers between devices: 65.1 us -> 75.9 us
  waiting for transfers between devices: 29.2 us -> 20.6 us
  Pallas kernels: 15.6 us -> 17.4 us
    all_to_all x3, waiting for transfers between devices: 9.92 us -> 0.01 us  [shuffle(): return lax.all_to_all(x, axis, split_axis=0, concat_axis=0, tiled=True)]
    ppermute x1, waiting for transfers between devices: 6.82 us -> 0.01 us  [gathered_weights(): moved.append(lax.ppermute(half, ('co', 'y'), ring))]
    ppermute x3, waiting for transfers between devices: 6.91 us -> 13.4 us  [gathered_weights(): moved.append(lax.ppermute(moved[-1], ('co', 'y'), ring))]
    ppermute x4, starting transfers between devices: 12.1 us -> 18.1 us  [gathered_weights(): swapped = [lax.ppermute(shard, 'co', swap) for shard in moved[1:]]]
    ppermute x1, starting transfers between devices: 3.31 us -> 5.64 us  [body(): far_before = lax.ppermute(far_after, TM, onward)]
    unnamed x18 -> x14, local copies, waits for them, and re-layouts: 4.98 us -> 2.82 us
    ppermute x4, waiting for transfers between devices: 0.01 us -> 1.62 us  [gathered_weights(): swapped = [lax.ppermute(shard, 'co', swap) for shard in moved[1:]]]
    all_to_all x2, blocking collectives: 34 us -> 35.5 us  [shuffle(): return lax.all_to_all(x, axis, split_axis=0, concat_axis=0, tiled=True)]
  transfers between devices with their start and end apart: 14 -> 14, of which waited for: 5 -> 5; matrix products, arithmetic and copies ran while one was open for 1% -> 2% of each run, Pallas kernels for 8% -> 9%
where the time goes in v6:
time: 156 us; the launch traced here: 155 us
  starting transfers between devices  75.9 us (49%)
  blocking collectives  35.5 us (23%)
  waiting for transfers between devices  20.6 us (13%)
  Pallas kernels  17.4 us (11%)
  local copies, waits for them, and re-layouts  3.62 us (2%)
  other arithmetic  1.73 us (1%)
    all_to_all x2, blocking collectives, shuffle(): return lax.all_to_all(x, axis, split_axis=0, concat_axis=0, tiled=True)  35.5 us
    all_to_all x3, starting transfers between devices, shuffle(): return lax.all_to_all(x, axis, split_axis=0, concat_axis=0, tiled=True)  20.5 us
    ppermute x4, starting transfers between devices, gathered_weights(): swapped = [lax.ppermute(shard, 'co', swap) for shard in moved[1:]]  18.1 us
    ppermute x3, waiting for transfers between devices, gathered_weights(): moved.append(lax.ppermute(moved[-1], ('co', 'y'), ring))  13.4 us
    ppermute x3, starting transfers between devices, gathered_weights(): moved.append(lax.ppermute(moved[-1], ('co', 'y'), ring))  13 us
    ppermute x1, starting transfers between devices, body(): far = lax.ppermute(far + far_before, 'zh', [(0, 1), (1, 0)])  8.96 us
    pallas_call x2, Pallas kernels, convolve(): pl.pallas_call(conv_kernel, out_shape=[jax.ShapeDtypeStruct((128, COUT),...  7.51 us
    ppermute x1, starting transfers between devices, body(): far_before = lax.ppermute(far_after, TM, onward)  5.64 us
  transfers between devices with their start and end apart: 14, of which 5 were waited for; matrix products, arithmetic and copies ran while one was open for 2% of the time, Pallas kernels for 9%

profile of v6, /device:TPU:1, one launch (start us, length us, event | category | flops | bytes accessed | tf_op | source)
XLA Modules:
  0.0 155.1 jit_solution(16467593278404634253)
XLA Ops:
  0.0 5.9 %collective-permute-start = (bf16[27,32,512]{2,1,0:T(8,128)(2,1)}, bf16[27,32,512]{2,1,0:T(8,128)(2,1)S(1)}, u32[]{:S(2)}, u32[]{:S(2)}) collective-permute-start(bf16[27,32,512]{2,1,0:T(8,128)(2,1)} %bitcast.6), channel_id=1, source_target_pairs={{0,1},{1,2},{2,3},{3,4},{4,5},{5,6},{6,7},{7,0},{16,23},{17,16},{1... | collective-permute-start | bytes 2654216 | tf_op jit(solution)/shard_map/ppermute | solution.py:263
  5.9 3.0 %shard_map.64 = bf16[32,144,128]{2,1,0:T(8,128)(2,1)} custom-call(s32[64]{0:T(128)} %target.1, bf16[64,32,128]{2,1,0:T(8,128)(2,1)} %arrived.1), custom_call_target="tpu_custom_call" | custom-call | tf_op jit(solution)/shard_map/pallas_call | solution.py:284
  9.0 10.1 %all-to-all-start = ((bf16[32,144,128]{2,1,0:T(8,128)(2,1)}), bf16[32,144,128]{2,1,0:T(8,128)(2,1)}, u32[]{:S(2)}, u32[]{:S(2)}) async-start(bf16[32,144,128]{2,1,0:T(8,128)(2,1)} %shard_map.64), calls=%async_computation | async-start | bytes 2359296 | tf_op jit(solution)/shard_map/all_to_all | solution.py:254
  19.0 0.0 collective-permute-done.rest_1_
  19.0 3.0 %collective-permute-start.1 = (bf16[27,32,512]{2,1,0:T(8,128)(2,1)S(1)}, bf16[27,32,512]{2,1,0:T(8,128)(2,1)S(1)}, u32[]{:S(2)}, u32[]{:S(2)}) collective-permute-start(bf16[27,32,512]{2,1,0:T(8,128)(2,1)S(1)} %collective-permute-done.rest_1_), channel_id=1, source_target_pairs={{0,1},{1,2},{2,3},{3,4},{4,5},{5,6},{6,7},{7,0},{16,23},{17,16},{1... | collective-permute-start | bytes 2654216 | tf_op jit(solution)/shard_map/ppermute | solution.py:263
  22.0 11.2 %collective-permute-done.1.rest_3_ = bf16[27,32,512]{2,1,0:T(8,128)(2,1)S(1)} collective-permute-done((bf16[27,32,512]{2,1,0:T(8,128)(2,1)S(1)}, bf16[27,32,512]{2,1,0:T(8,128)(2,1)S(1)}, u32[]{:S(2)}, u32[]{:S(2)}) %collective-permute-start.1) | collective-permute-done | bytes 884768 | tf_op jit(solution)/shard_map/ppermute | solution.py:263
  33.2 4.1 %collective-permute-start.4 = (bf16[27,32,512]{2,1,0:T(8,128)(2,1)S(1)}, bf16[27,32,512]{2,1,0:T(8,128)(2,1)S(1)}, u32[]{:S(2)}, u32[]{:S(2)}) collective-permute-start(bf16[27,32,512]{2,1,0:T(8,128)(2,1)S(1)} %collective-permute-done.1.rest_3_), channel_id=1, source_target_pairs={{0,1},{1,2},{2,3},{3,4},{4,5},{5,6},{6,7},{7,0},{16,23},{17,16},{1... | collective-permute-start | bytes 2654216 | tf_op jit(solution)/shard_map/ppermute | solution.py:263
  37.3 5.9 %collective-permute-start.2 = (bf16[27,32,512]{2,1,0:T(8,128)(2,1)S(1)}, bf16[27,32,512]{2,1,0:T(8,128)(2,1)}, u32[]{:S(2)}, u32[]{:S(2)}) collective-permute-start(bf16[27,32,512]{2,1,0:T(8,128)(2,1)S(1)} %collective-permute-done.rest_1_), channel_id=1, source_target_pairs={{0,16},{16,0},{1,17},{17,1},{2,18},{18,2},{3,19},{19,3},{4,20},{20... | collective-permute-start | bytes 2654216 | tf_op jit(solution)/shard_map/ppermute | solution.py:267
  43.2 1.9 %collective-permute-start.3 = (bf16[27,32,512]{2,1,0:T(8,128)(2,1)S(1)}, bf16[27,32,512]{2,1,0:T(8,128)(2,1)}, u32[]{:S(2)}, u32[]{:S(2)}) collective-permute-start(bf16[27,32,512]{2,1,0:T(8,128)(2,1)S(1)} %collective-permute-done.1.rest_3_), channel_id=1, source_target_pairs={{0,16},{16,0},{1,17},{17,1},{2,18},{18,2},{3,19},{19,3},{4,20},{20... | collective-permute-start | bytes 2654216 | tf_op jit(solution)/shard_map/ppermute | solution.py:267
  45.1 2.2 %collective-permute-done.4.rest_5_ = bf16[27,32,512]{2,1,0:T(8,128)(2,1)S(1)} collective-permute-done((bf16[27,32,512]{2,1,0:T(8,128)(2,1)S(1)}, bf16[27,32,512]{2,1,0:T(8,128)(2,1)S(1)}, u32[]{:S(2)}, u32[]{:S(2)}) %collective-permute-start.4) | collective-permute-done | bytes 884768 | tf_op jit(solution)/shard_map/ppermute | solution.py:263
  47.3 0.8 constant_dynamic-slice_fusion
  48.1 0.0 copy-start
  48.1 0.0 copy-start.4
  48.1 5.1 %collective-permute-start.5 = (bf16[27,16,512]{2,1,0:T(8,128)(2,1)}, bf16[27,16,512]{2,1,0:T(8,128)(2,1)}, u32[]{:S(2)}, u32[]{:S(2)}) collective-permute-start(bf16[27,16,512]{2,1,0:T(8,128)(2,1)} %constant_dynamic-slice_fusion), channel_id=1, source_target_pairs={{0,1},{1,2},{2,3},{3,4},{4,5},{5,6},{6,7},{7,0},{16,23},{17,16},{1... | collective-permute-start | bytes 1327112 | tf_op jit(solution)/shard_map/ppermute | solution.py:266
  53.3 0.0 collective-permute-done.2.rest_2_
  53.3 0.0 all-to-all-done.arrived
  53.3 0.0 collective-permute-done.3.rest_4_
  53.3 3.0 %shard_map.65 = (bf16[48,32,128]{2,1,0:T(8,128)(2,1)}, bf16[48,32,128]{2,1,0:T(8,128)(2,1)}) custom-call(bf16[32,144,128]{2,1,0:T(8,128)(2,1)} %all-to-all-done.arrived), custom_call_target="tpu_custom_call" | custom-call | tf_op jit(solution)/shard_map/pallas_call | solution.py:302
  56.3 6.1 %all-to-all-start.2 = ((bf16[8,6,32,128]{3,2,1,0:T(8,128)(2,1)}), bf16[8,6,32,128]{3,2,1,0:T(8,128)(2,1)}, u32[]{:S(2)}, u32[]{:S(2)}) async-start(bf16[8,6,32,128]{3,2,1,0:T(8,128)(2,1)} %bitcast.12), calls=%async_computation.2 | async-start | bytes 786432 | tf_op jit(solution)/shard_map/all_to_all | solution.py:254
  62.4 5.4 %collective-permute-start.7 = (bf16[27,32,512]{2,1,0:T(8,128)(2,1)S(1)}, bf16[27,32,512]{2,1,0:T(8,128)(2,1)}, u32[]{:S(2)}, u32[]{:S(2)}) collective-permute-start(bf16[27,32,512]{2,1,0:T(8,128)(2,1)S(1)} %collective-permute-done.4.rest_5_), channel_id=1, source_target_pairs={{0,16},{16,0},{1,17},{17,1},{2,18},{18,2},{3,19},{19,3},{4,20},{20... | collective-permute-start | bytes 2654216 | tf_op jit(solution)/shard_map/ppermute | solution.py:267
  67.8 0.0 collective-permute-done.5.rest_7_
  67.8 4.9 %collective-permute-start.6 = (bf16[27,16,512]{2,1,0:T(8,128)(2,1)}, bf16[27,16,512]{2,1,0:T(8,128)(2,1)S(1)}, u32[]{:S(2)}, u32[]{:S(2)}) collective-permute-start(bf16[27,16,512]{2,1,0:T(8,128)(2,1)} %collective-permute-done.5.rest_7_), channel_id=1, source_target_pairs={{0,16},{16,0},{1,17},{17,1},{2,18},{18,2},{3,19},{19,3},{4,20},{20... | collective-permute-start | bytes 1327112 | tf_op jit(solution)/shard_map/ppermute | solution.py:267
  72.7 1.6 %collective-permute-done.6.rest_8_ = bf16[27,16,512]{2,1,0:T(8,128)(2,1)S(1)} collective-permute-done((bf16[27,16,512]{2,1,0:T(8,128)(2,1)}, bf16[27,16,512]{2,1,0:T(8,128)(2,1)S(1)}, u32[]{:S(2)}, u32[]{:S(2)}) %collective-permute-start.6) | collective-permute-done | bytes 442400 | tf_op jit(solution)/shard_map/ppermute | solution.py:267
  74.3 0.0 copy-start.1
  74.3 0.8 copy-done.1
  75.1 0.0 all-to-all-done.2.frames
  75.1 4.3 %all-to-all-start.1 = ((bf16[8,6,32,128]{3,2,1,0:T(8,128)(2,1)}), bf16[8,6,32,128]{3,2,1,0:T(8,128)(2,1)}, u32[]{:S(2)}, u32[]{:S(2)}) async-start(bf16[8,6,32,128]{3,2,1,0:T(8,128)(2,1)} %bitcast.11), calls=%async_computation.1 | async-start | bytes 786432 | tf_op jit(solution)/shard_map/all_to_all | solution.py:254
  79.4 0.0 collective-permute-done.7.rest_6_
  79.4 0.0 copy-done
  79.5 0.0 copy-done.4
  79.5 0.0 copy-start.2
  79.5 1.0 copy-done.2
  80.5 3.8 %shard_map.67 = (f32[128,512]{1,0:T(8,128)S(1)}, f32[128,512]{1,0:T(8,128)S(1)}) custom-call(s32[4]{0:T(128)S(1)} %copy-done.4, bf16[8,6,32,128]{3,2,1,0:T(8,128)(2,1)} %all-to-all-done.2.frames, bf16[27,32,512]{2,1,0:T(8,128)(2,1)S(1)} %bitcast.7, bf16[27,32,512]{2,1,0:T(8,128)(2,1)S(1)} %collective-permute-done.rest_1_, ...), custom_call_target="tpu_custom_call" | custom-call | tf_op jit(solution)/shard_map/pallas_call | solution.py:272
  84.2 5.6 %collective-permute-start.8 = (f32[128,512]{1,0:T(8,128)S(1)}, f32[128,512]{1,0:T(8,128)S(1)}, u32[]{:S(2)}, u32[]{:S(2)}) collective-permute-start(f32[128,512]{1,0:T(8,128)S(1)} %get-tuple-element.29), channel_id=1, source_target_pairs={{0,16},{16,32},{32,48},{48,64},{64,80},{80,96},{96,112},{112,128},... | collective-permute-start | bytes 786440 | tf_op jit(solution)/shard_map/ppermute | solution.py:323
  89.9 3.3 %collective-permute-done.8 = f32[128,512]{1,0:T(8,128)S(1)} collective-permute-done((f32[128,512]{1,0:T(8,128)S(1)}, f32[128,512]{1,0:T(8,128)S(1)}, u32[]{:S(2)}, u32[]{:S(2)}) %collective-permute-start.8) | collective-permute-done | bytes 262176 | tf_op jit(solution)/shard_map/ppermute | solution.py:323
  93.2 0.7 add.10
  93.9 9.0 %collective-permute-start.9 = (f32[128,512]{1,0:T(8,128)}, f32[128,512]{1,0:T(8,128)}, u32[]{:S(2)}, u32[]{:S(2)}) collective-permute-start(f32[128,512]{1,0:T(8,128)} %add.10), channel_id=1, source_target_pairs={{0,8},{8,0},{1,9},{9,1},{2,10},{10,2},{3,11},{11,3},{4,12},{12,4},... | collective-permute-start | bytes 786440 | tf_op jit(solution)/shard_map/ppermute | solution.py:326
  102.9 0.0 all-to-all-done.1.frames
  102.9 0.0 copy-start.3
  102.9 1.0 copy-done.3
  103.9 3.8 %shard_map.66 = (f32[128,512]{1,0:T(8,128)S(1)}, f32[128,512]{1,0:T(8,128)S(1)}) custom-call(s32[4]{0:T(128)S(1)} %copy-done.4, bf16[8,6,32,128]{3,2,1,0:T(8,128)(2,1)} %all-to-all-done.1.frames, bf16[27,32,512]{2,1,0:T(8,128)(2,1)S(1)} %bitcast.8, bf16[27,32,512]{2,1,0:T(8,128)(2,1)S(1)} %collective-permute-done.rest_1_, ...), custom_call_target="tpu_custom_call" | custom-call | tf_op jit(solution)/shard_map/pallas_call | solution.py:272
  107.7 0.0 copy-start.5
  107.7 0.0 copy-start.6
  107.7 4.7 %collective-permute-start.10 = (f32[128,512]{1,0:T(8,128)S(1)}, f32[128,512]{1,0:T(8,128)S(1)}, u32[]{:S(2)}, u32[]{:S(2)}) collective-permute-start(f32[128,512]{1,0:T(8,128)S(1)} %get-tuple-element.30), channel_id=1, source_target_pairs={{0,16},{16,32},{32,48},{48,64},{64,80},{80,96},{96,112},{112,128},... | collective-permute-start | bytes 786440 | tf_op jit(solution)/shard_map/ppermute | solution.py:325
  112.4 0.0 collective-permute-done.9
  112.4 1.0 add.11.near
  113.4 2.3 %collective-permute-done.10.before = f32[128,512]{1,0:T(8,128)S(1)} collective-permute-done((f32[128,512]{1,0:T(8,128)S(1)}, f32[128,512]{1,0:T(8,128)S(1)}, u32[]{:S(2)}, u32[]{:S(2)}) %collective-permute-start.10) | collective-permute-done | bytes 262176 | tf_op jit(solution)/shard_map/ppermute | solution.py:325
  115.7 0.9 shard_map.68
  116.6 15.0 %all_to_all.25.got = f32[16,8,128]{2,1,0:T(8,128)} all-to-all(f32[16,8,128]{2,1,0:T(8,128)S(1)} %get-tuple-element.31), channel_id=1, replica_groups=mesh['zl'=4,'x'=4,'co'=2,'zh'=2,'y'=8] {'y','co'}, dimensions={0} | all-to-all | bytes 131072 | tf_op jit(solution)/shard_map/all_to_all | solution.py:254
  131.6 1.5 shard_map.69
  133.1 20.5 %all_to_all.26.got = f32[32,8,128]{2,1,0:T(8,128)S(1)} all-to-all(f32[32,8,128]{2,1,0:T(8,128)} %shard_map.69), channel_id=1, replica_groups=mesh['zl'=4,'x'=4,'co'=2,'zh'=2,'y'=8] {'zl','zh','x'}, dimensions={0} | all-to-all | bytes 262144 | tf_op jit(solution)/shard_map/all_to_all | solution.py:254
  153.6 0.0 copy-done.5
  153.6 0.0 copy-done.6
  153.6 1.5 shard_map.70
Async XLA Ops:
  0.0 19.0 %collective-permute-start = (bf16[27,32,512]{2,1,0:T(8,128)(2,1)}, bf16[27,32,512]{2,1,0:T(8,128)(2,1)S(1)}, u32[]{:S(2)}, u32[]{:S(2)}) collective-permute-start(bf16[27,32,512]{2,1,0:T(8,128)(2,1)} %bitcast.6), channel_id=1, source_target_pairs={{0,1},{1,2},{2,3},{3,4},{4,5},{5,6},{6,7},{7,0},{16,23},{17,16},{1... | collective-permute-start | bytes 2654216 | tf_op jit(solution)/shard_map/ppermute | solution.py:263
  9.0 44.3 %all-to-all-start = ((bf16[32,144,128]{2,1,0:T(8,128)(2,1)}), bf16[32,144,128]{2,1,0:T(8,128)(2,1)}, u32[]{:S(2)}, u32[]{:S(2)}) async-start(bf16[32,144,128]{2,1,0:T(8,128)(2,1)} %shard_map.64), calls=%async_computation | async-start | bytes 2359296 | tf_op jit(solution)/shard_map/all_to_all | solution.py:254
  19.0 14.2 %collective-permute-start.1 = (bf16[27,32,512]{2,1,0:T(8,128)(2,1)S(1)}, bf16[27,32,512]{2,1,0:T(8,128)(2,1)S(1)}, u32[]{:S(2)}, u32[]{:S(2)}) collective-permute-start(bf16[27,32,512]{2,1,0:T(8,128)(2,1)S(1)} %collective-permute-done.rest_1_), channel_id=1, source_target_pairs={{0,1},{1,2},{2,3},{3,4},{4,5},{5,6},{6,7},{7,0},{16,23},{17,16},{1... | collective-permute-start | bytes 2654216 | tf_op jit(solution)/shard_map/ppermute | solution.py:263
  33.2 14.1 %collective-permute-start.4 = (bf16[27,32,512]{2,1,0:T(8,128)(2,1)S(1)}, bf16[27,32,512]{2,1,0:T(8,128)(2,1)S(1)}, u32[]{:S(2)}, u32[]{:S(2)}) collective-permute-start(bf16[27,32,512]{2,1,0:T(8,128)(2,1)S(1)} %collective-permute-done.1.rest_3_), channel_id=1, source_target_pairs={{0,1},{1,2},{2,3},{3,4},{4,5},{5,6},{6,7},{7,0},{16,23},{17,16},{1... | collective-permute-start | bytes 2654216 | tf_op jit(solution)/shard_map/ppermute | solution.py:263
  37.3 15.9 %collective-permute-start.2 = (bf16[27,32,512]{2,1,0:T(8,128)(2,1)S(1)}, bf16[27,32,512]{2,1,0:T(8,128)(2,1)}, u32[]{:S(2)}, u32[]{:S(2)}) collective-permute-start(bf16[27,32,512]{2,1,0:T(8,128)(2,1)S(1)} %collective-permute-done.rest_1_), channel_id=1, source_target_pairs={{0,16},{16,0},{1,17},{17,1},{2,18},{18,2},{3,19},{19,3},{4,20},{20... | collective-permute-start | bytes 2654216 | tf_op jit(solution)/shard_map/ppermute | solution.py:267
  43.2 10.1 %collective-permute-start.3 = (bf16[27,32,512]{2,1,0:T(8,128)(2,1)S(1)}, bf16[27,32,512]{2,1,0:T(8,128)(2,1)}, u32[]{:S(2)}, u32[]{:S(2)}) collective-permute-start(bf16[27,32,512]{2,1,0:T(8,128)(2,1)S(1)} %collective-permute-done.1.rest_3_), channel_id=1, source_target_pairs={{0,16},{16,0},{1,17},{17,1},{2,18},{18,2},{3,19},{19,3},{4,20},{20... | collective-permute-start | bytes 2654216 | tf_op jit(solution)/shard_map/ppermute | solution.py:267
  48.1 31.3 %copy-start = (bf16[3,3,3,32,512]{4,3,2,1,0:T(8,128)(2,1)S(1)}, bf16[3,3,3,32,512]{4,3,2,1,0:T(8,128)(2,1)}, u32[]{:S(2)}) copy-start(bf16[3,3,3,32,512]{4,3,2,1,0:T(8,128)(2,1)} %param.9) | copy-start | bytes 2654212
  48.1 31.4 %copy-start.4 = (s32[4]{0:T(128)S(1)}, s32[4]{0:T(128)}, u32[]{:S(2)}) copy-start(s32[4]{0:T(128)} %lengths.7) | copy-start | bytes 52
  48.1 19.7 %collective-permute-start.5 = (bf16[27,16,512]{2,1,0:T(8,128)(2,1)}, bf16[27,16,512]{2,1,0:T(8,128)(2,1)}, u32[]{:S(2)}, u32[]{:S(2)}) collective-permute-start(bf16[27,16,512]{2,1,0:T(8,128)(2,1)} %constant_dynamic-slice_fusion), channel_id=1, source_target_pairs={{0,1},{1,2},{2,3},{3,4},{4,5},{5,6},{6,7},{7,0},{16,23},{17,16},{1... | collective-permute-start | bytes 1327112 | tf_op jit(solution)/shard_map/ppermute | solution.py:266
  56.3 18.8 %all-to-all-start.2 = ((bf16[8,6,32,128]{3,2,1,0:T(8,128)(2,1)}), bf16[8,6,32,128]{3,2,1,0:T(8,128)(2,1)}, u32[]{:S(2)}, u32[]{:S(2)}) async-start(bf16[8,6,32,128]{3,2,1,0:T(8,128)(2,1)} %bitcast.12), calls=%async_computation.2 | async-start | bytes 786432 | tf_op jit(solution)/shard_map/all_to_all | solution.py:254
  62.4 17.0 %collective-permute-start.7 = (bf16[27,32,512]{2,1,0:T(8,128)(2,1)S(1)}, bf16[27,32,512]{2,1,0:T(8,128)(2,1)}, u32[]{:S(2)}, u32[]{:S(2)}) collective-permute-start(bf16[27,32,512]{2,1,0:T(8,128)(2,1)S(1)} %collective-permute-done.4.rest_5_), channel_id=1, source_target_pairs={{0,16},{16,0},{1,17},{17,1},{2,18},{18,2},{3,19},{19,3},{4,20},{20... | collective-permute-start | bytes 2654216 | tf_op jit(solution)/shard_map/ppermute | solution.py:267
  67.8 6.5 %collective-permute-start.6 = (bf16[27,16,512]{2,1,0:T(8,128)(2,1)}, bf16[27,16,512]{2,1,0:T(8,128)(2,1)S(1)}, u32[]{:S(2)}, u32[]{:S(2)}) collective-permute-start(bf16[27,16,512]{2,1,0:T(8,128)(2,1)} %collective-permute-done.5.rest_7_), channel_id=1, source_target_pairs={{0,16},{16,0},{1,17},{17,1},{2,18},{18,2},{3,19},{19,3},{4,20},{20... | collective-permute-start | bytes 1327112 | tf_op jit(solution)/shard_map/ppermute | solution.py:267
  74.3 0.8 copy-start.1
  75.1 27.8 %all-to-all-start.1 = ((bf16[8,6,32,128]{3,2,1,0:T(8,128)(2,1)}), bf16[8,6,32,128]{3,2,1,0:T(8,128)(2,1)}, u32[]{:S(2)}, u32[]{:S(2)}) async-start(bf16[8,6,32,128]{3,2,1,0:T(8,128)(2,1)} %bitcast.11), calls=%async_computation.1 | async-start | bytes 786432 | tf_op jit(solution)/shard_map/all_to_all | solution.py:254
  79.5 1.0 copy-start.2
  84.2 8.9 %collective-permute-start.8 = (f32[128,512]{1,0:T(8,128)S(1)}, f32[128,512]{1,0:T(8,128)S(1)}, u32[]{:S(2)}, u32[]{:S(2)}) collective-permute-start(f32[128,512]{1,0:T(8,128)S(1)} %get-tuple-element.29), channel_id=1, source_target_pairs={{0,16},{16,32},{32,48},{48,64},{64,80},{80,96},{96,112},{112,128},... | collective-permute-start | bytes 786440 | tf_op jit(solution)/shard_map/ppermute | solution.py:323
  93.9 18.5 %collective-permute-start.9 = (f32[128,512]{1,0:T(8,128)}, f32[128,512]{1,0:T(8,128)}, u32[]{:S(2)}, u32[]{:S(2)}) collective-permute-start(f32[128,512]{1,0:T(8,128)} %add.10), channel_id=1, source_target_pairs={{0,8},{8,0},{1,9},{9,1},{2,10},{10,2},{3,11},{11,3},{4,12},{12,4},... | collective-permute-start | bytes 786440 | tf_op jit(solution)/shard_map/ppermute | solution.py:326
  102.9 1.0 copy-start.3
  107.7 46.0 %copy-start.5 = (f32[512]{0:T(512)S(1)}, f32[512]{0:T(512)}, u32[]{:S(2)}) copy-start(f32[512]{0:T(512)} %param.10) | copy-start | bytes 6148
  107.7 45.9 %copy-start.6 = (f32[512]{0:T(512)S(1)}, f32[512]{0:T(512)}, u32[]{:S(2)}) copy-start(f32[512]{0:T(512)} %param.11) | copy-start | bytes 6148
  107.7 8.0 %collective-permute-start.10 = (f32[128,512]{1,0:T(8,128)S(1)}, f32[128,512]{1,0:T(8,128)S(1)}, u32[]{:S(2)}, u32[]{:S(2)}) collective-permute-start(f32[128,512]{1,0:T(8,128)S(1)} %get-tuple-element.30), channel_id=1, source_target_pairs={{0,16},{16,32},{32,48},{48,64},{64,80},{80,96},{96,112},{112,128},... | collective-permute-start | bytes 786440 | tf_op jit(solution)/shard_map/ppermute | solution.py:325

commit v7 on v5

--- a/solution.py
+++ b/solution.py
@@ -19,6 +19,7 @@
 COUT = 512
 GROUPS = 32
 GROUP_SIZE = 16
+DEVICES = 512
 EPSILON = 1e-05
 BF = jnp.bfloat16
 F32 = jnp.float32
@@ -33,7 +34,9 @@
     return pltpu.CompilerParams(vmem_limit_bytes=mib * 1024 * 1024)
 
 
-def pack_kernel(target, arrived, send, counts, places, rounded, sems):
+def pack_kernel(target, arrived, send, rows, counts, places, rounded, sems):
+    fetch = pltpu.make_async_copy(arrived, rows, sems.at[0])
+    fetch.start()
     places[...] = jnp.full(places.shape, float(ROWS), F32)
 
     def clear(i, carry):
@@ -41,6 +44,7 @@
         return carry
 
     lax.fori_loop(0, SLABS, clear, 0)
+    fetch.wait()
 
     def one(i, carry):
         t = target[i]
@@ -48,7 +52,7 @@
         rank = counts[owner]
         counts[owner] = rank + 1
         slot = pl.ds(pl.multiple_of(rank * CH_DEV, CH_DEV), CH_DEV)
-        pltpu.make_async_copy(arrived.at[i], send.at[owner, slot], sems.at[0]).start()
+        pltpu.make_async_copy(rows.at[i], send.at[owner, slot], sems.at[0]).start()
         place = lax.bitwise_and(t, ROWS - 1).astype(F32)
         places[owner, pl.ds(rank, 1), :] = jnp.full((1, 128), place, F32)
         return carry
@@ -57,7 +61,7 @@
     rounded[...] = places[...].astype(BF)
     listed = pltpu.make_async_copy(rounded, send.at[:, pl.ds(CAP * CH_DEV, 16)], sems.at[1])
     listed.start()
-    pltpu.make_async_copy(arrived, arrived, sems.at[0]).wait()
+    pltpu.make_async_copy(rows, rows, sems.at[0]).wait()
     listed.wait()
 
 
@@ -175,11 +179,16 @@
     lax.fori_loop(0, 3, row_tap, 0)
 
 
-def group_matrix(channels_first):
-    shape = (COUT, 128) if channels_first else (128, COUT)
-    c = lax.broadcasted_iota(jnp.int32, shape, 0 if channels_first else 1)
-    g = lax.broadcasted_iota(jnp.int32, shape, 1 if channels_first else 0)
-    return (lax.shift_right_logical(c, 4) == g).astype(F32)
+def group_matrix():
+    c = lax.broadcasted_iota(jnp.int32, (COUT, 128), 0)
+    g = lax.broadcasted_iota(jnp.int32, (COUT, 128), 1)
+    return (lax.shift_right_logical(c, 4) == lax.bitwise_and(g, GROUPS - 1)).astype(F32)
+
+
+def spread_matrix():
+    g = lax.broadcasted_iota(jnp.int32, (128, COUT), 0)
+    c = lax.broadcasted_iota(jnp.int32, (128, COUT), 1)
+    return (lax.shift_right_logical(c, 4) == lax.bitwise_and(g, GROUPS - 1)).astype(F32)
 
 
 def member_of(lengths, frame):
@@ -202,36 +211,40 @@
         rows.append(jnp.sum(part, axis=0, keepdims=True))
         rows.append(jnp.sum(part * part, axis=0, keepdims=True))
     rows = jnp.concatenate(rows + rows, axis=0)
-    grouped = jnp.dot(rows, group_matrix(True), precision=HIGHEST, preferred_element_type=F32)
+    grouped = jnp.dot(rows, group_matrix(), precision=HIGHEST, preferred_element_type=F32)
     m0 = member_of(lengths, slab * 2)
     m1 = member_of(lengths, slab * 2 + 1)
     sums = [grouped[0:1] * m0[k] + grouped[2:3] * m1[k] for k in range(4)]
     squares = [grouped[1:2] * m0[k] + grouped[3:4] * m1[k] for k in range(4)]
-    tile = jnp.concatenate(sums + squares, axis=0)
+    lane = lax.broadcasted_iota(jnp.int32, (1, 128), 1)
+    clip_of = lax.shift_right_logical(lane, 5)
+    halves = []
+    for part in (sums, squares):
+        row = jnp.zeros((1, 128), F32)
+        for k in range(4):
+            row = jnp.where(clip_of == k, part[k], row)
+        halves.append(row)
+    tile = jnp.concatenate(halves, axis=1)
     stats[...] = jnp.broadcast_to(tile[None], stats.shape)
-
-
-def middle_kernel(got, out):
-    out[...] = jnp.broadcast_to(jnp.sum(got[...], axis=0)[None], out.shape)
 
 
 def final_kernel(lengths, got, conv, gain, bias, out):
     slab = my_slab()
     total = jnp.sum(got[...], axis=0)
-    spread = group_matrix(False)
+    spread = spread_matrix()
+    lane = lax.broadcasted_iota(jnp.int32, (1, 128), 1)
+    clip_of = lax.shift_right_logical(lane, 5)
     for f in range(2):
         flags = member_of(lengths, slab * 2 + f)
-        sums = jnp.zeros((1, 128), F32)
-        squares = jnp.zeros((1, 128), F32)
+        chosen = jnp.zeros((1, 128), F32)
         frames = jnp.float32(0)
         for k in range(4):
-            sums = sums + total[k:k + 1] * flags[k]
-            squares = squares + total[4 + k:5 + k] * flags[k]
+            chosen = jnp.where(clip_of == k, jnp.full((1, 128), flags[k], F32), chosen)
             frames = frames + flags[k] * lengths[k].astype(F32)
         entries = jnp.full((1, 128), frames * float(OUT_ROWS * 64 * GROUP_SIZE), F32)
-        mean = sums / entries
-        var = squares / entries - mean * mean
-        scale = lax.rsqrt(var + EPSILON)
+        mean = total[:, :128] * chosen / entries
+        var = total[:, 128:] * chosen / entries - mean * mean
+        scale = lax.rsqrt(var + EPSILON) * chosen
         both = jnp.concatenate([mean, scale] * 4, axis=0)
         wide = jnp.dot(both, spread, precision=HIGHEST, preferred_element_type=F32)
         part = conv[f * 64:(f + 1) * 64]
@@ -276,15 +289,18 @@
         in_specs=[SMEM, HBM],
         out_specs=HBM,
         scratch_shapes=[
+            pltpu.VMEM((ROWS, CH_DEV, 128), BF),
             pltpu.SMEM((SLABS,), jnp.int32),
             pltpu.VMEM((SLABS, 16, 128), F32),
             pltpu.VMEM((SLABS, 16, 128), BF),
             pltpu.SemaphoreType.DMA((2,)),
         ],
-        compiler_params=params(8),
+        compiler_params=params(60),
     )(row_target, arrived)
     got = shuffle(send, TM)
-    got, moved[2], swapped[0] = lax.optimization_barrier((got, moved[2], swapped[0]))
+    got, moved[2], swapped[0] = lax.optimization_barrier(
+        (got, moved[2], swapped[0])
+    )
     far, near = pl.pallas_call(
         place_kernel,
         out_shape=[jax.ShapeDtypeStruct((NY * 6, CH_DEV, 128), BF)] * 2,
@@ -311,19 +327,12 @@
     near = near + far
     conv, stats = pl.pallas_call(
         stat_kernel,
-        out_shape=[jax.ShapeDtypeStruct((128, COUT), F32), jax.ShapeDtypeStruct((16, 8, 128), F32)],
+        out_shape=[jax.ShapeDtypeStruct((128, COUT), F32), jax.ShapeDtypeStruct((DEVICES, 1, 256), F32)],
         in_specs=[SMEM, VMEM, VMEM],
         out_specs=[VMEM, VMEM],
         compiler_params=params(16),
     )(clip_lengths, near, near_before)
-    stats = shuffle(stats, ("y", "co"))
-    stats = pl.pallas_call(
-        middle_kernel,
-        out_shape=jax.ShapeDtypeStruct((SLABS, 8, 128), F32),
-        in_specs=[VMEM],
-        out_specs=VMEM,
-    )(stats)
-    stats = shuffle(stats, ("zl", "zh", "x"))
+    stats = shuffle(stats, TM + CH)
     out = pl.pallas_call(
         final_kernel,
         out_shape=jax.ShapeDtypeStruct((2, 64, COUT), BF),

time: 151 us -> 154 us (1.020)
  blocking collectives: 34 us -> 38.4 us
  local copies, waits for them, and re-layouts: 5.01 us -> 3.34 us
    all_to_all x2 -> x1, blocking collectives: 34 us -> 38.4 us  [shuffle(): return lax.all_to_all(x, axis, split_axis=0, concat_axis=0, tiled=True)]
    unnamed x18 -> x14, local copies, waits for them, and re-layouts: 4.98 us -> 3.3 us
where the time goes in v7:
time: 154 us; the launch traced here: 153 us
  starting transfers between devices  65.9 us (43%)
  blocking collectives  38.4 us (25%)
  waiting for transfers between devices  28.4 us (18%)
  Pallas kernels  15.8 us (10%)
  local copies, waits for them, and re-layouts  3.34 us (2%)
    all_to_all x1, blocking collectives, shuffle(): return lax.all_to_all(x, axis, split_axis=0, concat_axis=0, tiled=True)  38.4 us
    all_to_all x3, starting transfers between devices, shuffle(): return lax.all_to_all(x, axis, split_axis=0, concat_axis=0, tiled=True)  19.3 us
    ppermute x3, starting transfers between devices, gathered_weights(): moved.append(lax.ppermute(moved[-1], ('co', 'y'), ring))  12.9 us
    ppermute x4, starting transfers between devices, gathered_weights(): swapped = [lax.ppermute(shard, 'co', swap) for shard in moved[1:]]  12.9 us
    all_to_all x3, waiting for transfers between devices, shuffle(): return lax.all_to_all(x, axis, split_axis=0, concat_axis=0, tiled=True)  9.91 us
    ppermute x1, starting transfers between devices, body(): far = lax.ppermute(far + far_before, 'zh', [(0, 1), (1, 0)])  7.94 us
    pallas_call x2, Pallas kernels, convolve(): pl.pallas_call(conv_kernel, out_shape=[jax.ShapeDtypeStruct((128, COUT),...  7.52 us
    ppermute x1, waiting for transfers between devices, gathered_weights(): moved.append(lax.ppermute(half, ('co', 'y'), ring))  6.82 us
  transfers between devices with their start and end apart: 14, of which 5 were waited for; matrix products, arithmetic and copies ran while one was open for 1% of the time, Pallas kernels for 8%

profile of v7, /device:TPU:1, one launch (start us, length us, event | category | flops | bytes accessed | tf_op | source)
XLA Modules:
  0.0 153.1 jit_solution(3615393838635207728)
XLA Ops:
  0.0 5.9 %collective-permute-start = (bf16[27,32,512]{2,1,0:T(8,128)(2,1)}, bf16[27,32,512]{2,1,0:T(8,128)(2,1)S(1)}, u32[]{:S(2)}, u32[]{:S(2)}) collective-permute-start(bf16[27,32,512]{2,1,0:T(8,128)(2,1)} %bitcast.6), channel_id=1, source_target_pairs={{0,1},{1,2},{2,3},{3,4},{4,5},{5,6},{6,7},{7,0},{16,23},{17,16},{1... | collective-permute-start | bytes 2654216 | tf_op jit(solution)/shard_map/ppermute | solution.py:265
  5.9 3.0 %shard_map.64 = bf16[32,144,128]{2,1,0:T(8,128)(2,1)} custom-call(s32[64]{0:T(128)} %target.1, bf16[64,32,128]{2,1,0:T(8,128)(2,1)} %arrived.1), custom_call_target="tpu_custom_call" | custom-call | tf_op jit(solution)/shard_map/pallas_call | solution.py:286
  8.9 10.0 %all-to-all-start = ((bf16[32,144,128]{2,1,0:T(8,128)(2,1)}), bf16[32,144,128]{2,1,0:T(8,128)(2,1)S(1)}, u32[]{:S(2)}, u32[]{:S(2)}) async-start(bf16[32,144,128]{2,1,0:T(8,128)(2,1)} %shard_map.64), calls=%async_computation | async-start | bytes 2359296 | tf_op jit(solution)/shard_map/all_to_all | solution.py:256
  18.9 0.0 collective-permute-done.rest_1_
  19.0 3.0 %collective-permute-start.1 = (bf16[27,32,512]{2,1,0:T(8,128)(2,1)S(1)}, bf16[27,32,512]{2,1,0:T(8,128)(2,1)}, u32[]{:S(2)}, u32[]{:S(2)}) collective-permute-start(bf16[27,32,512]{2,1,0:T(8,128)(2,1)S(1)} %collective-permute-done.rest_1_), channel_id=1, source_target_pairs={{0,1},{1,2},{2,3},{3,4},{4,5},{5,6},{6,7},{7,0},{16,23},{17,16},{1... | collective-permute-start | bytes 2654216 | tf_op jit(solution)/shard_map/ppermute | solution.py:265
  21.9 5.1 %collective-permute-start.2 = (bf16[27,32,512]{2,1,0:T(8,128)(2,1)S(1)}, bf16[27,32,512]{2,1,0:T(8,128)(2,1)S(1)}, u32[]{:S(2)}, u32[]{:S(2)}) collective-permute-start(bf16[27,32,512]{2,1,0:T(8,128)(2,1)S(1)} %collective-permute-done.rest_1_), channel_id=1, source_target_pairs={{0,16},{16,0},{1,17},{17,1},{2,18},{18,2},{3,19},{19,3},{4,20},{20... | collective-permute-start | bytes 2654216 | tf_op jit(solution)/shard_map/ppermute | solution.py:269
  27.1 6.1 %collective-permute-done.1.rest_3_ = bf16[27,32,512]{2,1,0:T(8,128)(2,1)} collective-permute-done((bf16[27,32,512]{2,1,0:T(8,128)(2,1)S(1)}, bf16[27,32,512]{2,1,0:T(8,128)(2,1)}, u32[]{:S(2)}, u32[]{:S(2)}) %collective-permute-start.1) | collective-permute-done | bytes 884768 | tf_op jit(solution)/shard_map/ppermute | solution.py:265
  33.1 4.0 %collective-permute-start.4 = (bf16[27,32,512]{2,1,0:T(8,128)(2,1)}, bf16[27,32,512]{2,1,0:T(8,128)(2,1)S(1)}, u32[]{:S(2)}, u32[]{:S(2)}) collective-permute-start(bf16[27,32,512]{2,1,0:T(8,128)(2,1)} %collective-permute-done.1.rest_3_), channel_id=1, source_target_pairs={{0,1},{1,2},{2,3},{3,4},{4,5},{5,6},{6,7},{7,0},{16,23},{17,16},{1... | collective-permute-start | bytes 2654216 | tf_op jit(solution)/shard_map/ppermute | solution.py:265
  37.2 0.0 collective-permute-done.2.rest_2_
  37.2 0.0 copy-start.1
  37.2 1.0 copy-done.1
  38.2 9.9 %all-to-all-done.got = bf16[32,144,128]{2,1,0:T(8,128)(2,1)S(1)} async-done(((bf16[32,144,128]{2,1,0:T(8,128)(2,1)}), bf16[32,144,128]{2,1,0:T(8,128)(2,1)S(1)}, u32[]{:S(2)}, u32[]{:S(2)}) %all-to-all-start) | async-done | bytes 1179680 | tf_op jit(solution)/shard_map/all_to_all | solution.py:256
  48.1 2.1 %shard_map.65 = (bf16[48,32,128]{2,1,0:T(8,128)(2,1)}, bf16[48,32,128]{2,1,0:T(8,128)(2,1)}) custom-call(bf16[32,144,128]{2,1,0:T(8,128)(2,1)S(1)} %all-to-all-done.got), custom_call_target="tpu_custom_call" | custom-call | tf_op jit(solution)/shard_map/pallas_call | solution.py:304
  50.2 0.0 copy-start
  50.2 0.0 copy-start.4
  50.2 5.0 %all-to-all-start.2 = ((bf16[8,6,32,128]{3,2,1,0:T(8,128)(2,1)}), bf16[8,6,32,128]{3,2,1,0:T(8,128)(2,1)}, u32[]{:S(2)}, u32[]{:S(2)}) async-start(bf16[8,6,32,128]{3,2,1,0:T(8,128)(2,1)} %bitcast.2), calls=%async_computation.2 | async-start | bytes 786432 | tf_op jit(solution)/shard_map/all_to_all | solution.py:256
  55.2 2.4 %collective-permute-start.3 = (bf16[27,32,512]{2,1,0:T(8,128)(2,1)}, bf16[27,32,512]{2,1,0:T(8,128)(2,1)}, u32[]{:S(2)}, u32[]{:S(2)}) collective-permute-start(bf16[27,32,512]{2,1,0:T(8,128)(2,1)} %collective-permute-done.1.rest_3_), channel_id=1, source_target_pairs={{0,16},{16,0},{1,17},{17,1},{2,18},{18,2},{3,19},{19,3},{4,20},{20... | collective-permute-start | bytes 2654216 | tf_op jit(solution)/shard_map/ppermute | solution.py:269
  57.6 0.0 collective-permute-done.4.rest_5_
  57.7 4.9 %collective-permute-start.6 = (bf16[27,16,512]{2,1,0:T(8,128)(2,1)S(1)}, bf16[27,16,512]{2,1,0:T(8,128)(2,1)S(1)}, u32[]{:S(2)}, u32[]{:S(2)}) collective-permute-start(bf16[27,16,512]{2,1,0:T(8,128)(2,1)S(1)} %constant_dynamic-slice_fusion), channel_id=1, source_target_pairs={{0,1},{1,2},{2,3},{3,4},{4,5},{5,6},{6,7},{7,0},{16,23},{17,16},{1... | collective-permute-start | bytes 1327112 | tf_op jit(solution)/shard_map/ppermute | solution.py:268
  62.6 1.9 %collective-permute-start.5 = (bf16[27,32,512]{2,1,0:T(8,128)(2,1)S(1)}, bf16[27,32,512]{2,1,0:T(8,128)(2,1)}, u32[]{:S(2)}, u32[]{:S(2)}) collective-permute-start(bf16[27,32,512]{2,1,0:T(8,128)(2,1)S(1)} %collective-permute-done.4.rest_5_), channel_id=1, source_target_pairs={{0,16},{16,0},{1,17},{17,1},{2,18},{18,2},{3,19},{19,3},{4,20},{20... | collective-permute-start | bytes 2654216 | tf_op jit(solution)/shard_map/ppermute | solution.py:269
  64.5 6.8 %collective-permute-done.6.rest_7_ = bf16[27,16,512]{2,1,0:T(8,128)(2,1)S(1)} collective-permute-done((bf16[27,16,512]{2,1,0:T(8,128)(2,1)S(1)}, bf16[27,16,512]{2,1,0:T(8,128)(2,1)S(1)}, u32[]{:S(2)}, u32[]{:S(2)}) %collective-permute-start.6) | collective-permute-done | bytes 442400 | tf_op jit(solution)/shard_map/ppermute | solution.py:268
  71.3 3.5 %collective-permute-start.7 = (bf16[27,16,512]{2,1,0:T(8,128)(2,1)S(1)}, bf16[27,16,512]{2,1,0:T(8,128)(2,1)}, u32[]{:S(2)}, u32[]{:S(2)}) collective-permute-start(bf16[27,16,512]{2,1,0:T(8,128)(2,1)S(1)} %collective-permute-done.6.rest_7_), channel_id=1, source_target_pairs={{0,16},{16,0},{1,17},{17,1},{2,18},{18,2},{3,19},{19,3},{4,20},{20... | collective-permute-start | bytes 1327112 | tf_op jit(solution)/shard_map/ppermute | solution.py:269
  74.8 0.0 all-to-all-done.2.frames
  74.8 4.3 %all-to-all-start.1 = ((bf16[8,6,32,128]{3,2,1,0:T(8,128)(2,1)}), bf16[8,6,32,128]{3,2,1,0:T(8,128)(2,1)}, u32[]{:S(2)}, u32[]{:S(2)}) async-start(bf16[8,6,32,128]{3,2,1,0:T(8,128)(2,1)} %bitcast.1), calls=%async_computation.1 | async-start | bytes 786432 | tf_op jit(solution)/shard_map/all_to_all | solution.py:256
  79.1 0.0 collective-permute-done.3.rest_4_
  79.1 0.0 collective-permute-done.7.rest_8_
  79.1 0.0 collective-permute-done.5.rest_6_
  79.1 0.0 copy-done
  79.1 0.0 copy-done.4
  79.2 0.0 copy-start.2
  79.2 1.2 copy-done.2
  80.3 3.8 %shard_map.67 = (f32[128,512]{1,0:T(8,128)S(1)}, f32[128,512]{1,0:T(8,128)S(1)}) custom-call(s32[4]{0:T(128)S(1)} %copy-done.4, bf16[8,6,32,128]{3,2,1,0:T(8,128)(2,1)} %all-to-all-done.2.frames, bf16[27,32,512]{2,1,0:T(8,128)(2,1)S(1)} %bitcast.7, bf16[27,32,512]{2,1,0:T(8,128)(2,1)S(1)} %collective-permute-done.rest_1_, ...), custom_call_target="tpu_custom_call" | custom-call | tf_op jit(solution)/shard_map/pallas_call | solution.py:274
  84.1 3.3 %collective-permute-start.8 = (f32[128,512]{1,0:T(8,128)S(1)}, f32[128,512]{1,0:T(8,128)S(1)}, u32[]{:S(2)}, u32[]{:S(2)}) collective-permute-start(f32[128,512]{1,0:T(8,128)S(1)} %get-tuple-element.23), channel_id=1, source_target_pairs={{0,16},{16,32},{32,48},{48,64},{64,80},{80,96},{96,112},{112,128},... | collective-permute-start | bytes 786440 | tf_op jit(solution)/shard_map/ppermute | solution.py:323
  87.4 3.3 %collective-permute-done.8 = f32[128,512]{1,0:T(8,128)S(1)} collective-permute-done((f32[128,512]{1,0:T(8,128)S(1)}, f32[128,512]{1,0:T(8,128)S(1)}, u32[]{:S(2)}, u32[]{:S(2)}) %collective-permute-start.8) | collective-permute-done | bytes 262176 | tf_op jit(solution)/shard_map/ppermute | solution.py:323
  90.7 7.9 %collective-permute-start.9 = (f32[128,512]{1,0:T(8,128)S(1)}, f32[128,512]{1,0:T(8,128)}, u32[]{:S(2)}, u32[]{:S(2)}) collective-permute-start(f32[128,512]{1,0:T(8,128)S(1)} %add.10), channel_id=1, source_target_pairs={{0,8},{8,0},{1,9},{9,1},{2,10},{10,2},{3,11},{11,3},{4,12},{12,4},... | collective-permute-start | bytes 786440 | tf_op jit(solution)/shard_map/ppermute | solution.py:326
  98.7 0.0 all-to-all-done.1.frames
  98.7 0.0 copy-start.3
  98.7 1.2 copy-done.3
  99.9 3.8 %shard_map.66 = (f32[128,512]{1,0:T(8,128)S(1)}, f32[128,512]{1,0:T(8,128)S(1)}) custom-call(s32[4]{0:T(128)S(1)} %copy-done.4, bf16[8,6,32,128]{3,2,1,0:T(8,128)(2,1)} %all-to-all-done.1.frames, bf16[27,32,512]{2,1,0:T(8,128)(2,1)S(1)} %bitcast.8, bf16[27,32,512]{2,1,0:T(8,128)(2,1)S(1)} %collective-permute-done.rest_1_, ...), custom_call_target="tpu_custom_call" | custom-call | tf_op jit(solution)/shard_map/pallas_call | solution.py:274
  103.6 4.7 %collective-permute-start.10 = (f32[128,512]{1,0:T(8,128)S(1)}, f32[128,512]{1,0:T(8,128)S(1)}, u32[]{:S(2)}, u32[]{:S(2)}) collective-permute-start(f32[128,512]{1,0:T(8,128)S(1)} %get-tuple-element.24), channel_id=1, source_target_pairs={{0,16},{16,32},{32,48},{48,64},{64,80},{80,96},{96,112},{112,128},... | collective-permute-start | bytes 786440 | tf_op jit(solution)/shard_map/ppermute | solution.py:325
  108.3 0.0 collective-permute-done.9
  108.3 0.0 copy-start.5
  108.3 0.0 copy-start.6
  108.3 1.0 add.11.near
  109.3 2.2 %collective-permute-done.10.before = f32[128,512]{1,0:T(8,128)S(1)} collective-permute-done((f32[128,512]{1,0:T(8,128)S(1)}, f32[128,512]{1,0:T(8,128)S(1)}, u32[]{:S(2)}, u32[]{:S(2)}) %collective-permute-start.10) | collective-permute-done | bytes 262176 | tf_op jit(solution)/shard_map/ppermute | solution.py:325
  111.6 1.0 shard_map.68
  112.6 38.4 %all_to_all.20.got = f32[512,1,256]{2,1,0:T(1,128)S(1)} all-to-all(f32[512,1,256]{2,1,0:T(1,128)S(1)} %get-tuple-element.25), channel_id=1, replica_groups=mesh['zl'=4,'x'=4,'co'=2,'zh'=2,'y'=8] {'zl','x','co','zh','y'}, dimensions={0} | all-to-all | bytes 1048576 | tf_op jit(solution)/shard_map/all_to_all | solution.py:256
  151.0 0.0 copy-done.5
  151.0 0.0 copy-done.6
  151.0 2.1 %shard_map.69 = bf16[2,64,512]{2,1,0:T(8,128)(2,1)} custom-call(s32[4]{0:T(128)S(1)} %copy-done.4, f32[512,1,256]{2,1,0:T(1,128)S(1)} %all_to_all.20.got, f32[128,512]{1,0:T(8,128)S(1)} %get-tuple-element.26.conv, f32[1,512]{1,0:T(1,128)S(1)} %bitcast.9, f32[1,512]{1,0:T(1,128)S(1)} %bitcast.10), custom_call_target="tpu_custom_call" | custom-call | tf_op jit(solution)/shard_map/pallas_call | solution.py:336
  (2 shorter events, 0.1 us)
Async XLA Ops:
  0.0 19.0 %collective-permute-start = (bf16[27,32,512]{2,1,0:T(8,128)(2,1)}, bf16[27,32,512]{2,1,0:T(8,128)(2,1)S(1)}, u32[]{:S(2)}, u32[]{:S(2)}) collective-permute-start(bf16[27,32,512]{2,1,0:T(8,128)(2,1)} %bitcast.6), channel_id=1, source_target_pairs={{0,1},{1,2},{2,3},{3,4},{4,5},{5,6},{6,7},{7,0},{16,23},{17,16},{1... | collective-permute-start | bytes 2654216 | tf_op jit(solution)/shard_map/ppermute | solution.py:265
  8.9 39.1 %all-to-all-start = ((bf16[32,144,128]{2,1,0:T(8,128)(2,1)}), bf16[32,144,128]{2,1,0:T(8,128)(2,1)S(1)}, u32[]{:S(2)}, u32[]{:S(2)}) async-start(bf16[32,144,128]{2,1,0:T(8,128)(2,1)} %shard_map.64), calls=%async_computation | async-start | bytes 2359296 | tf_op jit(solution)/shard_map/all_to_all | solution.py:256
  19.0 14.2 %collective-permute-start.1 = (bf16[27,32,512]{2,1,0:T(8,128)(2,1)S(1)}, bf16[27,32,512]{2,1,0:T(8,128)(2,1)}, u32[]{:S(2)}, u32[]{:S(2)}) collective-permute-start(bf16[27,32,512]{2,1,0:T(8,128)(2,1)S(1)} %collective-permute-done.rest_1_), channel_id=1, source_target_pairs={{0,1},{1,2},{2,3},{3,4},{4,5},{5,6},{6,7},{7,0},{16,23},{17,16},{1... | collective-permute-start | bytes 2654216 | tf_op jit(solution)/shard_map/ppermute | solution.py:265
  21.9 15.3 %collective-permute-start.2 = (bf16[27,32,512]{2,1,0:T(8,128)(2,1)S(1)}, bf16[27,32,512]{2,1,0:T(8,128)(2,1)S(1)}, u32[]{:S(2)}, u32[]{:S(2)}) collective-permute-start(bf16[27,32,512]{2,1,0:T(8,128)(2,1)S(1)} %collective-permute-done.rest_1_), channel_id=1, source_target_pairs={{0,16},{16,0},{1,17},{17,1},{2,18},{18,2},{3,19},{19,3},{4,20},{20... | collective-permute-start | bytes 2654216 | tf_op jit(solution)/shard_map/ppermute | solution.py:269
  33.1 24.5 %collective-permute-start.4 = (bf16[27,32,512]{2,1,0:T(8,128)(2,1)}, bf16[27,32,512]{2,1,0:T(8,128)(2,1)S(1)}, u32[]{:S(2)}, u32[]{:S(2)}) collective-permute-start(bf16[27,32,512]{2,1,0:T(8,128)(2,1)} %collective-permute-done.1.rest_3_), channel_id=1, source_target_pairs={{0,1},{1,2},{2,3},{3,4},{4,5},{5,6},{6,7},{7,0},{16,23},{17,16},{1... | collective-permute-start | bytes 2654216 | tf_op jit(solution)/shard_map/ppermute | solution.py:265
  37.2 1.0 copy-start.1
  50.2 28.9 %copy-start = (bf16[3,3,3,32,512]{4,3,2,1,0:T(8,128)(2,1)S(1)}, bf16[3,3,3,32,512]{4,3,2,1,0:T(8,128)(2,1)}, u32[]{:S(2)}) copy-start(bf16[3,3,3,32,512]{4,3,2,1,0:T(8,128)(2,1)} %param.9) | copy-start | bytes 2654212
  50.2 28.9 %copy-start.4 = (s32[4]{0:T(128)S(1)}, s32[4]{0:T(128)}, u32[]{:S(2)}) copy-start(s32[4]{0:T(128)} %lengths.7) | copy-start | bytes 52
  50.2 24.6 %all-to-all-start.2 = ((bf16[8,6,32,128]{3,2,1,0:T(8,128)(2,1)}), bf16[8,6,32,128]{3,2,1,0:T(8,128)(2,1)}, u32[]{:S(2)}, u32[]{:S(2)}) async-start(bf16[8,6,32,128]{3,2,1,0:T(8,128)(2,1)} %bitcast.2), calls=%async_computation.2 | async-start | bytes 786432 | tf_op jit(solution)/shard_map/all_to_all | solution.py:256
  55.2 23.9 %collective-permute-start.3 = (bf16[27,32,512]{2,1,0:T(8,128)(2,1)}, bf16[27,32,512]{2,1,0:T(8,128)(2,1)}, u32[]{:S(2)}, u32[]{:S(2)}) collective-permute-start(bf16[27,32,512]{2,1,0:T(8,128)(2,1)} %collective-permute-done.1.rest_3_), channel_id=1, source_target_pairs={{0,16},{16,0},{1,17},{17,1},{2,18},{18,2},{3,19},{19,3},{4,20},{20... | collective-permute-start | bytes 2654216 | tf_op jit(solution)/shard_map/ppermute | solution.py:269
  57.7 13.6 %collective-permute-start.6 = (bf16[27,16,512]{2,1,0:T(8,128)(2,1)S(1)}, bf16[27,16,512]{2,1,0:T(8,128)(2,1)S(1)}, u32[]{:S(2)}, u32[]{:S(2)}) collective-permute-start(bf16[27,16,512]{2,1,0:T(8,128)(2,1)S(1)} %constant_dynamic-slice_fusion), channel_id=1, source_target_pairs={{0,1},{1,2},{2,3},{3,4},{4,5},{5,6},{6,7},{7,0},{16,23},{17,16},{1... | collective-permute-start | bytes 1327112 | tf_op jit(solution)/shard_map/ppermute | solution.py:268
  62.6 16.6 %collective-permute-start.5 = (bf16[27,32,512]{2,1,0:T(8,128)(2,1)S(1)}, bf16[27,32,512]{2,1,0:T(8,128)(2,1)}, u32[]{:S(2)}, u32[]{:S(2)}) collective-permute-start(bf16[27,32,512]{2,1,0:T(8,128)(2,1)S(1)} %collective-permute-done.4.rest_5_), channel_id=1, source_target_pairs={{0,16},{16,0},{1,17},{17,1},{2,18},{18,2},{3,19},{19,3},{4,20},{20... | collective-permute-start | bytes 2654216 | tf_op jit(solution)/shard_map/ppermute | solution.py:269
  71.3 7.8 %collective-permute-start.7 = (bf16[27,16,512]{2,1,0:T(8,128)(2,1)S(1)}, bf16[27,16,512]{2,1,0:T(8,128)(2,1)}, u32[]{:S(2)}, u32[]{:S(2)}) collective-permute-start(bf16[27,16,512]{2,1,0:T(8,128)(2,1)S(1)} %collective-permute-done.6.rest_7_), channel_id=1, source_target_pairs={{0,16},{16,0},{1,17},{17,1},{2,18},{18,2},{3,19},{19,3},{4,20},{20... | collective-permute-start | bytes 1327112 | tf_op jit(solution)/shard_map/ppermute | solution.py:269
  74.8 23.8 %all-to-all-start.1 = ((bf16[8,6,32,128]{3,2,1,0:T(8,128)(2,1)}), bf16[8,6,32,128]{3,2,1,0:T(8,128)(2,1)}, u32[]{:S(2)}, u32[]{:S(2)}) async-start(bf16[8,6,32,128]{3,2,1,0:T(8,128)(2,1)} %bitcast.1), calls=%async_computation.1 | async-start | bytes 786432 | tf_op jit(solution)/shard_map/all_to_all | solution.py:256
  79.2 1.2 copy-start.2
  84.1 6.6 %collective-permute-start.8 = (f32[128,512]{1,0:T(8,128)S(1)}, f32[128,512]{1,0:T(8,128)S(1)}, u32[]{:S(2)}, u32[]{:S(2)}) collective-permute-start(f32[128,512]{1,0:T(8,128)S(1)} %get-tuple-element.23), channel_id=1, source_target_pairs={{0,16},{16,32},{32,48},{48,64},{64,80},{80,96},{96,112},{112,128},... | collective-permute-start | bytes 786440 | tf_op jit(solution)/shard_map/ppermute | solution.py:323
  90.7 17.6 %collective-permute-start.9 = (f32[128,512]{1,0:T(8,128)S(1)}, f32[128,512]{1,0:T(8,128)}, u32[]{:S(2)}, u32[]{:S(2)}) collective-permute-start(f32[128,512]{1,0:T(8,128)S(1)} %add.10), channel_id=1, source_target_pairs={{0,8},{8,0},{1,9},{9,1},{2,10},{10,2},{3,11},{11,3},{4,12},{12,4},... | collective-permute-start | bytes 786440 | tf_op jit(solution)/shard_map/ppermute | solution.py:326
  98.7 1.2 copy-start.3
  103.6 8.0 %collective-permute-start.10 = (f32[128,512]{1,0:T(8,128)S(1)}, f32[128,512]{1,0:T(8,128)S(1)}, u32[]{:S(2)}, u32[]{:S(2)}) collective-permute-start(f32[128,512]{1,0:T(8,128)S(1)} %get-tuple-element.24), channel_id=1, source_target_pairs={{0,16},{16,32},{32,48},{48,64},{64,80},{80,96},{96,112},{112,128},... | collective-permute-start | bytes 786440 | tf_op jit(solution)/shard_map/ppermute | solution.py:325
  108.3 42.7 %copy-start.5 = (f32[512]{0:T(512)S(1)}, f32[512]{0:T(512)}, u32[]{:S(2)}) copy-start(f32[512]{0:T(512)} %param.10) | copy-start | bytes 6148
  108.3 42.7 %copy-start.6 = (f32[512]{0:T(512)S(1)}, f32[512]{0:T(512)}, u32[]{:S(2)}) copy-start(f32[512]{0:T(512)} %param.11) | copy-start | bytes 6148

commit v8 on v5

--- a/solution.py
+++ b/solution.py
@@ -33,7 +33,9 @@
     return pltpu.CompilerParams(vmem_limit_bytes=mib * 1024 * 1024)
 
 
-def pack_kernel(target, arrived, send, counts, places, rounded, sems):
+def pack_kernel(target, arrived, send, rows, counts, places, sem):
+    fetch = pltpu.make_async_copy(arrived, rows, sem)
+    fetch.start()
     places[...] = jnp.full(places.shape, float(ROWS), F32)
 
     def clear(i, carry):
@@ -41,24 +43,23 @@
         return carry
 
     lax.fori_loop(0, SLABS, clear, 0)
-
-    def one(i, carry):
-        t = target[i]
-        owner = lax.shift_right_logical(t, 6)
-        rank = counts[owner]
-        counts[owner] = rank + 1
-        slot = pl.ds(pl.multiple_of(rank * CH_DEV, CH_DEV), CH_DEV)
-        pltpu.make_async_copy(arrived.at[i], send.at[owner, slot], sems.at[0]).start()
-        place = lax.bitwise_and(t, ROWS - 1).astype(F32)
-        places[owner, pl.ds(rank, 1), :] = jnp.full((1, 128), place, F32)
+    fetch.wait()
+
+    def some(n, carry):
+        for k in range(4):
+            i = n * 4 + k
+            t = target[i]
+            owner = lax.shift_right_logical(t, 6)
+            rank = counts[owner]
+            counts[owner] = rank + 1
+            slot = pl.ds(pl.multiple_of(rank * CH_DEV, CH_DEV), CH_DEV)
+            send[owner, slot, :] = rows[i]
+            place = lax.bitwise_and(t, ROWS - 1).astype(F32)
+            places[owner, pl.ds(rank, 1), :] = jnp.full((1, 128), place, F32)
         return carry
 
-    lax.fori_loop(0, ROWS, one, 0)
-    rounded[...] = places[...].astype(BF)
-    listed = pltpu.make_async_copy(rounded, send.at[:, pl.ds(CAP * CH_DEV, 16)], sems.at[1])
-    listed.start()
-    pltpu.make_async_copy(arrived, arrived, sems.at[0]).wait()
-    listed.wait()
+    lax.fori_loop(0, ROWS // 4, some, 0)
+    send[:, CAP * CH_DEV:, :] = places[...].astype(BF)
 
 
 def my_slab():
@@ -72,8 +73,8 @@
 
 def place_kernel(got, far, near, both, table, moves, sems):
     zh = lax.axis_index("zh")
-    lane = lax.broadcasted_iota(jnp.int32, (16, 128), 1)
-    place = jnp.full((16, 128), float(ROWS), F32)
+    lane = lax.broadcasted_iota(jnp.int32, (8, 128), 1)
+    place = jnp.full((8, 128), float(ROWS), F32)
     for s in range(SLABS):
         place = jnp.where(lane == s, got[s, CAP * CH_DEV:, :].astype(F32), place)
     place = place.astype(jnp.int32)
@@ -272,19 +273,21 @@
     moved, swapped = gathered_weights(conv_weight.reshape(27, CH_DEV, COUT))
     send = pl.pallas_call(
         pack_kernel,
-        out_shape=jax.ShapeDtypeStruct((SLABS, 144, 128), BF),
+        out_shape=jax.ShapeDtypeStruct((SLABS, 136, 128), BF),
         in_specs=[SMEM, HBM],
-        out_specs=HBM,
+        out_specs=VMEM,
         scratch_shapes=[
+            pltpu.VMEM((ROWS, CH_DEV, 128), BF),
             pltpu.SMEM((SLABS,), jnp.int32),
-            pltpu.VMEM((SLABS, 16, 128), F32),
-            pltpu.VMEM((SLABS, 16, 128), BF),
-            pltpu.SemaphoreType.DMA((2,)),
+            pltpu.VMEM((SLABS, 8, 128), F32),
+            pltpu.SemaphoreType.DMA,
         ],
-        compiler_params=params(8),
+        compiler_params=params(60),
     )(row_target, arrived)
     got = shuffle(send, TM)
-    got, moved[2], swapped[0] = lax.optimization_barrier((got, moved[2], swapped[0]))
+    got, moved[2], swapped[0] = lax.optimization_barrier(
+        (got, moved[2], swapped[0])
+    )
     far, near = pl.pallas_call(
         place_kernel,
         out_shape=[jax.ShapeDtypeStruct((NY * 6, CH_DEV, 128), BF)] * 2,
@@ -292,8 +295,8 @@
         out_specs=[HBM, HBM],
         scratch_shapes=[
             pltpu.VMEM((97, CH_DEV, 128), BF),
-            pltpu.VMEM((16, 128), jnp.int32),
-            pltpu.SMEM((16, 128), jnp.int32),
+            pltpu.VMEM((8, 128), jnp.int32),
+            pltpu.SMEM((8, 128), jnp.int32),
             pltpu.SemaphoreType.DMA((2,)),
         ],
         compiler_params=params(8),

time: 151 us -> 150 us (level)
  local copies, waits for them, and re-layouts: 5.01 us -> 3.34 us
  waiting for transfers between devices: 29.2 us -> 27.6 us
    unnamed x18 -> x14, local copies, waits for them, and re-layouts: 4.98 us -> 3.3 us
  transfers between devices with their start and end apart: 14 -> 14, of which waited for: 5 -> 5; matrix products, arithmetic and copies ran while one was open for 1% -> 1% of each run, Pallas kernels for 8% -> 9%
where the time goes in v8:
time: 150 us; the launch traced here: 149 us
  starting transfers between devices  65.5 us (44%)
  blocking collectives  34.3 us (23%)
  waiting for transfers between devices  27.6 us (18%)
  Pallas kernels  16.5 us (11%)
  local copies, waits for them, and re-layouts  3.34 us (2%)
    all_to_all x2, blocking collectives, shuffle(): return lax.all_to_all(x, axis, split_axis=0, concat_axis=0, tiled=True)  34.3 us
    all_to_all x3, starting transfers between devices, shuffle(): return lax.all_to_all(x, axis, split_axis=0, concat_axis=0, tiled=True)  19.3 us
    ppermute x3, starting transfers between devices, gathered_weights(): moved.append(lax.ppermute(moved[-1], ('co', 'y'), ring))  12.8 us
    ppermute x4, starting transfers between devices, gathered_weights(): swapped = [lax.ppermute(shard, 'co', swap) for shard in moved[1:]]  12.7 us
    all_to_all x3, waiting for transfers between devices, shuffle(): return lax.all_to_all(x, axis, split_axis=0, concat_axis=0, tiled=True)  8.8 us
    ppermute x1, starting transfers between devices, body(): far = lax.ppermute(far + far_before, 'zh', [(0, 1), (1, 0)])  7.94 us
    pallas_call x2, Pallas kernels, convolve(): pl.pallas_call(conv_kernel, out_shape=[jax.ShapeDtypeStruct((128, COUT),...  7.52 us
    ppermute x1, waiting for transfers between devices, gathered_weights(): moved.append(lax.ppermute(half, ('co', 'y'), ring))  7 us
  transfers between devices with their start and end apart: 14, of which 5 were waited for; matrix products, arithmetic and copies ran while one was open for 1% of the time, Pallas kernels for 9%

profile of v8, /device:TPU:1, one launch (start us, length us, event | category | flops | bytes accessed | tf_op | source)
XLA Modules:
  0.0 148.5 jit_solution(12189102821183298696)
XLA Ops:
  0.0 5.9 %collective-permute-start = (bf16[27,32,512]{2,1,0:T(8,128)(2,1)}, bf16[27,32,512]{2,1,0:T(8,128)(2,1)S(1)}, u32[]{:S(2)}, u32[]{:S(2)}) collective-permute-start(bf16[27,32,512]{2,1,0:T(8,128)(2,1)} %bitcast.6), channel_id=1, source_target_pairs={{0,1},{1,2},{2,3},{3,4},{4,5},{5,6},{6,7},{7,0},{16,23},{17,16},{1... | collective-permute-start | bytes 2654216 | tf_op jit(solution)/shard_map/ppermute | solution.py:253
  5.9 3.1 %shard_map.64 = bf16[32,136,128]{2,1,0:T(8,128)(2,1)} custom-call(s32[64]{0:T(128)} %target.1, bf16[64,32,128]{2,1,0:T(8,128)(2,1)} %arrived.1), custom_call_target="tpu_custom_call" | custom-call | tf_op jit(solution)/shard_map/pallas_call | solution.py:274
  9.0 10.0 %all-to-all-start = ((bf16[32,136,128]{2,1,0:T(8,128)(2,1)}), bf16[32,136,128]{2,1,0:T(8,128)(2,1)S(1)}, u32[]{:S(2)}, u32[]{:S(2)}) async-start(bf16[32,136,128]{2,1,0:T(8,128)(2,1)} %shard_map.64), calls=%async_computation | async-start | bytes 2228224 | tf_op jit(solution)/shard_map/all_to_all | solution.py:244
  19.0 0.0 collective-permute-done.rest_1_
  19.0 3.0 %collective-permute-start.1 = (bf16[27,32,512]{2,1,0:T(8,128)(2,1)S(1)}, bf16[27,32,512]{2,1,0:T(8,128)(2,1)}, u32[]{:S(2)}, u32[]{:S(2)}) collective-permute-start(bf16[27,32,512]{2,1,0:T(8,128)(2,1)S(1)} %collective-permute-done.rest_1_), channel_id=1, source_target_pairs={{0,1},{1,2},{2,3},{3,4},{4,5},{5,6},{6,7},{7,0},{16,23},{17,16},{1... | collective-permute-start | bytes 2654216 | tf_op jit(solution)/shard_map/ppermute | solution.py:253
  22.0 5.0 %collective-permute-start.2 = (bf16[27,32,512]{2,1,0:T(8,128)(2,1)S(1)}, bf16[27,32,512]{2,1,0:T(8,128)(2,1)S(1)}, u32[]{:S(2)}, u32[]{:S(2)}) collective-permute-start(bf16[27,32,512]{2,1,0:T(8,128)(2,1)S(1)} %collective-permute-done.rest_1_), channel_id=1, source_target_pairs={{0,16},{16,0},{1,17},{17,1},{2,18},{18,2},{3,19},{19,3},{4,20},{20... | collective-permute-start | bytes 2654216 | tf_op jit(solution)/shard_map/ppermute | solution.py:257
  27.1 6.2 %collective-permute-done.1.rest_3_ = bf16[27,32,512]{2,1,0:T(8,128)(2,1)} collective-permute-done((bf16[27,32,512]{2,1,0:T(8,128)(2,1)S(1)}, bf16[27,32,512]{2,1,0:T(8,128)(2,1)}, u32[]{:S(2)}, u32[]{:S(2)}) %collective-permute-start.1) | collective-permute-done | bytes 884768 | tf_op jit(solution)/shard_map/ppermute | solution.py:253
  33.2 3.9 %collective-permute-start.4 = (bf16[27,32,512]{2,1,0:T(8,128)(2,1)}, bf16[27,32,512]{2,1,0:T(8,128)(2,1)S(1)}, u32[]{:S(2)}, u32[]{:S(2)}) collective-permute-start(bf16[27,32,512]{2,1,0:T(8,128)(2,1)} %collective-permute-done.1.rest_3_), channel_id=1, source_target_pairs={{0,1},{1,2},{2,3},{3,4},{4,5},{5,6},{6,7},{7,0},{16,23},{17,16},{1... | collective-permute-start | bytes 2654216 | tf_op jit(solution)/shard_map/ppermute | solution.py:253
  37.1 0.0 collective-permute-done.2.rest_2_
  37.1 0.0 copy-start.1
  37.1 1.0 copy-done.1
  38.1 8.8 %all-to-all-done.got = bf16[32,136,128]{2,1,0:T(8,128)(2,1)S(1)} async-done(((bf16[32,136,128]{2,1,0:T(8,128)(2,1)}), bf16[32,136,128]{2,1,0:T(8,128)(2,1)S(1)}, u32[]{:S(2)}, u32[]{:S(2)}) %all-to-all-start) | async-done | bytes 1114144 | tf_op jit(solution)/shard_map/all_to_all | solution.py:244
  46.9 2.0 %shard_map.65 = (bf16[48,32,128]{2,1,0:T(8,128)(2,1)}, bf16[48,32,128]{2,1,0:T(8,128)(2,1)}) custom-call(bf16[32,136,128]{2,1,0:T(8,128)(2,1)S(1)} %all-to-all-done.got), custom_call_target="tpu_custom_call" | custom-call | tf_op jit(solution)/shard_map/pallas_call | solution.py:291
  48.9 0.0 copy-start
  48.9 0.0 copy-start.4
  49.0 5.0 %all-to-all-start.2 = ((bf16[8,6,32,128]{3,2,1,0:T(8,128)(2,1)}), bf16[8,6,32,128]{3,2,1,0:T(8,128)(2,1)}, u32[]{:S(2)}, u32[]{:S(2)}) async-start(bf16[8,6,32,128]{3,2,1,0:T(8,128)(2,1)} %bitcast.2), calls=%async_computation.2 | async-start | bytes 786432 | tf_op jit(solution)/shard_map/all_to_all | solution.py:244
  54.0 2.2 %collective-permute-start.3 = (bf16[27,32,512]{2,1,0:T(8,128)(2,1)}, bf16[27,32,512]{2,1,0:T(8,128)(2,1)}, u32[]{:S(2)}, u32[]{:S(2)}) collective-permute-start(bf16[27,32,512]{2,1,0:T(8,128)(2,1)} %collective-permute-done.1.rest_3_), channel_id=1, source_target_pairs={{0,16},{16,0},{1,17},{17,1},{2,18},{18,2},{3,19},{19,3},{4,20},{20... | collective-permute-start | bytes 2654216 | tf_op jit(solution)/shard_map/ppermute | solution.py:257
  56.2 0.0 collective-permute-done.4.rest_5_
  56.3 4.9 %collective-permute-start.6 = (bf16[27,16,512]{2,1,0:T(8,128)(2,1)S(1)}, bf16[27,16,512]{2,1,0:T(8,128)(2,1)S(1)}, u32[]{:S(2)}, u32[]{:S(2)}) collective-permute-start(bf16[27,16,512]{2,1,0:T(8,128)(2,1)S(1)} %constant_dynamic-slice_fusion), channel_id=1, source_target_pairs={{0,1},{1,2},{2,3},{3,4},{4,5},{5,6},{6,7},{7,0},{16,23},{17,16},{1... | collective-permute-start | bytes 1327112 | tf_op jit(solution)/shard_map/ppermute | solution.py:256
  61.1 1.9 %collective-permute-start.5 = (bf16[27,32,512]{2,1,0:T(8,128)(2,1)S(1)}, bf16[27,32,512]{2,1,0:T(8,128)(2,1)}, u32[]{:S(2)}, u32[]{:S(2)}) collective-permute-start(bf16[27,32,512]{2,1,0:T(8,128)(2,1)S(1)} %collective-permute-done.4.rest_5_), channel_id=1, source_target_pairs={{0,16},{16,0},{1,17},{17,1},{2,18},{18,2},{3,19},{19,3},{4,20},{20... | collective-permute-start | bytes 2654216 | tf_op jit(solution)/shard_map/ppermute | solution.py:257
  63.1 7.0 %collective-permute-done.6.rest_7_ = bf16[27,16,512]{2,1,0:T(8,128)(2,1)S(1)} collective-permute-done((bf16[27,16,512]{2,1,0:T(8,128)(2,1)S(1)}, bf16[27,16,512]{2,1,0:T(8,128)(2,1)S(1)}, u32[]{:S(2)}, u32[]{:S(2)}) %collective-permute-start.6) | collective-permute-done | bytes 442400 | tf_op jit(solution)/shard_map/ppermute | solution.py:256
  70.0 3.5 %collective-permute-start.7 = (bf16[27,16,512]{2,1,0:T(8,128)(2,1)S(1)}, bf16[27,16,512]{2,1,0:T(8,128)(2,1)}, u32[]{:S(2)}, u32[]{:S(2)}) collective-permute-start(bf16[27,16,512]{2,1,0:T(8,128)(2,1)S(1)} %collective-permute-done.6.rest_7_), channel_id=1, source_target_pairs={{0,16},{16,0},{1,17},{17,1},{2,18},{18,2},{3,19},{19,3},{4,20},{20... | collective-permute-start | bytes 1327112 | tf_op jit(solution)/shard_map/ppermute | solution.py:257
  73.6 0.0 all-to-all-done.2.frames
  73.6 4.3 %all-to-all-start.1 = ((bf16[8,6,32,128]{3,2,1,0:T(8,128)(2,1)}), bf16[8,6,32,128]{3,2,1,0:T(8,128)(2,1)}, u32[]{:S(2)}, u32[]{:S(2)}) async-start(bf16[8,6,32,128]{3,2,1,0:T(8,128)(2,1)} %bitcast.1), calls=%async_computation.1 | async-start | bytes 786432 | tf_op jit(solution)/shard_map/all_to_all | solution.py:244
  77.8 0.0 collective-permute-done.3.rest_4_
  77.8 0.0 collective-permute-done.7.rest_8_
  77.9 0.0 collective-permute-done.5.rest_6_
  77.9 0.0 copy-done
  77.9 0.0 copy-done.4
  77.9 0.0 copy-start.2
  77.9 1.2 copy-done.2
  79.1 3.8 %shard_map.67 = (f32[128,512]{1,0:T(8,128)S(1)}, f32[128,512]{1,0:T(8,128)S(1)}) custom-call(s32[4]{0:T(128)S(1)} %copy-done.4, bf16[8,6,32,128]{3,2,1,0:T(8,128)(2,1)} %all-to-all-done.2.frames, bf16[27,32,512]{2,1,0:T(8,128)(2,1)S(1)} %bitcast.7, bf16[27,32,512]{2,1,0:T(8,128)(2,1)S(1)} %collective-permute-done.rest_1_, ...), custom_call_target="tpu_custom_call" | custom-call | tf_op jit(solution)/shard_map/pallas_call | solution.py:262
  82.8 3.3 %collective-permute-start.8 = (f32[128,512]{1,0:T(8,128)S(1)}, f32[128,512]{1,0:T(8,128)S(1)}, u32[]{:S(2)}, u32[]{:S(2)}) collective-permute-start(f32[128,512]{1,0:T(8,128)S(1)} %get-tuple-element.23), channel_id=1, source_target_pairs={{0,16},{16,32},{32,48},{48,64},{64,80},{80,96},{96,112},{112,128},... | collective-permute-start | bytes 786440 | tf_op jit(solution)/shard_map/ppermute | solution.py:310
  86.1 3.3 %collective-permute-done.8 = f32[128,512]{1,0:T(8,128)S(1)} collective-permute-done((f32[128,512]{1,0:T(8,128)S(1)}, f32[128,512]{1,0:T(8,128)S(1)}, u32[]{:S(2)}, u32[]{:S(2)}) %collective-permute-start.8) | collective-permute-done | bytes 262176 | tf_op jit(solution)/shard_map/ppermute | solution.py:310
  89.4 7.9 %collective-permute-start.9 = (f32[128,512]{1,0:T(8,128)S(1)}, f32[128,512]{1,0:T(8,128)}, u32[]{:S(2)}, u32[]{:S(2)}) collective-permute-start(f32[128,512]{1,0:T(8,128)S(1)} %add.10), channel_id=1, source_target_pairs={{0,8},{8,0},{1,9},{9,1},{2,10},{10,2},{3,11},{11,3},{4,12},{12,4},... | collective-permute-start | bytes 786440 | tf_op jit(solution)/shard_map/ppermute | solution.py:313
  97.4 0.0 all-to-all-done.1.frames
  97.4 0.0 copy-start.3
  97.4 1.2 copy-done.3
  98.6 3.8 %shard_map.66 = (f32[128,512]{1,0:T(8,128)S(1)}, f32[128,512]{1,0:T(8,128)S(1)}) custom-call(s32[4]{0:T(128)S(1)} %copy-done.4, bf16[8,6,32,128]{3,2,1,0:T(8,128)(2,1)} %all-to-all-done.1.frames, bf16[27,32,512]{2,1,0:T(8,128)(2,1)S(1)} %bitcast.8, bf16[27,32,512]{2,1,0:T(8,128)(2,1)S(1)} %collective-permute-done.rest_1_, ...), custom_call_target="tpu_custom_call" | custom-call | tf_op jit(solution)/shard_map/pallas_call | solution.py:262
  102.3 0.0 copy-start.5
  102.4 0.0 copy-start.6
  102.4 4.7 %collective-permute-start.10 = (f32[128,512]{1,0:T(8,128)S(1)}, f32[128,512]{1,0:T(8,128)S(1)}, u32[]{:S(2)}, u32[]{:S(2)}) collective-permute-start(f32[128,512]{1,0:T(8,128)S(1)} %get-tuple-element.24), channel_id=1, source_target_pairs={{0,16},{16,32},{32,48},{48,64},{64,80},{80,96},{96,112},{112,128},... | collective-permute-start | bytes 786440 | tf_op jit(solution)/shard_map/ppermute | solution.py:312
  107.0 0.0 collective-permute-done.9
  107.0 1.0 add.11.near
  108.0 2.3 %collective-permute-done.10.before = f32[128,512]{1,0:T(8,128)S(1)} collective-permute-done((f32[128,512]{1,0:T(8,128)S(1)}, f32[128,512]{1,0:T(8,128)S(1)}, u32[]{:S(2)}, u32[]{:S(2)}) %collective-permute-start.10) | collective-permute-done | bytes 262176 | tf_op jit(solution)/shard_map/ppermute | solution.py:312
  110.3 0.9 shard_map.68
  111.2 15.0 %all_to_all.25.got = f32[16,8,128]{2,1,0:T(8,128)} all-to-all(f32[16,8,128]{2,1,0:T(8,128)S(1)} %get-tuple-element.25), channel_id=1, replica_groups=mesh['zl'=4,'x'=4,'co'=2,'zh'=2,'y'=8] {'y','co'}, dimensions={0} | all-to-all | bytes 131072 | tf_op jit(solution)/shard_map/all_to_all | solution.py:244
  126.2 1.5 %shard_map.69 = f32[32,8,128]{2,1,0:T(8,128)} custom-call(f32[16,8,128]{2,1,0:T(8,128)} %all_to_all.25.got), custom_call_target="tpu_custom_call" | custom-call | tf_op jit(solution)/shard_map/pallas_call | solution.py:323
  127.8 19.2 %all_to_all.26.got = f32[32,8,128]{2,1,0:T(8,128)S(1)} all-to-all(f32[32,8,128]{2,1,0:T(8,128)} %shard_map.69), channel_id=1, replica_groups=mesh['zl'=4,'x'=4,'co'=2,'zh'=2,'y'=8] {'zl','zh','x'}, dimensions={0} | all-to-all | bytes 262144 | tf_op jit(solution)/shard_map/all_to_all | solution.py:244
  147.0 0.0 copy-done.5
  147.0 0.0 copy-done.6
  147.0 1.5 %shard_map.70 = bf16[2,64,512]{2,1,0:T(8,128)(2,1)} custom-call(s32[4]{0:T(128)S(1)} %copy-done.4, f32[32,8,128]{2,1,0:T(8,128)S(1)} %all_to_all.26.got, f32[128,512]{1,0:T(8,128)S(1)} %get-tuple-element.26.conv, f32[1,512]{1,0:T(1,128)S(1)} %bitcast.9, f32[1,512]{1,0:T(1,128)S(1)} %bitcast.10), custom_call_target="tpu_custom_call" | custom-call | tf_op jit(solution)/shard_map/pallas_call | solution.py:330
  (2 shorter events, 0.1 us)
Async XLA Ops:
  0.0 19.0 %collective-permute-start = (bf16[27,32,512]{2,1,0:T(8,128)(2,1)}, bf16[27,32,512]{2,1,0:T(8,128)(2,1)S(1)}, u32[]{:S(2)}, u32[]{:S(2)}) collective-permute-start(bf16[27,32,512]{2,1,0:T(8,128)(2,1)} %bitcast.6), channel_id=1, source_target_pairs={{0,1},{1,2},{2,3},{3,4},{4,5},{5,6},{6,7},{7,0},{16,23},{17,16},{1... | collective-permute-start | bytes 2654216 | tf_op jit(solution)/shard_map/ppermute | solution.py:253
  9.0 37.9 %all-to-all-start = ((bf16[32,136,128]{2,1,0:T(8,128)(2,1)}), bf16[32,136,128]{2,1,0:T(8,128)(2,1)S(1)}, u32[]{:S(2)}, u32[]{:S(2)}) async-start(bf16[32,136,128]{2,1,0:T(8,128)(2,1)} %shard_map.64), calls=%async_computation | async-start | bytes 2228224 | tf_op jit(solution)/shard_map/all_to_all | solution.py:244
  19.0 14.2 %collective-permute-start.1 = (bf16[27,32,512]{2,1,0:T(8,128)(2,1)S(1)}, bf16[27,32,512]{2,1,0:T(8,128)(2,1)}, u32[]{:S(2)}, u32[]{:S(2)}) collective-permute-start(bf16[27,32,512]{2,1,0:T(8,128)(2,1)S(1)} %collective-permute-done.rest_1_), channel_id=1, source_target_pairs={{0,1},{1,2},{2,3},{3,4},{4,5},{5,6},{6,7},{7,0},{16,23},{17,16},{1... | collective-permute-start | bytes 2654216 | tf_op jit(solution)/shard_map/ppermute | solution.py:253
  22.0 15.1 %collective-permute-start.2 = (bf16[27,32,512]{2,1,0:T(8,128)(2,1)S(1)}, bf16[27,32,512]{2,1,0:T(8,128)(2,1)S(1)}, u32[]{:S(2)}, u32[]{:S(2)}) collective-permute-start(bf16[27,32,512]{2,1,0:T(8,128)(2,1)S(1)} %collective-permute-done.rest_1_), channel_id=1, source_target_pairs={{0,16},{16,0},{1,17},{17,1},{2,18},{18,2},{3,19},{19,3},{4,20},{20... | collective-permute-start | bytes 2654216 | tf_op jit(solution)/shard_map/ppermute | solution.py:257
  33.2 23.0 %collective-permute-start.4 = (bf16[27,32,512]{2,1,0:T(8,128)(2,1)}, bf16[27,32,512]{2,1,0:T(8,128)(2,1)S(1)}, u32[]{:S(2)}, u32[]{:S(2)}) collective-permute-start(bf16[27,32,512]{2,1,0:T(8,128)(2,1)} %collective-permute-done.1.rest_3_), channel_id=1, source_target_pairs={{0,1},{1,2},{2,3},{3,4},{4,5},{5,6},{6,7},{7,0},{16,23},{17,16},{1... | collective-permute-start | bytes 2654216 | tf_op jit(solution)/shard_map/ppermute | solution.py:253
  37.1 1.0 copy-start.1
  48.9 28.9 %copy-start = (bf16[3,3,3,32,512]{4,3,2,1,0:T(8,128)(2,1)S(1)}, bf16[3,3,3,32,512]{4,3,2,1,0:T(8,128)(2,1)}, u32[]{:S(2)}) copy-start(bf16[3,3,3,32,512]{4,3,2,1,0:T(8,128)(2,1)} %param.9) | copy-start | bytes 2654212
  48.9 28.9 %copy-start.4 = (s32[4]{0:T(128)S(1)}, s32[4]{0:T(128)}, u32[]{:S(2)}) copy-start(s32[4]{0:T(128)} %lengths.7) | copy-start | bytes 52
  49.0 24.6 %all-to-all-start.2 = ((bf16[8,6,32,128]{3,2,1,0:T(8,128)(2,1)}), bf16[8,6,32,128]{3,2,1,0:T(8,128)(2,1)}, u32[]{:S(2)}, u32[]{:S(2)}) async-start(bf16[8,6,32,128]{3,2,1,0:T(8,128)(2,1)} %bitcast.2), calls=%async_computation.2 | async-start | bytes 786432 | tf_op jit(solution)/shard_map/all_to_all | solution.py:244
  54.0 23.9 %collective-permute-start.3 = (bf16[27,32,512]{2,1,0:T(8,128)(2,1)}, bf16[27,32,512]{2,1,0:T(8,128)(2,1)}, u32[]{:S(2)}, u32[]{:S(2)}) collective-permute-start(bf16[27,32,512]{2,1,0:T(8,128)(2,1)} %collective-permute-done.1.rest_3_), channel_id=1, source_target_pairs={{0,16},{16,0},{1,17},{17,1},{2,18},{18,2},{3,19},{19,3},{4,20},{20... | collective-permute-start | bytes 2654216 | tf_op jit(solution)/shard_map/ppermute | solution.py:257
  56.3 13.8 %collective-permute-start.6 = (bf16[27,16,512]{2,1,0:T(8,128)(2,1)S(1)}, bf16[27,16,512]{2,1,0:T(8,128)(2,1)S(1)}, u32[]{:S(2)}, u32[]{:S(2)}) collective-permute-start(bf16[27,16,512]{2,1,0:T(8,128)(2,1)S(1)} %constant_dynamic-slice_fusion), channel_id=1, source_target_pairs={{0,1},{1,2},{2,3},{3,4},{4,5},{5,6},{6,7},{7,0},{16,23},{17,16},{1... | collective-permute-start | bytes 1327112 | tf_op jit(solution)/shard_map/ppermute | solution.py:256
  61.1 16.7 %collective-permute-start.5 = (bf16[27,32,512]{2,1,0:T(8,128)(2,1)S(1)}, bf16[27,32,512]{2,1,0:T(8,128)(2,1)}, u32[]{:S(2)}, u32[]{:S(2)}) collective-permute-start(bf16[27,32,512]{2,1,0:T(8,128)(2,1)S(1)} %collective-permute-done.4.rest_5_), channel_id=1, source_target_pairs={{0,16},{16,0},{1,17},{17,1},{2,18},{18,2},{3,19},{19,3},{4,20},{20... | collective-permute-start | bytes 2654216 | tf_op jit(solution)/shard_map/ppermute | solution.py:257
  70.0 7.8 %collective-permute-start.7 = (bf16[27,16,512]{2,1,0:T(8,128)(2,1)S(1)}, bf16[27,16,512]{2,1,0:T(8,128)(2,1)}, u32[]{:S(2)}, u32[]{:S(2)}) collective-permute-start(bf16[27,16,512]{2,1,0:T(8,128)(2,1)S(1)} %collective-permute-done.6.rest_7_), channel_id=1, source_target_pairs={{0,16},{16,0},{1,17},{17,1},{2,18},{18,2},{3,19},{19,3},{4,20},{20... | collective-permute-start | bytes 1327112 | tf_op jit(solution)/shard_map/ppermute | solution.py:257
  73.6 23.8 %all-to-all-start.1 = ((bf16[8,6,32,128]{3,2,1,0:T(8,128)(2,1)}), bf16[8,6,32,128]{3,2,1,0:T(8,128)(2,1)}, u32[]{:S(2)}, u32[]{:S(2)}) async-start(bf16[8,6,32,128]{3,2,1,0:T(8,128)(2,1)} %bitcast.1), calls=%async_computation.1 | async-start | bytes 786432 | tf_op jit(solution)/shard_map/all_to_all | solution.py:244
  77.9 1.2 copy-start.2
  82.8 6.6 %collective-permute-start.8 = (f32[128,512]{1,0:T(8,128)S(1)}, f32[128,512]{1,0:T(8,128)S(1)}, u32[]{:S(2)}, u32[]{:S(2)}) collective-permute-start(f32[128,512]{1,0:T(8,128)S(1)} %get-tuple-element.23), channel_id=1, source_target_pairs={{0,16},{16,32},{32,48},{48,64},{64,80},{80,96},{96,112},{112,128},... | collective-permute-start | bytes 786440 | tf_op jit(solution)/shard_map/ppermute | solution.py:310
  89.4 17.6 %collective-permute-start.9 = (f32[128,512]{1,0:T(8,128)S(1)}, f32[128,512]{1,0:T(8,128)}, u32[]{:S(2)}, u32[]{:S(2)}) collective-permute-start(f32[128,512]{1,0:T(8,128)S(1)} %add.10), channel_id=1, source_target_pairs={{0,8},{8,0},{1,9},{9,1},{2,10},{10,2},{3,11},{11,3},{4,12},{12,4},... | collective-permute-start | bytes 786440 | tf_op jit(solution)/shard_map/ppermute | solution.py:313
  97.4 1.2 copy-start.3
  102.3 44.7 %copy-start.5 = (f32[512]{0:T(512)S(1)}, f32[512]{0:T(512)}, u32[]{:S(2)}) copy-start(f32[512]{0:T(512)} %param.10) | copy-start | bytes 6148
  102.4 44.7 %copy-start.6 = (f32[512]{0:T(512)S(1)}, f32[512]{0:T(512)}, u32[]{:S(2)}) copy-start(f32[512]{0:T(512)} %param.11) | copy-start | bytes 6148
  102.4 8.0 %collective-permute-start.10 = (f32[128,512]{1,0:T(8,128)S(1)}, f32[128,512]{1,0:T(8,128)S(1)}, u32[]{:S(2)}, u32[]{:S(2)}) collective-permute-start(f32[128,512]{1,0:T(8,128)S(1)} %get-tuple-element.24), channel_id=1, source_target_pairs={{0,16},{16,32},{32,48},{48,64},{64,80},{80,96},{96,112},{112,128},... | collective-permute-start | bytes 786440 | tf_op jit(solution)/shard_map/ppermute | solution.py:312

commit v9 on v8

--- a/solution.py
+++ b/solution.py
@@ -14,6 +14,7 @@
 CAP = 4
 CH_DEV = 32
 HALF = 16
+SHARDS = 11
 NY = 8
 OUT_ROWS = 16
 COUT = 512
@@ -122,20 +123,21 @@
 
 
 def conv_kernel(lengths, frames, *rest):
-    weights, (own, after, taps) = rest[:NY + 1], rest[NY + 1:]
+    weights, (own, after, taps) = rest[:SHARDS], rest[SHARDS:]
     y = lax.axis_index("y")
     core = lax.axis_index("co")
     slab = my_slab()
     sign = 2 * core - 1
-    sources = [y]
-    for s in range(1, 4):
-        sources += [y + sign * s, y - sign * s]
-    sources += [y + 4, y + 4]
-    sources = [lax.bitwise_and(s + NY, NY - 1) for s in sources]
     whole = pl.ds(0, CH_DEV)
     mine = pl.ds(pl.multiple_of(core * HALF, HALF), HALF)
     other = pl.ds(pl.multiple_of((1 - core) * HALF, HALF), HALF)
-    sources = list(zip(sources, [whole] * 7 + [mine, other]))
+    sources = [(y, whole)]
+    for s in (sign, 2 * sign):
+        sources += [(y + s, whole), (y - s, whole)]
+    s = 3 * sign
+    sources += [(y + s, mine), (y + s, other), (y - s, other), (y - s, mine)]
+    sources += [(y + 4, mine), (y + 4, other)]
+    sources = [(lax.bitwise_and(s + NY, NY - 1), c) for s, c in sources]
     j = lax.broadcasted_iota(jnp.int32, (192, 128), 0)
     w = lax.broadcasted_iota(jnp.int32, (192, 128), 1)
     wanted = jnp.where(j < 64, 2 * j - 1, jnp.where(j < 128, 2 * j - 128, 2 * j - 255))
@@ -247,22 +249,30 @@
 def gathered_weights(kernel):
     ring = [(c * NY + y, c * NY + (y + (1 if c == 0 else NY - 1)) % NY)
             for c in range(2) for y in range(NY)]
-    swap = [(0, 1), (1, 0)]
-    moved = [kernel]
-    for _ in range(3):
-        moved.append(lax.ppermute(moved[-1], ("co", "y"), ring))
-    first = lax.axis_index("co") * HALF
-    half = lax.dynamic_slice_in_dim(moved[3], first, HALF, axis=1)
-    moved.append(lax.ppermute(half, ("co", "y"), ring))
-    swapped = [lax.ppermute(shard, "co", swap) for shard in moved[1:]]
-    return moved, swapped
+    core = lax.axis_index("co")
+
+    def step(shard):
+        return lax.ppermute(shard, ("co", "y"), ring)
+
+    def swap(shard):
+        return lax.ppermute(shard, "co", [(0, 1), (1, 0)])
+
+    first = step(kernel)
+    second = step(first)
+    mine = step(lax.dynamic_slice_in_dim(second, core * HALF, HALF, axis=1))
+    other = step(lax.dynamic_slice_in_dim(second, (1 - core) * HALF, HALF, axis=1))
+    last = step(mine)
+    swapped = [swap(shard) for shard in (first, second, mine, other, last)]
+    return [kernel, first, swapped[0], second, swapped[1], mine, other] + swapped[2:4] + [
+        last, swapped[4]
+    ]
 
 
 def convolve(lengths, frames, weights):
     return pl.pallas_call(
         conv_kernel,
         out_shape=[jax.ShapeDtypeStruct((128, COUT), F32)] * 2,
-        in_specs=[SMEM] + [VMEM] * (2 + NY),
+        in_specs=[SMEM] + [VMEM] * (1 + SHARDS),
         out_specs=[VMEM, VMEM],
         scratch_shapes=[pltpu.VMEM((3, 128, 768), BF)],
         compiler_params=params(24),
@@ -270,7 +280,7 @@
 
 
 def body(arrived, row_target, clip_lengths, conv_weight, gn_gain, gn_bias):
-    moved, swapped = gathered_weights(conv_weight.reshape(27, CH_DEV, COUT))
+    weights = gathered_weights(conv_weight.reshape(27, CH_DEV, COUT))
     send = pl.pallas_call(
         pack_kernel,
         out_shape=jax.ShapeDtypeStruct((SLABS, 136, 128), BF),
@@ -285,8 +295,8 @@
         compiler_params=params(60),
     )(row_target, arrived)
     got = shuffle(send, TM)
-    got, moved[2], swapped[0] = lax.optimization_barrier(
-        (got, moved[2], swapped[0])
+    got, weights[2], weights[4] = lax.optimization_barrier(
+        (got, weights[2], weights[4])
     )
     far, near = pl.pallas_call(
         place_kernel,
@@ -301,10 +311,9 @@
         ],
         compiler_params=params(8),
     )(got)
-    weights = [moved[0], moved[1], swapped[0], moved[2], swapped[1], moved[3], swapped[2]]
-    weights += [moved[4], swapped[3]]
     onward = [(i, i + 1) for i in range(SLABS - 1)]
     far = shuffle(far.reshape(NY, 6, CH_DEV, 128), "y")
+    near, weights[8], weights[10] = lax.optimization_barrier((near, weights[8], weights[10]))
     near = shuffle(near.reshape(NY, 6, CH_DEV, 128), "y")
     far, far_after = convolve(clip_lengths, far, weights)
     far_before = lax.ppermute(far_after, TM, onward)

time: 150 us -> 154 us (1.027)
  starting transfers between devices: 65.5 us -> 74 us
  waiting for transfers between devices: 27.6 us -> 21.7 us
  blocking collectives: 34.3 us -> 37.2 us
    ppermute x8 -> x10, starting transfers between devices: 30.3 us -> 36.8 us  [the longest x5 21.2 us: swap(): return lax.ppermute(shard, 'co', [(0, 1), (1, 0)])]
    all_to_all x3, waiting for transfers between devices: 8.8 us -> 4.61 us  [shuffle(): return lax.all_to_all(x, axis, split_axis=0, concat_axis=0, tiled=True)]
    all_to_all x2, blocking collectives: 34.3 us -> 37.2 us  [shuffle(): return lax.all_to_all(x, axis, split_axis=0, concat_axis=0, tiled=True)]
    ppermute x1, starting transfers between devices: 7.94 us -> 9.89 us  [body(): far = lax.ppermute(far + far_before, 'zh', [(0, 1), (1, 0)])]
    unnamed x14 -> x12, local copies, waits for them, and re-layouts: 3.3 us -> 1.56 us
    ppermute x8 -> x10, waiting for transfers between devices: 13.2 us -> 11.5 us  [the longest x5 11.5 us: step(): return lax.ppermute(shard, ('co', 'y'), ring)]
  transfers between devices with their start and end apart: 14 -> 16, of which waited for: 5 -> 5; matrix products, arithmetic and copies ran while one was open for 1% -> 1% of each run, Pallas kernels for 9% -> 8%
where the time goes in v9:
time: 154 us; the launch traced here: 153 us
  starting transfers between devices  74 us (48%)
  blocking collectives  37.2 us (24%)
  waiting for transfers between devices  21.7 us (14%)
  Pallas kernels  16.5 us (11%)
  local copies, waits for them, and re-layouts  2.4 us (2%)
    all_to_all x2, blocking collectives, shuffle(): return lax.all_to_all(x, axis, split_axis=0, concat_axis=0, tiled=True)  37.2 us
    ppermute x5, starting transfers between devices, swap(): return lax.ppermute(shard, 'co', [(0, 1), (1, 0)])  21.2 us
    all_to_all x3, starting transfers between devices, shuffle(): return lax.all_to_all(x, axis, split_axis=0, concat_axis=0, tiled=True)  18.2 us
    ppermute x5, starting transfers between devices, step(): return lax.ppermute(shard, ('co', 'y'), ring)  15.7 us
    ppermute x5, waiting for transfers between devices, step(): return lax.ppermute(shard, ('co', 'y'), ring)  11.5 us
    ppermute x1, starting transfers between devices, body(): far = lax.ppermute(far + far_before, 'zh', [(0, 1), (1, 0)])  9.89 us
    pallas_call x2, Pallas kernels, convolve(): pl.pallas_call(conv_kernel, out_shape=[jax.ShapeDtypeStruct((128, COUT),...  8.02 us
    ppermute x1, starting transfers between devices, body(): near_before = lax.ppermute(near_after, TM, onward)  4.67 us
  transfers between devices with their start and end apart: 16, of which 5 were waited for; matrix products, arithmetic and copies ran while one was open for 1% of the time, Pallas kernels for 8%

profile of v9, /device:TPU:1, one launch (start us, length us, event | category | flops | bytes accessed | tf_op | source)
XLA Modules:
  0.0 153.1 jit_solution(16620738103477283024)
XLA Ops:
  0.0 5.9 %collective-permute-start = (bf16[27,32,512]{2,1,0:T(8,128)(2,1)}, bf16[27,32,512]{2,1,0:T(8,128)(2,1)}, u32[]{:S(2)}, u32[]{:S(2)}) collective-permute-start(bf16[27,32,512]{2,1,0:T(8,128)(2,1)} %bitcast.6), channel_id=1, source_target_pairs={{0,1},{1,2},{2,3},{3,4},{4,5},{5,6},{6,7},{7,0},{16,23},{17,16},{1... | collective-permute-start | bytes 2654216 | tf_op jit(solution)/shard_map/ppermute | solution.py:255
  5.9 3.1 %shard_map.64 = bf16[32,136,128]{2,1,0:T(8,128)(2,1)} custom-call(s32[64]{0:T(128)} %target.1, bf16[64,32,128]{2,1,0:T(8,128)(2,1)} %arrived.1), custom_call_target="tpu_custom_call" | custom-call | tf_op jit(solution)/shard_map/pallas_call | solution.py:284
  9.0 10.0 %all-to-all-start = ((bf16[32,136,128]{2,1,0:T(8,128)(2,1)}), bf16[32,136,128]{2,1,0:T(8,128)(2,1)S(1)}, u32[]{:S(2)}, u32[]{:S(2)}) async-start(bf16[32,136,128]{2,1,0:T(8,128)(2,1)} %shard_map.64), calls=%async_computation | async-start | bytes 2228224 | tf_op jit(solution)/shard_map/all_to_all | solution.py:246
  19.0 0.0 collective-permute-done.rest_1_
  19.0 3.0 %collective-permute-start.2 = (bf16[27,32,512]{2,1,0:T(8,128)(2,1)}, bf16[27,32,512]{2,1,0:T(8,128)(2,1)S(1)}, u32[]{:S(2)}, u32[]{:S(2)}) collective-permute-start(bf16[27,32,512]{2,1,0:T(8,128)(2,1)} %collective-permute-done.rest_1_), channel_id=1, source_target_pairs={{0,1},{1,2},{2,3},{3,4},{4,5},{5,6},{6,7},{7,0},{16,23},{17,16},{1... | collective-permute-start | bytes 2654216 | tf_op jit(solution)/shard_map/ppermute | solution.py:255
  22.0 5.1 %collective-permute-start.1 = (bf16[27,32,512]{2,1,0:T(8,128)(2,1)}, bf16[27,32,512]{2,1,0:T(8,128)(2,1)}, u32[]{:S(2)}, u32[]{:S(2)}) collective-permute-start(bf16[27,32,512]{2,1,0:T(8,128)(2,1)} %collective-permute-done.rest_1_), channel_id=1, source_target_pairs={{0,16},{16,0},{1,17},{17,1},{2,18},{18,2},{3,19},{19,3},{4,20},{20... | collective-permute-start | bytes 2654216 | tf_op jit(solution)/shard_map/ppermute | solution.py:258
  27.2 6.2 %collective-permute-done.2.rest_3_ = bf16[27,32,512]{2,1,0:T(8,128)(2,1)S(1)} collective-permute-done((bf16[27,32,512]{2,1,0:T(8,128)(2,1)}, bf16[27,32,512]{2,1,0:T(8,128)(2,1)S(1)}, u32[]{:S(2)}, u32[]{:S(2)}) %collective-permute-start.2) | collective-permute-done | bytes 884768 | tf_op jit(solution)/shard_map/ppermute | solution.py:255
  33.3 8.2 %collective-permute-start.3 = (bf16[27,32,512]{2,1,0:T(8,128)(2,1)S(1)}, bf16[27,32,512]{2,1,0:T(8,128)(2,1)}, u32[]{:S(2)}, u32[]{:S(2)}) collective-permute-start(bf16[27,32,512]{2,1,0:T(8,128)(2,1)S(1)} %collective-permute-done.2.rest_3_), channel_id=1, source_target_pairs={{0,16},{16,0},{1,17},{17,1},{2,18},{18,2},{3,19},{19,3},{4,20},{20... | collective-permute-start | bytes 2654216 | tf_op jit(solution)/shard_map/ppermute | solution.py:258
  41.6 0.8 constant_dynamic-slice_fusion
  42.4 1.9 %collective-permute-start.6 = (bf16[27,16,512]{2,1,0:T(8,128)(2,1)S(1)}, bf16[27,16,512]{2,1,0:T(8,128)(2,1)S(1)}, u32[]{:S(2)}, u32[]{:S(2)}) collective-permute-start(bf16[27,16,512]{2,1,0:T(8,128)(2,1)S(1)} %get-tuple-element.33), channel_id=1, source_target_pairs={{0,1},{1,2},{2,3},{3,4},{4,5},{5,6},{6,7},{7,0},{16,23},{17,16},{1... | collective-permute-start | bytes 1327112 | tf_op jit(solution)/shard_map/ppermute | solution.py:255
  44.4 0.0 copy-start
  44.4 0.0 copy-start.3
  44.4 2.1 %collective-permute-start.4 = (bf16[27,16,512]{2,1,0:T(8,128)(2,1)}, bf16[27,16,512]{2,1,0:T(8,128)(2,1)}, u32[]{:S(2)}, u32[]{:S(2)}) collective-permute-start(bf16[27,16,512]{2,1,0:T(8,128)(2,1)} %get-tuple-element.34), channel_id=1, source_target_pairs={{0,1},{1,2},{2,3},{3,4},{4,5},{5,6},{6,7},{7,0},{16,23},{17,16},{1... | collective-permute-start | bytes 1327112 | tf_op jit(solution)/shard_map/ppermute | solution.py:255
  46.4 5.3 %collective-permute-done.6.rest_5_ = bf16[27,16,512]{2,1,0:T(8,128)(2,1)S(1)} collective-permute-done((bf16[27,16,512]{2,1,0:T(8,128)(2,1)S(1)}, bf16[27,16,512]{2,1,0:T(8,128)(2,1)S(1)}, u32[]{:S(2)}, u32[]{:S(2)}) %collective-permute-start.6) | collective-permute-done | bytes 442400 | tf_op jit(solution)/shard_map/ppermute | solution.py:255
  51.8 2.8 %collective-permute-start.7 = (bf16[27,16,512]{2,1,0:T(8,128)(2,1)S(1)}, bf16[27,16,512]{2,1,0:T(8,128)(2,1)}, u32[]{:S(2)}, u32[]{:S(2)}) collective-permute-start(bf16[27,16,512]{2,1,0:T(8,128)(2,1)S(1)} %collective-permute-done.6.rest_5_), channel_id=1, source_target_pairs={{0,1},{1,2},{2,3},{3,4},{4,5},{5,6},{6,7},{7,0},{16,23},{17,16},{1... | collective-permute-start | bytes 1327112 | tf_op jit(solution)/shard_map/ppermute | solution.py:255
  54.6 0.0 collective-permute-done.1.rest_2_
  54.6 0.0 all-to-all-done.got
  54.6 0.0 collective-permute-done.3.rest_4_
  54.6 1.5 shard_map.65
  56.1 0.0 copy-start.1
  56.2 0.8 copy-done.1
  56.9 0.0 copy-start.2
  56.9 0.8 copy-done.2
  57.7 4.1 %all-to-all-start.2 = ((bf16[8,6,32,128]{3,2,1,0:T(8,128)(2,1)}), bf16[8,6,32,128]{3,2,1,0:T(8,128)(2,1)}, u32[]{:S(2)}, u32[]{:S(2)}) async-start(bf16[8,6,32,128]{3,2,1,0:T(8,128)(2,1)} %bitcast.10), calls=%async_computation.2 | async-start | bytes 786432 | tf_op jit(solution)/shard_map/all_to_all | solution.py:246
  61.8 0.0 collective-permute-done.4.rest_6_
  61.8 3.5 %collective-permute-start.5 = (bf16[27,16,512]{2,1,0:T(8,128)(2,1)}, bf16[27,16,512]{2,1,0:T(8,128)(2,1)S(1)}, u32[]{:S(2)}, u32[]{:S(2)}) collective-permute-start(bf16[27,16,512]{2,1,0:T(8,128)(2,1)} %collective-permute-done.4.rest_6_), channel_id=1, source_target_pairs={{0,16},{16,0},{1,17},{17,1},{2,18},{18,2},{3,19},{19,3},{4,20},{20... | collective-permute-start | bytes 1327112 | tf_op jit(solution)/shard_map/ppermute | solution.py:258
  65.3 0.0 collective-permute-done.7.rest_9_
  65.3 2.0 %collective-permute-start.8 = (bf16[27,16,512]{2,1,0:T(8,128)(2,1)}, bf16[27,16,512]{2,1,0:T(8,128)(2,1)S(1)}, u32[]{:S(2)}, u32[]{:S(2)}) collective-permute-start(bf16[27,16,512]{2,1,0:T(8,128)(2,1)} %collective-permute-done.7.rest_9_), channel_id=1, source_target_pairs={{0,16},{16,0},{1,17},{17,1},{2,18},{18,2},{3,19},{19,3},{4,20},{20... | collective-permute-start | bytes 1327112 | tf_op jit(solution)/shard_map/ppermute | solution.py:258
  67.2 2.4 %collective-permute-start.9 = (bf16[27,16,512]{2,1,0:T(8,128)(2,1)S(1)}, bf16[27,16,512]{2,1,0:T(8,128)(2,1)}, u32[]{:S(2)}, u32[]{:S(2)}) collective-permute-start(bf16[27,16,512]{2,1,0:T(8,128)(2,1)S(1)} %collective-permute-done.6.rest_5_), channel_id=1, source_target_pairs={{0,16},{16,0},{1,17},{17,1},{2,18},{18,2},{3,19},{19,3},{4,20},{20... | collective-permute-start | bytes 1327112 | tf_op jit(solution)/shard_map/ppermute | solution.py:258
  69.6 0.0 collective-permute-done.5.rest_8_
  69.6 0.0 collective-permute-done.8.rest_10_
  69.7 4.6 %all-to-all-done.2.frames = bf16[8,6,32,128]{3,2,1,0:T(8,128)(2,1)} async-done(((bf16[8,6,32,128]{3,2,1,0:T(8,128)(2,1)}), bf16[8,6,32,128]{3,2,1,0:T(8,128)(2,1)}, u32[]{:S(2)}, u32[]{:S(2)}) %all-to-all-start.2) | async-done | bytes 393248 | tf_op jit(solution)/shard_map/all_to_all | solution.py:246
  74.3 4.1 %all-to-all-start.1 = ((bf16[8,6,32,128]{3,2,1,0:T(8,128)(2,1)}), bf16[8,6,32,128]{3,2,1,0:T(8,128)(2,1)}, u32[]{:S(2)}, u32[]{:S(2)}) async-start(bf16[8,6,32,128]{3,2,1,0:T(8,128)(2,1)} %bitcast.9), calls=%async_computation.1 | async-start | bytes 786432 | tf_op jit(solution)/shard_map/all_to_all | solution.py:246
  78.4 0.0 collective-permute-done.9.rest_7_
  78.4 0.0 copy-done
  78.4 0.0 copy-done.3
  78.4 4.0 %shard_map.67 = (f32[128,512]{1,0:T(8,128)S(1)}, f32[128,512]{1,0:T(8,128)S(1)}) custom-call(s32[4]{0:T(128)S(1)} %copy-done.3, bf16[8,6,32,128]{3,2,1,0:T(8,128)(2,1)} %all-to-all-done.2.frames, bf16[27,32,512]{2,1,0:T(8,128)(2,1)S(1)} %bitcast.7, bf16[27,32,512]{2,1,0:T(8,128)(2,1)} %collective-permute-done.rest_1_, ...), custom_call_target="tpu_custom_call" | custom-call | tf_op jit(solution)/shard_map/pallas_call | solution.py:272
  82.4 4.4 %collective-permute-start.10 = (f32[128,512]{1,0:T(8,128)S(1)}, f32[128,512]{1,0:T(8,128)S(1)}, u32[]{:S(2)}, u32[]{:S(2)}) collective-permute-start(f32[128,512]{1,0:T(8,128)S(1)} %get-tuple-element.29), channel_id=1, source_target_pairs={{0,16},{16,32},{32,48},{48,64},{64,80},{80,96},{96,112},{112,128},... | collective-permute-start | bytes 786440 | tf_op jit(solution)/shard_map/ppermute | solution.py:319
  86.8 3.3 %collective-permute-done.10 = f32[128,512]{1,0:T(8,128)S(1)} collective-permute-done((f32[128,512]{1,0:T(8,128)S(1)}, f32[128,512]{1,0:T(8,128)S(1)}, u32[]{:S(2)}, u32[]{:S(2)}) %collective-permute-start.10) | collective-permute-done | bytes 262176 | tf_op jit(solution)/shard_map/ppermute | solution.py:319
  90.1 9.9 %collective-permute-start.11 = (f32[128,512]{1,0:T(8,128)S(1)}, f32[128,512]{1,0:T(8,128)}, u32[]{:S(2)}, u32[]{:S(2)}) collective-permute-start(f32[128,512]{1,0:T(8,128)S(1)} %add.14), channel_id=1, source_target_pairs={{0,8},{8,0},{1,9},{9,1},{2,10},{10,2},{3,11},{11,3},{4,12},{12,4},... | collective-permute-start | bytes 786440 | tf_op jit(solution)/shard_map/ppermute | solution.py:322
  100.0 0.0 all-to-all-done.1.frames
  100.0 4.0 %shard_map.66 = (f32[128,512]{1,0:T(8,128)S(1)}, f32[128,512]{1,0:T(8,128)S(1)}) custom-call(s32[4]{0:T(128)S(1)} %copy-done.3, bf16[8,6,32,128]{3,2,1,0:T(8,128)(2,1)} %all-to-all-done.1.frames, bf16[27,32,512]{2,1,0:T(8,128)(2,1)S(1)} %bitcast.8, bf16[27,32,512]{2,1,0:T(8,128)(2,1)} %collective-permute-done.rest_1_, ...), custom_call_target="tpu_custom_call" | custom-call | tf_op jit(solution)/shard_map/pallas_call | solution.py:272
  104.1 0.0 copy-start.4
  104.1 0.0 copy-start.5
  104.1 4.7 %collective-permute-start.12 = (f32[128,512]{1,0:T(8,128)S(1)}, f32[128,512]{1,0:T(8,128)S(1)}, u32[]{:S(2)}, u32[]{:S(2)}) collective-permute-start(f32[128,512]{1,0:T(8,128)S(1)} %get-tuple-element.30), channel_id=1, source_target_pairs={{0,16},{16,32},{32,48},{48,64},{64,80},{80,96},{96,112},{112,128},... | collective-permute-start | bytes 786440 | tf_op jit(solution)/shard_map/ppermute | solution.py:321
  108.8 0.0 collective-permute-done.11
  108.8 1.0 add.15.near
  109.8 2.3 %collective-permute-done.12.before = f32[128,512]{1,0:T(8,128)S(1)} collective-permute-done((f32[128,512]{1,0:T(8,128)S(1)}, f32[128,512]{1,0:T(8,128)S(1)}, u32[]{:S(2)}, u32[]{:S(2)}) %collective-permute-start.12) | collective-permute-done | bytes 262176 | tf_op jit(solution)/shard_map/ppermute | solution.py:321
  112.1 0.9 shard_map.68
  112.9 14.9 %all_to_all.25.got = f32[16,8,128]{2,1,0:T(8,128)} all-to-all(f32[16,8,128]{2,1,0:T(8,128)S(1)} %get-tuple-element.31), channel_id=1, replica_groups=mesh['zl'=4,'x'=4,'co'=2,'zh'=2,'y'=8] {'y','co'}, dimensions={0} | all-to-all | bytes 131072 | tf_op jit(solution)/shard_map/all_to_all | solution.py:246
  127.9 1.5 shard_map.69
  129.4 22.2 %all_to_all.26.got = f32[32,8,128]{2,1,0:T(8,128)S(1)} all-to-all(f32[32,8,128]{2,1,0:T(8,128)} %shard_map.69), channel_id=1, replica_groups=mesh['zl'=4,'x'=4,'co'=2,'zh'=2,'y'=8] {'zl','zh','x'}, dimensions={0} | all-to-all | bytes 262144 | tf_op jit(solution)/shard_map/all_to_all | solution.py:246
  151.6 0.0 copy-done.4
  151.6 0.0 copy-done.5
  151.6 1.5 shard_map.70
  (1 shorter events, 0.0 us)
Async XLA Ops:
  0.0 19.0 %collective-permute-start = (bf16[27,32,512]{2,1,0:T(8,128)(2,1)}, bf16[27,32,512]{2,1,0:T(8,128)(2,1)}, u32[]{:S(2)}, u32[]{:S(2)}) collective-permute-start(bf16[27,32,512]{2,1,0:T(8,128)(2,1)} %bitcast.6), channel_id=1, source_target_pairs={{0,1},{1,2},{2,3},{3,4},{4,5},{5,6},{6,7},{7,0},{16,23},{17,16},{1... | collective-permute-start | bytes 2654216 | tf_op jit(solution)/shard_map/ppermute | solution.py:255
  9.0 45.6 %all-to-all-start = ((bf16[32,136,128]{2,1,0:T(8,128)(2,1)}), bf16[32,136,128]{2,1,0:T(8,128)(2,1)S(1)}, u32[]{:S(2)}, u32[]{:S(2)}) async-start(bf16[32,136,128]{2,1,0:T(8,128)(2,1)} %shard_map.64), calls=%async_computation | async-start | bytes 2228224 | tf_op jit(solution)/shard_map/all_to_all | solution.py:246
  19.0 14.3 %collective-permute-start.2 = (bf16[27,32,512]{2,1,0:T(8,128)(2,1)}, bf16[27,32,512]{2,1,0:T(8,128)(2,1)S(1)}, u32[]{:S(2)}, u32[]{:S(2)}) collective-permute-start(bf16[27,32,512]{2,1,0:T(8,128)(2,1)} %collective-permute-done.rest_1_), channel_id=1, source_target_pairs={{0,1},{1,2},{2,3},{3,4},{4,5},{5,6},{6,7},{7,0},{16,23},{17,16},{1... | collective-permute-start | bytes 2654216 | tf_op jit(solution)/shard_map/ppermute | solution.py:255
  22.0 32.6 %collective-permute-start.1 = (bf16[27,32,512]{2,1,0:T(8,128)(2,1)}, bf16[27,32,512]{2,1,0:T(8,128)(2,1)}, u32[]{:S(2)}, u32[]{:S(2)}) collective-permute-start(bf16[27,32,512]{2,1,0:T(8,128)(2,1)} %collective-permute-done.rest_1_), channel_id=1, source_target_pairs={{0,16},{16,0},{1,17},{17,1},{2,18},{18,2},{3,19},{19,3},{4,20},{20... | collective-permute-start | bytes 2654216 | tf_op jit(solution)/shard_map/ppermute | solution.py:258
  33.3 21.3 %collective-permute-start.3 = (bf16[27,32,512]{2,1,0:T(8,128)(2,1)S(1)}, bf16[27,32,512]{2,1,0:T(8,128)(2,1)}, u32[]{:S(2)}, u32[]{:S(2)}) collective-permute-start(bf16[27,32,512]{2,1,0:T(8,128)(2,1)S(1)} %collective-permute-done.2.rest_3_), channel_id=1, source_target_pairs={{0,16},{16,0},{1,17},{17,1},{2,18},{18,2},{3,19},{19,3},{4,20},{20... | collective-permute-start | bytes 2654216 | tf_op jit(solution)/shard_map/ppermute | solution.py:258
  42.4 9.3 %collective-permute-start.6 = (bf16[27,16,512]{2,1,0:T(8,128)(2,1)S(1)}, bf16[27,16,512]{2,1,0:T(8,128)(2,1)S(1)}, u32[]{:S(2)}, u32[]{:S(2)}) collective-permute-start(bf16[27,16,512]{2,1,0:T(8,128)(2,1)S(1)} %get-tuple-element.33), channel_id=1, source_target_pairs={{0,1},{1,2},{2,3},{3,4},{4,5},{5,6},{6,7},{7,0},{16,23},{17,16},{1... | collective-permute-start | bytes 1327112 | tf_op jit(solution)/shard_map/ppermute | solution.py:255
  44.4 34.0 %copy-start = (bf16[3,3,3,32,512]{4,3,2,1,0:T(8,128)(2,1)S(1)}, bf16[3,3,3,32,512]{4,3,2,1,0:T(8,128)(2,1)}, u32[]{:S(2)}) copy-start(bf16[3,3,3,32,512]{4,3,2,1,0:T(8,128)(2,1)} %param.9) | copy-start | bytes 2654212
  44.4 34.0 %copy-start.3 = (s32[4]{0:T(128)S(1)}, s32[4]{0:T(128)}, u32[]{:S(2)}) copy-start(s32[4]{0:T(128)} %lengths.7) | copy-start | bytes 52
  44.4 17.4 %collective-permute-start.4 = (bf16[27,16,512]{2,1,0:T(8,128)(2,1)}, bf16[27,16,512]{2,1,0:T(8,128)(2,1)}, u32[]{:S(2)}, u32[]{:S(2)}) collective-permute-start(bf16[27,16,512]{2,1,0:T(8,128)(2,1)} %get-tuple-element.34), channel_id=1, source_target_pairs={{0,1},{1,2},{2,3},{3,4},{4,5},{5,6},{6,7},{7,0},{16,23},{17,16},{1... | collective-permute-start | bytes 1327112 | tf_op jit(solution)/shard_map/ppermute | solution.py:255
  51.8 13.5 %collective-permute-start.7 = (bf16[27,16,512]{2,1,0:T(8,128)(2,1)S(1)}, bf16[27,16,512]{2,1,0:T(8,128)(2,1)}, u32[]{:S(2)}, u32[]{:S(2)}) collective-permute-start(bf16[27,16,512]{2,1,0:T(8,128)(2,1)S(1)} %collective-permute-done.6.rest_5_), channel_id=1, source_target_pairs={{0,1},{1,2},{2,3},{3,4},{4,5},{5,6},{6,7},{7,0},{16,23},{17,16},{1... | collective-permute-start | bytes 1327112 | tf_op jit(solution)/shard_map/ppermute | solution.py:255
  56.1 0.8 copy-start.1
  56.9 0.8 copy-start.2
  57.7 16.6 %all-to-all-start.2 = ((bf16[8,6,32,128]{3,2,1,0:T(8,128)(2,1)}), bf16[8,6,32,128]{3,2,1,0:T(8,128)(2,1)}, u32[]{:S(2)}, u32[]{:S(2)}) async-start(bf16[8,6,32,128]{3,2,1,0:T(8,128)(2,1)} %bitcast.10), calls=%async_computation.2 | async-start | bytes 786432 | tf_op jit(solution)/shard_map/all_to_all | solution.py:246
  61.8 7.8 %collective-permute-start.5 = (bf16[27,16,512]{2,1,0:T(8,128)(2,1)}, bf16[27,16,512]{2,1,0:T(8,128)(2,1)S(1)}, u32[]{:S(2)}, u32[]{:S(2)}) collective-permute-start(bf16[27,16,512]{2,1,0:T(8,128)(2,1)} %collective-permute-done.4.rest_6_), channel_id=1, source_target_pairs={{0,16},{16,0},{1,17},{17,1},{2,18},{18,2},{3,19},{19,3},{4,20},{20... | collective-permute-start | bytes 1327112 | tf_op jit(solution)/shard_map/ppermute | solution.py:258
  65.3 4.4 %collective-permute-start.8 = (bf16[27,16,512]{2,1,0:T(8,128)(2,1)}, bf16[27,16,512]{2,1,0:T(8,128)(2,1)S(1)}, u32[]{:S(2)}, u32[]{:S(2)}) collective-permute-start(bf16[27,16,512]{2,1,0:T(8,128)(2,1)} %collective-permute-done.7.rest_9_), channel_id=1, source_target_pairs={{0,16},{16,0},{1,17},{17,1},{2,18},{18,2},{3,19},{19,3},{4,20},{20... | collective-permute-start | bytes 1327112 | tf_op jit(solution)/shard_map/ppermute | solution.py:258
  67.2 11.1 %collective-permute-start.9 = (bf16[27,16,512]{2,1,0:T(8,128)(2,1)S(1)}, bf16[27,16,512]{2,1,0:T(8,128)(2,1)}, u32[]{:S(2)}, u32[]{:S(2)}) collective-permute-start(bf16[27,16,512]{2,1,0:T(8,128)(2,1)S(1)} %collective-permute-done.6.rest_5_), channel_id=1, source_target_pairs={{0,16},{16,0},{1,17},{17,1},{2,18},{18,2},{3,19},{19,3},{4,20},{20... | collective-permute-start | bytes 1327112 | tf_op jit(solution)/shard_map/ppermute | solution.py:258
  74.3 25.8 %all-to-all-start.1 = ((bf16[8,6,32,128]{3,2,1,0:T(8,128)(2,1)}), bf16[8,6,32,128]{3,2,1,0:T(8,128)(2,1)}, u32[]{:S(2)}, u32[]{:S(2)}) async-start(bf16[8,6,32,128]{3,2,1,0:T(8,128)(2,1)} %bitcast.9), calls=%async_computation.1 | async-start | bytes 786432 | tf_op jit(solution)/shard_map/all_to_all | solution.py:246
  82.4 7.7 %collective-permute-start.10 = (f32[128,512]{1,0:T(8,128)S(1)}, f32[128,512]{1,0:T(8,128)S(1)}, u32[]{:S(2)}, u32[]{:S(2)}) collective-permute-start(f32[128,512]{1,0:T(8,128)S(1)} %get-tuple-element.29), channel_id=1, source_target_pairs={{0,16},{16,32},{32,48},{48,64},{64,80},{80,96},{96,112},{112,128},... | collective-permute-start | bytes 786440 | tf_op jit(solution)/shard_map/ppermute | solution.py:319
  90.1 18.6 %collective-permute-start.11 = (f32[128,512]{1,0:T(8,128)S(1)}, f32[128,512]{1,0:T(8,128)}, u32[]{:S(2)}, u32[]{:S(2)}) collective-permute-start(f32[128,512]{1,0:T(8,128)S(1)} %add.14), channel_id=1, source_target_pairs={{0,8},{8,0},{1,9},{9,1},{2,10},{10,2},{3,11},{11,3},{4,12},{12,4},... | collective-permute-start | bytes 786440 | tf_op jit(solution)/shard_map/ppermute | solution.py:322
  104.1 47.6 %copy-start.4 = (f32[512]{0:T(512)S(1)}, f32[512]{0:T(512)}, u32[]{:S(2)}) copy-start(f32[512]{0:T(512)} %param.10) | copy-start | bytes 6148
  104.1 47.6 %copy-start.5 = (f32[512]{0:T(512)S(1)}, f32[512]{0:T(512)}, u32[]{:S(2)}) copy-start(f32[512]{0:T(512)} %param.11) | copy-start | bytes 6148
  104.1 8.0 %collective-permute-start.12 = (f32[128,512]{1,0:T(8,128)S(1)}, f32[128,512]{1,0:T(8,128)S(1)}, u32[]{:S(2)}, u32[]{:S(2)}) collective-permute-start(f32[128,512]{1,0:T(8,128)S(1)} %get-tuple-element.30), channel_id=1, source_target_pairs={{0,16},{16,32},{32,48},{48,64},{64,80},{80,96},{96,112},{112,128},... | collective-permute-start | bytes 786440 | tf_op jit(solution)/shard_map/ppermute | solution.py:321

commit v10 on v8

--- a/solution.py
+++ b/solution.py
@@ -253,8 +253,9 @@
         moved.append(lax.ppermute(moved[-1], ("co", "y"), ring))
     first = lax.axis_index("co") * HALF
     half = lax.dynamic_slice_in_dim(moved[3], first, HALF, axis=1)
+    second, half = lax.optimization_barrier((moved[2], half))
     moved.append(lax.ppermute(half, ("co", "y"), ring))
-    swapped = [lax.ppermute(shard, "co", swap) for shard in moved[1:]]
+    swapped = [lax.ppermute(shard, "co", swap) for shard in (moved[1], second, moved[3], moved[4])]
     return moved, swapped
 
 

time: 150 us -> 150 us (level)
  no operation moved by 1% of the time
where the time goes in v10:
time: 150 us; the launch traced here: 149 us
  starting transfers between devices  65.4 us (44%)
  blocking collectives  34.3 us (23%)
  waiting for transfers between devices  27.7 us (18%)
  Pallas kernels  16.5 us (11%)
  local copies, waits for them, and re-layouts  3.34 us (2%)
    all_to_all x2, blocking collectives, shuffle(): return lax.all_to_all(x, axis, split_axis=0, concat_axis=0, tiled=True)  34.3 us
    all_to_all x3, starting transfers between devices, shuffle(): return lax.all_to_all(x, axis, split_axis=0, concat_axis=0, tiled=True)  19.3 us
    ppermute x4, starting transfers between devices, gathered_weights(): lax.ppermute(shard, 'co', swap)  12.9 us
    ppermute x3, starting transfers between devices, gathered_weights(): moved.append(lax.ppermute(moved[-1], ('co', 'y'), ring))  12.8 us
    all_to_all x3, waiting for transfers between devices, shuffle(): return lax.all_to_all(x, axis, split_axis=0, concat_axis=0, tiled=True)  8.8 us
    ppermute x1, starting transfers between devices, body(): far = lax.ppermute(far + far_before, 'zh', [(0, 1), (1, 0)])  7.95 us
    pallas_call x2, Pallas kernels, convolve(): pl.pallas_call(conv_kernel, out_shape=[jax.ShapeDtypeStruct((128, COUT),...  7.52 us
    ppermute x1, waiting for transfers between devices, gathered_weights(): moved.append(lax.ppermute(half, ('co', 'y'), ring))  7.1 us
  transfers between devices with their start and end apart: 14, of which 5 were waited for; matrix products, arithmetic and copies ran while one was open for 1% of the time, Pallas kernels for 9%

profile of v10, /device:TPU:1, one launch (start us, length us, event | category | flops | bytes accessed | tf_op | source)
XLA Modules:
  0.0 148.5 jit_solution(10626187820825127261)
XLA Ops:
  0.0 5.9 %collective-permute-start = (bf16[27,32,512]{2,1,0:T(8,128)(2,1)}, bf16[27,32,512]{2,1,0:T(8,128)(2,1)S(1)}, u32[]{:S(2)}, u32[]{:S(2)}) collective-permute-start(bf16[27,32,512]{2,1,0:T(8,128)(2,1)} %bitcast.6), channel_id=1, source_target_pairs={{0,1},{1,2},{2,3},{3,4},{4,5},{5,6},{6,7},{7,0},{16,23},{17,16},{1... | collective-permute-start | bytes 2654216 | tf_op jit(solution)/shard_map/ppermute | solution.py:253
  5.9 3.1 %shard_map.64 = bf16[32,136,128]{2,1,0:T(8,128)(2,1)} custom-call(s32[64]{0:T(128)} %target.1, bf16[64,32,128]{2,1,0:T(8,128)(2,1)} %arrived.1), custom_call_target="tpu_custom_call" | custom-call | tf_op jit(solution)/shard_map/pallas_call | solution.py:275
  9.0 10.0 %all-to-all-start = ((bf16[32,136,128]{2,1,0:T(8,128)(2,1)}), bf16[32,136,128]{2,1,0:T(8,128)(2,1)S(1)}, u32[]{:S(2)}, u32[]{:S(2)}) async-start(bf16[32,136,128]{2,1,0:T(8,128)(2,1)} %shard_map.64), calls=%async_computation | async-start | bytes 2228224 | tf_op jit(solution)/shard_map/all_to_all | solution.py:244
  19.0 0.0 collective-permute-done.rest_1_
  19.0 3.0 %collective-permute-start.1 = (bf16[27,32,512]{2,1,0:T(8,128)(2,1)S(1)}, bf16[27,32,512]{2,1,0:T(8,128)(2,1)}, u32[]{:S(2)}, u32[]{:S(2)}) collective-permute-start(bf16[27,32,512]{2,1,0:T(8,128)(2,1)S(1)} %collective-permute-done.rest_1_), channel_id=1, source_target_pairs={{0,1},{1,2},{2,3},{3,4},{4,5},{5,6},{6,7},{7,0},{16,23},{17,16},{1... | collective-permute-start | bytes 2654216 | tf_op jit(solution)/shard_map/ppermute | solution.py:253
  22.0 5.0 %collective-permute-start.2 = (bf16[27,32,512]{2,1,0:T(8,128)(2,1)S(1)}, bf16[27,32,512]{2,1,0:T(8,128)(2,1)S(1)}, u32[]{:S(2)}, u32[]{:S(2)}) collective-permute-start(bf16[27,32,512]{2,1,0:T(8,128)(2,1)S(1)} %collective-permute-done.rest_1_), channel_id=1, source_target_pairs={{0,16},{16,0},{1,17},{17,1},{2,18},{18,2},{3,19},{19,3},{4,20},{20... | collective-permute-start | bytes 2654216 | tf_op jit(solution)/shard_map/ppermute | solution.py:258
  27.1 6.2 %collective-permute-done.1.rest_3_ = bf16[27,32,512]{2,1,0:T(8,128)(2,1)} collective-permute-done((bf16[27,32,512]{2,1,0:T(8,128)(2,1)S(1)}, bf16[27,32,512]{2,1,0:T(8,128)(2,1)}, u32[]{:S(2)}, u32[]{:S(2)}) %collective-permute-start.1) | collective-permute-done | bytes 884768 | tf_op jit(solution)/shard_map/ppermute | solution.py:253
  33.2 3.9 %collective-permute-start.3 = (bf16[27,32,512]{2,1,0:T(8,128)(2,1)}, bf16[27,32,512]{2,1,0:T(8,128)(2,1)S(1)}, u32[]{:S(2)}, u32[]{:S(2)}) collective-permute-start(bf16[27,32,512]{2,1,0:T(8,128)(2,1)} %collective-permute-done.1.rest_3_), channel_id=1, source_target_pairs={{0,1},{1,2},{2,3},{3,4},{4,5},{5,6},{6,7},{7,0},{16,23},{17,16},{1... | collective-permute-start | bytes 2654216 | tf_op jit(solution)/shard_map/ppermute | solution.py:253
  37.1 0.0 collective-permute-done.2.rest_2_
  37.1 0.0 copy-start.1
  37.1 1.0 copy-done.1
  38.1 8.8 %all-to-all-done.got = bf16[32,136,128]{2,1,0:T(8,128)(2,1)S(1)} async-done(((bf16[32,136,128]{2,1,0:T(8,128)(2,1)}), bf16[32,136,128]{2,1,0:T(8,128)(2,1)S(1)}, u32[]{:S(2)}, u32[]{:S(2)}) %all-to-all-start) | async-done | bytes 1114144 | tf_op jit(solution)/shard_map/all_to_all | solution.py:244
  46.9 2.0 %shard_map.65 = (bf16[48,32,128]{2,1,0:T(8,128)(2,1)}, bf16[48,32,128]{2,1,0:T(8,128)(2,1)}) custom-call(bf16[32,136,128]{2,1,0:T(8,128)(2,1)S(1)} %all-to-all-done.got), custom_call_target="tpu_custom_call" | custom-call | tf_op jit(solution)/shard_map/pallas_call | solution.py:292
  48.9 0.0 copy-start
  48.9 0.0 copy-start.4
  49.0 5.0 %all-to-all-start.2 = ((bf16[8,6,32,128]{3,2,1,0:T(8,128)(2,1)}), bf16[8,6,32,128]{3,2,1,0:T(8,128)(2,1)}, u32[]{:S(2)}, u32[]{:S(2)}) async-start(bf16[8,6,32,128]{3,2,1,0:T(8,128)(2,1)} %bitcast.2), calls=%async_computation.2 | async-start | bytes 786432 | tf_op jit(solution)/shard_map/all_to_all | solution.py:244
  54.0 0.0 collective-permute-done.3.rest_5_
  54.0 4.6 %collective-permute-start.6 = (bf16[27,16,512]{2,1,0:T(8,128)(2,1)S(1)}, bf16[27,16,512]{2,1,0:T(8,128)(2,1)S(1)}, u32[]{:S(2)}, u32[]{:S(2)}) collective-permute-start(bf16[27,16,512]{2,1,0:T(8,128)(2,1)S(1)} %constant_dynamic-slice_fusion), channel_id=1, source_target_pairs={{0,1},{1,2},{2,3},{3,4},{4,5},{5,6},{6,7},{7,0},{16,23},{17,16},{1... | collective-permute-start | bytes 1327112 | tf_op jit(solution)/shard_map/ppermute | solution.py:257
  58.6 1.9 %collective-permute-start.4 = (bf16[27,32,512]{2,1,0:T(8,128)(2,1)}, bf16[27,32,512]{2,1,0:T(8,128)(2,1)}, u32[]{:S(2)}, u32[]{:S(2)}) collective-permute-start(bf16[27,32,512]{2,1,0:T(8,128)(2,1)} %collective-permute-done.1.rest_3_), channel_id=1, source_target_pairs={{0,16},{16,0},{1,17},{17,1},{2,18},{18,2},{3,19},{19,3},{4,20},{20... | collective-permute-start | bytes 2654216 | tf_op jit(solution)/shard_map/ppermute | solution.py:258
  60.5 2.4 %collective-permute-start.5 = (bf16[27,32,512]{2,1,0:T(8,128)(2,1)S(1)}, bf16[27,32,512]{2,1,0:T(8,128)(2,1)}, u32[]{:S(2)}, u32[]{:S(2)}) collective-permute-start(bf16[27,32,512]{2,1,0:T(8,128)(2,1)S(1)} %collective-permute-done.3.rest_5_), channel_id=1, source_target_pairs={{0,16},{16,0},{1,17},{17,1},{2,18},{18,2},{3,19},{19,3},{4,20},{20... | collective-permute-start | bytes 2654216 | tf_op jit(solution)/shard_map/ppermute | solution.py:258
  62.9 7.1 %collective-permute-done.6.rest_7_ = bf16[27,16,512]{2,1,0:T(8,128)(2,1)S(1)} collective-permute-done((bf16[27,16,512]{2,1,0:T(8,128)(2,1)S(1)}, bf16[27,16,512]{2,1,0:T(8,128)(2,1)S(1)}, u32[]{:S(2)}, u32[]{:S(2)}) %collective-permute-start.6) | collective-permute-done | bytes 442400 | tf_op jit(solution)/shard_map/ppermute | solution.py:257
  70.0 3.5 %collective-permute-start.7 = (bf16[27,16,512]{2,1,0:T(8,128)(2,1)S(1)}, bf16[27,16,512]{2,1,0:T(8,128)(2,1)}, u32[]{:S(2)}, u32[]{:S(2)}) collective-permute-start(bf16[27,16,512]{2,1,0:T(8,128)(2,1)S(1)} %collective-permute-done.6.rest_7_), channel_id=1, source_target_pairs={{0,16},{16,0},{1,17},{17,1},{2,18},{18,2},{3,19},{19,3},{4,20},{20... | collective-permute-start | bytes 1327112 | tf_op jit(solution)/shard_map/ppermute | solution.py:258
  73.6 0.0 all-to-all-done.2.frames
  73.6 4.3 %all-to-all-start.1 = ((bf16[8,6,32,128]{3,2,1,0:T(8,128)(2,1)}), bf16[8,6,32,128]{3,2,1,0:T(8,128)(2,1)}, u32[]{:S(2)}, u32[]{:S(2)}) async-start(bf16[8,6,32,128]{3,2,1,0:T(8,128)(2,1)} %bitcast.1), calls=%async_computation.1 | async-start | bytes 786432 | tf_op jit(solution)/shard_map/all_to_all | solution.py:244
  77.8 0.0 collective-permute-done.7.rest_8_
  77.8 0.0 collective-permute-done.4.rest_4_
  77.9 0.0 collective-permute-done.5.rest_6_
  77.9 0.0 copy-done
  77.9 0.0 copy-done.4
  77.9 0.0 copy-start.2
  77.9 1.2 copy-done.2
  79.1 3.8 %shard_map.67 = (f32[128,512]{1,0:T(8,128)S(1)}, f32[128,512]{1,0:T(8,128)S(1)}) custom-call(s32[4]{0:T(128)S(1)} %copy-done.4, bf16[8,6,32,128]{3,2,1,0:T(8,128)(2,1)} %all-to-all-done.2.frames, bf16[27,32,512]{2,1,0:T(8,128)(2,1)S(1)} %bitcast.7, bf16[27,32,512]{2,1,0:T(8,128)(2,1)S(1)} %collective-permute-done.rest_1_, ...), custom_call_target="tpu_custom_call" | custom-call | tf_op jit(solution)/shard_map/pallas_call | solution.py:263
  82.8 3.3 %collective-permute-start.8 = (f32[128,512]{1,0:T(8,128)S(1)}, f32[128,512]{1,0:T(8,128)S(1)}, u32[]{:S(2)}, u32[]{:S(2)}) collective-permute-start(f32[128,512]{1,0:T(8,128)S(1)} %get-tuple-element.27), channel_id=1, source_target_pairs={{0,16},{16,32},{32,48},{48,64},{64,80},{80,96},{96,112},{112,128},... | collective-permute-start | bytes 786440 | tf_op jit(solution)/shard_map/ppermute | solution.py:311
  86.1 3.3 %collective-permute-done.8 = f32[128,512]{1,0:T(8,128)S(1)} collective-permute-done((f32[128,512]{1,0:T(8,128)S(1)}, f32[128,512]{1,0:T(8,128)S(1)}, u32[]{:S(2)}, u32[]{:S(2)}) %collective-permute-start.8) | collective-permute-done | bytes 262176 | tf_op jit(solution)/shard_map/ppermute | solution.py:311
  89.4 7.9 %collective-permute-start.9 = (f32[128,512]{1,0:T(8,128)S(1)}, f32[128,512]{1,0:T(8,128)}, u32[]{:S(2)}, u32[]{:S(2)}) collective-permute-start(f32[128,512]{1,0:T(8,128)S(1)} %add.10), channel_id=1, source_target_pairs={{0,8},{8,0},{1,9},{9,1},{2,10},{10,2},{3,11},{11,3},{4,12},{12,4},... | collective-permute-start | bytes 786440 | tf_op jit(solution)/shard_map/ppermute | solution.py:314
  97.4 0.0 all-to-all-done.1.frames
  97.4 0.0 copy-start.3
  97.4 1.2 copy-done.3
  98.6 3.8 %shard_map.66 = (f32[128,512]{1,0:T(8,128)S(1)}, f32[128,512]{1,0:T(8,128)S(1)}) custom-call(s32[4]{0:T(128)S(1)} %copy-done.4, bf16[8,6,32,128]{3,2,1,0:T(8,128)(2,1)} %all-to-all-done.1.frames, bf16[27,32,512]{2,1,0:T(8,128)(2,1)S(1)} %bitcast.8, bf16[27,32,512]{2,1,0:T(8,128)(2,1)S(1)} %collective-permute-done.rest_1_, ...), custom_call_target="tpu_custom_call" | custom-call | tf_op jit(solution)/shard_map/pallas_call | solution.py:263
  102.3 0.0 copy-start.5
  102.4 0.0 copy-start.6
  102.4 4.7 %collective-permute-start.10 = (f32[128,512]{1,0:T(8,128)S(1)}, f32[128,512]{1,0:T(8,128)S(1)}, u32[]{:S(2)}, u32[]{:S(2)}) collective-permute-start(f32[128,512]{1,0:T(8,128)S(1)} %get-tuple-element.28), channel_id=1, source_target_pairs={{0,16},{16,32},{32,48},{48,64},{64,80},{80,96},{96,112},{112,128},... | collective-permute-start | bytes 786440 | tf_op jit(solution)/shard_map/ppermute | solution.py:313
  107.0 0.0 collective-permute-done.9
  107.0 1.0 add.11.near
  108.0 2.3 %collective-permute-done.10.before = f32[128,512]{1,0:T(8,128)S(1)} collective-permute-done((f32[128,512]{1,0:T(8,128)S(1)}, f32[128,512]{1,0:T(8,128)S(1)}, u32[]{:S(2)}, u32[]{:S(2)}) %collective-permute-start.10) | collective-permute-done | bytes 262176 | tf_op jit(solution)/shard_map/ppermute | solution.py:313
  110.3 0.9 shard_map.68
  111.2 15.0 %all_to_all.25.got = f32[16,8,128]{2,1,0:T(8,128)} all-to-all(f32[16,8,128]{2,1,0:T(8,128)S(1)} %get-tuple-element.29), channel_id=1, replica_groups=mesh['zl'=4,'x'=4,'co'=2,'zh'=2,'y'=8] {'y','co'}, dimensions={0} | all-to-all | bytes 131072 | tf_op jit(solution)/shard_map/all_to_all | solution.py:244
  126.2 1.5 %shard_map.69 = f32[32,8,128]{2,1,0:T(8,128)} custom-call(f32[16,8,128]{2,1,0:T(8,128)} %all_to_all.25.got), custom_call_target="tpu_custom_call" | custom-call | tf_op jit(solution)/shard_map/pallas_call | solution.py:324
  127.8 19.3 %all_to_all.26.got = f32[32,8,128]{2,1,0:T(8,128)S(1)} all-to-all(f32[32,8,128]{2,1,0:T(8,128)} %shard_map.69), channel_id=1, replica_groups=mesh['zl'=4,'x'=4,'co'=2,'zh'=2,'y'=8] {'zl','zh','x'}, dimensions={0} | all-to-all | bytes 262144 | tf_op jit(solution)/shard_map/all_to_all | solution.py:244
  147.0 0.0 copy-done.5
  147.0 0.0 copy-done.6
  147.0 1.5 %shard_map.70 = bf16[2,64,512]{2,1,0:T(8,128)(2,1)} custom-call(s32[4]{0:T(128)S(1)} %copy-done.4, f32[32,8,128]{2,1,0:T(8,128)S(1)} %all_to_all.26.got, f32[128,512]{1,0:T(8,128)S(1)} %get-tuple-element.30.conv, f32[1,512]{1,0:T(1,128)S(1)} %bitcast.9, f32[1,512]{1,0:T(1,128)S(1)} %bitcast.10), custom_call_target="tpu_custom_call" | custom-call | tf_op jit(solution)/shard_map/pallas_call | solution.py:331
  (2 shorter events, 0.1 us)
Async XLA Ops:
  0.0 19.0 %collective-permute-start = (bf16[27,32,512]{2,1,0:T(8,128)(2,1)}, bf16[27,32,512]{2,1,0:T(8,128)(2,1)S(1)}, u32[]{:S(2)}, u32[]{:S(2)}) collective-permute-start(bf16[27,32,512]{2,1,0:T(8,128)(2,1)} %bitcast.6), channel_id=1, source_target_pairs={{0,1},{1,2},{2,3},{3,4},{4,5},{5,6},{6,7},{7,0},{16,23},{17,16},{1... | collective-permute-start | bytes 2654216 | tf_op jit(solution)/shard_map/ppermute | solution.py:253
  9.0 37.9 %all-to-all-start = ((bf16[32,136,128]{2,1,0:T(8,128)(2,1)}), bf16[32,136,128]{2,1,0:T(8,128)(2,1)S(1)}, u32[]{:S(2)}, u32[]{:S(2)}) async-start(bf16[32,136,128]{2,1,0:T(8,128)(2,1)} %shard_map.64), calls=%async_computation | async-start | bytes 2228224 | tf_op jit(solution)/shard_map/all_to_all | solution.py:244
  19.0 14.2 %collective-permute-start.1 = (bf16[27,32,512]{2,1,0:T(8,128)(2,1)S(1)}, bf16[27,32,512]{2,1,0:T(8,128)(2,1)}, u32[]{:S(2)}, u32[]{:S(2)}) collective-permute-start(bf16[27,32,512]{2,1,0:T(8,128)(2,1)S(1)} %collective-permute-done.rest_1_), channel_id=1, source_target_pairs={{0,1},{1,2},{2,3},{3,4},{4,5},{5,6},{6,7},{7,0},{16,23},{17,16},{1... | collective-permute-start | bytes 2654216 | tf_op jit(solution)/shard_map/ppermute | solution.py:253
  22.0 15.1 %collective-permute-start.2 = (bf16[27,32,512]{2,1,0:T(8,128)(2,1)S(1)}, bf16[27,32,512]{2,1,0:T(8,128)(2,1)S(1)}, u32[]{:S(2)}, u32[]{:S(2)}) collective-permute-start(bf16[27,32,512]{2,1,0:T(8,128)(2,1)S(1)} %collective-permute-done.rest_1_), channel_id=1, source_target_pairs={{0,16},{16,0},{1,17},{17,1},{2,18},{18,2},{3,19},{19,3},{4,20},{20... | collective-permute-start | bytes 2654216 | tf_op jit(solution)/shard_map/ppermute | solution.py:258
  33.2 20.7 %collective-permute-start.3 = (bf16[27,32,512]{2,1,0:T(8,128)(2,1)}, bf16[27,32,512]{2,1,0:T(8,128)(2,1)S(1)}, u32[]{:S(2)}, u32[]{:S(2)}) collective-permute-start(bf16[27,32,512]{2,1,0:T(8,128)(2,1)} %collective-permute-done.1.rest_3_), channel_id=1, source_target_pairs={{0,1},{1,2},{2,3},{3,4},{4,5},{5,6},{6,7},{7,0},{16,23},{17,16},{1... | collective-permute-start | bytes 2654216 | tf_op jit(solution)/shard_map/ppermute | solution.py:253
  37.1 1.0 copy-start.1
  48.9 28.9 %copy-start = (bf16[3,3,3,32,512]{4,3,2,1,0:T(8,128)(2,1)S(1)}, bf16[3,3,3,32,512]{4,3,2,1,0:T(8,128)(2,1)}, u32[]{:S(2)}) copy-start(bf16[3,3,3,32,512]{4,3,2,1,0:T(8,128)(2,1)} %param.9) | copy-start | bytes 2654212
  48.9 28.9 %copy-start.4 = (s32[4]{0:T(128)S(1)}, s32[4]{0:T(128)}, u32[]{:S(2)}) copy-start(s32[4]{0:T(128)} %lengths.7) | copy-start | bytes 52
  49.0 24.6 %all-to-all-start.2 = ((bf16[8,6,32,128]{3,2,1,0:T(8,128)(2,1)}), bf16[8,6,32,128]{3,2,1,0:T(8,128)(2,1)}, u32[]{:S(2)}, u32[]{:S(2)}) async-start(bf16[8,6,32,128]{3,2,1,0:T(8,128)(2,1)} %bitcast.2), calls=%async_computation.2 | async-start | bytes 786432 | tf_op jit(solution)/shard_map/all_to_all | solution.py:244
  54.0 16.0 %collective-permute-start.6 = (bf16[27,16,512]{2,1,0:T(8,128)(2,1)S(1)}, bf16[27,16,512]{2,1,0:T(8,128)(2,1)S(1)}, u32[]{:S(2)}, u32[]{:S(2)}) collective-permute-start(bf16[27,16,512]{2,1,0:T(8,128)(2,1)S(1)} %constant_dynamic-slice_fusion), channel_id=1, source_target_pairs={{0,1},{1,2},{2,3},{3,4},{4,5},{5,6},{6,7},{7,0},{16,23},{17,16},{1... | collective-permute-start | bytes 1327112 | tf_op jit(solution)/shard_map/ppermute | solution.py:257
  58.6 19.3 %collective-permute-start.4 = (bf16[27,32,512]{2,1,0:T(8,128)(2,1)}, bf16[27,32,512]{2,1,0:T(8,128)(2,1)}, u32[]{:S(2)}, u32[]{:S(2)}) collective-permute-start(bf16[27,32,512]{2,1,0:T(8,128)(2,1)} %collective-permute-done.1.rest_3_), channel_id=1, source_target_pairs={{0,16},{16,0},{1,17},{17,1},{2,18},{18,2},{3,19},{19,3},{4,20},{20... | collective-permute-start | bytes 2654216 | tf_op jit(solution)/shard_map/ppermute | solution.py:258
  60.5 17.3 %collective-permute-start.5 = (bf16[27,32,512]{2,1,0:T(8,128)(2,1)S(1)}, bf16[27,32,512]{2,1,0:T(8,128)(2,1)}, u32[]{:S(2)}, u32[]{:S(2)}) collective-permute-start(bf16[27,32,512]{2,1,0:T(8,128)(2,1)S(1)} %collective-permute-done.3.rest_5_), channel_id=1, source_target_pairs={{0,16},{16,0},{1,17},{17,1},{2,18},{18,2},{3,19},{19,3},{4,20},{20... | collective-permute-start | bytes 2654216 | tf_op jit(solution)/shard_map/ppermute | solution.py:258
  70.0 7.8 %collective-permute-start.7 = (bf16[27,16,512]{2,1,0:T(8,128)(2,1)S(1)}, bf16[27,16,512]{2,1,0:T(8,128)(2,1)}, u32[]{:S(2)}, u32[]{:S(2)}) collective-permute-start(bf16[27,16,512]{2,1,0:T(8,128)(2,1)S(1)} %collective-permute-done.6.rest_7_), channel_id=1, source_target_pairs={{0,16},{16,0},{1,17},{17,1},{2,18},{18,2},{3,19},{19,3},{4,20},{20... | collective-permute-start | bytes 1327112 | tf_op jit(solution)/shard_map/ppermute | solution.py:258
  73.6 23.8 %all-to-all-start.1 = ((bf16[8,6,32,128]{3,2,1,0:T(8,128)(2,1)}), bf16[8,6,32,128]{3,2,1,0:T(8,128)(2,1)}, u32[]{:S(2)}, u32[]{:S(2)}) async-start(bf16[8,6,32,128]{3,2,1,0:T(8,128)(2,1)} %bitcast.1), calls=%async_computation.1 | async-start | bytes 786432 | tf_op jit(solution)/shard_map/all_to_all | solution.py:244
  77.9 1.2 copy-start.2
  82.8 6.6 %collective-permute-start.8 = (f32[128,512]{1,0:T(8,128)S(1)}, f32[128,512]{1,0:T(8,128)S(1)}, u32[]{:S(2)}, u32[]{:S(2)}) collective-permute-start(f32[128,512]{1,0:T(8,128)S(1)} %get-tuple-element.27), channel_id=1, source_target_pairs={{0,16},{16,32},{32,48},{48,64},{64,80},{80,96},{96,112},{112,128},... | collective-permute-start | bytes 786440 | tf_op jit(solution)/shard_map/ppermute | solution.py:311
  89.4 17.6 %collective-permute-start.9 = (f32[128,512]{1,0:T(8,128)S(1)}, f32[128,512]{1,0:T(8,128)}, u32[]{:S(2)}, u32[]{:S(2)}) collective-permute-start(f32[128,512]{1,0:T(8,128)S(1)} %add.10), channel_id=1, source_target_pairs={{0,8},{8,0},{1,9},{9,1},{2,10},{10,2},{3,11},{11,3},{4,12},{12,4},... | collective-permute-start | bytes 786440 | tf_op jit(solution)/shard_map/ppermute | solution.py:314
  97.4 1.2 copy-start.3
  102.3 44.7 %copy-start.5 = (f32[512]{0:T(512)S(1)}, f32[512]{0:T(512)}, u32[]{:S(2)}) copy-start(f32[512]{0:T(512)} %param.10) | copy-start | bytes 6148
  102.4 44.7 %copy-start.6 = (f32[512]{0:T(512)S(1)}, f32[512]{0:T(512)}, u32[]{:S(2)}) copy-start(f32[512]{0:T(512)} %param.11) | copy-start | bytes 6148
  102.4 8.0 %collective-permute-start.10 = (f32[128,512]{1,0:T(8,128)S(1)}, f32[128,512]{1,0:T(8,128)S(1)}, u32[]{:S(2)}, u32[]{:S(2)}) collective-permute-start(f32[128,512]{1,0:T(8,128)S(1)} %get-tuple-element.28), channel_id=1, source_target_pairs={{0,16},{16,32},{32,48},{48,64},{64,80},{80,96},{96,112},{112,128},... | collective-permute-start | bytes 786440 | tf_op jit(solution)/shard_map/ppermute | solution.py:313

commit v11 on v10

--- a/solution.py
+++ b/solution.py
@@ -286,9 +286,7 @@
         compiler_params=params(60),
     )(row_target, arrived)
     got = shuffle(send, TM)
-    got, moved[2], swapped[0] = lax.optimization_barrier(
-        (got, moved[2], swapped[0])
-    )
+    got, moved[2] = lax.optimization_barrier((got, moved[2]))
     far, near = pl.pallas_call(
         place_kernel,
         out_shape=[jax.ShapeDtypeStruct((NY * 6, CH_DEV, 128), BF)] * 2,

time: 150 us -> 149 us (level)
  waiting for transfers between devices: 27.7 us -> 31.2 us
  local copies, waits for them, and re-layouts: 3.34 us -> 0.06 us
  starting transfers between devices: 65.4 us -> 62.9 us
    ppermute x3, waiting for transfers between devices: 6.18 us -> 11.2 us  [gathered_weights(): moved.append(lax.ppermute(moved[-1], ('co', 'y'), ring))]
    unnamed x14 -> x8, local copies, waits for them, and re-layouts: 3.3 us -> 0.03 us
    ppermute x4, starting transfers between devices: 12.9 us -> 10.1 us  [gathered_weights(): lax.ppermute(shard, 'co', swap)]
    ppermute x1, waiting for transfers between devices: 7.1 us -> 4.58 us  [gathered_weights(): moved.append(lax.ppermute(half, ('co', 'y'), ring))]
  transfers between devices with their start and end apart: 14 -> 14, of which waited for: 5 -> 6; matrix products, arithmetic and copies ran while one was open for 1% -> 1% of each run, Pallas kernels for 9% -> 9%
where the time goes in v11:
time: 149 us; the launch traced here: 148 us
  starting transfers between devices  62.9 us (42%)
  blocking collectives  35.3 us (24%)
  waiting for transfers between devices  31.2 us (21%)
  Pallas kernels  17 us (11%)
    all_to_all x2, blocking collectives, shuffle(): return lax.all_to_all(x, axis, split_axis=0, concat_axis=0, tiled=True)  35.3 us
    all_to_all x3, starting transfers between devices, shuffle(): return lax.all_to_all(x, axis, split_axis=0, concat_axis=0, tiled=True)  19.3 us
    ppermute x3, starting transfers between devices, gathered_weights(): moved.append(lax.ppermute(moved[-1], ('co', 'y'), ring))  12.8 us
    ppermute x3, waiting for transfers between devices, gathered_weights(): moved.append(lax.ppermute(moved[-1], ('co', 'y'), ring))  11.2 us
    ppermute x4, starting transfers between devices, gathered_weights(): lax.ppermute(shard, 'co', swap)  10.1 us
    all_to_all x3, waiting for transfers between devices, shuffle(): return lax.all_to_all(x, axis, split_axis=0, concat_axis=0, tiled=True)  9.78 us
    pallas_call x2, Pallas kernels, convolve(): pl.pallas_call(conv_kernel, out_shape=[jax.ShapeDtypeStruct((128, COUT),...  7.99 us
    ppermute x1, starting transfers between devices, body(): far = lax.ppermute(far + far_before, 'zh', [(0, 1), (1, 0)])  7.94 us
  transfers between devices with their start and end apart: 14, of which 6 were waited for; matrix products, arithmetic and copies ran while one was open for 1% of the time, Pallas kernels for 9%

profile of v11, /device:TPU:1, one launch (start us, length us, event | category | flops | bytes accessed | tf_op | source)
XLA Modules:
  0.0 147.6 jit_solution(1415493359140107605)
XLA Ops:
  0.0 5.9 %collective-permute-start = (bf16[27,32,512]{2,1,0:T(8,128)(2,1)}, bf16[27,32,512]{2,1,0:T(8,128)(2,1)S(1)}, u32[]{:S(2)}, u32[]{:S(2)}) collective-permute-start(bf16[27,32,512]{2,1,0:T(8,128)(2,1)} %bitcast.6), channel_id=1, source_target_pairs={{0,1},{1,2},{2,3},{3,4},{4,5},{5,6},{6,7},{7,0},{16,23},{17,16},{1... | collective-permute-start | bytes 2654216 | tf_op jit(solution)/shard_map/ppermute | solution.py:253
  5.9 3.1 %shard_map.64 = bf16[32,136,128]{2,1,0:T(8,128)(2,1)} custom-call(s32[64]{0:T(128)} %target.1, bf16[64,32,128]{2,1,0:T(8,128)(2,1)} %arrived.1), custom_call_target="tpu_custom_call" | custom-call | tf_op jit(solution)/shard_map/pallas_call | solution.py:275
  9.0 10.0 %all-to-all-start = ((bf16[32,136,128]{2,1,0:T(8,128)(2,1)}), bf16[32,136,128]{2,1,0:T(8,128)(2,1)S(1)}, u32[]{:S(2)}, u32[]{:S(2)}) async-start(bf16[32,136,128]{2,1,0:T(8,128)(2,1)} %shard_map.64), calls=%async_computation | async-start | bytes 2228224 | tf_op jit(solution)/shard_map/all_to_all | solution.py:244
  19.1 0.0 collective-permute-done.rest_1_
  19.1 3.0 %collective-permute-start.1 = (bf16[27,32,512]{2,1,0:T(8,128)(2,1)S(1)}, bf16[27,32,512]{2,1,0:T(8,128)(2,1)}, u32[]{:S(2)}, u32[]{:S(2)}) collective-permute-start(bf16[27,32,512]{2,1,0:T(8,128)(2,1)S(1)} %collective-permute-done.rest_1_), channel_id=1, source_target_pairs={{0,1},{1,2},{2,3},{3,4},{4,5},{5,6},{6,7},{7,0},{16,23},{17,16},{1... | collective-permute-start | bytes 2654216 | tf_op jit(solution)/shard_map/ppermute | solution.py:253
  22.0 11.2 %collective-permute-done.1.rest_3_ = bf16[27,32,512]{2,1,0:T(8,128)(2,1)} collective-permute-done((bf16[27,32,512]{2,1,0:T(8,128)(2,1)S(1)}, bf16[27,32,512]{2,1,0:T(8,128)(2,1)}, u32[]{:S(2)}, u32[]{:S(2)}) %collective-permute-start.1) | collective-permute-done | bytes 884768 | tf_op jit(solution)/shard_map/ppermute | solution.py:253
  33.2 3.9 %collective-permute-start.3 = (bf16[27,32,512]{2,1,0:T(8,128)(2,1)}, bf16[27,32,512]{2,1,0:T(8,128)(2,1)S(1)}, u32[]{:S(2)}, u32[]{:S(2)}) collective-permute-start(bf16[27,32,512]{2,1,0:T(8,128)(2,1)} %collective-permute-done.1.rest_3_), channel_id=1, source_target_pairs={{0,1},{1,2},{2,3},{3,4},{4,5},{5,6},{6,7},{7,0},{16,23},{17,16},{1... | collective-permute-start | bytes 2654216 | tf_op jit(solution)/shard_map/ppermute | solution.py:253
  37.1 9.8 %all-to-all-done.got = bf16[32,136,128]{2,1,0:T(8,128)(2,1)S(1)} async-done(((bf16[32,136,128]{2,1,0:T(8,128)(2,1)}), bf16[32,136,128]{2,1,0:T(8,128)(2,1)S(1)}, u32[]{:S(2)}, u32[]{:S(2)}) %all-to-all-start) | async-done | bytes 1114144 | tf_op jit(solution)/shard_map/all_to_all | solution.py:244
  46.9 2.0 %shard_map.65 = (bf16[48,32,128]{2,1,0:T(8,128)(2,1)}, bf16[48,32,128]{2,1,0:T(8,128)(2,1)}) custom-call(bf16[32,136,128]{2,1,0:T(8,128)(2,1)S(1)} %all-to-all-done.got), custom_call_target="tpu_custom_call" | custom-call | tf_op jit(solution)/shard_map/pallas_call | solution.py:290
  48.9 0.0 copy-start
  48.9 0.0 copy-start.1
  48.9 5.0 %all-to-all-start.2 = ((bf16[8,6,32,128]{3,2,1,0:T(8,128)(2,1)}), bf16[8,6,32,128]{3,2,1,0:T(8,128)(2,1)}, u32[]{:S(2)}, u32[]{:S(2)}) async-start(bf16[8,6,32,128]{3,2,1,0:T(8,128)(2,1)} %bitcast.2), calls=%async_computation.2 | async-start | bytes 786432 | tf_op jit(solution)/shard_map/all_to_all | solution.py:244
  54.0 2.2 %collective-permute-start.2 = (bf16[27,32,512]{2,1,0:T(8,128)(2,1)S(1)}, bf16[27,32,512]{2,1,0:T(8,128)(2,1)}, u32[]{:S(2)}, u32[]{:S(2)}) collective-permute-start(bf16[27,32,512]{2,1,0:T(8,128)(2,1)S(1)} %collective-permute-done.rest_1_), channel_id=1, source_target_pairs={{0,16},{16,0},{1,17},{17,1},{2,18},{18,2},{3,19},{19,3},{4,20},{20... | collective-permute-start | bytes 2654216 | tf_op jit(solution)/shard_map/ppermute | solution.py:258
  56.2 0.0 collective-permute-done.3.rest_5_
  56.2 4.9 %collective-permute-start.6 = (bf16[27,16,512]{2,1,0:T(8,128)(2,1)S(1)}, bf16[27,16,512]{2,1,0:T(8,128)(2,1)S(1)}, u32[]{:S(2)}, u32[]{:S(2)}) collective-permute-start(bf16[27,16,512]{2,1,0:T(8,128)(2,1)S(1)} %constant_dynamic-slice_fusion), channel_id=1, source_target_pairs={{0,1},{1,2},{2,3},{3,4},{4,5},{5,6},{6,7},{7,0},{16,23},{17,16},{1... | collective-permute-start | bytes 1327112 | tf_op jit(solution)/shard_map/ppermute | solution.py:257
  61.1 1.9 %collective-permute-start.4 = (bf16[27,32,512]{2,1,0:T(8,128)(2,1)}, bf16[27,32,512]{2,1,0:T(8,128)(2,1)}, u32[]{:S(2)}, u32[]{:S(2)}) collective-permute-start(bf16[27,32,512]{2,1,0:T(8,128)(2,1)} %collective-permute-done.1.rest_3_), channel_id=1, source_target_pairs={{0,16},{16,0},{1,17},{17,1},{2,18},{18,2},{3,19},{19,3},{4,20},{20... | collective-permute-start | bytes 2654216 | tf_op jit(solution)/shard_map/ppermute | solution.py:258
  63.0 2.4 %collective-permute-start.5 = (bf16[27,32,512]{2,1,0:T(8,128)(2,1)S(1)}, bf16[27,32,512]{2,1,0:T(8,128)(2,1)}, u32[]{:S(2)}, u32[]{:S(2)}) collective-permute-start(bf16[27,32,512]{2,1,0:T(8,128)(2,1)S(1)} %collective-permute-done.3.rest_5_), channel_id=1, source_target_pairs={{0,16},{16,0},{1,17},{17,1},{2,18},{18,2},{3,19},{19,3},{4,20},{20... | collective-permute-start | bytes 2654216 | tf_op jit(solution)/shard_map/ppermute | solution.py:258
  65.5 4.6 %collective-permute-done.6.rest_7_ = bf16[27,16,512]{2,1,0:T(8,128)(2,1)S(1)} collective-permute-done((bf16[27,16,512]{2,1,0:T(8,128)(2,1)S(1)}, bf16[27,16,512]{2,1,0:T(8,128)(2,1)S(1)}, u32[]{:S(2)}, u32[]{:S(2)}) %collective-permute-start.6) | collective-permute-done | bytes 442400 | tf_op jit(solution)/shard_map/ppermute | solution.py:257
  70.0 3.5 %collective-permute-start.7 = (bf16[27,16,512]{2,1,0:T(8,128)(2,1)S(1)}, bf16[27,16,512]{2,1,0:T(8,128)(2,1)}, u32[]{:S(2)}, u32[]{:S(2)}) collective-permute-start(bf16[27,16,512]{2,1,0:T(8,128)(2,1)S(1)} %collective-permute-done.6.rest_7_), channel_id=1, source_target_pairs={{0,16},{16,0},{1,17},{17,1},{2,18},{18,2},{3,19},{19,3},{4,20},{20... | collective-permute-start | bytes 1327112 | tf_op jit(solution)/shard_map/ppermute | solution.py:258
  73.5 0.0 all-to-all-done.2.frames
  73.6 4.3 %all-to-all-start.1 = ((bf16[8,6,32,128]{3,2,1,0:T(8,128)(2,1)}), bf16[8,6,32,128]{3,2,1,0:T(8,128)(2,1)}, u32[]{:S(2)}, u32[]{:S(2)}) async-start(bf16[8,6,32,128]{3,2,1,0:T(8,128)(2,1)} %bitcast.1), calls=%async_computation.1 | async-start | bytes 786432 | tf_op jit(solution)/shard_map/all_to_all | solution.py:244
  77.8 0.0 collective-permute-done.2.rest_2_
  77.8 0.0 collective-permute-done.7.rest_8_
  77.8 0.0 collective-permute-done.4.rest_4_
  77.9 0.0 collective-permute-done.5.rest_6_
  77.9 0.0 copy-done
  77.9 0.0 copy-done.1
  77.9 4.0 %shard_map.67 = (f32[128,512]{1,0:T(8,128)S(1)}, f32[128,512]{1,0:T(8,128)S(1)}) custom-call(s32[4]{0:T(128)S(1)} %copy-done.1, bf16[8,6,32,128]{3,2,1,0:T(8,128)(2,1)} %all-to-all-done.2.frames, bf16[27,32,512]{2,1,0:T(8,128)(2,1)S(1)} %bitcast.7, bf16[27,32,512]{2,1,0:T(8,128)(2,1)S(1)} %collective-permute-done.rest_1_, ...), custom_call_target="tpu_custom_call" | custom-call | tf_op jit(solution)/shard_map/pallas_call | solution.py:263
  81.9 3.3 %collective-permute-start.8 = (f32[128,512]{1,0:T(8,128)S(1)}, f32[128,512]{1,0:T(8,128)S(1)}, u32[]{:S(2)}, u32[]{:S(2)}) collective-permute-start(f32[128,512]{1,0:T(8,128)S(1)} %get-tuple-element.25), channel_id=1, source_target_pairs={{0,16},{16,32},{32,48},{48,64},{64,80},{80,96},{96,112},{112,128},... | collective-permute-start | bytes 786440 | tf_op jit(solution)/shard_map/ppermute | solution.py:309
  85.2 3.3 %collective-permute-done.8 = f32[128,512]{1,0:T(8,128)S(1)} collective-permute-done((f32[128,512]{1,0:T(8,128)S(1)}, f32[128,512]{1,0:T(8,128)S(1)}, u32[]{:S(2)}, u32[]{:S(2)}) %collective-permute-start.8) | collective-permute-done | bytes 262176 | tf_op jit(solution)/shard_map/ppermute | solution.py:309
  88.5 7.9 %collective-permute-start.9 = (f32[128,512]{1,0:T(8,128)S(1)}, f32[128,512]{1,0:T(8,128)}, u32[]{:S(2)}, u32[]{:S(2)}) collective-permute-start(f32[128,512]{1,0:T(8,128)S(1)} %add.10), channel_id=1, source_target_pairs={{0,8},{8,0},{1,9},{9,1},{2,10},{10,2},{3,11},{11,3},{4,12},{12,4},... | collective-permute-start | bytes 786440 | tf_op jit(solution)/shard_map/ppermute | solution.py:312
  96.5 0.0 all-to-all-done.1.frames
  96.5 4.0 %shard_map.66 = (f32[128,512]{1,0:T(8,128)S(1)}, f32[128,512]{1,0:T(8,128)S(1)}) custom-call(s32[4]{0:T(128)S(1)} %copy-done.1, bf16[8,6,32,128]{3,2,1,0:T(8,128)(2,1)} %all-to-all-done.1.frames, bf16[27,32,512]{2,1,0:T(8,128)(2,1)S(1)} %bitcast.8, bf16[27,32,512]{2,1,0:T(8,128)(2,1)S(1)} %collective-permute-done.rest_1_, ...), custom_call_target="tpu_custom_call" | custom-call | tf_op jit(solution)/shard_map/pallas_call | solution.py:263
  100.5 0.0 copy-start.2
  100.5 0.0 copy-start.3
  100.5 4.7 %collective-permute-start.10 = (f32[128,512]{1,0:T(8,128)S(1)}, f32[128,512]{1,0:T(8,128)S(1)}, u32[]{:S(2)}, u32[]{:S(2)}) collective-permute-start(f32[128,512]{1,0:T(8,128)S(1)} %get-tuple-element.26), channel_id=1, source_target_pairs={{0,16},{16,32},{32,48},{48,64},{64,80},{80,96},{96,112},{112,128},... | collective-permute-start | bytes 786440 | tf_op jit(solution)/shard_map/ppermute | solution.py:311
  105.2 0.5 collective-permute-done.9
  105.6 1.0 add.11.near
  106.6 1.8 %collective-permute-done.10.before = f32[128,512]{1,0:T(8,128)S(1)} collective-permute-done((f32[128,512]{1,0:T(8,128)S(1)}, f32[128,512]{1,0:T(8,128)S(1)}, u32[]{:S(2)}, u32[]{:S(2)}) %collective-permute-start.10) | collective-permute-done | bytes 262176 | tf_op jit(solution)/shard_map/ppermute | solution.py:311
  108.5 0.9 shard_map.68
  109.3 15.0 %all_to_all.25.got = f32[16,8,128]{2,1,0:T(8,128)} all-to-all(f32[16,8,128]{2,1,0:T(8,128)S(1)} %get-tuple-element.27), channel_id=1, replica_groups=mesh['zl'=4,'x'=4,'co'=2,'zh'=2,'y'=8] {'y','co'}, dimensions={0} | all-to-all | bytes 131072 | tf_op jit(solution)/shard_map/all_to_all | solution.py:244
  124.4 1.5 %shard_map.69 = f32[32,8,128]{2,1,0:T(8,128)} custom-call(f32[16,8,128]{2,1,0:T(8,128)} %all_to_all.25.got), custom_call_target="tpu_custom_call" | custom-call | tf_op jit(solution)/shard_map/pallas_call | solution.py:322
  125.9 20.2 %all_to_all.26.got = f32[32,8,128]{2,1,0:T(8,128)S(1)} all-to-all(f32[32,8,128]{2,1,0:T(8,128)} %shard_map.69), channel_id=1, replica_groups=mesh['zl'=4,'x'=4,'co'=2,'zh'=2,'y'=8] {'zl','zh','x'}, dimensions={0} | all-to-all | bytes 262144 | tf_op jit(solution)/shard_map/all_to_all | solution.py:244
  146.1 0.0 copy-done.2
  146.1 0.0 copy-done.3
  146.1 1.5 %shard_map.70 = bf16[2,64,512]{2,1,0:T(8,128)(2,1)} custom-call(s32[4]{0:T(128)S(1)} %copy-done.1, f32[32,8,128]{2,1,0:T(8,128)S(1)} %all_to_all.26.got, f32[128,512]{1,0:T(8,128)S(1)} %get-tuple-element.28.conv, f32[1,512]{1,0:T(1,128)S(1)} %bitcast.9, f32[1,512]{1,0:T(1,128)S(1)} %bitcast.10), custom_call_target="tpu_custom_call" | custom-call | tf_op jit(solution)/shard_map/pallas_call | solution.py:329
  (2 shorter events, 0.1 us)
Async XLA Ops:
  0.0 19.1 %collective-permute-start = (bf16[27,32,512]{2,1,0:T(8,128)(2,1)}, bf16[27,32,512]{2,1,0:T(8,128)(2,1)S(1)}, u32[]{:S(2)}, u32[]{:S(2)}) collective-permute-start(bf16[27,32,512]{2,1,0:T(8,128)(2,1)} %bitcast.6), channel_id=1, source_target_pairs={{0,1},{1,2},{2,3},{3,4},{4,5},{5,6},{6,7},{7,0},{16,23},{17,16},{1... | collective-permute-start | bytes 2654216 | tf_op jit(solution)/shard_map/ppermute | solution.py:253
  9.0 37.9 %all-to-all-start = ((bf16[32,136,128]{2,1,0:T(8,128)(2,1)}), bf16[32,136,128]{2,1,0:T(8,128)(2,1)S(1)}, u32[]{:S(2)}, u32[]{:S(2)}) async-start(bf16[32,136,128]{2,1,0:T(8,128)(2,1)} %shard_map.64), calls=%async_computation | async-start | bytes 2228224 | tf_op jit(solution)/shard_map/all_to_all | solution.py:244
  19.1 14.2 %collective-permute-start.1 = (bf16[27,32,512]{2,1,0:T(8,128)(2,1)S(1)}, bf16[27,32,512]{2,1,0:T(8,128)(2,1)}, u32[]{:S(2)}, u32[]{:S(2)}) collective-permute-start(bf16[27,32,512]{2,1,0:T(8,128)(2,1)S(1)} %collective-permute-done.rest_1_), channel_id=1, source_target_pairs={{0,1},{1,2},{2,3},{3,4},{4,5},{5,6},{6,7},{7,0},{16,23},{17,16},{1... | collective-permute-start | bytes 2654216 | tf_op jit(solution)/shard_map/ppermute | solution.py:253
  33.2 22.9 %collective-permute-start.3 = (bf16[27,32,512]{2,1,0:T(8,128)(2,1)}, bf16[27,32,512]{2,1,0:T(8,128)(2,1)S(1)}, u32[]{:S(2)}, u32[]{:S(2)}) collective-permute-start(bf16[27,32,512]{2,1,0:T(8,128)(2,1)} %collective-permute-done.1.rest_3_), channel_id=1, source_target_pairs={{0,1},{1,2},{2,3},{3,4},{4,5},{5,6},{6,7},{7,0},{16,23},{17,16},{1... | collective-permute-start | bytes 2654216 | tf_op jit(solution)/shard_map/ppermute | solution.py:253
  48.9 28.9 %copy-start = (bf16[3,3,3,32,512]{4,3,2,1,0:T(8,128)(2,1)S(1)}, bf16[3,3,3,32,512]{4,3,2,1,0:T(8,128)(2,1)}, u32[]{:S(2)}) copy-start(bf16[3,3,3,32,512]{4,3,2,1,0:T(8,128)(2,1)} %param.9) | copy-start | bytes 2654212
  48.9 28.9 %copy-start.1 = (s32[4]{0:T(128)S(1)}, s32[4]{0:T(128)}, u32[]{:S(2)}) copy-start(s32[4]{0:T(128)} %lengths.7) | copy-start | bytes 52
  48.9 24.6 %all-to-all-start.2 = ((bf16[8,6,32,128]{3,2,1,0:T(8,128)(2,1)}), bf16[8,6,32,128]{3,2,1,0:T(8,128)(2,1)}, u32[]{:S(2)}, u32[]{:S(2)}) async-start(bf16[8,6,32,128]{3,2,1,0:T(8,128)(2,1)} %bitcast.2), calls=%async_computation.2 | async-start | bytes 786432 | tf_op jit(solution)/shard_map/all_to_all | solution.py:244
  54.0 23.9 %collective-permute-start.2 = (bf16[27,32,512]{2,1,0:T(8,128)(2,1)S(1)}, bf16[27,32,512]{2,1,0:T(8,128)(2,1)}, u32[]{:S(2)}, u32[]{:S(2)}) collective-permute-start(bf16[27,32,512]{2,1,0:T(8,128)(2,1)S(1)} %collective-permute-done.rest_1_), channel_id=1, source_target_pairs={{0,16},{16,0},{1,17},{17,1},{2,18},{18,2},{3,19},{19,3},{4,20},{20... | collective-permute-start | bytes 2654216 | tf_op jit(solution)/shard_map/ppermute | solution.py:258
  56.2 13.8 %collective-permute-start.6 = (bf16[27,16,512]{2,1,0:T(8,128)(2,1)S(1)}, bf16[27,16,512]{2,1,0:T(8,128)(2,1)S(1)}, u32[]{:S(2)}, u32[]{:S(2)}) collective-permute-start(bf16[27,16,512]{2,1,0:T(8,128)(2,1)S(1)} %constant_dynamic-slice_fusion), channel_id=1, source_target_pairs={{0,1},{1,2},{2,3},{3,4},{4,5},{5,6},{6,7},{7,0},{16,23},{17,16},{1... | collective-permute-start | bytes 1327112 | tf_op jit(solution)/shard_map/ppermute | solution.py:257
  61.1 16.7 %collective-permute-start.4 = (bf16[27,32,512]{2,1,0:T(8,128)(2,1)}, bf16[27,32,512]{2,1,0:T(8,128)(2,1)}, u32[]{:S(2)}, u32[]{:S(2)}) collective-permute-start(bf16[27,32,512]{2,1,0:T(8,128)(2,1)} %collective-permute-done.1.rest_3_), channel_id=1, source_target_pairs={{0,16},{16,0},{1,17},{17,1},{2,18},{18,2},{3,19},{19,3},{4,20},{20... | collective-permute-start | bytes 2654216 | tf_op jit(solution)/shard_map/ppermute | solution.py:258
  63.0 14.8 %collective-permute-start.5 = (bf16[27,32,512]{2,1,0:T(8,128)(2,1)S(1)}, bf16[27,32,512]{2,1,0:T(8,128)(2,1)}, u32[]{:S(2)}, u32[]{:S(2)}) collective-permute-start(bf16[27,32,512]{2,1,0:T(8,128)(2,1)S(1)} %collective-permute-done.3.rest_5_), channel_id=1, source_target_pairs={{0,16},{16,0},{1,17},{17,1},{2,18},{18,2},{3,19},{19,3},{4,20},{20... | collective-permute-start | bytes 2654216 | tf_op jit(solution)/shard_map/ppermute | solution.py:258
  70.0 7.8 %collective-permute-start.7 = (bf16[27,16,512]{2,1,0:T(8,128)(2,1)S(1)}, bf16[27,16,512]{2,1,0:T(8,128)(2,1)}, u32[]{:S(2)}, u32[]{:S(2)}) collective-permute-start(bf16[27,16,512]{2,1,0:T(8,128)(2,1)S(1)} %collective-permute-done.6.rest_7_), channel_id=1, source_target_pairs={{0,16},{16,0},{1,17},{17,1},{2,18},{18,2},{3,19},{19,3},{4,20},{20... | collective-permute-start | bytes 1327112 | tf_op jit(solution)/shard_map/ppermute | solution.py:258
  73.6 22.9 %all-to-all-start.1 = ((bf16[8,6,32,128]{3,2,1,0:T(8,128)(2,1)}), bf16[8,6,32,128]{3,2,1,0:T(8,128)(2,1)}, u32[]{:S(2)}, u32[]{:S(2)}) async-start(bf16[8,6,32,128]{3,2,1,0:T(8,128)(2,1)} %bitcast.1), calls=%async_computation.1 | async-start | bytes 786432 | tf_op jit(solution)/shard_map/all_to_all | solution.py:244
  81.9 6.6 %collective-permute-start.8 = (f32[128,512]{1,0:T(8,128)S(1)}, f32[128,512]{1,0:T(8,128)S(1)}, u32[]{:S(2)}, u32[]{:S(2)}) collective-permute-start(f32[128,512]{1,0:T(8,128)S(1)} %get-tuple-element.25), channel_id=1, source_target_pairs={{0,16},{16,32},{32,48},{48,64},{64,80},{80,96},{96,112},{112,128},... | collective-permute-start | bytes 786440 | tf_op jit(solution)/shard_map/ppermute | solution.py:309
  88.5 17.1 %collective-permute-start.9 = (f32[128,512]{1,0:T(8,128)S(1)}, f32[128,512]{1,0:T(8,128)}, u32[]{:S(2)}, u32[]{:S(2)}) collective-permute-start(f32[128,512]{1,0:T(8,128)S(1)} %add.10), channel_id=1, source_target_pairs={{0,8},{8,0},{1,9},{9,1},{2,10},{10,2},{3,11},{11,3},{4,12},{12,4},... | collective-permute-start | bytes 786440 | tf_op jit(solution)/shard_map/ppermute | solution.py:312
  100.5 45.7 %copy-start.2 = (f32[512]{0:T(512)S(1)}, f32[512]{0:T(512)}, u32[]{:S(2)}) copy-start(f32[512]{0:T(512)} %param.10) | copy-start | bytes 6148
  100.5 45.7 %copy-start.3 = (f32[512]{0:T(512)S(1)}, f32[512]{0:T(512)}, u32[]{:S(2)}) copy-start(f32[512]{0:T(512)} %param.11) | copy-start | bytes 6148
  100.5 8.0 %collective-permute-start.10 = (f32[128,512]{1,0:T(8,128)S(1)}, f32[128,512]{1,0:T(8,128)S(1)}, u32[]{:S(2)}, u32[]{:S(2)}) collective-permute-start(f32[128,512]{1,0:T(8,128)S(1)} %get-tuple-element.26), channel_id=1, source_target_pairs={{0,16},{16,32},{32,48},{48,64},{64,80},{80,96},{96,112},{112,128},... | collective-permute-start | bytes 786440 | tf_op jit(solution)/shard_map/ppermute | solution.py:311

commit v12 on v11

--- a/solution.py
+++ b/solution.py
@@ -121,8 +121,8 @@
     return first
 
 
-def conv_kernel(lengths, frames, *rest):
-    weights, (own, after, taps) = rest[:NY + 1], rest[NY + 1:]
+def conv_kernel(ahead, lengths, frames, *rest):
+    weights, (out, taps) = rest[:NY + 1], rest[NY + 1:]
     y = lax.axis_index("y")
     core = lax.axis_index("co")
     slab = my_slab()
@@ -147,8 +147,7 @@
                                      preferred_element_type=F32).astype(BF)
             for e in range(3):
                 taps[b, t * 64:(t + 1) * 64, e * 256:(e + 1) * 256] = picked[e * 64:(e + 1) * 64]
-    own[...] = jnp.zeros(own.shape, F32)
-    after[...] = jnp.zeros(after.shape, F32)
+    out[...] = jnp.zeros(out.shape, F32)
 
     def gates(a):
         parts = []
@@ -158,19 +157,15 @@
             parts.append(jnp.full((64, 768), jnp.where(allowed, 1.0, 0.0), F32).astype(BF))
         return jnp.concatenate(parts, axis=0)
 
+    first, second, both = slice(0, 64), slice(64, 128), slice(0, 128)
+    plan = [(0, both, both), (1, second, first)] if ahead else [(1, first, second), (2, both, both)]
+
     def row_tap(b, carry):
-        lhs = taps[b]
-        for a in range(3):
+        for a, meant, rows in plan:
             tap = (a * 3 + b) * 3
             kernel = jnp.concatenate([ref[tap + e] for e in range(3) for ref in weights], axis=0)
-            part = jnp.dot(lhs * gates(a), kernel, preferred_element_type=F32)
-            if a == 0:
-                after[...] += part
-            elif a == 1:
-                own[64:] += part[:64]
-                after[:64] += part[64:]
-            else:
-                own[...] += part
+            lhs = taps[b][meant] * gates(a)[meant]
+            out[rows] += jnp.dot(lhs, kernel, preferred_element_type=F32)
         return carry
 
     lax.fori_loop(0, 3, row_tap, 0)
@@ -259,12 +254,12 @@
     return moved, swapped
 
 
-def convolve(lengths, frames, weights):
+def convolve(ahead, lengths, frames, weights):
     return pl.pallas_call(
-        conv_kernel,
-        out_shape=[jax.ShapeDtypeStruct((128, COUT), F32)] * 2,
+        functools.partial(conv_kernel, ahead),
+        out_shape=jax.ShapeDtypeStruct((128, COUT), F32),
         in_specs=[SMEM] + [VMEM] * (2 + NY),
-        out_specs=[VMEM, VMEM],
+        out_specs=VMEM,
         scratch_shapes=[pltpu.VMEM((3, 128, 768), BF)],
         compiler_params=params(24),
     )(lengths, frames, *weights)
@@ -298,17 +293,17 @@
             pltpu.SMEM((8, 128), jnp.int32),
             pltpu.SemaphoreType.DMA((2,)),
         ],
-        compiler_params=params(8),
+        compiler_params=params(60),
     )(got)
     weights = [moved[0], moved[1], swapped[0], moved[2], swapped[1], moved[3], swapped[2]]
     weights += [moved[4], swapped[3]]
     onward = [(i, i + 1) for i in range(SLABS - 1)]
     far = shuffle(far.reshape(NY, 6, CH_DEV, 128), "y")
     near = shuffle(near.reshape(NY, 6, CH_DEV, 128), "y")
-    far, far_after = convolve(clip_lengths, far, weights)
-    far_before = lax.ppermute(far_after, TM, onward)
-    near, near_after = convolve(clip_lengths, near, weights)
-    near_before = lax.ppermute(near_after, TM, onward)
+    far_before = lax.ppermute(convolve(True, clip_lengths, far, weights), TM, onward)
+    far = convolve(False, clip_lengths, far, weights)
+    near_before = lax.ppermute(convolve(True, clip_lengths, near, weights), TM, onward)
+    near = convolve(False, clip_lengths, near, weights)
     far = lax.ppermute(far + far_before, "zh", [(0, 1), (1, 0)])
     near = near + far
     conv, stats = pl.pallas_call(

time: 149 us -> 151 us (1.013)
  Pallas kernels: 17 us -> 24.6 us
  waiting for transfers between devices: 31.2 us -> 26.3 us
    pallas_call x2 -> x4, Pallas kernels: 7.99 us -> 14.4 us  [convolve(): pl.pallas_call(functools.partial(conv_kernel, ahead), out_shape=jax.Shape...]
    ppermute x2, waiting for transfers between devices: 5.12 us -> 0.01 us  [the longest x1 0.01 us: body(): lax.ppermute(convolve(True, clip_lengths, far, weights), TM, onward)]
  transfers between devices with their start and end apart: 14 -> 14, of which waited for: 6 -> 3; matrix products, arithmetic and copies ran while one was open for 1% -> 1% of each run, Pallas kernels for 9% -> 14%
where the time goes in v12:
time: 151 us; the launch traced here: 150 us
  starting transfers between devices  63.1 us (42%)
  blocking collectives  34.2 us (23%)
  waiting for transfers between devices  26.3 us (17%)
  Pallas kernels  24.6 us (16%)
  other arithmetic  1.76 us (1%)
    all_to_all x2, blocking collectives, shuffle(): return lax.all_to_all(x, axis, split_axis=0, concat_axis=0, tiled=True)  34.2 us
    all_to_all x3, starting transfers between devices, shuffle(): return lax.all_to_all(x, axis, split_axis=0, concat_axis=0, tiled=True)  20.2 us
    pallas_call x4, Pallas kernels, convolve(): pl.pallas_call(functools.partial(conv_kernel, ahead), out_shape=jax.Shape...  14.4 us
    ppermute x3, starting transfers between devices, gathered_weights(): moved.append(lax.ppermute(moved[-1], ('co', 'y'), ring))  12.7 us
    ppermute x3, waiting for transfers between devices, gathered_weights(): moved.append(lax.ppermute(moved[-1], ('co', 'y'), ring))  11.2 us
    ppermute x4, starting transfers between devices, gathered_weights(): lax.ppermute(shard, 'co', swap)  9.99 us
    all_to_all x3, waiting for transfers between devices, shuffle(): return lax.all_to_all(x, axis, split_axis=0, concat_axis=0, tiled=True)  9.94 us
    ppermute x1, starting transfers between devices, body(): far = lax.ppermute(far + far_before, 'zh', [(0, 1), (1, 0)])  7.94 us
  transfers between devices with their start and end apart: 14, of which 3 were waited for; matrix products, arithmetic and copies ran while one was open for 1% of the time, Pallas kernels for 14%

profile of v12, /device:TPU:1, one launch (start us, length us, event | category | flops | bytes accessed | tf_op | source)
XLA Modules:
  0.0 150.3 jit_solution(7319644595779991288)
XLA Ops:
  0.0 5.9 %collective-permute-start = (bf16[27,32,512]{2,1,0:T(8,128)(2,1)}, bf16[27,32,512]{2,1,0:T(8,128)(2,1)S(1)}, u32[]{:S(2)}, u32[]{:S(2)}) collective-permute-start(bf16[27,32,512]{2,1,0:T(8,128)(2,1)} %bitcast.6), channel_id=1, source_target_pairs={{0,1},{1,2},{2,3},{3,4},{4,5},{5,6},{6,7},{7,0},{16,23},{17,16},{1... | collective-permute-start | bytes 2654216 | tf_op jit(solution)/shard_map/ppermute | solution.py:248
  5.9 3.1 %shard_map.64 = bf16[32,136,128]{2,1,0:T(8,128)(2,1)} custom-call(s32[64]{0:T(128)} %target.1, bf16[64,32,128]{2,1,0:T(8,128)(2,1)} %arrived.1), custom_call_target="tpu_custom_call" | custom-call | tf_op jit(solution)/shard_map/pallas_call | solution.py:270
  9.0 10.1 %all-to-all-start = ((bf16[32,136,128]{2,1,0:T(8,128)(2,1)}), bf16[32,136,128]{2,1,0:T(8,128)(2,1)}, u32[]{:S(2)}, u32[]{:S(2)}) async-start(bf16[32,136,128]{2,1,0:T(8,128)(2,1)} %shard_map.64), calls=%async_computation | async-start | bytes 2228224 | tf_op jit(solution)/shard_map/all_to_all | solution.py:239
  19.1 0.0 collective-permute-done.rest_1_
  19.1 3.0 %collective-permute-start.1 = (bf16[27,32,512]{2,1,0:T(8,128)(2,1)S(1)}, bf16[27,32,512]{2,1,0:T(8,128)(2,1)S(1)}, u32[]{:S(2)}, u32[]{:S(2)}) collective-permute-start(bf16[27,32,512]{2,1,0:T(8,128)(2,1)S(1)} %collective-permute-done.rest_1_), channel_id=1, source_target_pairs={{0,1},{1,2},{2,3},{3,4},{4,5},{5,6},{6,7},{7,0},{16,23},{17,16},{1... | collective-permute-start | bytes 2654216 | tf_op jit(solution)/shard_map/ppermute | solution.py:248
  22.1 11.2 %collective-permute-done.1.rest_3_ = bf16[27,32,512]{2,1,0:T(8,128)(2,1)S(1)} collective-permute-done((bf16[27,32,512]{2,1,0:T(8,128)(2,1)S(1)}, bf16[27,32,512]{2,1,0:T(8,128)(2,1)S(1)}, u32[]{:S(2)}, u32[]{:S(2)}) %collective-permute-start.1) | collective-permute-done | bytes 884768 | tf_op jit(solution)/shard_map/ppermute | solution.py:248
  33.3 3.8 %collective-permute-start.3 = (bf16[27,32,512]{2,1,0:T(8,128)(2,1)S(1)}, bf16[27,32,512]{2,1,0:T(8,128)(2,1)S(1)}, u32[]{:S(2)}, u32[]{:S(2)}) collective-permute-start(bf16[27,32,512]{2,1,0:T(8,128)(2,1)S(1)} %collective-permute-done.1.rest_3_), channel_id=1, source_target_pairs={{0,1},{1,2},{2,3},{3,4},{4,5},{5,6},{6,7},{7,0},{16,23},{17,16},{1... | collective-permute-start | bytes 2654216 | tf_op jit(solution)/shard_map/ppermute | solution.py:248
  37.1 9.9 %all-to-all-done.got = bf16[32,136,128]{2,1,0:T(8,128)(2,1)} async-done(((bf16[32,136,128]{2,1,0:T(8,128)(2,1)}), bf16[32,136,128]{2,1,0:T(8,128)(2,1)}, u32[]{:S(2)}, u32[]{:S(2)}) %all-to-all-start) | async-done | bytes 1114144 | tf_op jit(solution)/shard_map/all_to_all | solution.py:239
  47.0 3.3 %shard_map.65 = (bf16[48,32,128]{2,1,0:T(8,128)(2,1)}, bf16[48,32,128]{2,1,0:T(8,128)(2,1)}) custom-call(bf16[32,136,128]{2,1,0:T(8,128)(2,1)} %all-to-all-done.got), custom_call_target="tpu_custom_call" | custom-call | tf_op jit(solution)/shard_map/pallas_call | solution.py:285
  50.3 0.0 copy-start
  50.3 0.0 copy-start.1
  50.3 5.0 %all-to-all-start.2 = ((bf16[8,6,32,128]{3,2,1,0:T(8,128)(2,1)}), bf16[8,6,32,128]{3,2,1,0:T(8,128)(2,1)}, u32[]{:S(2)}, u32[]{:S(2)}) async-start(bf16[8,6,32,128]{3,2,1,0:T(8,128)(2,1)} %bitcast.14), calls=%async_computation.2 | async-start | bytes 786432 | tf_op jit(solution)/shard_map/all_to_all | solution.py:239
  55.3 2.2 %collective-permute-start.2 = (bf16[27,32,512]{2,1,0:T(8,128)(2,1)S(1)}, bf16[27,32,512]{2,1,0:T(8,128)(2,1)}, u32[]{:S(2)}, u32[]{:S(2)}) collective-permute-start(bf16[27,32,512]{2,1,0:T(8,128)(2,1)S(1)} %collective-permute-done.rest_1_), channel_id=1, source_target_pairs={{0,16},{16,0},{1,17},{17,1},{2,18},{18,2},{3,19},{19,3},{4,20},{20... | collective-permute-start | bytes 2654216 | tf_op jit(solution)/shard_map/ppermute | solution.py:253
  57.5 0.0 collective-permute-done.3.rest_5_
  57.6 2.1 %collective-permute-start.4 = (bf16[27,32,512]{2,1,0:T(8,128)(2,1)S(1)}, bf16[27,32,512]{2,1,0:T(8,128)(2,1)}, u32[]{:S(2)}, u32[]{:S(2)}) collective-permute-start(bf16[27,32,512]{2,1,0:T(8,128)(2,1)S(1)} %collective-permute-done.1.rest_3_), channel_id=1, source_target_pairs={{0,16},{16,0},{1,17},{17,1},{2,18},{18,2},{3,19},{19,3},{4,20},{20... | collective-permute-start | bytes 2654216 | tf_op jit(solution)/shard_map/ppermute | solution.py:253
  59.7 4.7 %collective-permute-start.6 = (bf16[27,16,512]{2,1,0:T(8,128)(2,1)S(1)}, bf16[27,16,512]{2,1,0:T(8,128)(2,1)}, u32[]{:S(2)}, u32[]{:S(2)}) collective-permute-start(bf16[27,16,512]{2,1,0:T(8,128)(2,1)S(1)} %constant_dynamic-slice_fusion), channel_id=1, source_target_pairs={{0,1},{1,2},{2,3},{3,4},{4,5},{5,6},{6,7},{7,0},{16,23},{17,16},{1... | collective-permute-start | bytes 1327112 | tf_op jit(solution)/shard_map/ppermute | solution.py:252
  64.4 1.9 %collective-permute-start.5 = (bf16[27,32,512]{2,1,0:T(8,128)(2,1)S(1)}, bf16[27,32,512]{2,1,0:T(8,128)(2,1)}, u32[]{:S(2)}, u32[]{:S(2)}) collective-permute-start(bf16[27,32,512]{2,1,0:T(8,128)(2,1)S(1)} %collective-permute-done.3.rest_5_), channel_id=1, source_target_pairs={{0,16},{16,0},{1,17},{17,1},{2,18},{18,2},{3,19},{19,3},{4,20},{20... | collective-permute-start | bytes 2654216 | tf_op jit(solution)/shard_map/ppermute | solution.py:253
  66.3 5.2 %collective-permute-done.6.rest_7_ = bf16[27,16,512]{2,1,0:T(8,128)(2,1)} collective-permute-done((bf16[27,16,512]{2,1,0:T(8,128)(2,1)S(1)}, bf16[27,16,512]{2,1,0:T(8,128)(2,1)}, u32[]{:S(2)}, u32[]{:S(2)}) %collective-permute-start.6) | collective-permute-done | bytes 442400 | tf_op jit(solution)/shard_map/ppermute | solution.py:252
  71.5 3.7 %collective-permute-start.7 = (bf16[27,16,512]{2,1,0:T(8,128)(2,1)}, bf16[27,16,512]{2,1,0:T(8,128)(2,1)}, u32[]{:S(2)}, u32[]{:S(2)}) collective-permute-start(bf16[27,16,512]{2,1,0:T(8,128)(2,1)} %collective-permute-done.6.rest_7_), channel_id=1, source_target_pairs={{0,16},{16,0},{1,17},{17,1},{2,18},{18,2},{3,19},{19,3},{4,20},{20... | collective-permute-start | bytes 1327112 | tf_op jit(solution)/shard_map/ppermute | solution.py:253
  75.2 0.0 all-to-all-done.2.frames
  75.3 5.1 %all-to-all-start.1 = ((bf16[8,6,32,128]{3,2,1,0:T(8,128)(2,1)}), bf16[8,6,32,128]{3,2,1,0:T(8,128)(2,1)}, u32[]{:S(2)}, u32[]{:S(2)}) async-start(bf16[8,6,32,128]{3,2,1,0:T(8,128)(2,1)} %bitcast.13), calls=%async_computation.1 | async-start | bytes 786432 | tf_op jit(solution)/shard_map/all_to_all | solution.py:239
  80.4 0.0 collective-permute-done.2.rest_2_
  80.4 0.0 collective-permute-done.4.rest_4_
  80.4 0.0 collective-permute-done.5.rest_6_
  80.4 0.0 collective-permute-done.7.rest_8_
  80.4 0.0 copy-done
  80.4 0.0 copy-done.1
  80.4 3.6 %shard_map.68 = f32[128,512]{1,0:T(8,128)S(1)} custom-call(s32[4]{0:T(128)S(1)} %copy-done.1, bf16[8,6,32,128]{3,2,1,0:T(8,128)(2,1)} %all-to-all-done.2.frames, bf16[27,32,512]{2,1,0:T(8,128)(2,1)S(1)} %bitcast.7, bf16[27,32,512]{2,1,0:T(8,128)(2,1)S(1)} %collective-permute-done.rest_1_, bf16[27,32,512]{2,1,0:T(8,128)(2,1)} %collective-permute-done.2.rest_2_, ...), custom_call_target="tpu_custom_call" | custom-call | tf_op jit(solution)/shard_map/pallas_call | solution.py:258
  84.0 3.3 %collective-permute-start.8 = (f32[128,512]{1,0:T(8,128)S(1)}, f32[128,512]{1,0:T(8,128)S(1)}, u32[]{:S(2)}, u32[]{:S(2)}) collective-permute-start(f32[128,512]{1,0:T(8,128)S(1)} %shard_map.68), channel_id=1, source_target_pairs={{0,16},{16,32},{32,48},{48,64},{64,80},{80,96},{96,112},{112,128},... | collective-permute-start | bytes 786440 | tf_op jit(solution)/shard_map/ppermute | solution.py:303
  87.3 3.6 %shard_map.67 = f32[128,512]{1,0:T(8,128)S(1)} custom-call(s32[4]{0:T(128)S(1)} %copy-done.1, bf16[8,6,32,128]{3,2,1,0:T(8,128)(2,1)} %all-to-all-done.2.frames, bf16[27,32,512]{2,1,0:T(8,128)(2,1)S(1)} %bitcast.8, bf16[27,32,512]{2,1,0:T(8,128)(2,1)S(1)} %collective-permute-done.rest_1_, bf16[27,32,512]{2,1,0:T(8,128)(2,1)} %collective-permute-done.2.rest_2_, ...), custom_call_target="tpu_custom_call" | custom-call | tf_op jit(solution)/shard_map/pallas_call | solution.py:258
  90.9 0.0 collective-permute-done.8
  90.9 0.8 add.10
  91.7 7.9 %collective-permute-start.9 = (f32[128,512]{1,0:T(8,128)}, f32[128,512]{1,0:T(8,128)}, u32[]{:S(2)}, u32[]{:S(2)}) collective-permute-start(f32[128,512]{1,0:T(8,128)} %add.10), channel_id=1, source_target_pairs={{0,8},{8,0},{1,9},{9,1},{2,10},{10,2},{3,11},{11,3},{4,12},{12,4},... | collective-permute-start | bytes 786440 | tf_op jit(solution)/shard_map/ppermute | solution.py:307
  99.6 0.0 all-to-all-done.1.frames
  99.6 3.6 %shard_map.69 = f32[128,512]{1,0:T(8,128)S(1)} custom-call(s32[4]{0:T(128)S(1)} %copy-done.1, bf16[8,6,32,128]{3,2,1,0:T(8,128)(2,1)} %all-to-all-done.1.frames, bf16[27,32,512]{2,1,0:T(8,128)(2,1)S(1)} %bitcast.9, bf16[27,32,512]{2,1,0:T(8,128)(2,1)S(1)} %collective-permute-done.rest_1_, bf16[27,32,512]{2,1,0:T(8,128)(2,1)} %collective-permute-done.2.rest_2_, ...), custom_call_target="tpu_custom_call" | custom-call | tf_op jit(solution)/shard_map/pallas_call | solution.py:258
  103.2 4.3 %collective-permute-start.10 = (f32[128,512]{1,0:T(8,128)S(1)}, f32[128,512]{1,0:T(8,128)S(1)}, u32[]{:S(2)}, u32[]{:S(2)}) collective-permute-start(f32[128,512]{1,0:T(8,128)S(1)} %shard_map.69), channel_id=1, source_target_pairs={{0,16},{16,32},{32,48},{48,64},{64,80},{80,96},{96,112},{112,128},... | collective-permute-start | bytes 786440 | tf_op jit(solution)/shard_map/ppermute | solution.py:305
  107.5 3.6 %shard_map.66 = f32[128,512]{1,0:T(8,128)S(1)} custom-call(s32[4]{0:T(128)S(1)} %copy-done.1, bf16[8,6,32,128]{3,2,1,0:T(8,128)(2,1)} %all-to-all-done.1.frames, bf16[27,32,512]{2,1,0:T(8,128)(2,1)S(1)} %bitcast.10, bf16[27,32,512]{2,1,0:T(8,128)(2,1)S(1)} %collective-permute-done.rest_1_, bf16[27,32,512]{2,1,0:T(8,128)(2,1)} %collective-permute-done.2.rest_2_, ...), custom_call_target="tpu_custom_call" | custom-call | tf_op jit(solution)/shard_map/pallas_call | solution.py:258
  111.2 0.0 copy-start.2
  111.2 0.0 copy-start.3
  111.2 0.0 collective-permute-done.9
  111.2 1.0 add.11.near
  112.2 0.0 collective-permute-done.10.before
  112.2 0.9 shard_map.70
  113.1 15.0 %all_to_all.25.got = f32[16,8,128]{2,1,0:T(8,128)} all-to-all(f32[16,8,128]{2,1,0:T(8,128)S(1)} %get-tuple-element.19), channel_id=1, replica_groups=mesh['zl'=4,'x'=4,'co'=2,'zh'=2,'y'=8] {'y','co'}, dimensions={0} | all-to-all | bytes 131072 | tf_op jit(solution)/shard_map/all_to_all | solution.py:239
  128.1 1.5 %shard_map.71 = f32[32,8,128]{2,1,0:T(8,128)} custom-call(f32[16,8,128]{2,1,0:T(8,128)} %all_to_all.25.got), custom_call_target="tpu_custom_call" | custom-call | tf_op jit(solution)/shard_map/pallas_call | solution.py:317
  129.6 19.2 %all_to_all.26.got = f32[32,8,128]{2,1,0:T(8,128)S(1)} all-to-all(f32[32,8,128]{2,1,0:T(8,128)} %shard_map.71), channel_id=1, replica_groups=mesh['zl'=4,'x'=4,'co'=2,'zh'=2,'y'=8] {'zl','zh','x'}, dimensions={0} | all-to-all | bytes 262144 | tf_op jit(solution)/shard_map/all_to_all | solution.py:239
  148.8 0.0 copy-done.2
  148.8 0.0 copy-done.3
  148.8 1.5 shard_map.72
  (1 shorter events, 0.0 us)
Async XLA Ops:
  0.0 19.1 %collective-permute-start = (bf16[27,32,512]{2,1,0:T(8,128)(2,1)}, bf16[27,32,512]{2,1,0:T(8,128)(2,1)S(1)}, u32[]{:S(2)}, u32[]{:S(2)}) collective-permute-start(bf16[27,32,512]{2,1,0:T(8,128)(2,1)} %bitcast.6), channel_id=1, source_target_pairs={{0,1},{1,2},{2,3},{3,4},{4,5},{5,6},{6,7},{7,0},{16,23},{17,16},{1... | collective-permute-start | bytes 2654216 | tf_op jit(solution)/shard_map/ppermute | solution.py:248
  9.0 38.0 %all-to-all-start = ((bf16[32,136,128]{2,1,0:T(8,128)(2,1)}), bf16[32,136,128]{2,1,0:T(8,128)(2,1)}, u32[]{:S(2)}, u32[]{:S(2)}) async-start(bf16[32,136,128]{2,1,0:T(8,128)(2,1)} %shard_map.64), calls=%async_computation | async-start | bytes 2228224 | tf_op jit(solution)/shard_map/all_to_all | solution.py:239
  19.1 14.2 %collective-permute-start.1 = (bf16[27,32,512]{2,1,0:T(8,128)(2,1)S(1)}, bf16[27,32,512]{2,1,0:T(8,128)(2,1)S(1)}, u32[]{:S(2)}, u32[]{:S(2)}) collective-permute-start(bf16[27,32,512]{2,1,0:T(8,128)(2,1)S(1)} %collective-permute-done.rest_1_), channel_id=1, source_target_pairs={{0,1},{1,2},{2,3},{3,4},{4,5},{5,6},{6,7},{7,0},{16,23},{17,16},{1... | collective-permute-start | bytes 2654216 | tf_op jit(solution)/shard_map/ppermute | solution.py:248
  33.3 24.3 %collective-permute-start.3 = (bf16[27,32,512]{2,1,0:T(8,128)(2,1)S(1)}, bf16[27,32,512]{2,1,0:T(8,128)(2,1)S(1)}, u32[]{:S(2)}, u32[]{:S(2)}) collective-permute-start(bf16[27,32,512]{2,1,0:T(8,128)(2,1)S(1)} %collective-permute-done.1.rest_3_), channel_id=1, source_target_pairs={{0,1},{1,2},{2,3},{3,4},{4,5},{5,6},{6,7},{7,0},{16,23},{17,16},{1... | collective-permute-start | bytes 2654216 | tf_op jit(solution)/shard_map/ppermute | solution.py:248
  50.3 30.2 %copy-start = (bf16[3,3,3,32,512]{4,3,2,1,0:T(8,128)(2,1)S(1)}, bf16[3,3,3,32,512]{4,3,2,1,0:T(8,128)(2,1)}, u32[]{:S(2)}) copy-start(bf16[3,3,3,32,512]{4,3,2,1,0:T(8,128)(2,1)} %param.9) | copy-start | bytes 2654212
  50.3 30.2 %copy-start.1 = (s32[4]{0:T(128)S(1)}, s32[4]{0:T(128)}, u32[]{:S(2)}) copy-start(s32[4]{0:T(128)} %lengths.11) | copy-start | bytes 52
  50.3 25.0 %all-to-all-start.2 = ((bf16[8,6,32,128]{3,2,1,0:T(8,128)(2,1)}), bf16[8,6,32,128]{3,2,1,0:T(8,128)(2,1)}, u32[]{:S(2)}, u32[]{:S(2)}) async-start(bf16[8,6,32,128]{3,2,1,0:T(8,128)(2,1)} %bitcast.14), calls=%async_computation.2 | async-start | bytes 786432 | tf_op jit(solution)/shard_map/all_to_all | solution.py:239
  55.3 25.1 %collective-permute-start.2 = (bf16[27,32,512]{2,1,0:T(8,128)(2,1)S(1)}, bf16[27,32,512]{2,1,0:T(8,128)(2,1)}, u32[]{:S(2)}, u32[]{:S(2)}) collective-permute-start(bf16[27,32,512]{2,1,0:T(8,128)(2,1)S(1)} %collective-permute-done.rest_1_), channel_id=1, source_target_pairs={{0,16},{16,0},{1,17},{17,1},{2,18},{18,2},{3,19},{19,3},{4,20},{20... | collective-permute-start | bytes 2654216 | tf_op jit(solution)/shard_map/ppermute | solution.py:253
  57.6 22.8 %collective-permute-start.4 = (bf16[27,32,512]{2,1,0:T(8,128)(2,1)S(1)}, bf16[27,32,512]{2,1,0:T(8,128)(2,1)}, u32[]{:S(2)}, u32[]{:S(2)}) collective-permute-start(bf16[27,32,512]{2,1,0:T(8,128)(2,1)S(1)} %collective-permute-done.1.rest_3_), channel_id=1, source_target_pairs={{0,16},{16,0},{1,17},{17,1},{2,18},{18,2},{3,19},{19,3},{4,20},{20... | collective-permute-start | bytes 2654216 | tf_op jit(solution)/shard_map/ppermute | solution.py:253
  59.7 11.8 %collective-permute-start.6 = (bf16[27,16,512]{2,1,0:T(8,128)(2,1)S(1)}, bf16[27,16,512]{2,1,0:T(8,128)(2,1)}, u32[]{:S(2)}, u32[]{:S(2)}) collective-permute-start(bf16[27,16,512]{2,1,0:T(8,128)(2,1)S(1)} %constant_dynamic-slice_fusion), channel_id=1, source_target_pairs={{0,1},{1,2},{2,3},{3,4},{4,5},{5,6},{6,7},{7,0},{16,23},{17,16},{1... | collective-permute-start | bytes 1327112 | tf_op jit(solution)/shard_map/ppermute | solution.py:252
  64.4 16.0 %collective-permute-start.5 = (bf16[27,32,512]{2,1,0:T(8,128)(2,1)S(1)}, bf16[27,32,512]{2,1,0:T(8,128)(2,1)}, u32[]{:S(2)}, u32[]{:S(2)}) collective-permute-start(bf16[27,32,512]{2,1,0:T(8,128)(2,1)S(1)} %collective-permute-done.3.rest_5_), channel_id=1, source_target_pairs={{0,16},{16,0},{1,17},{17,1},{2,18},{18,2},{3,19},{19,3},{4,20},{20... | collective-permute-start | bytes 2654216 | tf_op jit(solution)/shard_map/ppermute | solution.py:253
  71.5 8.9 %collective-permute-start.7 = (bf16[27,16,512]{2,1,0:T(8,128)(2,1)}, bf16[27,16,512]{2,1,0:T(8,128)(2,1)}, u32[]{:S(2)}, u32[]{:S(2)}) collective-permute-start(bf16[27,16,512]{2,1,0:T(8,128)(2,1)} %collective-permute-done.6.rest_7_), channel_id=1, source_target_pairs={{0,16},{16,0},{1,17},{17,1},{2,18},{18,2},{3,19},{19,3},{4,20},{20... | collective-permute-start | bytes 1327112 | tf_op jit(solution)/shard_map/ppermute | solution.py:253
  75.3 24.4 %all-to-all-start.1 = ((bf16[8,6,32,128]{3,2,1,0:T(8,128)(2,1)}), bf16[8,6,32,128]{3,2,1,0:T(8,128)(2,1)}, u32[]{:S(2)}, u32[]{:S(2)}) async-start(bf16[8,6,32,128]{3,2,1,0:T(8,128)(2,1)} %bitcast.13), calls=%async_computation.1 | async-start | bytes 786432 | tf_op jit(solution)/shard_map/all_to_all | solution.py:239
  84.0 6.9 %collective-permute-start.8 = (f32[128,512]{1,0:T(8,128)S(1)}, f32[128,512]{1,0:T(8,128)S(1)}, u32[]{:S(2)}, u32[]{:S(2)}) collective-permute-start(f32[128,512]{1,0:T(8,128)S(1)} %shard_map.68), channel_id=1, source_target_pairs={{0,16},{16,32},{32,48},{48,64},{64,80},{80,96},{96,112},{112,128},... | collective-permute-start | bytes 786440 | tf_op jit(solution)/shard_map/ppermute | solution.py:303
  91.7 19.5 %collective-permute-start.9 = (f32[128,512]{1,0:T(8,128)}, f32[128,512]{1,0:T(8,128)}, u32[]{:S(2)}, u32[]{:S(2)}) collective-permute-start(f32[128,512]{1,0:T(8,128)} %add.10), channel_id=1, source_target_pairs={{0,8},{8,0},{1,9},{9,1},{2,10},{10,2},{3,11},{11,3},{4,12},{12,4},... | collective-permute-start | bytes 786440 | tf_op jit(solution)/shard_map/ppermute | solution.py:307
  103.2 9.0 %collective-permute-start.10 = (f32[128,512]{1,0:T(8,128)S(1)}, f32[128,512]{1,0:T(8,128)S(1)}, u32[]{:S(2)}, u32[]{:S(2)}) collective-permute-start(f32[128,512]{1,0:T(8,128)S(1)} %shard_map.69), channel_id=1, source_target_pairs={{0,16},{16,32},{32,48},{48,64},{64,80},{80,96},{96,112},{112,128},... | collective-permute-start | bytes 786440 | tf_op jit(solution)/shard_map/ppermute | solution.py:305
  111.2 37.6 %copy-start.2 = (f32[512]{0:T(512)S(1)}, f32[512]{0:T(512)}, u32[]{:S(2)}) copy-start(f32[512]{0:T(512)} %param.10) | copy-start | bytes 6148
  111.2 37.6 %copy-start.3 = (f32[512]{0:T(512)S(1)}, f32[512]{0:T(512)}, u32[]{:S(2)}) copy-start(f32[512]{0:T(512)} %param.11) | copy-start | bytes 6148

commit v13 on v11

--- a/solution.py
+++ b/solution.py
@@ -193,9 +193,9 @@
     return flags
 
 
-def stat_kernel(lengths, near, before, conv_out, stats):
+def stat_kernel(lengths, near, far, token, before, conv_out, stats):
     slab = my_slab()
-    conv = near[...] + before[...]
+    conv = near[...] + before[...] + far[...]
     conv_out[...] = conv
     rows = []
     for f in range(2):
@@ -307,17 +307,18 @@
     near = shuffle(near.reshape(NY, 6, CH_DEV, 128), "y")
     far, far_after = convolve(clip_lengths, far, weights)
     far_before = lax.ppermute(far_after, TM, onward)
+    near, far_sum = lax.optimization_barrier((near, far + far_before))
     near, near_after = convolve(clip_lengths, near, weights)
     near_before = lax.ppermute(near_after, TM, onward)
-    far = lax.ppermute(far + far_before, "zh", [(0, 1), (1, 0)])
-    near = near + far
+    far = lax.ppermute(far_sum, "zh", [(0, 1), (1, 0)])
+    token = far[:8, :128]
     conv, stats = pl.pallas_call(
         stat_kernel,
         out_shape=[jax.ShapeDtypeStruct((128, COUT), F32), jax.ShapeDtypeStruct((16, 8, 128), F32)],
-        in_specs=[SMEM, VMEM, VMEM],
+        in_specs=[SMEM, VMEM, VMEM, VMEM, VMEM],
         out_specs=[VMEM, VMEM],
         compiler_params=params(16),
-    )(clip_lengths, near, near_before)
+    )(clip_lengths, near, far, token, near_before)
     stats = shuffle(stats, ("y", "co"))
     stats = pl.pallas_call(
         middle_kernel,

time: 149 us -> 150 us (level)
  waiting for transfers between devices: 31.2 us -> 37.2 us
  blocking collectives: 35.3 us -> 32.4 us
    all_to_all x3, waiting for transfers between devices: 9.78 us -> 14.4 us  [shuffle(): return lax.all_to_all(x, axis, split_axis=0, concat_axis=0, tiled=True)]
    all_to_all x2, blocking collectives: 35.3 us -> 32.4 us  [shuffle(): return lax.all_to_all(x, axis, split_axis=0, concat_axis=0, tiled=True)]
  transfers between devices with their start and end apart: 14 -> 14, of which waited for: 6 -> 6; matrix products, arithmetic and copies ran while one was open for 1% -> 0% of each run, Pallas kernels for 9% -> 9%
where the time goes in v13:
time: 150 us
  starting transfers between devices  62.5 us (42%)
  waiting for transfers between devices  37.2 us (25%)
  blocking collectives  32.4 us (22%)
  Pallas kernels  17 us (11%)
    all_to_all x2, blocking collectives, shuffle(): return lax.all_to_all(x, axis, split_axis=0, concat_axis=0, tiled=True)  32.4 us
    all_to_all x3, starting transfers between devices, shuffle(): return lax.all_to_all(x, axis, split_axis=0, concat_axis=0, tiled=True)  20.1 us
    all_to_all x3, waiting for transfers between devices, shuffle(): return lax.all_to_all(x, axis, split_axis=0, concat_axis=0, tiled=True)  14.4 us
    ppermute x3, starting transfers between devices, gathered_weights(): moved.append(lax.ppermute(moved[-1], ('co', 'y'), ring))  12.8 us
    ppermute x3, waiting for transfers between devices, gathered_weights(): moved.append(lax.ppermute(moved[-1], ('co', 'y'), ring))  11.2 us
    ppermute x4, starting transfers between devices, gathered_weights(): lax.ppermute(shard, 'co', swap)  9.99 us
    pallas_call x2, Pallas kernels, convolve(): pl.pallas_call(conv_kernel, out_shape=[jax.ShapeDtypeStruct((128, COUT),...  8 us
    ppermute x1, starting transfers between devices, body(): far = lax.ppermute(far_sum, 'zh', [(0, 1), (1, 0)])  7.93 us
  transfers between devices with their start and end apart: 14, of which 6 were waited for; matrix products, arithmetic and copies ran while one was open for 0% of the time, Pallas kernels for 9%

profile of v13, /device:TPU:1, one launch (start us, length us, event | category | flops | bytes accessed | tf_op | source)
XLA Modules:
  0.0 149.6 jit_solution(4324664346425242087)
XLA Ops:
  0.0 5.9 %collective-permute-start = (bf16[27,32,512]{2,1,0:T(8,128)(2,1)}, bf16[27,32,512]{2,1,0:T(8,128)(2,1)S(1)}, u32[]{:S(2)}, u32[]{:S(2)}) collective-permute-start(bf16[27,32,512]{2,1,0:T(8,128)(2,1)} %bitcast.6), channel_id=1, source_target_pairs={{0,1},{1,2},{2,3},{3,4},{4,5},{5,6},{6,7},{7,0},{16,23},{17,16},{1... | collective-permute-start | bytes 2654216 | tf_op jit(solution)/shard_map/ppermute | solution.py:253
  5.9 3.1 %shard_map.64 = bf16[32,136,128]{2,1,0:T(8,128)(2,1)} custom-call(s32[64]{0:T(128)} %target.1, bf16[64,32,128]{2,1,0:T(8,128)(2,1)} %arrived.1), custom_call_target="tpu_custom_call" | custom-call | tf_op jit(solution)/shard_map/pallas_call | solution.py:275
  9.0 10.0 %all-to-all-start = ((bf16[32,136,128]{2,1,0:T(8,128)(2,1)}), bf16[32,136,128]{2,1,0:T(8,128)(2,1)S(1)}, u32[]{:S(2)}, u32[]{:S(2)}) async-start(bf16[32,136,128]{2,1,0:T(8,128)(2,1)} %shard_map.64), calls=%async_computation | async-start | bytes 2228224 | tf_op jit(solution)/shard_map/all_to_all | solution.py:244
  19.0 0.0 collective-permute-done.rest_1_
  19.1 3.0 %collective-permute-start.1 = (bf16[27,32,512]{2,1,0:T(8,128)(2,1)S(1)}, bf16[27,32,512]{2,1,0:T(8,128)(2,1)}, u32[]{:S(2)}, u32[]{:S(2)}) collective-permute-start(bf16[27,32,512]{2,1,0:T(8,128)(2,1)S(1)} %collective-permute-done.rest_1_), channel_id=1, source_target_pairs={{0,1},{1,2},{2,3},{3,4},{4,5},{5,6},{6,7},{7,0},{16,23},{17,16},{1... | collective-permute-start | bytes 2654216 | tf_op jit(solution)/shard_map/ppermute | solution.py:253
  22.0 11.2 %collective-permute-done.1.rest_3_ = bf16[27,32,512]{2,1,0:T(8,128)(2,1)} collective-permute-done((bf16[27,32,512]{2,1,0:T(8,128)(2,1)S(1)}, bf16[27,32,512]{2,1,0:T(8,128)(2,1)}, u32[]{:S(2)}, u32[]{:S(2)}) %collective-permute-start.1) | collective-permute-done | bytes 884768 | tf_op jit(solution)/shard_map/ppermute | solution.py:253
  33.2 3.9 %collective-permute-start.3 = (bf16[27,32,512]{2,1,0:T(8,128)(2,1)}, bf16[27,32,512]{2,1,0:T(8,128)(2,1)S(1)}, u32[]{:S(2)}, u32[]{:S(2)}) collective-permute-start(bf16[27,32,512]{2,1,0:T(8,128)(2,1)} %collective-permute-done.1.rest_3_), channel_id=1, source_target_pairs={{0,1},{1,2},{2,3},{3,4},{4,5},{5,6},{6,7},{7,0},{16,23},{17,16},{1... | collective-permute-start | bytes 2654216 | tf_op jit(solution)/shard_map/ppermute | solution.py:253
  37.1 9.8 %all-to-all-done.got = bf16[32,136,128]{2,1,0:T(8,128)(2,1)S(1)} async-done(((bf16[32,136,128]{2,1,0:T(8,128)(2,1)}), bf16[32,136,128]{2,1,0:T(8,128)(2,1)S(1)}, u32[]{:S(2)}, u32[]{:S(2)}) %all-to-all-start) | async-done | bytes 1114144 | tf_op jit(solution)/shard_map/all_to_all | solution.py:244
  46.9 2.0 %shard_map.65 = (bf16[48,32,128]{2,1,0:T(8,128)(2,1)}, bf16[48,32,128]{2,1,0:T(8,128)(2,1)}) custom-call(bf16[32,136,128]{2,1,0:T(8,128)(2,1)S(1)} %all-to-all-done.got), custom_call_target="tpu_custom_call" | custom-call | tf_op jit(solution)/shard_map/pallas_call | solution.py:290
  48.9 0.0 copy-start
  48.9 0.0 copy-start.1
  48.9 5.0 %all-to-all-start.2 = ((bf16[8,6,32,128]{3,2,1,0:T(8,128)(2,1)}), bf16[8,6,32,128]{3,2,1,0:T(8,128)(2,1)}, u32[]{:S(2)}, u32[]{:S(2)}) async-start(bf16[8,6,32,128]{3,2,1,0:T(8,128)(2,1)} %bitcast.2), calls=%async_computation.2 | async-start | bytes 786432 | tf_op jit(solution)/shard_map/all_to_all | solution.py:244
  54.0 2.2 %collective-permute-start.2 = (bf16[27,32,512]{2,1,0:T(8,128)(2,1)S(1)}, bf16[27,32,512]{2,1,0:T(8,128)(2,1)}, u32[]{:S(2)}, u32[]{:S(2)}) collective-permute-start(bf16[27,32,512]{2,1,0:T(8,128)(2,1)S(1)} %collective-permute-done.rest_1_), channel_id=1, source_target_pairs={{0,16},{16,0},{1,17},{17,1},{2,18},{18,2},{3,19},{19,3},{4,20},{20... | collective-permute-start | bytes 2654216 | tf_op jit(solution)/shard_map/ppermute | solution.py:258
  56.2 0.0 collective-permute-done.3.rest_5_
  56.2 2.1 %collective-permute-start.4 = (bf16[27,32,512]{2,1,0:T(8,128)(2,1)}, bf16[27,32,512]{2,1,0:T(8,128)(2,1)}, u32[]{:S(2)}, u32[]{:S(2)}) collective-permute-start(bf16[27,32,512]{2,1,0:T(8,128)(2,1)} %collective-permute-done.1.rest_3_), channel_id=1, source_target_pairs={{0,16},{16,0},{1,17},{17,1},{2,18},{18,2},{3,19},{19,3},{4,20},{20... | collective-permute-start | bytes 2654216 | tf_op jit(solution)/shard_map/ppermute | solution.py:258
  58.3 4.7 %collective-permute-start.6 = (bf16[27,16,512]{2,1,0:T(8,128)(2,1)S(1)}, bf16[27,16,512]{2,1,0:T(8,128)(2,1)S(1)}, u32[]{:S(2)}, u32[]{:S(2)}) collective-permute-start(bf16[27,16,512]{2,1,0:T(8,128)(2,1)S(1)} %constant_dynamic-slice_fusion), channel_id=1, source_target_pairs={{0,1},{1,2},{2,3},{3,4},{4,5},{5,6},{6,7},{7,0},{16,23},{17,16},{1... | collective-permute-start | bytes 1327112 | tf_op jit(solution)/shard_map/ppermute | solution.py:257
  63.0 1.9 %collective-permute-start.5 = (bf16[27,32,512]{2,1,0:T(8,128)(2,1)S(1)}, bf16[27,32,512]{2,1,0:T(8,128)(2,1)}, u32[]{:S(2)}, u32[]{:S(2)}) collective-permute-start(bf16[27,32,512]{2,1,0:T(8,128)(2,1)S(1)} %collective-permute-done.3.rest_5_), channel_id=1, source_target_pairs={{0,16},{16,0},{1,17},{17,1},{2,18},{18,2},{3,19},{19,3},{4,20},{20... | collective-permute-start | bytes 2654216 | tf_op jit(solution)/shard_map/ppermute | solution.py:258
  65.0 5.1 %collective-permute-done.6.rest_7_ = bf16[27,16,512]{2,1,0:T(8,128)(2,1)S(1)} collective-permute-done((bf16[27,16,512]{2,1,0:T(8,128)(2,1)S(1)}, bf16[27,16,512]{2,1,0:T(8,128)(2,1)S(1)}, u32[]{:S(2)}, u32[]{:S(2)}) %collective-permute-start.6) | collective-permute-done | bytes 442400 | tf_op jit(solution)/shard_map/ppermute | solution.py:257
  70.0 3.7 %collective-permute-start.7 = (bf16[27,16,512]{2,1,0:T(8,128)(2,1)S(1)}, bf16[27,16,512]{2,1,0:T(8,128)(2,1)}, u32[]{:S(2)}, u32[]{:S(2)}) collective-permute-start(bf16[27,16,512]{2,1,0:T(8,128)(2,1)S(1)} %collective-permute-done.6.rest_7_), channel_id=1, source_target_pairs={{0,16},{16,0},{1,17},{17,1},{2,18},{18,2},{3,19},{19,3},{4,20},{20... | collective-permute-start | bytes 1327112 | tf_op jit(solution)/shard_map/ppermute | solution.py:258
  73.8 0.0 all-to-all-done.2.frames
  73.8 5.1 %all-to-all-start.1 = ((bf16[8,6,32,128]{3,2,1,0:T(8,128)(2,1)}), bf16[8,6,32,128]{3,2,1,0:T(8,128)(2,1)}, u32[]{:S(2)}, u32[]{:S(2)}) async-start(bf16[8,6,32,128]{3,2,1,0:T(8,128)(2,1)} %bitcast.1), calls=%async_computation.1 | async-start | bytes 786432 | tf_op jit(solution)/shard_map/all_to_all | solution.py:244
  78.9 0.0 collective-permute-done.2.rest_2_
  78.9 0.0 collective-permute-done.4.rest_4_
  78.9 0.0 collective-permute-done.5.rest_6_
  79.0 0.0 collective-permute-done.7.rest_8_
  79.0 0.0 copy-done
  79.0 0.0 copy-done.1
  79.0 4.0 %shard_map.66 = (f32[128,512]{1,0:T(8,128)S(1)}, f32[128,512]{1,0:T(8,128)S(1)}) custom-call(s32[4]{0:T(128)S(1)} %copy-done.1, bf16[8,6,32,128]{3,2,1,0:T(8,128)(2,1)} %all-to-all-done.2.frames, bf16[27,32,512]{2,1,0:T(8,128)(2,1)S(1)} %bitcast.7, bf16[27,32,512]{2,1,0:T(8,128)(2,1)S(1)} %collective-permute-done.rest_1_, ...), custom_call_target="tpu_custom_call" | custom-call | tf_op jit(solution)/shard_map/pallas_call | solution.py:263
  83.0 3.3 %collective-permute-start.8 = (f32[128,512]{1,0:T(8,128)S(1)}, f32[128,512]{1,0:T(8,128)S(1)}, u32[]{:S(2)}, u32[]{:S(2)}) collective-permute-start(f32[128,512]{1,0:T(8,128)S(1)} %get-tuple-element.26), channel_id=1, source_target_pairs={{0,16},{16,32},{32,48},{48,64},{64,80},{80,96},{96,112},{112,128},... | collective-permute-start | bytes 786440 | tf_op jit(solution)/shard_map/ppermute | solution.py:309
  86.3 3.3 %collective-permute-done.8 = f32[128,512]{1,0:T(8,128)S(1)} collective-permute-done((f32[128,512]{1,0:T(8,128)S(1)}, f32[128,512]{1,0:T(8,128)S(1)}, u32[]{:S(2)}, u32[]{:S(2)}) %collective-permute-start.8) | collective-permute-done | bytes 262176 | tf_op jit(solution)/shard_map/ppermute | solution.py:309
  89.6 4.6 %all-to-all-done.1.frames = bf16[8,6,32,128]{3,2,1,0:T(8,128)(2,1)} async-done(((bf16[8,6,32,128]{3,2,1,0:T(8,128)(2,1)}), bf16[8,6,32,128]{3,2,1,0:T(8,128)(2,1)}, u32[]{:S(2)}, u32[]{:S(2)}) %all-to-all-start.1) | async-done | bytes 393248 | tf_op jit(solution)/shard_map/all_to_all | solution.py:244
  94.2 7.9 %collective-permute-start.9 = (f32[128,512]{1,0:T(8,128)S(1)}, f32[128,512]{1,0:T(8,128)S(1)}, u32[]{:S(2)}, u32[]{:S(2)}) collective-permute-start(f32[128,512]{1,0:T(8,128)S(1)} %add.7), channel_id=1, source_target_pairs={{0,8},{8,0},{1,9},{9,1},{2,10},{10,2},{3,11},{11,3},{4,12},{12,4},... | collective-permute-start | bytes 786440 | tf_op jit(solution)/shard_map/ppermute | solution.py:313
  102.2 4.0 %shard_map.67 = (f32[128,512]{1,0:T(8,128)S(1)}, f32[128,512]{1,0:T(8,128)S(1)}) custom-call(s32[4]{0:T(128)S(1)} %copy-done.1, bf16[8,6,32,128]{3,2,1,0:T(8,128)(2,1)} %all-to-all-done.1.frames, bf16[27,32,512]{2,1,0:T(8,128)(2,1)S(1)} %bitcast.8, bf16[27,32,512]{2,1,0:T(8,128)(2,1)S(1)} %collective-permute-done.rest_1_, ...), custom_call_target="tpu_custom_call" | custom-call | tf_op jit(solution)/shard_map/pallas_call | solution.py:263
  106.2 0.0 copy-start.2
  106.2 0.0 copy-start.3
  106.2 3.7 %collective-permute-start.10 = (f32[128,512]{1,0:T(8,128)S(1)}, f32[128,512]{1,0:T(8,128)S(1)}, u32[]{:S(2)}, u32[]{:S(2)}) collective-permute-start(f32[128,512]{1,0:T(8,128)S(1)} %get-tuple-element.30), channel_id=1, source_target_pairs={{0,16},{16,32},{32,48},{48,64},{64,80},{80,96},{96,112},{112,128},... | collective-permute-start | bytes 786440 | tf_op jit(solution)/shard_map/ppermute | solution.py:312
  109.9 0.0 collective-permute-done.9.far
  109.9 3.3 %collective-permute-done.10.before = f32[128,512]{1,0:T(8,128)S(1)} collective-permute-done((f32[128,512]{1,0:T(8,128)S(1)}, f32[128,512]{1,0:T(8,128)S(1)}, u32[]{:S(2)}, u32[]{:S(2)}) %collective-permute-start.10) | collective-permute-done | bytes 262176 | tf_op jit(solution)/shard_map/ppermute | solution.py:312
  113.2 0.9 shard_map.68
  114.1 11.4 %all_to_all.25.got = f32[16,8,128]{2,1,0:T(8,128)} all-to-all(f32[16,8,128]{2,1,0:T(8,128)S(1)} %get-tuple-element.31), channel_id=1, replica_groups=mesh['zl'=4,'x'=4,'co'=2,'zh'=2,'y'=8] {'y','co'}, dimensions={0} | all-to-all | bytes 131072 | tf_op jit(solution)/shard_map/all_to_all | solution.py:244
  125.5 1.5 %shard_map.69 = f32[32,8,128]{2,1,0:T(8,128)} custom-call(f32[16,8,128]{2,1,0:T(8,128)} %all_to_all.25.got), custom_call_target="tpu_custom_call" | custom-call | tf_op jit(solution)/shard_map/pallas_call | solution.py:323
  127.0 21.1 %all_to_all.26.got = f32[32,8,128]{2,1,0:T(8,128)S(1)} all-to-all(f32[32,8,128]{2,1,0:T(8,128)} %shard_map.69), channel_id=1, replica_groups=mesh['zl'=4,'x'=4,'co'=2,'zh'=2,'y'=8] {'zl','zh','x'}, dimensions={0} | all-to-all | bytes 262144 | tf_op jit(solution)/shard_map/all_to_all | solution.py:244
  148.1 0.0 copy-done.2
  148.1 0.0 copy-done.3
  148.1 1.5 %shard_map.70 = bf16[2,64,512]{2,1,0:T(8,128)(2,1)} custom-call(s32[4]{0:T(128)S(1)} %copy-done.1, f32[32,8,128]{2,1,0:T(8,128)S(1)} %all_to_all.26.got, f32[128,512]{1,0:T(8,128)S(1)} %get-tuple-element.32.conv, f32[1,512]{1,0:T(1,128)S(1)} %bitcast.9, f32[1,512]{1,0:T(1,128)S(1)} %bitcast.10), custom_call_target="tpu_custom_call" | custom-call | tf_op jit(solution)/shard_map/pallas_call | solution.py:330
  (3 shorter events, 0.1 us)
Async XLA Ops:
  0.0 19.0 %collective-permute-start = (bf16[27,32,512]{2,1,0:T(8,128)(2,1)}, bf16[27,32,512]{2,1,0:T(8,128)(2,1)S(1)}, u32[]{:S(2)}, u32[]{:S(2)}) collective-permute-start(bf16[27,32,512]{2,1,0:T(8,128)(2,1)} %bitcast.6), channel_id=1, source_target_pairs={{0,1},{1,2},{2,3},{3,4},{4,5},{5,6},{6,7},{7,0},{16,23},{17,16},{1... | collective-permute-start | bytes 2654216 | tf_op jit(solution)/shard_map/ppermute | solution.py:253
  9.0 37.9 %all-to-all-start = ((bf16[32,136,128]{2,1,0:T(8,128)(2,1)}), bf16[32,136,128]{2,1,0:T(8,128)(2,1)S(1)}, u32[]{:S(2)}, u32[]{:S(2)}) async-start(bf16[32,136,128]{2,1,0:T(8,128)(2,1)} %shard_map.64), calls=%async_computation | async-start | bytes 2228224 | tf_op jit(solution)/shard_map/all_to_all | solution.py:244
  19.1 14.2 %collective-permute-start.1 = (bf16[27,32,512]{2,1,0:T(8,128)(2,1)S(1)}, bf16[27,32,512]{2,1,0:T(8,128)(2,1)}, u32[]{:S(2)}, u32[]{:S(2)}) collective-permute-start(bf16[27,32,512]{2,1,0:T(8,128)(2,1)S(1)} %collective-permute-done.rest_1_), channel_id=1, source_target_pairs={{0,1},{1,2},{2,3},{3,4},{4,5},{5,6},{6,7},{7,0},{16,23},{17,16},{1... | collective-permute-start | bytes 2654216 | tf_op jit(solution)/shard_map/ppermute | solution.py:253
  33.2 22.9 %collective-permute-start.3 = (bf16[27,32,512]{2,1,0:T(8,128)(2,1)}, bf16[27,32,512]{2,1,0:T(8,128)(2,1)S(1)}, u32[]{:S(2)}, u32[]{:S(2)}) collective-permute-start(bf16[27,32,512]{2,1,0:T(8,128)(2,1)} %collective-permute-done.1.rest_3_), channel_id=1, source_target_pairs={{0,1},{1,2},{2,3},{3,4},{4,5},{5,6},{6,7},{7,0},{16,23},{17,16},{1... | collective-permute-start | bytes 2654216 | tf_op jit(solution)/shard_map/ppermute | solution.py:253
  48.9 30.1 %copy-start = (bf16[3,3,3,32,512]{4,3,2,1,0:T(8,128)(2,1)S(1)}, bf16[3,3,3,32,512]{4,3,2,1,0:T(8,128)(2,1)}, u32[]{:S(2)}) copy-start(bf16[3,3,3,32,512]{4,3,2,1,0:T(8,128)(2,1)} %param.9) | copy-start | bytes 2654212
  48.9 30.0 %copy-start.1 = (s32[4]{0:T(128)S(1)}, s32[4]{0:T(128)}, u32[]{:S(2)}) copy-start(s32[4]{0:T(128)} %lengths.7) | copy-start | bytes 52
  48.9 24.9 %all-to-all-start.2 = ((bf16[8,6,32,128]{3,2,1,0:T(8,128)(2,1)}), bf16[8,6,32,128]{3,2,1,0:T(8,128)(2,1)}, u32[]{:S(2)}, u32[]{:S(2)}) async-start(bf16[8,6,32,128]{3,2,1,0:T(8,128)(2,1)} %bitcast.2), calls=%async_computation.2 | async-start | bytes 786432 | tf_op jit(solution)/shard_map/all_to_all | solution.py:244
  54.0 25.0 %collective-permute-start.2 = (bf16[27,32,512]{2,1,0:T(8,128)(2,1)S(1)}, bf16[27,32,512]{2,1,0:T(8,128)(2,1)}, u32[]{:S(2)}, u32[]{:S(2)}) collective-permute-start(bf16[27,32,512]{2,1,0:T(8,128)(2,1)S(1)} %collective-permute-done.rest_1_), channel_id=1, source_target_pairs={{0,16},{16,0},{1,17},{17,1},{2,18},{18,2},{3,19},{19,3},{4,20},{20... | collective-permute-start | bytes 2654216 | tf_op jit(solution)/shard_map/ppermute | solution.py:258
  56.2 22.7 %collective-permute-start.4 = (bf16[27,32,512]{2,1,0:T(8,128)(2,1)}, bf16[27,32,512]{2,1,0:T(8,128)(2,1)}, u32[]{:S(2)}, u32[]{:S(2)}) collective-permute-start(bf16[27,32,512]{2,1,0:T(8,128)(2,1)} %collective-permute-done.1.rest_3_), channel_id=1, source_target_pairs={{0,16},{16,0},{1,17},{17,1},{2,18},{18,2},{3,19},{19,3},{4,20},{20... | collective-permute-start | bytes 2654216 | tf_op jit(solution)/shard_map/ppermute | solution.py:258
  58.3 11.7 %collective-permute-start.6 = (bf16[27,16,512]{2,1,0:T(8,128)(2,1)S(1)}, bf16[27,16,512]{2,1,0:T(8,128)(2,1)S(1)}, u32[]{:S(2)}, u32[]{:S(2)}) collective-permute-start(bf16[27,16,512]{2,1,0:T(8,128)(2,1)S(1)} %constant_dynamic-slice_fusion), channel_id=1, source_target_pairs={{0,1},{1,2},{2,3},{3,4},{4,5},{5,6},{6,7},{7,0},{16,23},{17,16},{1... | collective-permute-start | bytes 1327112 | tf_op jit(solution)/shard_map/ppermute | solution.py:257
  63.0 15.9 %collective-permute-start.5 = (bf16[27,32,512]{2,1,0:T(8,128)(2,1)S(1)}, bf16[27,32,512]{2,1,0:T(8,128)(2,1)}, u32[]{:S(2)}, u32[]{:S(2)}) collective-permute-start(bf16[27,32,512]{2,1,0:T(8,128)(2,1)S(1)} %collective-permute-done.3.rest_5_), channel_id=1, source_target_pairs={{0,16},{16,0},{1,17},{17,1},{2,18},{18,2},{3,19},{19,3},{4,20},{20... | collective-permute-start | bytes 2654216 | tf_op jit(solution)/shard_map/ppermute | solution.py:258
  70.0 8.9 %collective-permute-start.7 = (bf16[27,16,512]{2,1,0:T(8,128)(2,1)S(1)}, bf16[27,16,512]{2,1,0:T(8,128)(2,1)}, u32[]{:S(2)}, u32[]{:S(2)}) collective-permute-start(bf16[27,16,512]{2,1,0:T(8,128)(2,1)S(1)} %collective-permute-done.6.rest_7_), channel_id=1, source_target_pairs={{0,16},{16,0},{1,17},{17,1},{2,18},{18,2},{3,19},{19,3},{4,20},{20... | collective-permute-start | bytes 1327112 | tf_op jit(solution)/shard_map/ppermute | solution.py:258
  73.8 20.4 %all-to-all-start.1 = ((bf16[8,6,32,128]{3,2,1,0:T(8,128)(2,1)}), bf16[8,6,32,128]{3,2,1,0:T(8,128)(2,1)}, u32[]{:S(2)}, u32[]{:S(2)}) async-start(bf16[8,6,32,128]{3,2,1,0:T(8,128)(2,1)} %bitcast.1), calls=%async_computation.1 | async-start | bytes 786432 | tf_op jit(solution)/shard_map/all_to_all | solution.py:244
  83.0 6.6 %collective-permute-start.8 = (f32[128,512]{1,0:T(8,128)S(1)}, f32[128,512]{1,0:T(8,128)S(1)}, u32[]{:S(2)}, u32[]{:S(2)}) collective-permute-start(f32[128,512]{1,0:T(8,128)S(1)} %get-tuple-element.26), channel_id=1, source_target_pairs={{0,16},{16,32},{32,48},{48,64},{64,80},{80,96},{96,112},{112,128},... | collective-permute-start | bytes 786440 | tf_op jit(solution)/shard_map/ppermute | solution.py:309
  94.2 15.7 %collective-permute-start.9 = (f32[128,512]{1,0:T(8,128)S(1)}, f32[128,512]{1,0:T(8,128)S(1)}, u32[]{:S(2)}, u32[]{:S(2)}) collective-permute-start(f32[128,512]{1,0:T(8,128)S(1)} %add.7), channel_id=1, source_target_pairs={{0,8},{8,0},{1,9},{9,1},{2,10},{10,2},{3,11},{11,3},{4,12},{12,4},... | collective-permute-start | bytes 786440 | tf_op jit(solution)/shard_map/ppermute | solution.py:313
  106.2 41.9 %copy-start.2 = (f32[512]{0:T(512)S(1)}, f32[512]{0:T(512)}, u32[]{:S(2)}) copy-start(f32[512]{0:T(512)} %param.10) | copy-start | bytes 6148
  106.2 41.9 %copy-start.3 = (f32[512]{0:T(512)S(1)}, f32[512]{0:T(512)}, u32[]{:S(2)}) copy-start(f32[512]{0:T(512)} %param.11) | copy-start | bytes 6148
  106.2 7.0 %collective-permute-start.10 = (f32[128,512]{1,0:T(8,128)S(1)}, f32[128,512]{1,0:T(8,128)S(1)}, u32[]{:S(2)}, u32[]{:S(2)}) collective-permute-start(f32[128,512]{1,0:T(8,128)S(1)} %get-tuple-element.30), channel_id=1, source_target_pairs={{0,16},{16,32},{32,48},{48,64},{64,80},{80,96},{96,112},{112,128},... | collective-permute-start | bytes 786440 | tf_op jit(solution)/shard_map/ppermute | solution.py:312

commit v14 on v11

--- a/solution.py
+++ b/solution.py
@@ -313,19 +313,19 @@
     near = near + far
     conv, stats = pl.pallas_call(
         stat_kernel,
-        out_shape=[jax.ShapeDtypeStruct((128, COUT), F32), jax.ShapeDtypeStruct((16, 8, 128), F32)],
+        out_shape=[jax.ShapeDtypeStruct((128, COUT), F32), jax.ShapeDtypeStruct((32, 8, 128), F32)],
         in_specs=[SMEM, VMEM, VMEM],
         out_specs=[VMEM, VMEM],
         compiler_params=params(16),
     )(clip_lengths, near, near_before)
-    stats = shuffle(stats, ("y", "co"))
+    stats = shuffle(stats, ("zl", "zh", "x"))
     stats = pl.pallas_call(
         middle_kernel,
-        out_shape=jax.ShapeDtypeStruct((SLABS, 8, 128), F32),
+        out_shape=jax.ShapeDtypeStruct((16, 8, 128), F32),
         in_specs=[VMEM],
         out_specs=VMEM,
     )(stats)
-    stats = shuffle(stats, ("zl", "zh", "x"))
+    stats = shuffle(stats, ("y", "co"))
     out = pl.pallas_call(
         final_kernel,
         out_shape=jax.ShapeDtypeStruct((2, 64, COUT), BF),

time: 149 us -> 150 us (level)
  no operation moved by 1% of the time
where the time goes in v14:
time: 150 us; the launch traced here: 149 us
  starting transfers between devices  62.9 us (42%)
  blocking collectives  36.6 us (24%)
  waiting for transfers between devices  31.2 us (21%)
  Pallas kernels  17.1 us (11%)
    all_to_all x2, blocking collectives, shuffle(): return lax.all_to_all(x, axis, split_axis=0, concat_axis=0, tiled=True)  36.6 us
    all_to_all x3, starting transfers between devices, shuffle(): return lax.all_to_all(x, axis, split_axis=0, concat_axis=0, tiled=True)  19.3 us
    ppermute x3, starting transfers between devices, gathered_weights(): moved.append(lax.ppermute(moved[-1], ('co', 'y'), ring))  12.8 us
    ppermute x3, waiting for transfers between devices, gathered_weights(): moved.append(lax.ppermute(moved[-1], ('co', 'y'), ring))  11.2 us
    ppermute x4, starting transfers between devices, gathered_weights(): lax.ppermute(shard, 'co', swap)  10.1 us
    all_to_all x3, waiting for transfers between devices, shuffle(): return lax.all_to_all(x, axis, split_axis=0, concat_axis=0, tiled=True)  9.78 us
    pallas_call x2, Pallas kernels, convolve(): pl.pallas_call(conv_kernel, out_shape=[jax.ShapeDtypeStruct((128, COUT),...  8 us
    ppermute x1, starting transfers between devices, body(): far = lax.ppermute(far + far_before, 'zh', [(0, 1), (1, 0)])  7.94 us
  transfers between devices with their start and end apart: 14, of which 6 were waited for; matrix products, arithmetic and copies ran while one was open for 1% of the time, Pallas kernels for 9%

profile of v14, /device:TPU:1, one launch (start us, length us, event | category | flops | bytes accessed | tf_op | source)
XLA Modules:
  0.0 149.0 jit_solution(1244737927221599621)
XLA Ops:
  0.0 5.9 %collective-permute-start = (bf16[27,32,512]{2,1,0:T(8,128)(2,1)}, bf16[27,32,512]{2,1,0:T(8,128)(2,1)S(1)}, u32[]{:S(2)}, u32[]{:S(2)}) collective-permute-start(bf16[27,32,512]{2,1,0:T(8,128)(2,1)} %bitcast.6), channel_id=1, source_target_pairs={{0,1},{1,2},{2,3},{3,4},{4,5},{5,6},{6,7},{7,0},{16,23},{17,16},{1... | collective-permute-start | bytes 2654216 | tf_op jit(solution)/shard_map/ppermute | solution.py:253
  5.9 3.1 %shard_map.64 = bf16[32,136,128]{2,1,0:T(8,128)(2,1)} custom-call(s32[64]{0:T(128)} %target.1, bf16[64,32,128]{2,1,0:T(8,128)(2,1)} %arrived.1), custom_call_target="tpu_custom_call" | custom-call | tf_op jit(solution)/shard_map/pallas_call | solution.py:275
  9.0 10.0 %all-to-all-start = ((bf16[32,136,128]{2,1,0:T(8,128)(2,1)}), bf16[32,136,128]{2,1,0:T(8,128)(2,1)S(1)}, u32[]{:S(2)}, u32[]{:S(2)}) async-start(bf16[32,136,128]{2,1,0:T(8,128)(2,1)} %shard_map.64), calls=%async_computation | async-start | bytes 2228224 | tf_op jit(solution)/shard_map/all_to_all | solution.py:244
  19.0 0.0 collective-permute-done.rest_1_
  19.1 3.0 %collective-permute-start.1 = (bf16[27,32,512]{2,1,0:T(8,128)(2,1)S(1)}, bf16[27,32,512]{2,1,0:T(8,128)(2,1)}, u32[]{:S(2)}, u32[]{:S(2)}) collective-permute-start(bf16[27,32,512]{2,1,0:T(8,128)(2,1)S(1)} %collective-permute-done.rest_1_), channel_id=1, source_target_pairs={{0,1},{1,2},{2,3},{3,4},{4,5},{5,6},{6,7},{7,0},{16,23},{17,16},{1... | collective-permute-start | bytes 2654216 | tf_op jit(solution)/shard_map/ppermute | solution.py:253
  22.0 11.2 %collective-permute-done.1.rest_3_ = bf16[27,32,512]{2,1,0:T(8,128)(2,1)} collective-permute-done((bf16[27,32,512]{2,1,0:T(8,128)(2,1)S(1)}, bf16[27,32,512]{2,1,0:T(8,128)(2,1)}, u32[]{:S(2)}, u32[]{:S(2)}) %collective-permute-start.1) | collective-permute-done | bytes 884768 | tf_op jit(solution)/shard_map/ppermute | solution.py:253
  33.2 3.9 %collective-permute-start.3 = (bf16[27,32,512]{2,1,0:T(8,128)(2,1)}, bf16[27,32,512]{2,1,0:T(8,128)(2,1)S(1)}, u32[]{:S(2)}, u32[]{:S(2)}) collective-permute-start(bf16[27,32,512]{2,1,0:T(8,128)(2,1)} %collective-permute-done.1.rest_3_), channel_id=1, source_target_pairs={{0,1},{1,2},{2,3},{3,4},{4,5},{5,6},{6,7},{7,0},{16,23},{17,16},{1... | collective-permute-start | bytes 2654216 | tf_op jit(solution)/shard_map/ppermute | solution.py:253
  37.1 9.8 %all-to-all-done.got = bf16[32,136,128]{2,1,0:T(8,128)(2,1)S(1)} async-done(((bf16[32,136,128]{2,1,0:T(8,128)(2,1)}), bf16[32,136,128]{2,1,0:T(8,128)(2,1)S(1)}, u32[]{:S(2)}, u32[]{:S(2)}) %all-to-all-start) | async-done | bytes 1114144 | tf_op jit(solution)/shard_map/all_to_all | solution.py:244
  46.9 2.0 %shard_map.65 = (bf16[48,32,128]{2,1,0:T(8,128)(2,1)}, bf16[48,32,128]{2,1,0:T(8,128)(2,1)}) custom-call(bf16[32,136,128]{2,1,0:T(8,128)(2,1)S(1)} %all-to-all-done.got), custom_call_target="tpu_custom_call" | custom-call | tf_op jit(solution)/shard_map/pallas_call | solution.py:290
  48.9 0.0 copy-start
  48.9 0.0 copy-start.1
  48.9 5.0 %all-to-all-start.2 = ((bf16[8,6,32,128]{3,2,1,0:T(8,128)(2,1)}), bf16[8,6,32,128]{3,2,1,0:T(8,128)(2,1)}, u32[]{:S(2)}, u32[]{:S(2)}) async-start(bf16[8,6,32,128]{3,2,1,0:T(8,128)(2,1)} %bitcast.2), calls=%async_computation.2 | async-start | bytes 786432 | tf_op jit(solution)/shard_map/all_to_all | solution.py:244
  54.0 2.2 %collective-permute-start.2 = (bf16[27,32,512]{2,1,0:T(8,128)(2,1)S(1)}, bf16[27,32,512]{2,1,0:T(8,128)(2,1)}, u32[]{:S(2)}, u32[]{:S(2)}) collective-permute-start(bf16[27,32,512]{2,1,0:T(8,128)(2,1)S(1)} %collective-permute-done.rest_1_), channel_id=1, source_target_pairs={{0,16},{16,0},{1,17},{17,1},{2,18},{18,2},{3,19},{19,3},{4,20},{20... | collective-permute-start | bytes 2654216 | tf_op jit(solution)/shard_map/ppermute | solution.py:258
  56.2 0.0 collective-permute-done.3.rest_5_
  56.2 4.9 %collective-permute-start.6 = (bf16[27,16,512]{2,1,0:T(8,128)(2,1)S(1)}, bf16[27,16,512]{2,1,0:T(8,128)(2,1)S(1)}, u32[]{:S(2)}, u32[]{:S(2)}) collective-permute-start(bf16[27,16,512]{2,1,0:T(8,128)(2,1)S(1)} %constant_dynamic-slice_fusion), channel_id=1, source_target_pairs={{0,1},{1,2},{2,3},{3,4},{4,5},{5,6},{6,7},{7,0},{16,23},{17,16},{1... | collective-permute-start | bytes 1327112 | tf_op jit(solution)/shard_map/ppermute | solution.py:257
  61.1 1.9 %collective-permute-start.4 = (bf16[27,32,512]{2,1,0:T(8,128)(2,1)}, bf16[27,32,512]{2,1,0:T(8,128)(2,1)}, u32[]{:S(2)}, u32[]{:S(2)}) collective-permute-start(bf16[27,32,512]{2,1,0:T(8,128)(2,1)} %collective-permute-done.1.rest_3_), channel_id=1, source_target_pairs={{0,16},{16,0},{1,17},{17,1},{2,18},{18,2},{3,19},{19,3},{4,20},{20... | collective-permute-start | bytes 2654216 | tf_op jit(solution)/shard_map/ppermute | solution.py:258
  63.0 2.4 %collective-permute-start.5 = (bf16[27,32,512]{2,1,0:T(8,128)(2,1)S(1)}, bf16[27,32,512]{2,1,0:T(8,128)(2,1)}, u32[]{:S(2)}, u32[]{:S(2)}) collective-permute-start(bf16[27,32,512]{2,1,0:T(8,128)(2,1)S(1)} %collective-permute-done.3.rest_5_), channel_id=1, source_target_pairs={{0,16},{16,0},{1,17},{17,1},{2,18},{18,2},{3,19},{19,3},{4,20},{20... | collective-permute-start | bytes 2654216 | tf_op jit(solution)/shard_map/ppermute | solution.py:258
  65.5 4.6 %collective-permute-done.6.rest_7_ = bf16[27,16,512]{2,1,0:T(8,128)(2,1)S(1)} collective-permute-done((bf16[27,16,512]{2,1,0:T(8,128)(2,1)S(1)}, bf16[27,16,512]{2,1,0:T(8,128)(2,1)S(1)}, u32[]{:S(2)}, u32[]{:S(2)}) %collective-permute-start.6) | collective-permute-done | bytes 442400 | tf_op jit(solution)/shard_map/ppermute | solution.py:257
  70.0 3.5 %collective-permute-start.7 = (bf16[27,16,512]{2,1,0:T(8,128)(2,1)S(1)}, bf16[27,16,512]{2,1,0:T(8,128)(2,1)}, u32[]{:S(2)}, u32[]{:S(2)}) collective-permute-start(bf16[27,16,512]{2,1,0:T(8,128)(2,1)S(1)} %collective-permute-done.6.rest_7_), channel_id=1, source_target_pairs={{0,16},{16,0},{1,17},{17,1},{2,18},{18,2},{3,19},{19,3},{4,20},{20... | collective-permute-start | bytes 1327112 | tf_op jit(solution)/shard_map/ppermute | solution.py:258
  73.5 0.0 all-to-all-done.2.frames
  73.6 4.3 %all-to-all-start.1 = ((bf16[8,6,32,128]{3,2,1,0:T(8,128)(2,1)}), bf16[8,6,32,128]{3,2,1,0:T(8,128)(2,1)}, u32[]{:S(2)}, u32[]{:S(2)}) async-start(bf16[8,6,32,128]{3,2,1,0:T(8,128)(2,1)} %bitcast.1), calls=%async_computation.1 | async-start | bytes 786432 | tf_op jit(solution)/shard_map/all_to_all | solution.py:244
  77.8 0.0 collective-permute-done.2.rest_2_
  77.8 0.0 collective-permute-done.7.rest_8_
  77.8 0.0 collective-permute-done.4.rest_4_
  77.9 0.0 collective-permute-done.5.rest_6_
  77.9 0.0 copy-done
  77.9 0.0 copy-done.1
  77.9 4.0 %shard_map.67 = (f32[128,512]{1,0:T(8,128)S(1)}, f32[128,512]{1,0:T(8,128)S(1)}) custom-call(s32[4]{0:T(128)S(1)} %copy-done.1, bf16[8,6,32,128]{3,2,1,0:T(8,128)(2,1)} %all-to-all-done.2.frames, bf16[27,32,512]{2,1,0:T(8,128)(2,1)S(1)} %bitcast.7, bf16[27,32,512]{2,1,0:T(8,128)(2,1)S(1)} %collective-permute-done.rest_1_, ...), custom_call_target="tpu_custom_call" | custom-call | tf_op jit(solution)/shard_map/pallas_call | solution.py:263
  81.9 3.3 %collective-permute-start.8 = (f32[128,512]{1,0:T(8,128)S(1)}, f32[128,512]{1,0:T(8,128)S(1)}, u32[]{:S(2)}, u32[]{:S(2)}) collective-permute-start(f32[128,512]{1,0:T(8,128)S(1)} %get-tuple-element.25), channel_id=1, source_target_pairs={{0,16},{16,32},{32,48},{48,64},{64,80},{80,96},{96,112},{112,128},... | collective-permute-start | bytes 786440 | tf_op jit(solution)/shard_map/ppermute | solution.py:309
  85.2 3.3 %collective-permute-done.8 = f32[128,512]{1,0:T(8,128)S(1)} collective-permute-done((f32[128,512]{1,0:T(8,128)S(1)}, f32[128,512]{1,0:T(8,128)S(1)}, u32[]{:S(2)}, u32[]{:S(2)}) %collective-permute-start.8) | collective-permute-done | bytes 262176 | tf_op jit(solution)/shard_map/ppermute | solution.py:309
  88.5 7.9 %collective-permute-start.9 = (f32[128,512]{1,0:T(8,128)S(1)}, f32[128,512]{1,0:T(8,128)}, u32[]{:S(2)}, u32[]{:S(2)}) collective-permute-start(f32[128,512]{1,0:T(8,128)S(1)} %add.10), channel_id=1, source_target_pairs={{0,8},{8,0},{1,9},{9,1},{2,10},{10,2},{3,11},{11,3},{4,12},{12,4},... | collective-permute-start | bytes 786440 | tf_op jit(solution)/shard_map/ppermute | solution.py:312
  96.5 0.0 all-to-all-done.1.frames
  96.5 4.0 %shard_map.66 = (f32[128,512]{1,0:T(8,128)S(1)}, f32[128,512]{1,0:T(8,128)S(1)}) custom-call(s32[4]{0:T(128)S(1)} %copy-done.1, bf16[8,6,32,128]{3,2,1,0:T(8,128)(2,1)} %all-to-all-done.1.frames, bf16[27,32,512]{2,1,0:T(8,128)(2,1)S(1)} %bitcast.8, bf16[27,32,512]{2,1,0:T(8,128)(2,1)S(1)} %collective-permute-done.rest_1_, ...), custom_call_target="tpu_custom_call" | custom-call | tf_op jit(solution)/shard_map/pallas_call | solution.py:263
  100.5 0.0 copy-start.2
  100.5 0.0 copy-start.3
  100.5 4.7 %collective-permute-start.10 = (f32[128,512]{1,0:T(8,128)S(1)}, f32[128,512]{1,0:T(8,128)S(1)}, u32[]{:S(2)}, u32[]{:S(2)}) collective-permute-start(f32[128,512]{1,0:T(8,128)S(1)} %get-tuple-element.26), channel_id=1, source_target_pairs={{0,16},{16,32},{32,48},{48,64},{64,80},{80,96},{96,112},{112,128},... | collective-permute-start | bytes 786440 | tf_op jit(solution)/shard_map/ppermute | solution.py:311
  105.2 0.5 collective-permute-done.9
  105.6 1.0 add.11.near
  106.6 1.8 %collective-permute-done.10.before = f32[128,512]{1,0:T(8,128)S(1)} collective-permute-done((f32[128,512]{1,0:T(8,128)S(1)}, f32[128,512]{1,0:T(8,128)S(1)}, u32[]{:S(2)}, u32[]{:S(2)}) %collective-permute-start.10) | collective-permute-done | bytes 262176 | tf_op jit(solution)/shard_map/ppermute | solution.py:311
  108.5 0.9 shard_map.68
  109.4 18.8 %all_to_all.25.got = f32[32,8,128]{2,1,0:T(8,128)} all-to-all(f32[32,8,128]{2,1,0:T(8,128)S(1)} %get-tuple-element.27), channel_id=1, replica_groups=mesh['zl'=4,'x'=4,'co'=2,'zh'=2,'y'=8] {'zl','zh','x'}, dimensions={0} | all-to-all | bytes 262144 | tf_op jit(solution)/shard_map/all_to_all | solution.py:244
  128.1 1.6 %shard_map.69 = f32[16,8,128]{2,1,0:T(8,128)} custom-call(f32[32,8,128]{2,1,0:T(8,128)} %all_to_all.25.got), custom_call_target="tpu_custom_call" | custom-call | tf_op jit(solution)/shard_map/pallas_call | solution.py:322
  129.7 17.8 %all_to_all.26.got = f32[16,8,128]{2,1,0:T(8,128)S(1)} all-to-all(f32[16,8,128]{2,1,0:T(8,128)} %shard_map.69), channel_id=1, replica_groups=mesh['zl'=4,'x'=4,'co'=2,'zh'=2,'y'=8] {'y','co'}, dimensions={0} | all-to-all | bytes 131072 | tf_op jit(solution)/shard_map/all_to_all | solution.py:244
  147.5 0.0 copy-done.2
  147.5 0.0 copy-done.3
  147.5 1.5 %shard_map.70 = bf16[2,64,512]{2,1,0:T(8,128)(2,1)} custom-call(s32[4]{0:T(128)S(1)} %copy-done.1, f32[16,8,128]{2,1,0:T(8,128)S(1)} %all_to_all.26.got, f32[128,512]{1,0:T(8,128)S(1)} %get-tuple-element.28.conv, f32[1,512]{1,0:T(1,128)S(1)} %bitcast.9, f32[1,512]{1,0:T(1,128)S(1)} %bitcast.10), custom_call_target="tpu_custom_call" | custom-call | tf_op jit(solution)/shard_map/pallas_call | solution.py:329
  (2 shorter events, 0.1 us)
Async XLA Ops:
  0.0 19.0 %collective-permute-start = (bf16[27,32,512]{2,1,0:T(8,128)(2,1)}, bf16[27,32,512]{2,1,0:T(8,128)(2,1)S(1)}, u32[]{:S(2)}, u32[]{:S(2)}) collective-permute-start(bf16[27,32,512]{2,1,0:T(8,128)(2,1)} %bitcast.6), channel_id=1, source_target_pairs={{0,1},{1,2},{2,3},{3,4},{4,5},{5,6},{6,7},{7,0},{16,23},{17,16},{1... | collective-permute-start | bytes 2654216 | tf_op jit(solution)/shard_map/ppermute | solution.py:253
  9.0 37.9 %all-to-all-start = ((bf16[32,136,128]{2,1,0:T(8,128)(2,1)}), bf16[32,136,128]{2,1,0:T(8,128)(2,1)S(1)}, u32[]{:S(2)}, u32[]{:S(2)}) async-start(bf16[32,136,128]{2,1,0:T(8,128)(2,1)} %shard_map.64), calls=%async_computation | async-start | bytes 2228224 | tf_op jit(solution)/shard_map/all_to_all | solution.py:244
  19.1 14.2 %collective-permute-start.1 = (bf16[27,32,512]{2,1,0:T(8,128)(2,1)S(1)}, bf16[27,32,512]{2,1,0:T(8,128)(2,1)}, u32[]{:S(2)}, u32[]{:S(2)}) collective-permute-start(bf16[27,32,512]{2,1,0:T(8,128)(2,1)S(1)} %collective-permute-done.rest_1_), channel_id=1, source_target_pairs={{0,1},{1,2},{2,3},{3,4},{4,5},{5,6},{6,7},{7,0},{16,23},{17,16},{1... | collective-permute-start | bytes 2654216 | tf_op jit(solution)/shard_map/ppermute | solution.py:253
  33.2 22.9 %collective-permute-start.3 = (bf16[27,32,512]{2,1,0:T(8,128)(2,1)}, bf16[27,32,512]{2,1,0:T(8,128)(2,1)S(1)}, u32[]{:S(2)}, u32[]{:S(2)}) collective-permute-start(bf16[27,32,512]{2,1,0:T(8,128)(2,1)} %collective-permute-done.1.rest_3_), channel_id=1, source_target_pairs={{0,1},{1,2},{2,3},{3,4},{4,5},{5,6},{6,7},{7,0},{16,23},{17,16},{1... | collective-permute-start | bytes 2654216 | tf_op jit(solution)/shard_map/ppermute | solution.py:253
  48.9 28.9 %copy-start = (bf16[3,3,3,32,512]{4,3,2,1,0:T(8,128)(2,1)S(1)}, bf16[3,3,3,32,512]{4,3,2,1,0:T(8,128)(2,1)}, u32[]{:S(2)}) copy-start(bf16[3,3,3,32,512]{4,3,2,1,0:T(8,128)(2,1)} %param.9) | copy-start | bytes 2654212
  48.9 28.9 %copy-start.1 = (s32[4]{0:T(128)S(1)}, s32[4]{0:T(128)}, u32[]{:S(2)}) copy-start(s32[4]{0:T(128)} %lengths.7) | copy-start | bytes 52
  48.9 24.6 %all-to-all-start.2 = ((bf16[8,6,32,128]{3,2,1,0:T(8,128)(2,1)}), bf16[8,6,32,128]{3,2,1,0:T(8,128)(2,1)}, u32[]{:S(2)}, u32[]{:S(2)}) async-start(bf16[8,6,32,128]{3,2,1,0:T(8,128)(2,1)} %bitcast.2), calls=%async_computation.2 | async-start | bytes 786432 | tf_op jit(solution)/shard_map/all_to_all | solution.py:244
  54.0 23.9 %collective-permute-start.2 = (bf16[27,32,512]{2,1,0:T(8,128)(2,1)S(1)}, bf16[27,32,512]{2,1,0:T(8,128)(2,1)}, u32[]{:S(2)}, u32[]{:S(2)}) collective-permute-start(bf16[27,32,512]{2,1,0:T(8,128)(2,1)S(1)} %collective-permute-done.rest_1_), channel_id=1, source_target_pairs={{0,16},{16,0},{1,17},{17,1},{2,18},{18,2},{3,19},{19,3},{4,20},{20... | collective-permute-start | bytes 2654216 | tf_op jit(solution)/shard_map/ppermute | solution.py:258
  56.2 13.8 %collective-permute-start.6 = (bf16[27,16,512]{2,1,0:T(8,128)(2,1)S(1)}, bf16[27,16,512]{2,1,0:T(8,128)(2,1)S(1)}, u32[]{:S(2)}, u32[]{:S(2)}) collective-permute-start(bf16[27,16,512]{2,1,0:T(8,128)(2,1)S(1)} %constant_dynamic-slice_fusion), channel_id=1, source_target_pairs={{0,1},{1,2},{2,3},{3,4},{4,5},{5,6},{6,7},{7,0},{16,23},{17,16},{1... | collective-permute-start | bytes 1327112 | tf_op jit(solution)/shard_map/ppermute | solution.py:257
  61.1 16.7 %collective-permute-start.4 = (bf16[27,32,512]{2,1,0:T(8,128)(2,1)}, bf16[27,32,512]{2,1,0:T(8,128)(2,1)}, u32[]{:S(2)}, u32[]{:S(2)}) collective-permute-start(bf16[27,32,512]{2,1,0:T(8,128)(2,1)} %collective-permute-done.1.rest_3_), channel_id=1, source_target_pairs={{0,16},{16,0},{1,17},{17,1},{2,18},{18,2},{3,19},{19,3},{4,20},{20... | collective-permute-start | bytes 2654216 | tf_op jit(solution)/shard_map/ppermute | solution.py:258
  63.0 14.8 %collective-permute-start.5 = (bf16[27,32,512]{2,1,0:T(8,128)(2,1)S(1)}, bf16[27,32,512]{2,1,0:T(8,128)(2,1)}, u32[]{:S(2)}, u32[]{:S(2)}) collective-permute-start(bf16[27,32,512]{2,1,0:T(8,128)(2,1)S(1)} %collective-permute-done.3.rest_5_), channel_id=1, source_target_pairs={{0,16},{16,0},{1,17},{17,1},{2,18},{18,2},{3,19},{19,3},{4,20},{20... | collective-permute-start | bytes 2654216 | tf_op jit(solution)/shard_map/ppermute | solution.py:258
  70.0 7.8 %collective-permute-start.7 = (bf16[27,16,512]{2,1,0:T(8,128)(2,1)S(1)}, bf16[27,16,512]{2,1,0:T(8,128)(2,1)}, u32[]{:S(2)}, u32[]{:S(2)}) collective-permute-start(bf16[27,16,512]{2,1,0:T(8,128)(2,1)S(1)} %collective-permute-done.6.rest_7_), channel_id=1, source_target_pairs={{0,16},{16,0},{1,17},{17,1},{2,18},{18,2},{3,19},{19,3},{4,20},{20... | collective-permute-start | bytes 1327112 | tf_op jit(solution)/shard_map/ppermute | solution.py:258
  73.6 22.9 %all-to-all-start.1 = ((bf16[8,6,32,128]{3,2,1,0:T(8,128)(2,1)}), bf16[8,6,32,128]{3,2,1,0:T(8,128)(2,1)}, u32[]{:S(2)}, u32[]{:S(2)}) async-start(bf16[8,6,32,128]{3,2,1,0:T(8,128)(2,1)} %bitcast.1), calls=%async_computation.1 | async-start | bytes 786432 | tf_op jit(solution)/shard_map/all_to_all | solution.py:244
  81.9 6.6 %collective-permute-start.8 = (f32[128,512]{1,0:T(8,128)S(1)}, f32[128,512]{1,0:T(8,128)S(1)}, u32[]{:S(2)}, u32[]{:S(2)}) collective-permute-start(f32[128,512]{1,0:T(8,128)S(1)} %get-tuple-element.25), channel_id=1, source_target_pairs={{0,16},{16,32},{32,48},{48,64},{64,80},{80,96},{96,112},{112,128},... | collective-permute-start | bytes 786440 | tf_op jit(solution)/shard_map/ppermute | solution.py:309
  88.5 17.1 %collective-permute-start.9 = (f32[128,512]{1,0:T(8,128)S(1)}, f32[128,512]{1,0:T(8,128)}, u32[]{:S(2)}, u32[]{:S(2)}) collective-permute-start(f32[128,512]{1,0:T(8,128)S(1)} %add.10), channel_id=1, source_target_pairs={{0,8},{8,0},{1,9},{9,1},{2,10},{10,2},{3,11},{11,3},{4,12},{12,4},... | collective-permute-start | bytes 786440 | tf_op jit(solution)/shard_map/ppermute | solution.py:312
  100.5 47.0 %copy-start.2 = (f32[512]{0:T(512)S(1)}, f32[512]{0:T(512)}, u32[]{:S(2)}) copy-start(f32[512]{0:T(512)} %param.10) | copy-start | bytes 6148
  100.5 47.0 %copy-start.3 = (f32[512]{0:T(512)S(1)}, f32[512]{0:T(512)}, u32[]{:S(2)}) copy-start(f32[512]{0:T(512)} %param.11) | copy-start | bytes 6148
  100.5 8.0 %collective-permute-start.10 = (f32[128,512]{1,0:T(8,128)S(1)}, f32[128,512]{1,0:T(8,128)S(1)}, u32[]{:S(2)}, u32[]{:S(2)}) collective-permute-start(f32[128,512]{1,0:T(8,128)S(1)} %get-tuple-element.26), channel_id=1, source_target_pairs={{0,16},{16,32},{32,48},{48,64},{64,80},{80,96},{96,112},{112,128},... | collective-permute-start | bytes 786440 | tf_op jit(solution)/shard_map/ppermute | solution.py:311

commit v15 on v11

--- a/solution.py
+++ b/solution.py
@@ -304,8 +304,9 @@
     weights += [moved[4], swapped[3]]
     onward = [(i, i + 1) for i in range(SLABS - 1)]
     far = shuffle(far.reshape(NY, 6, CH_DEV, 128), "y")
+    far, far_after = convolve(clip_lengths, far, weights)
+    near, far_after = lax.optimization_barrier((near, far_after))
     near = shuffle(near.reshape(NY, 6, CH_DEV, 128), "y")
-    far, far_after = convolve(clip_lengths, far, weights)
     far_before = lax.ppermute(far_after, TM, onward)
     near, near_after = convolve(clip_lengths, near, weights)
     near_before = lax.ppermute(near_after, TM, onward)

time: 149 us -> 166 us (1.11)
  starting transfers between devices: 62.9 us -> 71 us
  local copies, waits for them, and re-layouts: 0.06 us -> 5.21 us
  waiting for transfers between devices: 31.2 us -> 34.5 us
    ppermute x4, starting transfers between devices: 10.1 us -> 18.2 us  [gathered_weights(): lax.ppermute(shard, 'co', swap)]
    ppermute x1, waiting for transfers between devices: 4.58 us -> 0.01 us  [gathered_weights(): moved.append(lax.ppermute(half, ('co', 'y'), ring))]
    unnamed x8 -> x22, local copies, waits for them, and re-layouts: 0.03 us -> 4.4 us
    ppermute x3, waiting for transfers between devices: 11.2 us -> 15.2 us  [gathered_weights(): moved.append(lax.ppermute(moved[-1], ('co', 'y'), ring))]
    all_to_all x3, waiting for transfers between devices: 9.78 us -> 12.4 us  [shuffle(): return lax.all_to_all(x, axis, split_axis=0, concat_axis=0, tiled=True)]
    ppermute x1, starting transfers between devices: 7.94 us -> 10.1 us  [body(): far = lax.ppermute(far + far_before, 'zh', [(0, 1), (1, 0)])]
  transfers between devices with their start and end apart: 14 -> 14, of which waited for: 6 -> 5; matrix products, arithmetic and copies ran while one was open for 1% -> 1% of each run, Pallas kernels for 9% -> 6%
where the time goes in v15:
time: 166 us; the launch traced here: 165 us
  starting transfers between devices  71 us (43%)
  blocking collectives  36.6 us (22%)
  waiting for transfers between devices  34.5 us (21%)
  Pallas kernels  16.7 us (10%)
  local copies, waits for them, and re-layouts  5.21 us (3%)
    all_to_all x2, blocking collectives, shuffle(): return lax.all_to_all(x, axis, split_axis=0, concat_axis=0, tiled=True)  36.6 us
    all_to_all x3, starting transfers between devices, shuffle(): return lax.all_to_all(x, axis, split_axis=0, concat_axis=0, tiled=True)  18.5 us
    ppermute x4, starting transfers between devices, gathered_weights(): lax.ppermute(shard, 'co', swap)  18.2 us
    ppermute x3, waiting for transfers between devices, gathered_weights(): moved.append(lax.ppermute(moved[-1], ('co', 'y'), ring))  15.2 us
    ppermute x3, starting transfers between devices, gathered_weights(): moved.append(lax.ppermute(moved[-1], ('co', 'y'), ring))  12.8 us
    all_to_all x3, waiting for transfers between devices, shuffle(): return lax.all_to_all(x, axis, split_axis=0, concat_axis=0, tiled=True)  12.4 us
    ppermute x1, starting transfers between devices, body(): far = lax.ppermute(far + far_before, 'zh', [(0, 1), (1, 0)])  10.1 us
    pallas_call x2, Pallas kernels, convolve(): pl.pallas_call(conv_kernel, out_shape=[jax.ShapeDtypeStruct((128, COUT),...  7.65 us
  transfers between devices with their start and end apart: 14, of which 5 were waited for; matrix products, arithmetic and copies ran while one was open for 1% of the time, Pallas kernels for 6%

profile of v15, /device:TPU:1, one launch (start us, length us, event | category | flops | bytes accessed | tf_op | source)
XLA Modules:
  0.0 165.0 jit_solution(2499461675313138236)
XLA Ops:
  0.0 5.9 %collective-permute-start = (bf16[27,32,512]{2,1,0:T(8,128)(2,1)}, bf16[27,32,512]{2,1,0:T(8,128)(2,1)}, u32[]{:S(2)}, u32[]{:S(2)}) collective-permute-start(bf16[27,32,512]{2,1,0:T(8,128)(2,1)} %bitcast.6), channel_id=1, source_target_pairs={{0,1},{1,2},{2,3},{3,4},{4,5},{5,6},{6,7},{7,0},{16,23},{17,16},{1... | collective-permute-start | bytes 2654216 | tf_op jit(solution)/shard_map/ppermute | solution.py:253
  5.9 3.1 %shard_map.64 = bf16[32,136,128]{2,1,0:T(8,128)(2,1)} custom-call(s32[64]{0:T(128)} %target.1, bf16[64,32,128]{2,1,0:T(8,128)(2,1)} %arrived.1), custom_call_target="tpu_custom_call" | custom-call | tf_op jit(solution)/shard_map/pallas_call | solution.py:275
  9.1 10.0 %all-to-all-start = ((bf16[32,136,128]{2,1,0:T(8,128)(2,1)}), bf16[32,136,128]{2,1,0:T(8,128)(2,1)S(1)}, u32[]{:S(2)}, u32[]{:S(2)}) async-start(bf16[32,136,128]{2,1,0:T(8,128)(2,1)} %shard_map.64), calls=%async_computation | async-start | bytes 2228224 | tf_op jit(solution)/shard_map/all_to_all | solution.py:244
  19.1 0.0 collective-permute-done.rest_1_
  19.1 3.0 %collective-permute-start.1 = (bf16[27,32,512]{2,1,0:T(8,128)(2,1)}, bf16[27,32,512]{2,1,0:T(8,128)(2,1)S(1)}, u32[]{:S(2)}, u32[]{:S(2)}) collective-permute-start(bf16[27,32,512]{2,1,0:T(8,128)(2,1)} %collective-permute-done.rest_1_), channel_id=1, source_target_pairs={{0,1},{1,2},{2,3},{3,4},{4,5},{5,6},{6,7},{7,0},{16,23},{17,16},{1... | collective-permute-start | bytes 2654216 | tf_op jit(solution)/shard_map/ppermute | solution.py:253
  22.1 11.3 %collective-permute-done.1.rest_3_ = bf16[27,32,512]{2,1,0:T(8,128)(2,1)S(1)} collective-permute-done((bf16[27,32,512]{2,1,0:T(8,128)(2,1)}, bf16[27,32,512]{2,1,0:T(8,128)(2,1)S(1)}, u32[]{:S(2)}, u32[]{:S(2)}) %collective-permute-start.1) | collective-permute-done | bytes 884768 | tf_op jit(solution)/shard_map/ppermute | solution.py:253
  33.4 0.0 copy-start.1
  33.4 3.9 %collective-permute-start.3 = (bf16[27,32,512]{2,1,0:T(8,128)(2,1)S(1)}, bf16[27,32,512]{2,1,0:T(8,128)(2,1)S(1)}, u32[]{:S(2)}, u32[]{:S(2)}) collective-permute-start(bf16[27,32,512]{2,1,0:T(8,128)(2,1)S(1)} %collective-permute-done.1.rest_3_), channel_id=1, source_target_pairs={{0,1},{1,2},{2,3},{3,4},{4,5},{5,6},{6,7},{7,0},{16,23},{17,16},{1... | collective-permute-start | bytes 2654216 | tf_op jit(solution)/shard_map/ppermute | solution.py:253
  37.3 6.2 %collective-permute-start.2 = (bf16[27,32,512]{2,1,0:T(8,128)(2,1)}, bf16[27,32,512]{2,1,0:T(8,128)(2,1)}, u32[]{:S(2)}, u32[]{:S(2)}) collective-permute-start(bf16[27,32,512]{2,1,0:T(8,128)(2,1)} %collective-permute-done.rest_1_), channel_id=1, source_target_pairs={{0,16},{16,0},{1,17},{17,1},{2,18},{18,2},{3,19},{19,3},{4,20},{20... | collective-permute-start | bytes 2654216 | tf_op jit(solution)/shard_map/ppermute | solution.py:258
  43.5 3.9 %collective-permute-done.3.rest_5_ = bf16[27,32,512]{2,1,0:T(8,128)(2,1)S(1)} collective-permute-done((bf16[27,32,512]{2,1,0:T(8,128)(2,1)S(1)}, bf16[27,32,512]{2,1,0:T(8,128)(2,1)S(1)}, u32[]{:S(2)}, u32[]{:S(2)}) %collective-permute-start.3) | collective-permute-done | bytes 884768 | tf_op jit(solution)/shard_map/ppermute | solution.py:253
  47.4 0.0 copy-done.1
  47.5 0.8 constant_dynamic-slice_fusion
  48.3 0.0 copy-start
  48.3 0.0 copy-start.7
  48.3 4.9 %collective-permute-start.6 = (bf16[27,16,512]{2,1,0:T(8,128)(2,1)}, bf16[27,16,512]{2,1,0:T(8,128)(2,1)S(1)}, u32[]{:S(2)}, u32[]{:S(2)}) collective-permute-start(bf16[27,16,512]{2,1,0:T(8,128)(2,1)} %constant_dynamic-slice_fusion), channel_id=1, source_target_pairs={{0,1},{1,2},{2,3},{3,4},{4,5},{5,6},{6,7},{7,0},{16,23},{17,16},{1... | collective-permute-start | bytes 1327112 | tf_op jit(solution)/shard_map/ppermute | solution.py:257
  53.2 7.4 %collective-permute-start.4 = (bf16[27,32,512]{2,1,0:T(8,128)(2,1)}, bf16[27,32,512]{2,1,0:T(8,128)(2,1)}, u32[]{:S(2)}, u32[]{:S(2)}) collective-permute-start(bf16[27,32,512]{2,1,0:T(8,128)(2,1)} %copy-done.1), channel_id=1, source_target_pairs={{0,16},{16,0},{1,17},{17,1},{2,18},{18,2},{3,19},{19,3},{4,20},{20... | collective-permute-start | bytes 2654216 | tf_op jit(solution)/shard_map/ppermute | solution.py:258
  60.6 1.9 %collective-permute-start.5 = (bf16[27,32,512]{2,1,0:T(8,128)(2,1)S(1)}, bf16[27,32,512]{2,1,0:T(8,128)(2,1)}, u32[]{:S(2)}, u32[]{:S(2)}) collective-permute-start(bf16[27,32,512]{2,1,0:T(8,128)(2,1)S(1)} %collective-permute-done.3.rest_5_), channel_id=1, source_target_pairs={{0,16},{16,0},{1,17},{17,1},{2,18},{18,2},{3,19},{19,3},{4,20},{20... | collective-permute-start | bytes 2654216 | tf_op jit(solution)/shard_map/ppermute | solution.py:258
  62.5 0.0 all-to-all-done.got
  62.5 2.1 %shard_map.65 = (bf16[48,32,128]{2,1,0:T(8,128)(2,1)S(1)}, bf16[48,32,128]{2,1,0:T(8,128)(2,1)}) custom-call(bf16[32,136,128]{2,1,0:T(8,128)(2,1)S(1)} %all-to-all-done.got), custom_call_target="tpu_custom_call" | custom-call | tf_op jit(solution)/shard_map/pallas_call | solution.py:290
  64.6 0.0 copy-start.6
  64.6 0.7 copy-done.6
  65.4 4.2 %all-to-all-start.1 = ((bf16[8,6,32,128]{3,2,1,0:T(8,128)(2,1)}), bf16[8,6,32,128]{3,2,1,0:T(8,128)(2,1)S(1)}, u32[]{:S(2)}, u32[]{:S(2)}) async-start(bf16[8,6,32,128]{3,2,1,0:T(8,128)(2,1)} %bitcast.9), calls=%async_computation.1 | async-start | bytes 786432 | tf_op jit(solution)/shard_map/all_to_all | solution.py:244
  69.6 0.0 collective-permute-done.6.rest_7_
  69.6 2.7 %collective-permute-start.7 = (bf16[27,16,512]{2,1,0:T(8,128)(2,1)S(1)}, bf16[27,16,512]{2,1,0:T(8,128)(2,1)S(1)}, u32[]{:S(2)}, u32[]{:S(2)}) collective-permute-start(bf16[27,16,512]{2,1,0:T(8,128)(2,1)S(1)} %collective-permute-done.6.rest_7_), channel_id=1, source_target_pairs={{0,16},{16,0},{1,17},{17,1},{2,18},{18,2},{3,19},{19,3},{4,20},{20... | collective-permute-start | bytes 1327112 | tf_op jit(solution)/shard_map/ppermute | solution.py:258
  72.3 0.0 collective-permute-done.2.rest_2_
  72.3 12.4 %all-to-all-done.1.frames = bf16[8,6,32,128]{3,2,1,0:T(8,128)(2,1)S(1)} async-done(((bf16[8,6,32,128]{3,2,1,0:T(8,128)(2,1)}), bf16[8,6,32,128]{3,2,1,0:T(8,128)(2,1)S(1)}, u32[]{:S(2)}, u32[]{:S(2)}) %all-to-all-start.1) | async-done | bytes 393248 | tf_op jit(solution)/shard_map/all_to_all | solution.py:244
  84.7 0.0 collective-permute-done.7.rest_8_
  84.7 0.0 collective-permute-done.4.rest_4_
  84.7 0.0 collective-permute-done.5.rest_6_
  84.7 0.0 copy-done
  84.7 0.0 copy-done.7
  84.7 0.0 copy-start.2
  84.7 1.2 copy-done.2
  85.9 3.8 %shard_map.66 = (f32[128,512]{1,0:T(8,128)S(1)}, f32[128,512]{1,0:T(8,128)S(1)}) custom-call(s32[4]{0:T(128)S(1)} %copy-done.7, bf16[8,6,32,128]{3,2,1,0:T(8,128)(2,1)S(1)} %all-to-all-done.1.frames, bf16[27,32,512]{2,1,0:T(8,128)(2,1)S(1)} %bitcast.7, bf16[27,32,512]{2,1,0:T(8,128)(2,1)} %collective-permute-done.rest_1_, ...), custom_call_target="tpu_custom_call" | custom-call | tf_op jit(solution)/shard_map/pallas_call | solution.py:263
  89.6 0.0 copy-start.4
  89.7 0.7 copy-done.4
  90.4 0.0 copy-start.10
  90.4 0.7 copy-done.10
  91.1 0.0 copy-start.3
  91.1 4.2 %all-to-all-start.2 = ((bf16[8,6,32,128]{3,2,1,0:T(8,128)(2,1)}), bf16[8,6,32,128]{3,2,1,0:T(8,128)(2,1)}, u32[]{:S(2)}, u32[]{:S(2)}) async-start(bf16[8,6,32,128]{3,2,1,0:T(8,128)(2,1)} %bitcast.2), calls=%async_computation.2 | async-start | bytes 786432 | tf_op jit(solution)/shard_map/all_to_all | solution.py:244
  95.4 1.9 %collective-permute-start.8 = (f32[128,512]{1,0:T(8,128)}, f32[128,512]{1,0:T(8,128)S(1)}, u32[]{:S(2)}, u32[]{:S(2)}) collective-permute-start(f32[128,512]{1,0:T(8,128)} %copy-done.10), channel_id=1, source_target_pairs={{0,16},{16,32},{32,48},{48,64},{64,80},{80,96},{96,112},{112,128},... | collective-permute-start | bytes 786440 | tf_op jit(solution)/shard_map/ppermute | solution.py:310
  97.3 3.6 %collective-permute-done.8 = f32[128,512]{1,0:T(8,128)S(1)} collective-permute-done((f32[128,512]{1,0:T(8,128)}, f32[128,512]{1,0:T(8,128)S(1)}, u32[]{:S(2)}, u32[]{:S(2)}) %collective-permute-start.8) | collective-permute-done | bytes 262176 | tf_op jit(solution)/shard_map/ppermute | solution.py:310
  100.9 0.8 add.10
  101.6 10.1 %collective-permute-start.9 = (f32[128,512]{1,0:T(8,128)}, f32[128,512]{1,0:T(8,128)S(1)}, u32[]{:S(2)}, u32[]{:S(2)}) collective-permute-start(f32[128,512]{1,0:T(8,128)} %add.10), channel_id=1, source_target_pairs={{0,8},{8,0},{1,9},{9,1},{2,10},{10,2},{3,11},{11,3},{4,12},{12,4},... | collective-permute-start | bytes 786440 | tf_op jit(solution)/shard_map/ppermute | solution.py:313
  111.7 0.0 all-to-all-done.2.frames
  111.7 0.0 copy-done.3
  111.7 0.0 copy-start.5
  111.8 1.0 copy-done.5
  112.8 3.9 %shard_map.67 = (f32[128,512]{1,0:T(8,128)S(1)}, f32[128,512]{1,0:T(8,128)S(1)}) custom-call(s32[4]{0:T(128)S(1)} %copy-done.7, bf16[8,6,32,128]{3,2,1,0:T(8,128)(2,1)} %all-to-all-done.2.frames, bf16[27,32,512]{2,1,0:T(8,128)(2,1)S(1)} %bitcast.8, bf16[27,32,512]{2,1,0:T(8,128)(2,1)} %collective-permute-done.rest_1_, ...), custom_call_target="tpu_custom_call" | custom-call | tf_op jit(solution)/shard_map/pallas_call | solution.py:263
  116.6 0.0 copy-start.8
  116.7 0.0 copy-start.9
  116.7 4.6 %collective-permute-start.10 = (f32[128,512]{1,0:T(8,128)S(1)}, f32[128,512]{1,0:T(8,128)S(1)}, u32[]{:S(2)}, u32[]{:S(2)}) collective-permute-start(f32[128,512]{1,0:T(8,128)S(1)} %get-tuple-element.30), channel_id=1, source_target_pairs={{0,16},{16,32},{32,48},{48,64},{64,80},{80,96},{96,112},{112,128},... | collective-permute-start | bytes 786440 | tf_op jit(solution)/shard_map/ppermute | solution.py:312
  121.2 0.0 collective-permute-done.9
  121.3 3.2 %collective-permute-done.10.before = f32[128,512]{1,0:T(8,128)S(1)} collective-permute-done((f32[128,512]{1,0:T(8,128)S(1)}, f32[128,512]{1,0:T(8,128)S(1)}, u32[]{:S(2)}, u32[]{:S(2)}) %collective-permute-start.10) | collective-permute-done | bytes 262176 | tf_op jit(solution)/shard_map/ppermute | solution.py:312
  124.5 0.9 shard_map.68
  125.4 14.9 %all_to_all.25.got = f32[16,8,128]{2,1,0:T(8,128)} all-to-all(f32[16,8,128]{2,1,0:T(8,128)S(1)} %get-tuple-element.31), channel_id=1, replica_groups=mesh['zl'=4,'x'=4,'co'=2,'zh'=2,'y'=8] {'y','co'}, dimensions={0} | all-to-all | bytes 131072 | tf_op jit(solution)/shard_map/all_to_all | solution.py:244
  140.3 1.5 shard_map.69
  141.9 21.7 %all_to_all.26.got = f32[32,8,128]{2,1,0:T(8,128)S(1)} all-to-all(f32[32,8,128]{2,1,0:T(8,128)} %shard_map.69), channel_id=1, replica_groups=mesh['zl'=4,'x'=4,'co'=2,'zh'=2,'y'=8] {'zl','zh','x'}, dimensions={0} | all-to-all | bytes 262144 | tf_op jit(solution)/shard_map/all_to_all | solution.py:244
  163.5 0.0 copy-done.8
  163.5 0.0 copy-done.9
  163.5 1.5 shard_map.70
  (1 shorter events, 0.0 us)
Async XLA Ops:
  0.0 19.1 %collective-permute-start = (bf16[27,32,512]{2,1,0:T(8,128)(2,1)}, bf16[27,32,512]{2,1,0:T(8,128)(2,1)}, u32[]{:S(2)}, u32[]{:S(2)}) collective-permute-start(bf16[27,32,512]{2,1,0:T(8,128)(2,1)} %bitcast.6), channel_id=1, source_target_pairs={{0,1},{1,2},{2,3},{3,4},{4,5},{5,6},{6,7},{7,0},{16,23},{17,16},{1... | collective-permute-start | bytes 2654216 | tf_op jit(solution)/shard_map/ppermute | solution.py:253
  9.1 53.5 %all-to-all-start = ((bf16[32,136,128]{2,1,0:T(8,128)(2,1)}), bf16[32,136,128]{2,1,0:T(8,128)(2,1)S(1)}, u32[]{:S(2)}, u32[]{:S(2)}) async-start(bf16[32,136,128]{2,1,0:T(8,128)(2,1)} %shard_map.64), calls=%async_computation | async-start | bytes 2228224 | tf_op jit(solution)/shard_map/all_to_all | solution.py:244
  19.1 14.3 %collective-permute-start.1 = (bf16[27,32,512]{2,1,0:T(8,128)(2,1)}, bf16[27,32,512]{2,1,0:T(8,128)(2,1)S(1)}, u32[]{:S(2)}, u32[]{:S(2)}) collective-permute-start(bf16[27,32,512]{2,1,0:T(8,128)(2,1)} %collective-permute-done.rest_1_), channel_id=1, source_target_pairs={{0,1},{1,2},{2,3},{3,4},{4,5},{5,6},{6,7},{7,0},{16,23},{17,16},{1... | collective-permute-start | bytes 2654216 | tf_op jit(solution)/shard_map/ppermute | solution.py:253
  33.4 14.1 %copy-start.1 = (bf16[27,32,512]{2,1,0:T(8,128)(2,1)}, bf16[27,32,512]{2,1,0:T(8,128)(2,1)S(1)}, u32[]{:S(2)}) copy-start(bf16[27,32,512]{2,1,0:T(8,128)(2,1)S(1)} %collective-permute-done.1.rest_3_) | copy-start | bytes 2654212
  33.4 14.1 %collective-permute-start.3 = (bf16[27,32,512]{2,1,0:T(8,128)(2,1)S(1)}, bf16[27,32,512]{2,1,0:T(8,128)(2,1)S(1)}, u32[]{:S(2)}, u32[]{:S(2)}) collective-permute-start(bf16[27,32,512]{2,1,0:T(8,128)(2,1)S(1)} %collective-permute-done.1.rest_3_), channel_id=1, source_target_pairs={{0,1},{1,2},{2,3},{3,4},{4,5},{5,6},{6,7},{7,0},{16,23},{17,16},{1... | collective-permute-start | bytes 2654216 | tf_op jit(solution)/shard_map/ppermute | solution.py:253
  37.3 35.0 %collective-permute-start.2 = (bf16[27,32,512]{2,1,0:T(8,128)(2,1)}, bf16[27,32,512]{2,1,0:T(8,128)(2,1)}, u32[]{:S(2)}, u32[]{:S(2)}) collective-permute-start(bf16[27,32,512]{2,1,0:T(8,128)(2,1)} %collective-permute-done.rest_1_), channel_id=1, source_target_pairs={{0,16},{16,0},{1,17},{17,1},{2,18},{18,2},{3,19},{19,3},{4,20},{20... | collective-permute-start | bytes 2654216 | tf_op jit(solution)/shard_map/ppermute | solution.py:258
  48.3 36.4 %copy-start = (bf16[3,3,3,32,512]{4,3,2,1,0:T(8,128)(2,1)S(1)}, bf16[3,3,3,32,512]{4,3,2,1,0:T(8,128)(2,1)}, u32[]{:S(2)}) copy-start(bf16[3,3,3,32,512]{4,3,2,1,0:T(8,128)(2,1)} %param.9) | copy-start | bytes 2654212
  48.3 36.4 %copy-start.7 = (s32[4]{0:T(128)S(1)}, s32[4]{0:T(128)}, u32[]{:S(2)}) copy-start(s32[4]{0:T(128)} %lengths.7) | copy-start | bytes 52
  48.3 21.3 %collective-permute-start.6 = (bf16[27,16,512]{2,1,0:T(8,128)(2,1)}, bf16[27,16,512]{2,1,0:T(8,128)(2,1)S(1)}, u32[]{:S(2)}, u32[]{:S(2)}) collective-permute-start(bf16[27,16,512]{2,1,0:T(8,128)(2,1)} %constant_dynamic-slice_fusion), channel_id=1, source_target_pairs={{0,1},{1,2},{2,3},{3,4},{4,5},{5,6},{6,7},{7,0},{16,23},{17,16},{1... | collective-permute-start | bytes 1327112 | tf_op jit(solution)/shard_map/ppermute | solution.py:257
  53.2 31.5 %collective-permute-start.4 = (bf16[27,32,512]{2,1,0:T(8,128)(2,1)}, bf16[27,32,512]{2,1,0:T(8,128)(2,1)}, u32[]{:S(2)}, u32[]{:S(2)}) collective-permute-start(bf16[27,32,512]{2,1,0:T(8,128)(2,1)} %copy-done.1), channel_id=1, source_target_pairs={{0,16},{16,0},{1,17},{17,1},{2,18},{18,2},{3,19},{19,3},{4,20},{20... | collective-permute-start | bytes 2654216 | tf_op jit(solution)/shard_map/ppermute | solution.py:258
  60.6 24.1 %collective-permute-start.5 = (bf16[27,32,512]{2,1,0:T(8,128)(2,1)S(1)}, bf16[27,32,512]{2,1,0:T(8,128)(2,1)}, u32[]{:S(2)}, u32[]{:S(2)}) collective-permute-start(bf16[27,32,512]{2,1,0:T(8,128)(2,1)S(1)} %collective-permute-done.3.rest_5_), channel_id=1, source_target_pairs={{0,16},{16,0},{1,17},{17,1},{2,18},{18,2},{3,19},{19,3},{4,20},{20... | collective-permute-start | bytes 2654216 | tf_op jit(solution)/shard_map/ppermute | solution.py:258
  64.6 0.8 copy-start.6
  65.4 19.3 %all-to-all-start.1 = ((bf16[8,6,32,128]{3,2,1,0:T(8,128)(2,1)}), bf16[8,6,32,128]{3,2,1,0:T(8,128)(2,1)S(1)}, u32[]{:S(2)}, u32[]{:S(2)}) async-start(bf16[8,6,32,128]{3,2,1,0:T(8,128)(2,1)} %bitcast.9), calls=%async_computation.1 | async-start | bytes 786432 | tf_op jit(solution)/shard_map/all_to_all | solution.py:244
  69.6 15.1 %collective-permute-start.7 = (bf16[27,16,512]{2,1,0:T(8,128)(2,1)S(1)}, bf16[27,16,512]{2,1,0:T(8,128)(2,1)S(1)}, u32[]{:S(2)}, u32[]{:S(2)}) collective-permute-start(bf16[27,16,512]{2,1,0:T(8,128)(2,1)S(1)} %collective-permute-done.6.rest_7_), channel_id=1, source_target_pairs={{0,16},{16,0},{1,17},{17,1},{2,18},{18,2},{3,19},{19,3},{4,20},{20... | collective-permute-start | bytes 1327112 | tf_op jit(solution)/shard_map/ppermute | solution.py:258
  84.7 1.2 copy-start.2
  89.6 0.8 copy-start.4
  90.4 0.7 copy-start.10
  91.1 20.6 %copy-start.3 = (bf16[27,32,512]{2,1,0:T(8,128)(2,1)S(1)}, bf16[27,32,512]{2,1,0:T(8,128)(2,1)}, u32[]{:S(2)}) copy-start(bf16[27,32,512]{2,1,0:T(8,128)(2,1)} %copy-done.1) | copy-start | bytes 2654212
  91.1 20.6 %all-to-all-start.2 = ((bf16[8,6,32,128]{3,2,1,0:T(8,128)(2,1)}), bf16[8,6,32,128]{3,2,1,0:T(8,128)(2,1)}, u32[]{:S(2)}, u32[]{:S(2)}) async-start(bf16[8,6,32,128]{3,2,1,0:T(8,128)(2,1)} %bitcast.2), calls=%async_computation.2 | async-start | bytes 786432 | tf_op jit(solution)/shard_map/all_to_all | solution.py:244
  95.4 5.5 %collective-permute-start.8 = (f32[128,512]{1,0:T(8,128)}, f32[128,512]{1,0:T(8,128)S(1)}, u32[]{:S(2)}, u32[]{:S(2)}) collective-permute-start(f32[128,512]{1,0:T(8,128)} %copy-done.10), channel_id=1, source_target_pairs={{0,16},{16,32},{32,48},{48,64},{64,80},{80,96},{96,112},{112,128},... | collective-permute-start | bytes 786440 | tf_op jit(solution)/shard_map/ppermute | solution.py:310
  101.6 19.6 %collective-permute-start.9 = (f32[128,512]{1,0:T(8,128)}, f32[128,512]{1,0:T(8,128)S(1)}, u32[]{:S(2)}, u32[]{:S(2)}) collective-permute-start(f32[128,512]{1,0:T(8,128)} %add.10), channel_id=1, source_target_pairs={{0,8},{8,0},{1,9},{9,1},{2,10},{10,2},{3,11},{11,3},{4,12},{12,4},... | collective-permute-start | bytes 786440 | tf_op jit(solution)/shard_map/ppermute | solution.py:313
  111.7 1.0 copy-start.5
  116.6 46.9 %copy-start.8 = (f32[512]{0:T(512)S(1)}, f32[512]{0:T(512)}, u32[]{:S(2)}) copy-start(f32[512]{0:T(512)} %param.10) | copy-start | bytes 6148
  116.7 46.9 %copy-start.9 = (f32[512]{0:T(512)S(1)}, f32[512]{0:T(512)}, u32[]{:S(2)}) copy-start(f32[512]{0:T(512)} %param.11) | copy-start | bytes 6148
  116.7 7.9 %collective-permute-start.10 = (f32[128,512]{1,0:T(8,128)S(1)}, f32[128,512]{1,0:T(8,128)S(1)}, u32[]{:S(2)}, u32[]{:S(2)}) collective-permute-start(f32[128,512]{1,0:T(8,128)S(1)} %get-tuple-element.30), channel_id=1, source_target_pairs={{0,16},{16,32},{32,48},{48,64},{64,80},{80,96},{96,112},{112,128},... | collective-permute-start | bytes 786440 | tf_op jit(solution)/shard_map/ppermute | solution.py:312
